TPU v7x, 32 devices: a whole 2x2x4 slice. The times are simulated.
32 devices in a mesh: groups: 2 (over y), req: 4 (over z), tensor: 4 (over x, core).
Axes of the slice: x: 2, y: 2, z: 4, core: 2. Of those that a mesh axis runs over, the one named last changes fastest.
Arguments:
- tokens: bfloat16 [2048, 5120], P(('groups', 'req')), parts along dimension 0, may hold values from -6 to 6
- w_x: bfloat16 [5120, 4096], P('req', 'tensor'), may hold values from -0.078125 to 0.078125
- w_bc: bfloat16 [5120, 256], P('req'), may hold values from -0.0078125 to 0.0078125
- w_dt: bfloat16 [5120, 64], P('req', 'tensor'), may hold values from -0.078125 to 0.078125
- dt_bias: float32 [64], P('tensor'), may hold values from -2 to 0.5
- decay_rate: float32 [64], P('tensor'), may hold values from 0.004 to 1
- skip_gain: float32 [64], P('tensor'), may hold values from 0.3 to 1.5
- w_out: bfloat16 [4096, 5120], P('tensor', 'req'), may hold values from -0.09375 to 0.09375
- suffix_lengths: int32 [8, 8], P(('groups', 'req')), parts along dimension 0, may hold values from 1 to 96, 256 in all within a row
- checkpoint_slot: int32 [64], P('groups'), parts along dimension 0, may hold values from 0 to 47, as said below
- cache: float32 [96, 64, 64, 128], P(('groups', 'req'), 'tensor'), parts along dimension 0, may hold values from -6 to 6
Outputs:
- layer_out: bfloat16 [2048, 5120], P(('groups', 'req'), 'tensor'), parts along dimension 0
- new_cache: float32 [96, 64, 64, 128], P(('groups', 'req'), 'tensor'), parts along dimension 0
There are 2 independent parts, one for each index of `groups`. A program takes and returns all parts, laid end to end along the dimension named above; an argument that names none is the same for every part. Nothing has to cross between parts.
Inputs may be any that keep to these rules, and one draw needn't show every extreme that they name: `checkpoint_slot`: entries are distinct. Slot k lies on req index k // 12. At most 3 requests of one req index have their checkpoints on one req index, and this is reached in every draw; some req index has all its 12 slots in use. `suffix_lengths`: each row sums to 256.
All inputs are finite; a program needn't handle non-finite values.
Results may differ from a plain program's by a relative error of at most 0.013.
Values may be sent and summed in bfloat16 or wider, within the bound.
No kernel may reach another device: no remote copies, remote signals or barrier semaphores. Data moves between devices by JAX's collectives and lax.ppermute only.
A program may use at most 128 MiB of HBM per device.

v0:
```python
import jax
import jax.numpy as jnp
from jax import lax
from jax.sharding import PartitionSpec as P

HIGH = lax.Precision.HIGHEST


def suffix_scan(inputs_ssm, state_maps, step_size, decay_rate, skip_gain, lengths, initial):
    num_tok = inputs_ssm.shape[0]
    state_dim = state_maps.shape[1] // 2
    head_count = step_size.shape[1]
    head_width = inputs_ssm.shape[1] // head_count
    places = jnp.arange(num_tok, dtype=jnp.int32)
    seg_end = jnp.cumsum(lengths)
    starts = seg_end - lengths
    member = ((places[:, None] >= starts[None, :]) & (places[:, None] < seg_end[None, :])).astype(
        jnp.float32
    )
    same_seg = jnp.dot(member, member.T, precision=HIGH)
    causal = same_seg * (places[:, None] >= places[None, :]).astype(jnp.float32)
    log_decay = -step_size * decay_rate[None, :]
    running = jnp.dot(causal, log_decay, precision=HIGH)
    totals = jnp.dot(member.T, log_decay, precision=HIGH)
    b_part = state_maps[:, :state_dim]
    c_part = state_maps[:, state_dim:]
    scores = jnp.dot(c_part, b_part.T, precision=HIGH)
    spread = jnp.minimum(running[:, None, :] - running[None, :, :], 0.0)
    mixing = (
        jnp.where(causal[:, :, None] > 0, jnp.exp(spread), 0.0)
        * scores[:, :, None]
        * step_size[None, :, :]
    )
    mixing = mixing.astype(jnp.bfloat16)
    values = inputs_ssm.reshape(num_tok, head_count, head_width)
    within = jnp.einsum("tsh,shp->thp", mixing, values, preferred_element_type=jnp.float32)
    from_cache = jnp.einsum("tn,rhpn->trhp", c_part, initial, precision=HIGH)
    carried = jnp.einsum("tr,trhp->thp", member, from_cache, precision=HIGH)
    values_f = values.astype(jnp.float32)
    outputs = within + jnp.exp(running)[:, :, None] * carried + skip_gain[None, :, None] * values_f
    weights = (
        jnp.where(
            member[:, :, None] > 0,
            jnp.exp(jnp.minimum(totals[None, :, :] - running[:, None, :], 0.0)),
            0.0,
        )
        * step_size[:, None, :]
    )
    scaled = weights[:, :, :, None] * values_f[:, None, :, :]
    increment = jnp.einsum("trhp,tn->rhpn", scaled, b_part, precision=HIGH)
    new_states = jnp.exp(totals)[:, :, None, None] * initial + increment
    return (outputs.astype(jnp.bfloat16).reshape(num_tok, head_count * head_width), new_states)


def body(
    tokens,
    w_x,
    w_bc,
    w_dt,
    dt_bias,
    decay_rate,
    skip_gain,
    w_out,
    suffix_lengths,
    checkpoint_slot,
    cache,
):
    blocks = (
        lax.all_gather(w_x, "req", axis=0, tiled=True),
        lax.all_gather(w_bc, "req", axis=0, tiled=True),
        lax.all_gather(w_dt, "req", axis=0, tiled=True),
    )
    proj_x, state_maps, raw_step = tuple(
        (jnp.dot(tokens, block_w, preferred_element_type=jnp.float32) for block_w in blocks)
    )
    inputs_ssm = proj_x.astype(jnp.bfloat16)
    step_size = jax.nn.softplus(raw_step + dt_bias[None, :])
    req_count = lax.axis_size("req")
    own_index = lax.axis_index("req")
    slots_dev = cache.shape[0]
    per_pair = (slots_dev + req_count - 1) // req_count
    total_reqs = checkpoint_slot.shape[0]
    req_dev = total_reqs // req_count
    holder = checkpoint_slot // slots_dev
    owner = jnp.arange(total_reqs, dtype=jnp.int32) // req_dev
    pair_key = holder * req_count + owner
    rank_in_pair = jnp.sum(
        (pair_key[:, None] == pair_key[None, :])
        & (checkpoint_slot[None, :] < checkpoint_slot[:, None]),
        axis=1,
    )
    slot_local = checkpoint_slot % slots_dev
    targets = jnp.arange(req_count, dtype=jnp.int32)[:, None, None]
    rank_slots = jnp.arange(per_pair, dtype=jnp.int32)[None, :, None]
    match_send = (
        (holder[None, None, :] == own_index)
        & (owner[None, None, :] == targets)
        & (rank_in_pair[None, None, :] == rank_slots)
    )
    send_used = jnp.any(match_send, axis=2).reshape(-1)
    send_slot = jnp.sum(jnp.where(match_send, slot_local[None, None, :], 0), axis=2).reshape(-1)
    outgoing = jnp.where(send_used[:, None, None, None], jnp.take(cache, send_slot, axis=0), 0.0)
    fetched = lax.all_to_all(
        outgoing.astype(jnp.bfloat16), "req", split_axis=0, concat_axis=0, tiled=True
    ).astype(outgoing.dtype)
    fetch_index = lax.dynamic_slice_in_dim(
        holder * per_pair + rank_in_pair, own_index * req_dev, req_dev
    )
    initial = jnp.take(fetched, fetch_index, axis=0)
    outputs, new_states = suffix_scan(
        inputs_ssm, state_maps, step_size, decay_rate, skip_gain, suffix_lengths[0], initial
    )
    partial_out = jnp.dot(
        outputs,
        lax.all_gather(w_out, "req", axis=1, tiled=True),
        preferred_element_type=jnp.float32,
    )
    layer_out = lax.psum_scatter(
        partial_out.astype(jnp.bfloat16), "tensor", scatter_dimension=1, tiled=True
    )
    holder_mine = lax.dynamic_slice_in_dim(holder, own_index * req_dev, req_dev)
    rank_mine = lax.dynamic_slice_in_dim(rank_in_pair, own_index * req_dev, req_dev)
    match_back = (holder_mine[None, None, :] == targets) & (rank_mine[None, None, :] == rank_slots)
    back_used = jnp.any(match_back, axis=2).reshape(-1)
    back_index = jnp.sum(
        jnp.where(match_back, jnp.arange(req_dev, dtype=jnp.int32)[None, None, :], 0), axis=2
    ).reshape(-1)
    returning = jnp.where(
        back_used[:, None, None, None], jnp.take(new_states, back_index, axis=0), 0.0
    )
    arrived = lax.all_to_all(
        returning.astype(jnp.bfloat16), "req", split_axis=0, concat_axis=0, tiled=True
    ).astype(returning.dtype)
    slot_ids = own_index * slots_dev + jnp.arange(slots_dev, dtype=jnp.int32)
    match_slot = checkpoint_slot[None, :] == slot_ids[:, None]
    slot_used = jnp.any(match_slot, axis=1)
    slot_source = jnp.sum(
        jnp.where(match_slot, (owner * per_pair + rank_in_pair)[None, :], 0), axis=1
    )
    new_cache = jnp.where(
        slot_used[:, None, None, None], jnp.take(arrived, slot_source, axis=0), cache
    )
    return (layer_out, new_cache)


def solution(mesh):
    placed = (
        P(("groups", "req"), None),
        P("req", "tensor"),
        P("req", None),
        P("req", "tensor"),
        P("tensor"),
        P("tensor"),
        P("tensor"),
        P("tensor", "req"),
        P(("groups", "req"), None),
        P("groups"),
        P(("groups", "req"), "tensor", None, None),
    )
    return jax.shard_map(
        body,
        mesh=mesh,
        in_specs=placed,
        out_specs=(P(("groups", "req"), "tensor"), P(("groups", "req"), "tensor", None, None)),
        check_vma=False,
    )
```

profile of v0, /device:TPU:0, one launch (start us, length us, event | category | flops | bytes accessed | tf_op | source)
XLA Modules:
  0.0 604.9 jit_solution(5794083958238240605)
XLA Ops:
  7.2 0.7 all-gather.6.cloned.1.call-update
  8.0 0.7 all-gather.4.cloned.1.call-update
  8.7 0.7 all-gather.8.cloned.1.call-update
  10.4 5.8 gather_fusion.2
  16.2 4.8 fusion.3
  21.0 6.6 %all-to-all-start = ((bf16[12,16,64,128]{3,2,1,0:T(8,128)(2,1)}), bf16[12,16,64,128]{3,2,1,0:T(8,128)(2,1)}, u32[]{:S(2)}, u32[]{:S(2)}) async-start(bf16[12,16,64,128]{3,2,1,0:T(8,128)(2,1)} %fusion.3), calls=%async_computation | async-start | bytes 6291456 | tf_op jit(solution)/shard_map/all_to_all | solution.py:103
  28.7 0.7 broadcast_in_dim.166
  29.4 121.0 %all_gather.13 = bf16[5120,16]{0,1:T(8,128)(2,1)S(1)} all-gather(bf16[1280,16]{0,1:T(8,128)(2,1)S(1)} %copy-done.6), channel_id=1, replica_groups=mesh['groups'=2,'req'=4,'tensor'=4] {'req'}, dimensions={0}, use_global_device_ids=true | all-gather | bytes 204800 | tf_op jit(solution)/shard_map/all_gather | solution.py:71
  151.1 0.6 pad_clamp_fusion.1
  152.2 0.8 compare_select_fusion
  153.1 0.8 fusion.51
  153.9 0.9 broadcast_compare_fusion
  154.8 0.9 fusion.50
  155.8 2.6 fusion.52
  158.4 1.1 fusion.26
  159.5 5.4 convert_element_type.46
  164.9 5.6 gather_fusion
  170.5 11.1 %fusion.6 = f32[256,8,16,64]{0,3,2,1:T(8,128)S(1)} fusion(f32[8,16,64,128]{3,2,1,0:T(8,128)} %gather_fusion, pred[8]{0:T(512)(128)(4,1)S(1)} %get-tuple-element.3, f32[256,256]{1,0:T(8,128)S(1)} %fusion.52), kind=kOutput, calls=%fused_computation.17 | convolution fusion | flops 3222274048 | bytes 12714496 | tf_op jit(solution)/shard_map/tn,rhpn->trhp/dot_general | solution.py:37
  181.6 2.3 fusion
  183.9 121.9 %all-gather.4.cloned.1.call-done = bf16[5120,1024]{1,0:T(8,128)(2,1)} async-done(((bf16[1280,1024]{1,0:T(8,128)(2,1)}), bf16[5120,1024]{1,0:T(8,128)(2,1)}) %all-gather.4.cloned.1.call-update) | async-done | bytes 10485776 | tf_op jit(solution)/shard_map/all_gather | solution.py:69
  305.8 6.8 %convolution_convert_fusion.1 = bf16[256,1024]{1,0:T(8,128)(2,1)S(1)} fusion(bf16[256,5120]{1,0:T(8,128)(2,1)S(1)} %copy-done, bf16[5120,1024]{1,0:T(8,128)(2,1)} %all-gather.4.cloned.1.call-done), kind=kOutput, calls=%fused_computation.31 | convolution fusion | flops 2684616704 | bytes 13631488 | tf_op jit(solution)/shard_map/dot_general | solution.py:74
  312.9 9.1 %multiply_add_fusion = bf16[8,16,64,128]{3,2,1,0:T(8,128)(2,1)S(1)} fusion(f32[8,16,64,128]{3,2,1,0:T(8,128)} %gather_fusion, f32[256,16,64]{0,2,1:T(8,128)S(1)} %convert_element_type.47, f32[256,8,16]{0,2,1:T(8,128)S(1)} %select_multiply_fusion, f32[8,16]{1,0:T(8,128)} %get-tuple-element.15, pred[8]{0:T(512)(128)(4,1)} %copy-done.10, ...), kind=kOutput, calls=%fused_computation.15 | convolution fusion | flops 3227516928 | bytes 7602696 | tf_op jit(solution)/shard_map/trhp,tn->rhpn/dot_general | solution.py:50
  322.0 2.8 gather_fusion.1
  324.9 4.8 select_convert_fusion
  329.7 4.8 all-to-all-start.1
  334.6 1.7 fusion.22
  336.3 220.8 %all-gather.8.cloned.1.call-done = bf16[1024,5120]{1,0:T(8,128)(2,1)} async-done(((bf16[1024,1280]{1,0:T(8,128)(2,1)}), bf16[1024,5120]{1,0:T(8,128)(2,1)}) %all-gather.8.cloned.1.call-update) | async-done | bytes 10485776 | tf_op jit(solution)/shard_map/all_gather | solution.py:115
  557.1 8.3 %convolution_convert_fusion = bf16[256,5120]{1,0:T(8,128)(2,1)} fusion(bf16[256,1024]{0,1:T(8,128)(2,1)S(1)} %bitcast.50, bf16[1024,5120]{1,0:T(8,128)(2,1)} %all-gather.8.cloned.1.call-done), kind=kOutput, calls=%fused_computation.8 | convolution fusion | flops 2685665280 | bytes 13631488 | tf_op jit(solution)/shard_map/dot_general | solution.py:113
  565.8 5.4 convert_element_type.52
  571.2 6.9 %gather_fusion.3 = f32[12,16,64,128]{3,2,1,0:T(8,128)} fusion(f32[12,16,64,128]{3,2,1,0:T(8,128)} %convert_element_type.52, s32[1024]{0:T(1024)S(1)} %pad_clamp_fusion), kind=kCustom, calls=%fused_computation.1.clone | custom fusion | bytes 12582960 | tf_op jit(solution)/shard_map/jit(_take)/gather | solution.py:141
  578.0 10.2 %select_select_fusion = f32[12,16,64,128]{3,2,1,0:T(8,128)} fusion(f32[12,16,64,128]{3,2,1,0:T(8,128)} %param.23, f32[12,16,64,128]{3,2,1,0:T(8,128)} %gather_fusion.3, pred[12]{0:T(512)(128)(4,1)S(1)} %compare_and_fusion, pred[12]{0:T(512)(128)(4,1)S(1)} %compare_reduce_fusion), kind=kLoop, calls=%fused_computation.9 | loop fusion | flops 3145728 | bytes 18874392 | tf_op jit(solution)/shard_map/jit(_where)/select_n | solution.py:140
  588.3 10.1 %reduce-scatter.2.cloned.1.call-done = bf16[256,1280]{1,0:T(8,128)(2,1)} async-done(((bf16[256,5120]{1,0:T(8,128)(2,1)}), bf16[256,1280]{1,0:T(8,128)(2,1)}) %reduce-scatter.2.cloned.1.call-update) | async-done | bytes 655376 | tf_op jit(solution)/shard_map/reduce_scatter | solution.py:118
  (89 shorter events, 4.2 us)
Async XLA Ops:
  7.2 145.1 %copy-start = (bf16[256,5120]{1,0:T(8,128)(2,1)S(1)}, bf16[256,5120]{1,0:T(8,128)(2,1)}, u32[]{:S(2)}) copy-start(bf16[256,5120]{1,0:T(8,128)(2,1)} %param.13) | copy-start | bytes 7864324
  7.2 2.2 copy-start.8
  7.2 148.6 %all-gather.6.cloned.1.call-start = ((), (), s32[]{:S(2)}) async-start(), calls=%async_computation.4 | async-start | bytes 3276800 | tf_op jit(solution)/shard_map/all_gather | solution.py:70
  7.9 297.8 %all-gather.4.cloned.1.call-start = ((), (), s32[]{:S(2)}) async-start(), calls=%async_computation.3 | async-start | bytes 13107200 | tf_op jit(solution)/shard_map/all_gather | solution.py:69
  8.7 548.4 %all-gather.8.cloned.1.call-start = ((), (), s32[]{:S(2)}) async-start(), calls=%async_computation.5 | async-start | bytes 13107200 | tf_op jit(solution)/shard_map/all_gather | solution.py:115
  21.0 7.2 %copy-start.16 = (s32[1,8]{1,0:T(1,128)S(1)}, s32[1,8]{1,0:T(1,128)}, u32[]{:S(2)}) copy-start(s32[1,8]{1,0:T(1,128)} %param.21) | copy-start | bytes 100
  21.0 8.4 %copy-start.6 = (bf16[1280,16]{0,1:T(8,128)(2,1)S(1)}, bf16[1280,16]{0,1:T(8,128)(2,1)}, u32[]{:S(2)}) copy-start(bf16[1280,16]{0,1:T(8,128)(2,1)} %param.16) | copy-start | bytes 122884
  21.0 131.2 %copy-start.11 = (f32[16]{0:T(128)S(1)}, f32[16]{0:T(128)}, u32[]{:S(2)}) copy-start(f32[16]{0:T(128)} %param.17) | copy-start | bytes 196
  21.0 132.0 %copy-start.13 = (f32[16]{0:T(128)S(1)}, f32[16]{0:T(128)}, u32[]{:S(2)}) copy-start(f32[16]{0:T(128)} %param.18) | copy-start | bytes 196
  21.0 138.5 %all-to-all-start = ((bf16[12,16,64,128]{3,2,1,0:T(8,128)(2,1)}), bf16[12,16,64,128]{3,2,1,0:T(8,128)(2,1)}, u32[]{:S(2)}, u32[]{:S(2)}) async-start(bf16[12,16,64,128]{3,2,1,0:T(8,128)(2,1)} %fusion.3), calls=%async_computation | async-start | bytes 6291456 | tf_op jit(solution)/shard_map/all_to_all | solution.py:103
  151.0 19.5 %copy-start.10 = (pred[8]{0:T(512)(128)(4,1)}, pred[8]{0:T(512)(128)(4,1)S(1)}, u32[]{:S(2)}) copy-start(pred[8]{0:T(512)(128)(4,1)S(1)} %get-tuple-element.3) | copy-start | bytes 28
  155.7 9.2 %copy-start.4 = (f32[256,16]{0,1:T(8,128)}, f32[256,16]{0,1:T(8,128)S(1)}, u32[]{:S(2)}) copy-start(f32[256,16]{0,1:T(8,128)S(1)} %get-tuple-element.14) | copy-start | bytes 49156
  322.0 2.9 copy-start.14
  322.0 2.9 copy-start.15
  329.7 4.9 copy-start.2
  329.7 4.9 copy-start.3
  329.7 4.9 copy-start.5
  329.7 4.9 copy-start.7
  329.7 4.9 copy-start.17
  329.7 4.9 copy-start.18
  329.7 236.1 %all-to-all-start.1 = ((bf16[12,16,64,128]{3,2,1,0:T(8,128)(2,1)}), bf16[12,16,64,128]{3,2,1,0:T(8,128)(2,1)}, u32[]{:S(2)}, u32[]{:S(2)}) async-start(bf16[12,16,64,128]{3,2,1,0:T(8,128)(2,1)} %select_convert_fusion), calls=%async_computation.2 | async-start | bytes 6291456 | tf_op jit(solution)/shard_map/all_to_all | solution.py:131
  334.5 263.9 %reduce-scatter.2.cloned.1.call-start = ((), (), s32[]{:S(2)}) async-start(), calls=%async_computation.6 | async-start | bytes 3276800 | tf_op jit(solution)/shard_map/reduce_scatter | solution.py:118
  557.1 8.3 %copy-start.9 = (s32[32]{0:T(128)S(1)}, s32[32]{0:T(128)}, u32[]{:S(2)}) copy-start(s32[32]{0:T(128)} %param.22) | copy-start | bytes 388
  557.1 8.3 %copy-start.12 = (s32[32]{0:T(128)S(1)}, s32[32]{0:T(128)}, u32[]{:S(2)}) copy-start(s32[32]{0:T(128)} %get-tuple-element.9) | copy-start | bytes 388
  578.0 20.3 %copy-start.1 = (bf16[256,5120]{1,0:T(8,128)(2,1)S(1)}, bf16[256,5120]{1,0:T(8,128)(2,1)}, u32[]{:S(2)}) copy-start(bf16[256,5120]{1,0:T(8,128)(2,1)} %param.13) | copy-start | bytes 7864324
Sparse Core Ops, SparseCore 0:
  9.6 109.1 all-gather.5
  120.3 185.3 all-gather.3
  307.3 249.7 all-gather.7
  565.5 32.8 reduce-scatter.1
where the time goes:
time: 606 us; the launch traced here: 605 us
  waiting for transfers between devices  355 us (59%)
  blocking collectives  121 us (20%)
  matrix products  44 us (7%)
  other arithmetic  36.4 us (6%)
  local copies, waits for them, and re-layouts  22.9 us (4%)
  between operations  14.1 us (2%)
  starting transfers between devices  11.6 us (2%)
    all_gather x1, waiting for transfers between devices, body(): lax.all_gather(w_out, 'req', axis=1, tiled=True)  221 us
    all_gather x1, waiting for transfers between devices, body(): lax.all_gather(w_x, 'req', axis=0, tiled=True)  122 us
    all_gather x1, blocking collectives, body(): lax.all_gather(w_dt, 'req', axis=0, tiled=True)  121 us
  transfers between devices with their start and end apart: 6, of which 3 were waited for; matrix products, arithmetic and copies ran while one was open for 17% of the time, Pallas kernels for 0%

commit v1 on v0

v1 whole, which is shorter than its diff:
```python
import functools

import jax
import jax.numpy as jnp
from jax import lax
from jax.experimental import pallas as pl
from jax.experimental.pallas import tpu as pltpu
from jax.sharding import PartitionSpec as P

HIGH = lax.Precision.HIGHEST
BF = jnp.bfloat16
F32 = jnp.float32
NT = (((1,), (1,)), ((), ()))
TN = (((0,), (0,)), ((), ()))


def params():
    return pltpu.CompilerParams(vmem_limit_bytes=48 * 1024 * 1024)


def exchange(x, axis="req"):
    return lax.all_to_all(x, axis, split_axis=0, concat_axis=0, tiled=True)


def spread_out(x, axis="req"):
    count = lax.axis_size(axis)
    return exchange(jnp.broadcast_to(x[None], (count,) + x.shape), axis)


def swap_core(x):
    count = lax.axis_size("tensor")
    return lax.ppermute(x, "tensor", [(i, i ^ 1) for i in range(count)])


def chip_turn(x, turn):
    count = lax.axis_size("tensor")
    return lax.ppermute(x, "tensor", [(i, (i + 2 * turn) % count) for i in range(count)])


def sum_tensor(x):
    x = x + swap_core(x)
    total = x
    for turn in range(1, lax.axis_size("tensor") // 2):
        total = total + chip_turn(x, turn)
    return total


def carried_kernel(slot, start, stop, c_ref, *refs):
    *states, out = refs
    owner = pl.program_id(0)
    rows = lax.broadcasted_iota(jnp.int32, (c_ref.shape[1], 1), 0)
    c_part = c_ref[0]
    total = jnp.zeros(out.shape[1:], F32)
    for rank, state in enumerate(states):
        at = owner * len(states) + rank
        inside = (rows >= start[at]) & (rows < stop[at])
        mine = jnp.where(inside, c_part, jnp.zeros_like(c_part))
        heads, width, dim = state.shape[1:]
        flat = state[0].reshape(heads * width, dim).astype(BF)
        total += lax.dot_general(mine, flat, NT, preferred_element_type=F32)
    out[0] = total.astype(BF)


def carried_part(slot, start, stop, c_all, cache, per_pair):
    owners, num_tok, dim = c_all.shape
    _, heads, width, _ = cache.shape

    def state_map(rank, o, slot, start, stop):
        return (slot[o * per_pair + rank], 0, 0, 0)

    return pl.pallas_call(
        carried_kernel,
        out_shape=jax.ShapeDtypeStruct((owners, num_tok, heads * width), BF),
        grid_spec=pltpu.PrefetchScalarGridSpec(
            num_scalar_prefetch=3,
            grid=(owners,),
            in_specs=[pl.BlockSpec((1, num_tok, dim), lambda o, *_: (o, 0, 0))]
            + [
                pl.BlockSpec((1, heads, width, dim), functools.partial(state_map, rank))
                for rank in range(per_pair)
            ],
            out_specs=pl.BlockSpec((1, num_tok, heads * width), lambda o, *_: (o, 0, 0)),
        ),
        compiler_params=params(),
        cost_estimate=pl.CostEstimate(
            flops=2 * owners * num_tok * dim * heads * width * per_pair,
            bytes_accessed=cache.size * 4 + owners * num_tok * heads * width * 2,
            transcendentals=0,
        ),
    )(slot, start, stop, c_all, *([cache] * per_pair))


def outputs_kernel(
    parts, carried, b_ref, c_ref, seg_row, seg_col, run_ref, run_t, step_t, gain, out, x_out, scores
):
    num_tok = b_ref.shape[0]

    @pl.when(pl.program_id(0) == 0)
    def _():
        raw = lax.dot_general(c_ref[...], b_ref[...], NT, preferred_element_type=F32)
        down = lax.broadcasted_iota(jnp.int32, (num_tok, num_tok), 0)
        along = lax.broadcasted_iota(jnp.int32, (num_tok, num_tok), 1)
        keep = (seg_row[...] == seg_col[...]) & (down >= along)
        scores[...] = jnp.where(keep, raw, 0.0)

    values = parts[0].astype(F32)
    for i in range(1, parts.shape[0]):
        values += parts[i].astype(F32)
    values = values.astype(BF)
    x_out[...] = values
    held = carried[0].astype(F32)
    for i in range(1, carried.shape[0]):
        held += carried[i].astype(F32)
    pair = run_ref.shape[2]
    width = values.shape[1] // pair
    lane = lax.broadcasted_iota(jnp.int32, values.shape, 1) // width
    total = jnp.zeros(values.shape, F32)
    grown = jnp.zeros(values.shape, F32)
    gains = jnp.zeros((1, values.shape[1]), F32)
    for i in range(pair):
        run_col = run_ref[0, :, i : i + 1]
        run_row = run_t[0, i : i + 1, :]
        step_row = step_t[0, i : i + 1, :]
        decay = jnp.exp(jnp.minimum(run_col - run_row, 0.0))
        mixing = (decay * scores[...] * step_row).astype(BF)
        within = jnp.dot(mixing, values, preferred_element_type=F32)
        total = jnp.where(lane == i, within, total)
        grown = jnp.where(lane == i, jnp.exp(run_col), grown)
        gains = jnp.where(lane[:1] == i, gain[0, :, i : i + 1], gains)
    out[...] = (total + grown * held + gains * values.astype(F32)).astype(BF)


def outputs_part(parts, carried, b_part, c_part, seg, running, step_size, gain):
    owners, num_tok, columns = parts.shape
    heads = running.shape[1]
    dim = b_part.shape[1]
    pair = 2
    steps = heads // pair
    lanes = columns // steps
    run_p = running.reshape(num_tok, steps, pair).transpose(1, 0, 2)
    run_t = running.T.reshape(steps, pair, num_tok)
    step_t = step_size.T.reshape(steps, pair, num_tok)

    def whole(*shape):
        return pl.BlockSpec(shape, lambda i: (0,) * len(shape))

    def per_step(*shape):
        return pl.BlockSpec((1,) + shape, lambda i: (i, 0, 0))

    wide = pl.BlockSpec((owners, num_tok, lanes), lambda i: (0, 0, i))
    slab = pl.BlockSpec((num_tok, lanes), lambda i: (0, i))
    return pl.pallas_call(
        outputs_kernel,
        out_shape=[jax.ShapeDtypeStruct((num_tok, columns), BF)] * 2,
        grid=(steps,),
        in_specs=[
            wide,
            wide,
            whole(num_tok, dim),
            whole(num_tok, dim),
            whole(num_tok, 1),
            whole(1, num_tok),
            per_step(num_tok, pair),
            per_step(pair, num_tok),
            per_step(pair, num_tok),
            per_step(1, pair),
        ],
        out_specs=[slab, slab],
        scratch_shapes=[pltpu.VMEM((num_tok, num_tok), F32)],
        compiler_params=params(),
        cost_estimate=pl.CostEstimate(
            flops=2 * num_tok * num_tok * columns * 2,
            bytes_accessed=parts.size * 4 + num_tok * columns * 4,
            transcendentals=num_tok * num_tok * heads,
        ),
    )(
        parts,
        carried,
        b_part,
        c_part,
        seg[:, None],
        seg[None, :],
        run_p,
        run_t,
        step_t,
        gain.reshape(steps, 1, pair),
    )


def states_kernel(owner, start, stop, state, x_ref, b_ref, run_ref, step_ref, out):
    at = pl.program_id(0)
    num_tok, heads = run_ref.shape[1:]
    width = state.shape[2]
    rows = lax.broadcasted_iota(jnp.int32, (num_tok, 1), 0)
    inside = (rows >= start[at]) & (rows < stop[at])
    last = rows == stop[at] - 1
    running = run_ref[0]
    totals = jnp.sum(jnp.where(last, running, 0.0), axis=0, keepdims=True)
    weights = jnp.where(inside, jnp.exp(jnp.minimum(totals - running, 0.0)), 0.0) * step_ref[0]
    head = lax.broadcasted_iota(jnp.int32, (heads, heads * width), 0)
    lane = lax.broadcasted_iota(jnp.int32, (heads, heads * width), 1) // width
    widen = (head == lane).astype(BF)
    wide = jnp.dot(weights.astype(BF), widen, preferred_element_type=F32)
    scaled = (x_ref[0].astype(F32) * wide).astype(BF)
    increment = lax.dot_general(scaled, b_ref[0], TN, preferred_element_type=F32)
    grown = jnp.exp(totals)
    for h in range(heads):
        out[0, h] = state[0, h] * grown[:, h : h + 1] + increment[h * width : (h + 1) * width]


def states_part(owner, start, stop, cache, x_all, b_all, run_all, step_all):
    slots, heads, width, dim = cache.shape
    _, num_tok, columns = x_all.shape

    def own(*shape):
        return pl.BlockSpec((1,) + shape, lambda s, owner, *_: (owner[s], 0, 0))

    slab = pl.BlockSpec((1, heads, width, dim), lambda s, *_: (s, 0, 0, 0))
    return pl.pallas_call(
        states_kernel,
        out_shape=jax.ShapeDtypeStruct(cache.shape, cache.dtype),
        grid_spec=pltpu.PrefetchScalarGridSpec(
            num_scalar_prefetch=3,
            grid=(slots,),
            in_specs=[
                slab,
                own(num_tok, columns),
                own(num_tok, dim),
                own(num_tok, heads),
                own(num_tok, heads),
            ],
            out_specs=slab,
        ),
        compiler_params=params(),
        cost_estimate=pl.CostEstimate(
            flops=2 * slots * num_tok * columns * dim,
            bytes_accessed=cache.size * 8 + slots * num_tok * columns * 2,
            transcendentals=slots * num_tok * heads,
        ),
    )(owner, start, stop, cache, x_all, b_all, run_all, step_all)


def body(
    tokens,
    w_x,
    w_bc,
    w_dt,
    dt_bias,
    decay_rate,
    skip_gain,
    w_out,
    suffix_lengths,
    checkpoint_slot,
    cache,
):
    reqs = lax.axis_size("req")
    tensors = lax.axis_size("tensor")
    chips = tensors // 2
    own_req = lax.axis_index("req")
    own_tensor = lax.axis_index("tensor")
    core = own_tensor % 2
    num_tok = tokens.shape[0]
    depth = w_x.shape[0]
    slots_dev, heads, width, state_dim = cache.shape
    columns = heads * width

    half = depth // 2
    outgoing = lax.dynamic_index_in_dim(
        tokens.reshape(num_tok, reqs, 2, half), core, axis=2, keepdims=False
    ).transpose(1, 0, 2)
    near = exchange(outgoing).reshape(reqs * num_tok, half)

    share = depth // tensors
    bc_rows = spread_out(lax.dynamic_slice_in_dim(w_bc, own_tensor * share, share))
    bc_tokens = lax.dynamic_index_in_dim(
        tokens.reshape(num_tok, reqs, tensors, share), own_tensor, axis=2, keepdims=False
    )
    state_maps = sum_tensor(
        jnp.dot(
            bc_tokens.reshape(num_tok, reqs * share),
            bc_rows.reshape(reqs * share, -1),
            preferred_element_type=F32,
        )
    ).astype(BF)
    b_part, c_part = state_maps[:, :state_dim], state_maps[:, state_dim:]
    c_all = spread_out(c_part)

    dt_rows = spread_out(w_dt.T)
    raw_step = jnp.einsum(
        "trk,rhk->th",
        tokens.reshape(num_tok, reqs, depth),
        dt_rows,
        preferred_element_type=F32,
    )
    step_size = jax.nn.softplus(raw_step + dt_bias[None, :])
    lengths = lax.all_gather(suffix_lengths[0], "req", axis=0)
    ends = jnp.cumsum(lengths, axis=1)
    begins = ends - lengths
    places = jnp.arange(num_tok, dtype=jnp.int32)
    own_ends = jnp.cumsum(suffix_lengths[0])
    seg = jnp.sum((places[:, None] >= own_ends[None, :]).astype(jnp.int32), axis=1)
    causal = ((seg[:, None] == seg[None, :]) & (places[:, None] >= places[None, :])).astype(F32)
    running = jnp.dot(causal, -step_size * decay_rate[None, :], precision=HIGH)
    timing = spread_out(jnp.concatenate([running, step_size], axis=1))
    b_all = spread_out(b_part)

    per_pair = (slots_dev + reqs - 1) // reqs
    total_reqs = checkpoint_slot.shape[0]
    req_dev = total_reqs // reqs
    holder = checkpoint_slot // slots_dev
    owner = jnp.arange(total_reqs, dtype=jnp.int32) // req_dev
    pair_key = holder * reqs + owner
    rank_in_pair = jnp.sum(
        (pair_key[:, None] == pair_key[None, :])
        & (checkpoint_slot[None, :] < checkpoint_slot[:, None]),
        axis=1,
    )
    slot_local = checkpoint_slot % slots_dev
    begin = begins.reshape(-1)
    end = ends.reshape(-1)
    pairs = jnp.arange(reqs * per_pair, dtype=jnp.int32)
    mine = holder == own_req
    match = mine[None, :] & ((owner * per_pair + rank_in_pair)[None, :] == pairs[:, None])

    def pick(match, values):
        return jnp.sum(jnp.where(match, values[None, :], 0), axis=1)

    carried = carried_part(
        pick(match, slot_local), pick(match, begin), pick(match, end), c_all, cache, per_pair
    )
    carried = exchange(carried)

    w_near = lax.dynamic_slice_in_dim(w_x, core * half, half)
    w_far = lax.dynamic_slice_in_dim(w_x, (1 - core) * half, half)
    far = swap_core(near)
    partial = jnp.dot(near, w_near, preferred_element_type=F32) + jnp.dot(
        far, w_far, preferred_element_type=F32
    )
    parts = exchange(partial.astype(BF).reshape(reqs, num_tok, columns))

    outputs, values = outputs_part(
        parts, carried, b_part, c_part, seg, running, step_size, skip_gain
    )
    all_outputs = spread_out(outputs).reshape(reqs * num_tok, columns)
    x_all = spread_out(values)

    product = jnp.dot(all_outputs, w_out, preferred_element_type=F32).astype(BF)
    rows_half = num_tok // 2
    out_columns = w_out.shape[1]
    product = product.reshape(reqs, 2, rows_half, out_columns)
    kept = lax.dynamic_index_in_dim(product, core, axis=1, keepdims=False)
    given = lax.dynamic_index_in_dim(product, 1 - core, axis=1, keepdims=False)
    summed = (kept.astype(F32) + swap_core(given).astype(F32)).astype(BF)
    arrived = exchange(summed).reshape(chips, 2, rows_half, out_columns)
    own_chip = own_tensor // 2
    total = lax.dynamic_index_in_dim(arrived, own_chip, axis=0, keepdims=False).astype(F32)
    for turn in range(1, chips):
        to_chip = (own_chip + turn) % chips
        given = lax.dynamic_index_in_dim(arrived, to_chip, axis=0, keepdims=False)
        total = total + chip_turn(given, turn).astype(F32)
    total = total.astype(BF)
    kept = lax.dynamic_index_in_dim(total, core, axis=0, keepdims=False)
    other = swap_core(lax.dynamic_index_in_dim(total, 1 - core, axis=0, keepdims=False))
    low = jnp.where(core == 0, kept, other)
    high = jnp.where(core == 0, other, kept)
    layer_out = jnp.concatenate([low, high], axis=0)

    slot_ids = own_req * slots_dev + jnp.arange(slots_dev, dtype=jnp.int32)
    match_slot = checkpoint_slot[None, :] == slot_ids[:, None]
    new_cache = states_part(
        pick(match_slot, owner),
        pick(match_slot, begin),
        pick(match_slot, end),
        cache,
        x_all,
        b_all,
        timing[:, :, :heads],
        timing[:, :, heads:],
    )
    return (layer_out, new_cache)


def solution(mesh):
    placed = (
        P(("groups", "req"), None),
        P("req", "tensor"),
        P("req", None),
        P("req", "tensor"),
        P("tensor"),
        P("tensor"),
        P("tensor"),
        P("tensor", "req"),
        P(("groups", "req"), None),
        P("groups"),
        P(("groups", "req"), "tensor", None, None),
    )
    return jax.shard_map(
        body,
        mesh=mesh,
        in_specs=placed,
        out_specs=(P(("groups", "req"), "tensor"), P(("groups", "req"), "tensor", None, None)),
        check_vma=False,
    )
```

time: 606 us -> 396 us (0.65)
  waiting for transfers between devices: 355 us -> 200 us
  blocking collectives: 121 us -> 66.8 us
  starting transfers between devices: 11.6 us -> 43.8 us
  other arithmetic: 36.4 us -> 6.37 us
  matrix products: 44 us -> 17 us
  Pallas kernels: 0 us -> 24.3 us
  between operations: 14.1 us -> 1.04 us
  local copies, waits for them, and re-layouts: 22.9 us -> 35.1 us
    all_gather x3 -> x0, waiting for transfers between devices: 343 us -> none  [the longest x1 221 us: body(): lax.all_gather(w_out, 'req', axis=1, tiled=True)]
    all_to_all x2 -> x9, waiting for transfers between devices: 0.01 us -> 180 us  [exchange(): return lax.all_to_all(x, axis, split_axis=0, concat_axis=0, tiled=True)]
    all_gather x1, blocking collectives: 121 us -> 24.6 us  [body(): lengths = lax.all_gather(suffix_lengths[0], 'req', axis=0)]
    all_to_all x0 -> x2, blocking collectives: none -> 42.3 us  [exchange(): return lax.all_to_all(x, axis, split_axis=0, concat_axis=0, tiled=True)]
    all_to_all x2 -> x9, starting transfers between devices: 11.4 us -> 41.6 us  [exchange(): return lax.all_to_all(x, axis, split_axis=0, concat_axis=0, tiled=True)]
    dot_general x11 -> x6, matrix products: 44 us -> 17 us  [the longest x1 5.24 us: body(): product = jnp.dot(all_outputs, w_out, preferred_element_type=F32).astype(BF)]
    pallas_call x0 -> x3, Pallas kernels: none -> 24.3 us  [the longest x1 13.6 us: states_part(): pl.pallas_call(states_kernel, out_shape=jax.ShapeDtypeStruct(cache.shape,...]
    gather x4 -> x0, local copies, waits for them, and re-layouts: 21.1 us -> none  [the longest x1 6.87 us: body(): jnp.take(arrived, slot_source, axis=0)]
  transfers between devices with their start and end apart: 6 -> 15, of which waited for: 3 -> 12; matrix products, arithmetic and copies ran while one was open for 17% -> 8% of each run, Pallas kernels for 0% -> 5%
where the time goes in v1:
time: 396 us; the launch traced here: 394 us
  waiting for transfers between devices  200 us (51%)
  blocking collectives  66.8 us (17%)
  starting transfers between devices  43.8 us (11%)
  local copies, waits for them, and re-layouts  35.1 us (9%)
  Pallas kernels  24.3 us (6%)
  matrix products  17 us (4%)
  other arithmetic  6.37 us (2%)
    all_to_all x9, waiting for transfers between devices, exchange(): return lax.all_to_all(x, axis, split_axis=0, concat_axis=0, tiled=True)  180 us
    all_to_all x2, blocking collectives, exchange(): return lax.all_to_all(x, axis, split_axis=0, concat_axis=0, tiled=True)  42.3 us
    all_to_all x9, starting transfers between devices, exchange(): return lax.all_to_all(x, axis, split_axis=0, concat_axis=0, tiled=True)  41.6 us
    all_gather x1, blocking collectives, body(): lengths = lax.all_gather(suffix_lengths[0], 'req', axis=0)  24.6 us
    ppermute x2, waiting for transfers between devices, chip_turn(): lax.ppermute(x, 'tensor', [(i, (i + 2 * turn) % count) for i in range(cou...  17.7 us
    unnamed x41, local copies, waits for them, and re-layouts  15 us
    pallas_call x1, Pallas kernels, states_part(): pl.pallas_call(states_kernel, out_shape=jax.ShapeDtypeStruct(cache.shape,...  13.6 us
  transfers between devices with their start and end apart: 15, of which 12 were waited for; matrix products, arithmetic and copies ran while one was open for 8% of the time, Pallas kernels for 5%

profile of v1, /device:TPU:0, one launch (start us, length us, event | category | flops | bytes accessed | tf_op | source)
XLA Modules:
  0.0 394.2 jit_solution(13482050561810000394)
XLA Ops:
  2.6 6.3 %all-to-all-start.2 = ((bf16[4,320,256]{2,1,0:T(8,128)(2,1)}), bf16[4,320,256]{2,1,0:T(8,128)(2,1)S(1)}, u32[]{:S(2)}, u32[]{:S(2)}) async-start(bf16[4,320,256]{2,1,0:T(8,128)(2,1)} %broadcast_in_dim.115), calls=%async_computation.2 | async-start | bytes 1310720 | tf_op jit(solution)/shard_map/all_to_all | solution.py:22
  9.0 4.4 %copy.39 = bf16[256,5120]{0,1:T(8,128)(2,1)} copy(bf16[256,5120]{1,0:T(8,128)(2,1)} %param.11) | data formatting | bytes 5242880 | tf_op args[0]
  15.3 11.0 %all-to-all-done.2 = bf16[4,320,256]{2,1,0:T(8,128)(2,1)S(1)} async-done(((bf16[4,320,256]{2,1,0:T(8,128)(2,1)}), bf16[4,320,256]{2,1,0:T(8,128)(2,1)S(1)}, u32[]{:S(2)}, u32[]{:S(2)}) %all-to-all-start.2) | async-done | bytes 655392 | tf_op jit(solution)/shard_map/all_to_all | solution.py:22
  31.6 3.3 all-to-all-start.5
  35.0 2.8 collective-permute-done.2
  37.8 3.7 all-to-all-done.5
  42.3 3.4 all-to-all-start.3
  45.7 2.5 constant_dynamic-slice_fusion.2
  48.2 2.4 copy.40
  50.7 3.2 all-to-all-done.3.c_ref
  53.9 4.3 %all-to-all-start = ((bf16[4,256,640]{2,1,0:T(8,128)(2,1)}), bf16[4,256,640]{2,1,0:T(8,128)(2,1)}, u32[]{:S(2)}, u32[]{:S(2)}) async-start(bf16[4,256,640]{2,1,0:T(8,128)(2,1)} %bitcast.84), calls=%async_computation | async-start | bytes 2621440 | tf_op jit(solution)/shard_map/all_to_all | solution.py:22
  58.2 24.6 %all-gather = s32[4,1,8]{2,1,0:T(1,128)S(1)} all-gather(s32[1,1,8]{2,1,0:T(1,128)S(1)} %bitcast.96), channel_id=1, replica_groups=mesh['groups'=2,'req'=4,'tensor'=4] {'req'}, dimensions={0}, use_global_device_ids=true | all-gather | bytes 160 | tf_op jit(solution)/shard_map/all_gather | solution.py:296
  83.6 4.5 %shard_map.122 = bf16[4,256,1024]{2,1,0:T(8,128)(2,1)S(1)} custom-call(s32[12]{0:T(128)S(1)} %get-tuple-element.14.slot, s32[12]{0:T(128)S(1)} %get-tuple-element.10.start, s32[12]{0:T(128)S(1)} %get-tuple-element.9.stop, bf16[4,256,128]{2,1,0:T(8,128)(2,1)S(1)} %all-to-all-done.3.c_ref, f32[12,16,64,128]{3,2,1,0:T(8,128)} %state.1, ...), custom_call_target="tpu_custom_call" | custom-call | flops 805306368 | bytes 8388608 | tf_op jit(solution)/shard_map/pallas_call | solution.py:71
  89.4 9.9 %all-to-all-start.4 = ((bf16[4,256,1024]{2,1,0:T(8,128)(2,1)}), bf16[4,256,1024]{2,1,0:T(8,128)(2,1)}, u32[]{:S(2)}, u32[]{:S(2)}) async-start(bf16[4,256,1024]{2,1,0:T(8,128)(2,1)} %copy-done.4), calls=%async_computation.4 | async-start | bytes 4194304 | tf_op jit(solution)/shard_map/all_to_all | solution.py:22
  99.3 3.1 fusion.6
  102.7 4.4 %add_convert_fusion = bf16[1024,1024]{1,0:T(8,128)(2,1)} fusion(f32[1024,1024]{1,0:T(8,128)S(1)} %fusion.6, bf16[1024,640]{1,0:T(8,128)(2,1)} %collective-permute-done, bf16[1280,1024]{1,0:T(8,128)(2,1)S(1)} %copy-done, s32[]{:T(128)S(6)} %select_n.114), kind=kOutput, calls=%fused_computation | convolution fusion | flops 1344274432 | bytes 8912900 | tf_op jit(solution)/shard_map/dot_general | solution.py:336
  107.1 39.2 %all-to-all-done.4.carried = bf16[4,256,1024]{2,1,0:T(8,128)(2,1)} async-done(((bf16[4,256,1024]{2,1,0:T(8,128)(2,1)}), bf16[4,256,1024]{2,1,0:T(8,128)(2,1)}, u32[]{:S(2)}, u32[]{:S(2)}) %all-to-all-start.4) | async-done | bytes 2097184 | tf_op jit(solution)/shard_map/all_to_all | solution.py:22
  146.2 3.7 all-to-all-start.1
  150.5 2.6 compare_select_fusion
  154.8 43.7 %all-to-all-done.1.parts = bf16[4,256,1024]{2,1,0:T(8,128)(2,1)S(1)} async-done(((bf16[4,256,1024]{2,1,0:T(8,128)(2,1)}), bf16[4,256,1024]{2,1,0:T(8,128)(2,1)S(1)}, u32[]{:S(2)}, u32[]{:S(2)}) %all-to-all-start.1) | async-done | bytes 2097184 | tf_op jit(solution)/shard_map/all_to_all | solution.py:22
  199.7 6.2 %shard_map.123 = (bf16[256,1024]{1,0:T(8,128)(2,1)S(1)}, bf16[256,1024]{1,0:T(8,128)(2,1)S(1)}) custom-call(bf16[4,256,1024]{2,1,0:T(8,128)(2,1)S(1)} %all-to-all-done.1.parts, bf16[4,256,1024]{2,1,0:T(8,128)(2,1)} %all-to-all-done.4.carried, bf16[256,128]{1,0:T(8,128)(2,1)S(1)} %get-tuple-element.21.b_ref, bf16[256,128]{1,0:T(8,128)(2,1)S(1)} %get-tuple-element.22.c_ref, ...), custom_call_target="tpu_custom_call" | custom-call | flops 268435456 | bytes 5242880 | tf_op jit(solution)/shard_map/pallas_call | solution.py:152
  208.3 3.6 all-to-all-start.6
  212.0 47.7 %all-to-all-done.6 = bf16[4,256,1024]{2,1,0:T(8,128)(2,1)S(1)} async-done(((bf16[4,256,1024]{2,1,0:T(8,128)(2,1)}), bf16[4,256,1024]{2,1,0:T(8,128)(2,1)S(1)}, u32[]{:S(2)}, u32[]{:S(2)}) %all-to-all-start.6) | async-done | bytes 2097184 | tf_op jit(solution)/shard_map/all_to_all | solution.py:22
  261.0 5.2 %convolution_convert_fusion = bf16[1024,1280]{1,0:T(8,128)(2,1)S(1)} fusion(bf16[1024,1024]{1,0:T(8,128)(2,1)} %bitcast.89, bf16[1024,1280]{1,0:T(8,128)(2,1)} %param.18), kind=kOutput, calls=%fused_computation.1 | convolution fusion | flops 2685665280 | bytes 7340032 | tf_op jit(solution)/shard_map/dot_general | solution.py:347
  267.6 9.0 %all_to_all.55 = f32[4,256,32]{1,2,0:T(8,128)S(1)} all-to-all(f32[4,256,32]{1,2,0:T(8,128)S(1)} %broadcast_in_dim.124), channel_id=1, replica_groups=mesh['groups'=2,'req'=4,'tensor'=4] {'req'}, dimensions={0} | all-to-all | bytes 262144 | tf_op jit(solution)/shard_map/all_to_all | solution.py:22
  277.4 3.4 all-to-all-start.9
  282.8 6.4 %all-to-all-done.9.b_ref = bf16[4,256,128]{2,1,0:T(8,128)(2,1)S(1)} async-done(((bf16[4,256,128]{2,1,0:T(8,128)(2,1)}), bf16[4,256,128]{2,1,0:T(8,128)(2,1)S(1)}, u32[]{:S(2)}, u32[]{:S(2)}) %all-to-all-start.9) | async-done | bytes 262176 | tf_op jit(solution)/shard_map/all_to_all | solution.py:22
  289.3 33.2 %all_to_all.56 = bf16[4,128,1280]{2,1,0:T(8,128)(2,1)} all-to-all(bf16[4,128,1280]{2,1,0:T(8,128)(2,1)S(1)} %fusion.3), channel_id=1, replica_groups=mesh['groups'=2,'req'=4,'tensor'=4] {'req'}, dimensions={0} | all-to-all | bytes 2621440 | tf_op jit(solution)/shard_map/all_to_all | solution.py:22
  324.1 3.6 all-to-all-start.8
  330.2 14.9 %collective-permute-done.4 = bf16[2,128,1280]{2,1,0:T(8,128)(2,1)} collective-permute-done((bf16[2,128,1280]{2,1,0:T(8,128)(2,1)}, bf16[2,128,1280]{2,1,0:T(8,128)(2,1)}, u32[]{:S(2)}, u32[]{:S(2)}) %collective-permute-start.4) | collective-permute-done | bytes 655392 | tf_op jit(solution)/shard_map/ppermute | solution.py:37
  349.4 25.4 %all-to-all-done.8.x_ref = bf16[4,256,1024]{2,1,0:T(8,128)(2,1)S(1)} async-done(((bf16[4,256,1024]{2,1,0:T(8,128)(2,1)}), bf16[4,256,1024]{2,1,0:T(8,128)(2,1)S(1)}, u32[]{:S(2)}, u32[]{:S(2)}) %all-to-all-start.8) | async-done | bytes 2097184 | tf_op jit(solution)/shard_map/all_to_all | solution.py:22
  378.7 13.6 %shard_map.124 = f32[12,16,64,128]{3,2,1,0:T(8,128)} custom-call(s32[12]{0:T(128)S(1)} %get-tuple-element.11.owner, s32[12]{0:T(128)S(1)} %get-tuple-element.12.start, s32[12]{0:T(128)S(1)} %get-tuple-element.13.stop, f32[12,16,64,128]{3,2,1,0:T(8,128)} %state.1, bf16[4,256,1024]{2,1,0:T(8,128)(2,1)S(1)} %copy-done.3, ...), custom_call_target="tpu_custom_call" | custom-call | flops 805306368 | bytes 18874368 | tf_op jit(solution)/shard_map/pallas_call | solution.py:219
  (94 shorter events, 37.9 us)
Async XLA Ops:
  0.6 98.7 %copy-start = (bf16[1280,1024]{1,0:T(8,128)(2,1)S(1)}, bf16[1280,1024]{1,0:T(8,128)(2,1)}, u32[]{:S(2)}) copy-start(bf16[1280,1024]{1,0:T(8,128)(2,1)} %param.12) | copy-start | bytes 7864324
  2.6 23.6 %all-to-all-start.2 = ((bf16[4,320,256]{2,1,0:T(8,128)(2,1)}), bf16[4,320,256]{2,1,0:T(8,128)(2,1)S(1)}, u32[]{:S(2)}, u32[]{:S(2)}) async-start(bf16[4,320,256]{2,1,0:T(8,128)(2,1)} %broadcast_in_dim.115), calls=%async_computation.2 | async-start | bytes 1310720 | tf_op jit(solution)/shard_map/all_to_all | solution.py:22
  13.3 17.6 %copy-start.13 = (bf16[1280,16]{0,1:T(8,128)(2,1)S(1)}, bf16[1280,16]{0,1:T(8,128)(2,1)}, u32[]{:S(2)}) copy-start(bf16[1280,16]{0,1:T(8,128)(2,1)} %param.14) | copy-start | bytes 122884
  27.7 1.6 collective-permute-start.1
  29.4 8.4 %collective-permute-start.2 = (f32[256,256]{1,0:T(8,128)S(1)}, f32[256,256]{1,0:T(8,128)S(1)}, u32[]{:S(2)}, u32[]{:S(2)}) collective-permute-start(f32[256,256]{1,0:T(8,128)S(1)} %add.123), channel_id=1, source_target_pairs={{0,2},{1,3},{2,0},{3,1},{4,6},{5,7},{6,4},{7,5},{8,10},{9,11},{10,... | collective-permute-start | bytes 786440 | tf_op jit(solution)/shard_map/ppermute | solution.py:37
  31.6 10.0 %all-to-all-start.5 = ((bf16[4,16,1280]{2,1,0:T(8,128)(2,1)}), bf16[4,16,1280]{2,1,0:T(8,128)(2,1)S(1)}, u32[]{:S(2)}, u32[]{:S(2)}) async-start(bf16[4,16,1280]{2,1,0:T(8,128)(2,1)} %broadcast_in_dim.119), calls=%async_computation.5 | async-start | bytes 327680 | tf_op jit(solution)/shard_map/all_to_all | solution.py:22
  42.3 11.6 %all-to-all-start.3 = ((bf16[4,256,128]{2,1,0:T(8,128)(2,1)}), bf16[4,256,128]{2,1,0:T(8,128)(2,1)S(1)}, u32[]{:S(2)}, u32[]{:S(2)}) async-start(bf16[4,256,128]{2,1,0:T(8,128)(2,1)} %broadcast_in_dim.116), calls=%async_computation.3 | async-start | bytes 524288 | tf_op jit(solution)/shard_map/all_to_all | solution.py:22
  48.2 10.0 %copy-start.15 = (s32[1,8]{1,0:T(1,128)S(1)}, s32[1,8]{1,0:T(1,128)}, u32[]{:S(2)}) copy-start(s32[1,8]{1,0:T(1,128)} %param.19) | copy-start | bytes 100
  48.2 34.9 %copy-start.14 = (s32[32]{0:T(128)S(1)}, s32[32]{0:T(128)}, u32[]{:S(2)}) copy-start(s32[32]{0:T(128)} %param.20) | copy-start | bytes 388
  53.9 35.5 %all-to-all-start = ((bf16[4,256,640]{2,1,0:T(8,128)(2,1)}), bf16[4,256,640]{2,1,0:T(8,128)(2,1)}, u32[]{:S(2)}, u32[]{:S(2)}) async-start(bf16[4,256,640]{2,1,0:T(8,128)(2,1)} %bitcast.84), calls=%async_computation | async-start | bytes 2621440 | tf_op jit(solution)/shard_map/all_to_all | solution.py:22
  88.1 1.3 copy-start.4
  89.4 56.8 %all-to-all-start.4 = ((bf16[4,256,1024]{2,1,0:T(8,128)(2,1)}), bf16[4,256,1024]{2,1,0:T(8,128)(2,1)}, u32[]{:S(2)}, u32[]{:S(2)}) async-start(bf16[4,256,1024]{2,1,0:T(8,128)(2,1)} %copy-done.4), calls=%async_computation.4 | async-start | bytes 4194304 | tf_op jit(solution)/shard_map/all_to_all | solution.py:22
  99.3 3.4 collective-permute-start
  146.2 4.2 %copy-start.16 = (f32[16]{0:T(128)S(1)}, f32[16]{0:T(128)}, u32[]{:S(2)}) copy-start(f32[16]{0:T(128)} %param.17) | copy-start | bytes 196
  146.2 4.3 %copy-start.17 = (f32[16]{0:T(128)S(1)}, f32[16]{0:T(128)}, u32[]{:S(2)}) copy-start(f32[16]{0:T(128)} %param.15) | copy-start | bytes 196
  146.2 52.3 %all-to-all-start.1 = ((bf16[4,256,1024]{2,1,0:T(8,128)(2,1)}), bf16[4,256,1024]{2,1,0:T(8,128)(2,1)S(1)}, u32[]{:S(2)}, u32[]{:S(2)}) async-start(bf16[4,256,1024]{2,1,0:T(8,128)(2,1)} %bitcast.88), calls=%async_computation.1 | async-start | bytes 4194304 | tf_op jit(solution)/shard_map/all_to_all | solution.py:22
  150.0 3.1 copy-start.18
  198.5 1.2 copy-start.5
  208.3 51.3 %all-to-all-start.6 = ((bf16[4,256,1024]{2,1,0:T(8,128)(2,1)}), bf16[4,256,1024]{2,1,0:T(8,128)(2,1)S(1)}, u32[]{:S(2)}, u32[]{:S(2)}) async-start(bf16[4,256,1024]{2,1,0:T(8,128)(2,1)} %broadcast_in_dim.120), calls=%async_computation.6 | async-start | bytes 4194304 | tf_op jit(solution)/shard_map/all_to_all | solution.py:22
  259.7 1.3 copy-start.12
  266.2 14.6 %copy-start.9 = (bf16[1024,1280]{1,0:T(8,128)(2,1)}, bf16[1024,1280]{1,0:T(8,128)(2,1)S(1)}, u32[]{:S(2)}) copy-start(bf16[1024,1280]{1,0:T(8,128)(2,1)S(1)} %convolution_convert_fusion) | copy-start | bytes 7864324
  267.5 13.3 %collective-permute-start.3 = (bf16[4,128,1280]{2,1,0:T(8,128)(2,1)}, bf16[4,128,1280]{2,1,0:T(8,128)(2,1)}, u32[]{:S(2)}, u32[]{:S(2)}) collective-permute-start(bf16[4,128,1280]{2,1,0:T(8,128)(2,1)} %dynamic-slice_bitcast_fusion), channel_id=1, source_target_pairs={{0,1},{1,0},{2,3},{3,2},{4,5},{5,4},{6,7},{7,6},{8,9},{9,8},{10,11... | collective-permute-start | bytes 3932168 | tf_op jit(solution)/shard_map/ppermute | solution.py:32
  277.4 11.9 %all-to-all-start.9 = ((bf16[4,256,128]{2,1,0:T(8,128)(2,1)}), bf16[4,256,128]{2,1,0:T(8,128)(2,1)S(1)}, u32[]{:S(2)}, u32[]{:S(2)}) async-start(bf16[4,256,128]{2,1,0:T(8,128)(2,1)} %broadcast_in_dim.123), calls=%async_computation.9 | async-start | bytes 524288 | tf_op jit(solution)/shard_map/all_to_all | solution.py:22
  282.8 39.7 %copy-start.8 = (bf16[256,1024]{1,0:T(8,128)(2,1)S(1)}, bf16[256,1024]{1,0:T(8,128)(2,1)}, u32[]{:S(2)}) copy-start(bf16[256,1024]{1,0:T(8,128)(2,1)} %copy-done.7) | copy-start | bytes 1572868
  324.1 50.7 %all-to-all-start.8 = ((bf16[4,256,1024]{2,1,0:T(8,128)(2,1)}), bf16[4,256,1024]{2,1,0:T(8,128)(2,1)S(1)}, u32[]{:S(2)}, u32[]{:S(2)}) async-start(bf16[4,256,1024]{2,1,0:T(8,128)(2,1)} %broadcast_in_dim.122), calls=%async_computation.8 | async-start | bytes 4194304 | tf_op jit(solution)/shard_map/all_to_all | solution.py:22
  329.7 15.4 %collective-permute-start.4 = (bf16[2,128,1280]{2,1,0:T(8,128)(2,1)}, bf16[2,128,1280]{2,1,0:T(8,128)(2,1)}, u32[]{:S(2)}, u32[]{:S(2)}) collective-permute-start(bf16[2,128,1280]{2,1,0:T(8,128)(2,1)} %dynamic-slice_bitcast_fusion.1), channel_id=1, source_target_pairs={{0,2},{1,3},{2,0},{3,1},{4,6},{5,7},{6,4},{7,5},{8,10},{9,11},{10,... | collective-permute-start | bytes 1966088 | tf_op jit(solution)/shard_map/ppermute | solution.py:37
  348.1 44.2 %collective-permute-start.5 = (bf16[128,1280]{1,0:T(8,128)(2,1)}, bf16[128,1280]{1,0:T(8,128)(2,1)}, u32[]{:S(2)}, u32[]{:S(2)}) collective-permute-start(bf16[128,1280]{1,0:T(8,128)(2,1)} %dynamic-slice_bitcast_fusion.2), channel_id=1, source_target_pairs={{0,1},{1,0},{2,3},{3,2},{4,5},{5,4},{6,7},{7,6},{8,9},{9,8},{10,11... | collective-permute-start | bytes 983048 | tf_op jit(solution)/shard_map/ppermute | solution.py:32
  374.8 1.3 copy-start.2
  376.1 1.6 copy-start.3
  377.7 1.0 copy-start.6
  378.7 13.6 %copy-start.11 = (bf16[2,128,1280]{2,1,0:T(8,128)(2,1)S(1)}, bf16[2,128,1280]{2,1,0:T(8,128)(2,1)}, u32[]{:S(2)}) copy-start(bf16[2,128,1280]{2,1,0:T(8,128)(2,1)} %copy-done.10) | copy-start | bytes 1966084
  378.7 15.5 %copy-start.1 = (bf16[1280,1024]{1,0:T(8,128)(2,1)S(1)}, bf16[1280,1024]{1,0:T(8,128)(2,1)}, u32[]{:S(2)}) copy-start(bf16[1280,1024]{1,0:T(8,128)(2,1)} %param.12) | copy-start | bytes 7864324
  (2 other events, 1.6 us)

commit v2 on v0

v2 whole, which is shorter than its diff:
```python
import functools

import jax
import jax.numpy as jnp
from jax import lax
from jax.experimental import pallas as pl
from jax.experimental.pallas import tpu as pltpu
from jax.sharding import PartitionSpec as P

HIGH = lax.Precision.HIGHEST
BF = jnp.bfloat16
F32 = jnp.float32
NN = (((1,), (0,)), ((), ()))
NT = (((1,), (1,)), ((), ()))
TN = (((0,), (0,)), ((), ()))
LANES = 128


def turn_req(x, turn):
    count = lax.axis_size("req")
    return lax.ppermute(x, "req", [(i, (i + turn) % count) for i in range(count)])


def swap_core(x):
    count = lax.axis_size("tensor")
    return lax.ppermute(x, "tensor", [(i, i ^ 1) for i in range(count)])


def turn_chip(x, turn):
    count = lax.axis_size("tensor")
    return lax.ppermute(x, "tensor", [(i, (i + 2 * turn) % count) for i in range(count)])


def spread_out(x):
    count = lax.axis_size("req")
    wide = jnp.broadcast_to(x[None], (count,) + x.shape)
    return lax.all_to_all(wide, "req", split_axis=0, concat_axis=0, tiled=True)


def sum_tensor(x):
    x = x + swap_core(x)
    total = x
    for turn in range(1, lax.axis_size("tensor") // 2):
        total = total + turn_chip(x, turn)
    return total


def dot32(a, b, dims):
    return lax.dot_general(a, b, dims, precision=HIGH, preferred_element_type=F32)


def dot16(a, b, dims):
    return lax.dot_general(a, b, dims, preferred_element_type=F32)


def prep_kernel(maps, raw, bias, rate, seg_row, seg_col, payload, run, run_t, step_t):
    num_tok, heads = raw.shape
    dim = maps.shape[1] // 2
    z = raw[...] + bias[...]
    step = jnp.maximum(z, 0.0) + jnp.log1p(jnp.exp(-jnp.abs(z)))
    log_decay = -step * rate[...]
    down = lax.broadcasted_iota(jnp.int32, (num_tok, num_tok), 0)
    along = lax.broadcasted_iota(jnp.int32, (num_tok, num_tok), 1)
    same = seg_row[...] == seg_col[...]
    causal = (same & (down >= along)).astype(F32)
    running = dot32(causal, log_decay, NN)
    totals = dot32(same.astype(F32), log_decay, NN)
    run[...] = running
    run_t[...] = dot32(log_decay, causal, (((0,), (1,)), ((), ())))
    step_t[...] = dot32(step, (down == along).astype(F32), TN)
    weights = jnp.exp(jnp.minimum(totals - running, 0.0)) * step
    grown = jnp.exp(totals)
    high = grown.astype(BF)
    low = (grown - high.astype(F32)).astype(BF)
    payload[:, :dim] = maps[:, dim:].astype(BF)
    payload[:, dim : 2 * dim] = maps[:, :dim].astype(BF)
    head = lax.broadcasted_iota(jnp.int32, (heads, LANES), 0)
    lane = lax.broadcasted_iota(jnp.int32, (heads, LANES), 1)
    tail = jnp.zeros((num_tok, LANES), F32)
    for i, part in enumerate((weights.astype(BF), high, low)):
        tail += dot16(part, (lane == head + i * heads).astype(BF), NN)
    seg_lane = lax.broadcasted_iota(jnp.int32, (num_tok, LANES), 1) == 3 * heads
    tail = jnp.where(seg_lane, seg_row[...].astype(F32), tail)
    payload[:, 2 * dim :] = tail.astype(BF)


def prep(maps, raw, bias, rate, seg):
    num_tok, heads = raw.shape
    return pl.pallas_call(
        prep_kernel,
        out_shape=[
            jax.ShapeDtypeStruct((num_tok, maps.shape[1] + LANES), BF),
            jax.ShapeDtypeStruct((num_tok, heads), F32),
            jax.ShapeDtypeStruct((heads, num_tok), F32),
            jax.ShapeDtypeStruct((heads, num_tok), F32),
        ],
        cost_estimate=pl.CostEstimate(flops=1 << 28, bytes_accessed=1 << 20, transcendentals=1 << 14),
    )(maps, raw, bias[None], rate[None], seg[:, None], seg[None, :])


def carried_kernel(slot, member, payload, *refs):
    *states, out = refs
    heads, width, dim = states[0].shape[1:]
    at = lax.broadcasted_iota(jnp.int32, (1, LANES), 1)
    seg_at = payload.shape[1] - LANES
    tail = payload[:, seg_at:].astype(F32)
    c_part = payload[:, :dim].astype(F32)
    total = jnp.zeros(out.shape, F32)
    seg = jnp.sum(jnp.where(at == member[len(states)], tail, 0.0), axis=1, keepdims=True)
    for rank, state in enumerate(states):
        inside = seg == member[rank].astype(F32)
        mine = jnp.where(inside, c_part, 0.0).astype(BF)
        flat = state[0].reshape(heads * width, dim).astype(BF)
        total += dot16(mine, flat, NT)
    out[...] = total.astype(BF)


def carried_part(slot, member, payload, cache):
    num_tok = payload.shape[0]
    _, heads, width, dim = cache.shape
    chunk = min(heads, 4)
    ranks = slot.shape[0]

    def state_map(rank, i, slot, member):
        return (slot[rank], i, 0, 0)

    return pl.pallas_call(
        carried_kernel,
        out_shape=jax.ShapeDtypeStruct((num_tok, heads * width), BF),
        grid_spec=pltpu.PrefetchScalarGridSpec(
            num_scalar_prefetch=2,
            grid=(heads // chunk,),
            in_specs=[pl.BlockSpec(payload.shape, lambda i, *_: (0, 0))]
            + [
                pl.BlockSpec((1, chunk, width, dim), functools.partial(state_map, rank))
                for rank in range(ranks)
            ],
            out_specs=pl.BlockSpec((num_tok, chunk * width), lambda i, *_: (0, i)),
        ),
        cost_estimate=pl.CostEstimate(
            flops=2 * num_tok * dim * heads * width * ranks,
            bytes_accessed=ranks * heads * width * dim * 4 + num_tok * heads * width * 2,
            transcendentals=0,
        ),
    )(slot, member, payload, *([cache] * ranks))


def within_kernel(owners, *refs):
    parts = refs[:owners]
    payload, seg_row, seg_col, run, run_t, step_t, gain, base, grown, x_t = refs[owners:]
    num_tok, columns = base.shape
    heads = run.shape[1]
    width = columns // heads
    dim = (payload.shape[1] - LANES) // 2
    down = lax.broadcasted_iota(jnp.int32, (num_tok, num_tok), 0)
    along = lax.broadcasted_iota(jnp.int32, (num_tok, num_tok), 1)
    keep = (seg_row[...] == seg_col[...]) & (down >= along)
    raw = dot16(payload[:, :dim], payload[:, dim : 2 * dim], NT)
    scores = jnp.where(keep, raw, 0.0)
    pair = LANES // width
    lane = lax.broadcasted_iota(jnp.int32, (num_tok, LANES), 1) // width
    for first in range(0, heads, pair):
        at = slice(first * width, (first + pair) * width)
        values = parts[0][:, at].astype(F32)
        for part in parts[1:]:
            values += part[:, at].astype(F32)
        values = values.astype(BF)
        exact = values.astype(F32)
        x_t[at, :] = exact.T.astype(BF)
        total = jnp.zeros((num_tok, LANES), F32)
        rise = jnp.zeros((num_tok, LANES), F32)
        for i in range(pair):
            h = first + i
            run_col = run[:, h : h + 1]
            decay = jnp.exp(jnp.minimum(run_col - run_t[h : h + 1, :], 0.0))
            mixing = (decay * scores * step_t[h : h + 1, :]).astype(BF)
            inner = dot16(mixing, values, NN) + gain[:, h : h + 1] * exact
            total = jnp.where(lane == i, inner, total)
            rise = jnp.where(lane == i, jnp.exp(run_col), rise)
        base[:, at] = total
        grown[:, at] = rise


def within_part(parts, payload, seg, run, run_t, step_t, gain):
    num_tok, columns = parts[0].shape
    heads = run.shape[1]
    return pl.pallas_call(
        functools.partial(within_kernel, len(parts)),
        out_shape=[
            jax.ShapeDtypeStruct((num_tok, columns), F32),
            jax.ShapeDtypeStruct((num_tok, columns), F32),
            jax.ShapeDtypeStruct((columns, num_tok), BF),
        ],
        cost_estimate=pl.CostEstimate(
            flops=2 * num_tok * num_tok * columns * 2,
            bytes_accessed=num_tok * columns * (2 * len(parts) + 10),
            transcendentals=num_tok * num_tok * heads,
        ),
    )(*parts, payload, seg[:, None], seg[None, :], run, run_t, step_t, gain[None])


def states_kernel(owners, which, member, state, *refs):
    x_refs, payloads, out = refs[:owners], refs[owners:-1], refs[-1]
    heads, width, dim = state.shape[1:]
    at = pl.program_id(0)

    def update(x_ref, payload):
        tail = payload[:, 2 * dim :].astype(F32).T
        inside = tail[3 * heads : 3 * heads + 1] == member[at].astype(F32)
        weights = jnp.where(inside, tail[:heads], 0.0)
        rise = tail[heads : 2 * heads] + tail[2 * heads : 3 * heads]
        rise = jnp.max(jnp.where(inside, rise, 0.0), axis=1, keepdims=True)
        b_part = payload[:, dim : 2 * dim]
        for h in range(heads):
            rows = slice(h * width, (h + 1) * width)
            scaled = (x_ref[rows, :].astype(F32) * weights[h : h + 1]).astype(BF)
            out[0, h] = state[0, h] * rise[h : h + 1] + dot16(scaled, b_part, NN)

    for i in range(owners):
        pl.when(which[at] == i)(functools.partial(update, x_refs[i], payloads[i]))

    @pl.when(which[at] < 0)
    def _():
        out[...] = state[...]


def states_part(which, member, cache, x_all, payloads):
    slots, heads, width, dim = cache.shape
    columns, num_tok = x_all[0].shape
    slab = pl.BlockSpec((1, heads, width, dim), lambda s, *_: (s, 0, 0, 0))
    return pl.pallas_call(
        functools.partial(states_kernel, len(x_all)),
        out_shape=jax.ShapeDtypeStruct(cache.shape, cache.dtype),
        grid_spec=pltpu.PrefetchScalarGridSpec(
            num_scalar_prefetch=2,
            grid=(slots,),
            in_specs=[slab]
            + [pl.BlockSpec(x.shape, lambda s, *_: (0, 0)) for x in x_all]
            + [pl.BlockSpec(p.shape, lambda s, *_: (0, 0)) for p in payloads],
            out_specs=slab,
        ),
        cost_estimate=pl.CostEstimate(
            flops=2 * slots * num_tok * columns * dim,
            bytes_accessed=cache.size * 8 + len(x_all) * num_tok * columns * 2,
            transcendentals=0,
        ),
    )(which, member, cache, *x_all, *payloads)


def body(
    tokens,
    w_x,
    w_bc,
    w_dt,
    dt_bias,
    decay_rate,
    skip_gain,
    w_out,
    suffix_lengths,
    checkpoint_slot,
    cache,
):
    reqs = lax.axis_size("req")
    tensors = lax.axis_size("tensor")
    chips = tensors // 2
    own_req = lax.axis_index("req")
    own_tensor = lax.axis_index("tensor")
    own_chip = own_tensor // 2
    core = own_tensor % 2
    num_tok = tokens.shape[0]
    depth = w_x.shape[0]
    slots_dev, heads, width, state_dim = cache.shape
    columns = heads * width
    half = depth // 2

    def token_block(req, start, size):
        return lax.dynamic_slice(tokens, (0, req * depth + start), (num_tok, size))

    near = [token_block(own_req, core * half, half)]
    for k in range(1, reqs):
        near.append(turn_req(token_block((own_req + k) % reqs, core * half, half), k))

    share = depth // tensors
    bc_share = lax.dynamic_slice_in_dim(w_bc, own_tensor * share, share)
    small = spread_out(jnp.concatenate([bc_share, w_dt.T.reshape(-1, w_bc.shape[1])], axis=0))
    bc_tokens = lax.dynamic_index_in_dim(
        tokens.reshape(num_tok, reqs, tensors, share), own_tensor, axis=2, keepdims=False
    )
    state_maps = sum_tensor(
        jnp.dot(
            bc_tokens.reshape(num_tok, reqs * share),
            small[:, :share].reshape(reqs * share, -1),
            preferred_element_type=F32,
        )
    )
    raw_step = jnp.einsum(
        "trk,rhk->th",
        tokens.reshape(num_tok, reqs, depth),
        small[:, share:].reshape(reqs, heads, depth),
        preferred_element_type=F32,
    )
    places = jnp.arange(num_tok, dtype=jnp.int32)
    ends = jnp.cumsum(suffix_lengths[0])
    seg = jnp.sum((places[:, None] >= ends[None, :]).astype(jnp.int32), axis=1)
    payload, run, run_t, step_t = prep(state_maps, raw_step, dt_bias, decay_rate, seg)
    payloads = [payload] + [turn_req(payload, k) for k in range(1, reqs)]

    per_pair = (slots_dev + reqs - 1) // reqs
    total_reqs = checkpoint_slot.shape[0]
    req_dev = total_reqs // reqs
    holder = checkpoint_slot // slots_dev
    index = jnp.arange(total_reqs, dtype=jnp.int32)
    owner = index // req_dev
    pair_key = holder * reqs + owner
    rank_in_pair = jnp.sum(
        (pair_key[:, None] == pair_key[None, :])
        & (checkpoint_slot[None, :] < checkpoint_slot[:, None]),
        axis=1,
    )
    away = (own_req - owner) % reqs
    pairs = jnp.arange(reqs * per_pair, dtype=jnp.int32)
    match = (holder == own_req)[None, :] & (
        (away * per_pair + rank_in_pair)[None, :] == pairs[:, None]
    )

    def pick(match, values, missing):
        found = jnp.sum(jnp.where(match, values[None, :], 0), axis=1)
        return jnp.where(jnp.any(match, axis=1), found, missing).astype(jnp.int32)

    pair_slot = pick(match, checkpoint_slot % slots_dev, 0).reshape(reqs, per_pair)
    pair_member = pick(match, index % req_dev, -1).reshape(reqs, per_pair)
    seg_lane = jnp.full((reqs, 1), 3 * heads, jnp.int32)
    pair_member = jnp.concatenate([pair_member, seg_lane], axis=1)

    w_near = lax.dynamic_slice_in_dim(w_x, core * half, half)
    w_far = lax.dynamic_slice_in_dim(w_x, (1 - core) * half, half)
    parts = []
    for k in range(reqs):
        partial = jnp.dot(near[k], w_near, preferred_element_type=F32) + jnp.dot(
            swap_core(near[k]), w_far, preferred_element_type=F32
        )
        parts.append(partial.astype(BF))
    parts = [parts[0]] + [turn_req(parts[k], -k) for k in range(1, reqs)]

    carried = [
        carried_part(pair_slot[k], pair_member[k], payloads[k], cache) for k in range(reqs)
    ]
    carried = [carried[0]] + [turn_req(carried[k], -k) for k in range(1, reqs)]

    base, grown, x_t = within_part(parts, payload, seg, run, run_t, step_t, skip_gain)
    held = carried[0].astype(F32)
    for k in range(1, reqs):
        held = held + carried[k].astype(F32)
    outputs = (base + grown * held).astype(BF)

    rows_half = num_tok // 2
    arrived = []
    for k in range(reqs):
        block = outputs if k == 0 else turn_req(outputs, k)
        product = jnp.dot(block, w_out, preferred_element_type=F32).astype(BF)
        kept = lax.dynamic_slice_in_dim(product, core * rows_half, rows_half)
        given = lax.dynamic_slice_in_dim(product, (1 - core) * rows_half, rows_half)
        summed = (kept.astype(F32) + swap_core(given).astype(F32)).astype(BF)
        arrived.append(summed if k == 0 else turn_req(summed, -k))

    def column_block(req):
        chosen = arrived[0]
        for k in range(1, reqs):
            chosen = jnp.where((req - own_req) % reqs == k, arrived[k], chosen)
        return chosen

    pair_blocks = [
        jnp.stack([column_block(2 * ((own_chip + turn) % chips) + c) for c in range(2)])
        for turn in range(chips)
    ]
    total = pair_blocks[0].astype(F32)
    for turn in range(1, chips):
        total = total + turn_chip(pair_blocks[turn], turn).astype(F32)
    total = total.astype(BF)
    kept = lax.dynamic_index_in_dim(total, core, axis=0, keepdims=False)
    other = swap_core(lax.dynamic_index_in_dim(total, 1 - core, axis=0, keepdims=False))
    layer_out = jnp.concatenate(
        [jnp.where(core == 0, kept, other), jnp.where(core == 0, other, kept)], axis=0
    )

    x_all = [x_t] + [turn_req(x_t, k) for k in range(1, reqs)]
    slot_ids = own_req * slots_dev + jnp.arange(slots_dev, dtype=jnp.int32)
    match_slot = checkpoint_slot[None, :] == slot_ids[:, None]
    new_cache = states_part(
        pick(match_slot, away, -1), pick(match_slot, index % req_dev, -1), cache, x_all, payloads
    )
    return (layer_out, new_cache)


def solution(mesh):
    placed = (
        P(("groups", "req"), None),
        P("req", "tensor"),
        P("req", None),
        P("req", "tensor"),
        P("tensor"),
        P("tensor"),
        P("tensor"),
        P("tensor", "req"),
        P(("groups", "req"), None),
        P("groups"),
        P(("groups", "req"), "tensor", None, None),
    )
    return jax.shard_map(
        body,
        mesh=mesh,
        in_specs=placed,
        out_specs=(P(("groups", "req"), "tensor"), P(("groups", "req"), "tensor", None, None)),
        check_vma=False,
    )
```

time: 606 us -> 340 us (0.56)
  waiting for transfers between devices: 355 us -> 174 us
  blocking collectives: 121 us -> 0 us
  starting transfers between devices: 11.6 us -> 65.1 us
  Pallas kernels: 0 us -> 40.1 us
  other arithmetic: 36.4 us -> 15.5 us
  matrix products: 44 us -> 25.8 us
  between operations: 14.1 us -> 0.92 us
    all_gather x3 -> x0, waiting for transfers between devices: 343 us -> none  [the longest x1 221 us: body(): lax.all_gather(w_out, 'req', axis=1, tiled=True)]
    ppermute x0 -> x33, waiting for transfers between devices: none -> 174 us  [the longest x21 163 us: turn_req(): lax.ppermute(x, 'req', [(i, (i + turn) % count) for i in range(count)])]
    all_gather x1 -> x0, blocking collectives: 121 us -> none  [body(): lax.all_gather(w_dt, 'req', axis=0, tiled=True)]
    ppermute x0 -> x33, starting transfers between devices: none -> 58.7 us  [the longest x21 53.9 us: turn_req(): lax.ppermute(x, 'req', [(i, (i + turn) % count) for i in range(count)])]
    pallas_call x0 -> x7, Pallas kernels: none -> 40.1 us  [the longest x4 19.6 us: carried_part(): pl.pallas_call(carried_kernel, out_shape=jax.ShapeDtypeStruct((num_tok, h...]
    gather x4 -> x0, local copies, waits for them, and re-layouts: 21.1 us -> none  [the longest x1 6.87 us: body(): jnp.take(arrived, slot_source, axis=0)]
    dot_general x11 -> x14, matrix products: 44 us -> 25.8 us  [the longest x4 8.79 us: body(): jnp.dot(swap_core(near[k]), w_far, preferred_element_type=F32)]
    convert_element_type x5, other arithmetic: 20.5 us -> 6.33 us  [the longest x1 2.46 us: body(): outputs = (base + grown * held).astype(BF)]
  transfers between devices with their start and end apart: 6 -> 34, of which waited for: 3 -> 11; matrix products, arithmetic and copies ran while one was open for 17% -> 14% of each run, Pallas kernels for 0% -> 12%
where the time goes in v2:
time: 340 us
  waiting for transfers between devices  174 us (51%)
  starting transfers between devices  65.1 us (19%)
  Pallas kernels  40.1 us (12%)
  matrix products  25.8 us (8%)
  local copies, waits for them, and re-layouts  17.8 us (5%)
  other arithmetic  15.5 us (5%)
    ppermute x21, waiting for transfers between devices, turn_req(): lax.ppermute(x, 'req', [(i, (i + turn) % count) for i in range(count)])  163 us
    ppermute x21, starting transfers between devices, turn_req(): lax.ppermute(x, 'req', [(i, (i + turn) % count) for i in range(count)])  53.9 us
    pallas_call x4, Pallas kernels, carried_part(): pl.pallas_call(carried_kernel, out_shape=jax.ShapeDtypeStruct((num_tok, h...  19.6 us
    pallas_call x1, Pallas kernels, states_part(): pl.pallas_call(functools.partial(states_kernel, len(x_all)), out_shape=ja...  12.7 us
    ppermute x2, waiting for transfers between devices, turn_chip(): lax.ppermute(x, 'tensor', [(i, (i + 2 * turn) % count) for i in range(cou...  11.6 us
    dot_general x4, matrix products, body(): jnp.dot(swap_core(near[k]), w_far, preferred_element_type=F32)  8.79 us
    dot_general x4, matrix products, body(): jnp.dot(near[k], w_near, preferred_element_type=F32)  8.13 us
  transfers between devices with their start and end apart: 34, of which 11 were waited for; matrix products, arithmetic and copies ran while one was open for 14% of the time, Pallas kernels for 12%

profile of v2, /device:TPU:0, one launch (start us, length us, event | category | flops | bytes accessed | tf_op | source)
XLA Modules:
  0.0 339.8 jit_solution(6242715023035848209)
XLA Ops:
  3.6 6.3 %all-to-all-start = ((bf16[4,400,256]{2,1,0:T(8,128)(2,1)}), bf16[4,400,256]{2,1,0:T(8,128)(2,1)S(1)}, u32[]{:S(2)}, u32[]{:S(2)}) async-start(bf16[4,400,256]{2,1,0:T(8,128)(2,1)} %broadcast_in_dim.77), calls=%async_computation | async-start | bytes 1638400 | tf_op jit(solution)/shard_map/all_to_all | solution.py:37
  9.9 2.4 constant_dynamic-slice_fusion.6
  12.3 3.8 %collective-permute-start.7 = (bf16[256,640]{1,0:T(8,128)(2,1)}, bf16[256,640]{1,0:T(8,128)(2,1)}, u32[]{:S(2)}, u32[]{:S(2)}) collective-permute-start(bf16[256,640]{1,0:T(8,128)(2,1)} %get-tuple-element.26), channel_id=1, source_target_pairs={{0,12},{4,0},{8,4},{12,8},{1,13},{5,1},{9,5},{13,9},{2,14},{6,2},{... | collective-permute-start | bytes 983048 | tf_op jit(solution)/shard_map/ppermute | solution.py:21
  17.3 4.4 %copy.20 = bf16[256,5120]{0,1:T(8,128)(2,1)} copy(bf16[256,5120]{1,0:T(8,128)(2,1)} %param.11) | data formatting | bytes 5242880 | tf_op args[0]
  26.6 32.3 %collective-permute-done.4 = bf16[256,640]{1,0:T(8,128)(2,1)} collective-permute-done((bf16[256,640]{1,0:T(8,128)(2,1)}, bf16[256,640]{1,0:T(8,128)(2,1)}, u32[]{:S(2)}, u32[]{:S(2)}) %collective-permute-start.4) | collective-permute-done | bytes 327712 | tf_op jit(solution)/shard_map/ppermute | solution.py:21
  61.0 2.5 fusion.16
  63.5 2.5 fusion.14
  76.9 3.2 fusion.7.raw
  80.1 3.5 %collective-permute-done.11 = f32[256,256]{1,0:T(8,128)S(1)} collective-permute-done((f32[256,256]{1,0:T(8,128)S(1)}, f32[256,256]{1,0:T(8,128)S(1)}, u32[]{:S(2)}, u32[]{:S(2)}) %collective-permute-start.11) | collective-permute-done | bytes 262176 | tf_op jit(solution)/shard_map/ppermute | solution.py:31
  84.4 2.7 shard_map.122
  90.6 2.7 fusion.6
  93.3 9.3 %collective-permute-done.12.payload.refs_5_ = bf16[256,384]{1,0:T(8,128)(2,1)S(1)} collective-permute-done((bf16[256,384]{1,0:T(8,128)(2,1)}, bf16[256,384]{1,0:T(8,128)(2,1)S(1)}, u32[]{:S(2)}, u32[]{:S(2)}) %collective-permute-start.12) | collective-permute-done | bytes 196640 | tf_op jit(solution)/shard_map/ppermute | solution.py:21
  102.7 6.0 %collective-permute-start.6 = (bf16[256,1024]{1,0:T(8,128)(2,1)}, bf16[256,1024]{1,0:T(8,128)(2,1)}, u32[]{:S(2)}, u32[]{:S(2)}) collective-permute-start(bf16[256,1024]{1,0:T(8,128)(2,1)} %fusion.5), channel_id=1, source_target_pairs={{0,8},{4,12},{8,0},{12,4},{1,9},{5,13},{9,1},{13,5},{2,10},{6,14},... | collective-permute-start | bytes 1572872 | tf_op jit(solution)/shard_map/ppermute | solution.py:21
  108.7 4.9 %shard_map.125 = bf16[256,1024]{1,0:T(8,128)(2,1)} custom-call(s32[3]{0:T(128)} %get-tuple-element.44.slot, s32[4]{0:T(128)} %get-tuple-element.36.member, bf16[256,384]{1,0:T(8,128)(2,1)} %copy-done.5, f32[12,16,64,128]{3,2,1,0:T(8,128)} %state.1, f32[12,16,64,128]{3,2,1,0:T(8,128)} %state.1, f32[12,16,64,128]{3,2,1,0:T(8,128)} %state.1), custom_call_target="tpu_custom_call" | custom-call | flops 201326592 | bytes 2097152 | tf_op jit(solution)/shard_map/pallas_call | solution.py:127
  114.3 4.9 %shard_map.127 = bf16[256,1024]{1,0:T(8,128)(2,1)} custom-call(s32[3]{0:T(128)} %get-tuple-element.42.slot, s32[4]{0:T(128)} %get-tuple-element.38.member, bf16[256,384]{1,0:T(8,128)(2,1)} %copy-done.3, f32[12,16,64,128]{3,2,1,0:T(8,128)} %state.1, f32[12,16,64,128]{3,2,1,0:T(8,128)} %state.1, f32[12,16,64,128]{3,2,1,0:T(8,128)} %state.1), custom_call_target="tpu_custom_call" | custom-call | flops 201326592 | bytes 2097152 | tf_op jit(solution)/shard_map/pallas_call | solution.py:127
  120.0 4.9 %shard_map.126 = bf16[256,1024]{1,0:T(8,128)(2,1)} custom-call(s32[3]{0:T(128)} %get-tuple-element.43.slot, s32[4]{0:T(128)} %get-tuple-element.37.member, bf16[256,384]{1,0:T(8,128)(2,1)} %copy-done.4, f32[12,16,64,128]{3,2,1,0:T(8,128)} %state.1, f32[12,16,64,128]{3,2,1,0:T(8,128)} %state.1, f32[12,16,64,128]{3,2,1,0:T(8,128)} %state.1), custom_call_target="tpu_custom_call" | custom-call | flops 201326592 | bytes 2097152 | tf_op jit(solution)/shard_map/pallas_call | solution.py:127
  124.9 3.1 collective-permute-start.15
  132.0 4.9 %shard_map.124 = bf16[256,1024]{1,0:T(8,128)(2,1)} custom-call(s32[3]{0:T(128)} %get-tuple-element.41.slot, s32[4]{0:T(128)} %get-tuple-element.35.member, bf16[256,384]{1,0:T(8,128)(2,1)} %get-tuple-element.9.refs_4_.payload, f32[12,16,64,128]{3,2,1,0:T(8,128)} %state.1, f32[12,16,64,128]{3,2,1,0:T(8,128)} %state.1, f32[12,16,64,128]{3,2,1,0:T(8,128)} %state.1), custom_call_target="tpu_custom_call" | custom-call | flops 201326592 | bytes 2097152 | tf_op jit(solution)/shard_map/pallas_call | solution.py:127
  136.9 28.7 %collective-permute-done.6.refs_2_ = bf16[256,1024]{1,0:T(8,128)(2,1)} collective-permute-done((bf16[256,1024]{1,0:T(8,128)(2,1)}, bf16[256,1024]{1,0:T(8,128)(2,1)}, u32[]{:S(2)}, u32[]{:S(2)}) %collective-permute-start.6) | collective-permute-done | bytes 524320 | tf_op jit(solution)/shard_map/ppermute | solution.py:21
  165.6 5.1 %shard_map.123 = (f32[256,1024]{1,0:T(8,128)}, f32[256,1024]{1,0:T(8,128)}, bf16[1024,256]{1,0:T(8,128)(2,1)}) custom-call(bf16[256,1024]{1,0:T(8,128)(2,1)} %fusion.3.refs_0_, bf16[256,1024]{1,0:T(8,128)(2,1)} %collective-permute-done.3.refs_1_, bf16[256,1024]{1,0:T(8,128)(2,1)} %collective-permute-done.6.refs_2_, ...), custom_call_target="tpu_custom_call" | custom-call | flops 268435456 | bytes 4718592 | tf_op jit(solution)/shard_map/pallas_call | solution.py:187
  170.7 6.1 %collective-permute-done.15 = bf16[256,1024]{1,0:T(8,128)(2,1)} collective-permute-done((bf16[256,1024]{1,0:T(8,128)(2,1)}, bf16[256,1024]{1,0:T(8,128)(2,1)}, u32[]{:S(2)}, u32[]{:S(2)}) %collective-permute-start.15) | collective-permute-done | bytes 524320 | tf_op jit(solution)/shard_map/ppermute | solution.py:21
  176.9 2.5 add_convert_fusion.1
  179.3 11.6 %collective-permute-start.24 = (bf16[256,1024]{1,0:T(8,128)(2,1)S(1)}, bf16[256,1024]{1,0:T(8,128)(2,1)S(1)}, u32[]{:S(2)}, u32[]{:S(2)}) collective-permute-start(bf16[256,1024]{1,0:T(8,128)(2,1)S(1)} %add_convert_fusion.1), channel_id=1, source_target_pairs={{0,4},{4,8},{8,12},{12,0},{1,5},{5,9},{9,13},{13,1},{2,6},{6,10},{... | collective-permute-start | bytes 1572872 | tf_op jit(solution)/shard_map/ppermute | solution.py:21
  195.1 9.0 %collective-permute-done.24 = bf16[256,1024]{1,0:T(8,128)(2,1)S(1)} collective-permute-done((bf16[256,1024]{1,0:T(8,128)(2,1)S(1)}, bf16[256,1024]{1,0:T(8,128)(2,1)S(1)}, u32[]{:S(2)}, u32[]{:S(2)}) %collective-permute-start.24) | collective-permute-done | bytes 524320 | tf_op jit(solution)/shard_map/ppermute | solution.py:21
  205.1 19.3 %collective-permute-done.21 = bf16[256,1024]{1,0:T(8,128)(2,1)S(1)} collective-permute-done((bf16[256,1024]{1,0:T(8,128)(2,1)S(1)}, bf16[256,1024]{1,0:T(8,128)(2,1)S(1)}, u32[]{:S(2)}, u32[]{:S(2)}) %collective-permute-start.21) | collective-permute-done | bytes 524320 | tf_op jit(solution)/shard_map/ppermute | solution.py:21
  227.6 14.4 %collective-permute-start.26 = (bf16[128,1280]{1,0:T(8,128)(2,1)}, bf16[128,1280]{1,0:T(8,128)(2,1)S(1)}, u32[]{:S(2)}, u32[]{:S(2)}) collective-permute-start(bf16[128,1280]{1,0:T(8,128)(2,1)} %add_convert_fusion.3), channel_id=1, source_target_pairs={{0,12},{4,0},{8,4},{12,8},{1,13},{5,1},{9,5},{13,9},{2,14},{6,2},{... | collective-permute-start | bytes 983048 | tf_op jit(solution)/shard_map/ppermute | solution.py:21
  244.3 6.3 %collective-permute-done.26 = bf16[128,1280]{1,0:T(8,128)(2,1)S(1)} collective-permute-done((bf16[128,1280]{1,0:T(8,128)(2,1)}, bf16[128,1280]{1,0:T(8,128)(2,1)S(1)}, u32[]{:S(2)}, u32[]{:S(2)}) %collective-permute-start.26) | collective-permute-done | bytes 327712 | tf_op jit(solution)/shard_map/ppermute | solution.py:21
  250.6 19.0 %collective-permute-done.23 = bf16[128,1280]{1,0:T(8,128)(2,1)S(1)} collective-permute-done((bf16[128,1280]{1,0:T(8,128)(2,1)}, bf16[128,1280]{1,0:T(8,128)(2,1)S(1)}, u32[]{:S(2)}, u32[]{:S(2)}) %collective-permute-start.23) | collective-permute-done | bytes 327712 | tf_op jit(solution)/shard_map/ppermute | solution.py:21
  275.0 4.4 %collective-permute-start.31 = (bf16[1024,256]{1,0:T(8,128)(2,1)}, bf16[1024,256]{1,0:T(8,128)(2,1)}, u32[]{:S(2)}, u32[]{:S(2)}) collective-permute-start(bf16[1024,256]{1,0:T(8,128)(2,1)} %get-tuple-element.15.refs_0_), channel_id=1, source_target_pairs={{0,8},{4,12},{8,0},{12,4},{1,9},{5,13},{9,1},{13,5},{2,10},{6,14},... | collective-permute-start | bytes 1572872 | tf_op jit(solution)/shard_map/ppermute | solution.py:21
  281.4 8.0 %collective-permute-done.28 = bf16[2,128,1280]{2,1,0:T(8,128)(2,1)} collective-permute-done((bf16[2,128,1280]{2,1,0:T(8,128)(2,1)S(1)}, bf16[2,128,1280]{2,1,0:T(8,128)(2,1)}, u32[]{:S(2)}, u32[]{:S(2)}) %collective-permute-start.28) | collective-permute-done | bytes 655392 | tf_op jit(solution)/shard_map/ppermute | solution.py:31
  292.4 32.8 %collective-permute-done.31.refs_2_ = bf16[1024,256]{1,0:T(8,128)(2,1)} collective-permute-done((bf16[1024,256]{1,0:T(8,128)(2,1)}, bf16[1024,256]{1,0:T(8,128)(2,1)}, u32[]{:S(2)}, u32[]{:S(2)}) %collective-permute-start.31) | collective-permute-done | bytes 524320 | tf_op jit(solution)/shard_map/ppermute | solution.py:21
  325.2 12.7 %shard_map.128 = f32[12,16,64,128]{3,2,1,0:T(8,128)} custom-call(s32[12]{0:T(128)} %get-tuple-element.40.which, s32[12]{0:T(128)} %get-tuple-element.39.member, f32[12,16,64,128]{3,2,1,0:T(8,128)} %state.1, bf16[1024,256]{1,0:T(8,128)(2,1)} %get-tuple-element.15.refs_0_, bf16[1024,256]{1,0:T(8,128)(2,1)} %collective-permute-done.30.refs_1_, ...), custom_call_target="tpu_custom_call" | custom-call | flops 805306368 | bytes 14680064 | tf_op jit(solution)/shard_map/pallas_call | solution.py:231
  (123 shorter events, 54.5 us)
Async XLA Ops:
  3.6 63.9 %all-to-all-start = ((bf16[4,400,256]{2,1,0:T(8,128)(2,1)}), bf16[4,400,256]{2,1,0:T(8,128)(2,1)S(1)}, u32[]{:S(2)}, u32[]{:S(2)}) async-start(bf16[4,400,256]{2,1,0:T(8,128)(2,1)} %broadcast_in_dim.77), calls=%async_computation | async-start | bytes 1638400 | tf_op jit(solution)/shard_map/all_to_all | solution.py:37
  12.3 51.2 %collective-permute-start.7 = (bf16[256,640]{1,0:T(8,128)(2,1)}, bf16[256,640]{1,0:T(8,128)(2,1)}, u32[]{:S(2)}, u32[]{:S(2)}) collective-permute-start(bf16[256,640]{1,0:T(8,128)(2,1)} %get-tuple-element.26), channel_id=1, source_target_pairs={{0,12},{4,0},{8,4},{12,8},{1,13},{5,1},{9,5},{13,9},{2,14},{6,2},{... | collective-permute-start | bytes 983048 | tf_op jit(solution)/shard_map/ppermute | solution.py:21
  16.1 42.8 %collective-permute-start.4 = (bf16[256,640]{1,0:T(8,128)(2,1)}, bf16[256,640]{1,0:T(8,128)(2,1)}, u32[]{:S(2)}, u32[]{:S(2)}) collective-permute-start(bf16[256,640]{1,0:T(8,128)(2,1)} %get-tuple-element.27), channel_id=1, source_target_pairs={{0,8},{4,12},{8,0},{12,4},{1,9},{5,13},{9,1},{13,5},{2,10},{6,14},... | collective-permute-start | bytes 983048 | tf_op jit(solution)/shard_map/ppermute | solution.py:21
  16.1 42.8 %collective-permute-start.1 = (bf16[256,640]{1,0:T(8,128)(2,1)}, bf16[256,640]{1,0:T(8,128)(2,1)}, u32[]{:S(2)}, u32[]{:S(2)}) collective-permute-start(bf16[256,640]{1,0:T(8,128)(2,1)} %get-tuple-element.28), channel_id=1, source_target_pairs={{0,4},{4,8},{8,12},{12,0},{1,5},{5,9},{9,13},{13,1},{2,6},{6,10},{... | collective-permute-start | bytes 983048 | tf_op jit(solution)/shard_map/ppermute | solution.py:21
  17.2 107.7 %collective-permute-start = (bf16[256,640]{1,0:T(8,128)(2,1)}, bf16[256,640]{1,0:T(8,128)(2,1)}, u32[]{:S(2)}, u32[]{:S(2)}) collective-permute-start(bf16[256,640]{1,0:T(8,128)(2,1)} %get-tuple-element.29), channel_id=1, source_target_pairs={{0,1},{1,0},{2,3},{3,2},{4,5},{5,4},{6,7},{7,6},{8,9},{9,8},{10,11... | collective-permute-start | bytes 983048 | tf_op jit(solution)/shard_map/ppermute | solution.py:26
  58.9 11.3 %collective-permute-start.5 = (bf16[256,640]{1,0:T(8,128)(2,1)}, bf16[256,640]{1,0:T(8,128)(2,1)}, u32[]{:S(2)}, u32[]{:S(2)}) collective-permute-start(bf16[256,640]{1,0:T(8,128)(2,1)} %collective-permute-done.4), channel_id=1, source_target_pairs={{0,1},{1,0},{2,3},{3,2},{4,5},{5,4},{6,7},{7,6},{8,9},{9,8},{10,11... | collective-permute-start | bytes 983048 | tf_op jit(solution)/shard_map/ppermute | solution.py:26
  63.5 27.1 %collective-permute-start.8 = (bf16[256,640]{1,0:T(8,128)(2,1)}, bf16[256,640]{1,0:T(8,128)(2,1)}, u32[]{:S(2)}, u32[]{:S(2)}) collective-permute-start(bf16[256,640]{1,0:T(8,128)(2,1)} %collective-permute-done.7), channel_id=1, source_target_pairs={{0,1},{1,0},{2,3},{3,2},{4,5},{5,4},{6,7},{7,6},{8,9},{9,8},{10,11... | collective-permute-start | bytes 983048 | tf_op jit(solution)/shard_map/ppermute | solution.py:26
  67.4 60.6 %collective-permute-start.3 = (bf16[256,1024]{1,0:T(8,128)(2,1)}, bf16[256,1024]{1,0:T(8,128)(2,1)}, u32[]{:S(2)}, u32[]{:S(2)}) collective-permute-start(bf16[256,1024]{1,0:T(8,128)(2,1)} %fusion.4), channel_id=1, source_target_pairs={{0,12},{4,0},{8,4},{12,8},{1,13},{5,1},{9,5},{13,9},{2,14},{6,2},{... | collective-permute-start | bytes 1572872 | tf_op jit(solution)/shard_map/ppermute | solution.py:21
  75.4 8.3 %collective-permute-start.11 = (f32[256,256]{1,0:T(8,128)S(1)}, f32[256,256]{1,0:T(8,128)S(1)}, u32[]{:S(2)}, u32[]{:S(2)}) collective-permute-start(f32[256,256]{1,0:T(8,128)S(1)} %add.248), channel_id=1, source_target_pairs={{0,2},{1,3},{2,0},{3,1},{4,6},{5,7},{6,4},{7,5},{8,10},{9,11},{10,... | collective-permute-start | bytes 786440 | tf_op jit(solution)/shard_map/ppermute | solution.py:31
  87.1 26.5 %collective-permute-start.16 = (bf16[256,384]{1,0:T(8,128)(2,1)}, bf16[256,384]{1,0:T(8,128)(2,1)S(1)}, u32[]{:S(2)}, u32[]{:S(2)}) collective-permute-start(bf16[256,384]{1,0:T(8,128)(2,1)} %get-tuple-element.9.refs_4_.payload), channel_id=1, source_target_pairs={{0,12},{4,0},{8,4},{12,8},{1,13},{5,1},{9,5},{13,9},{2,14},{6,2},{... | collective-permute-start | bytes 589832 | tf_op jit(solution)/shard_map/ppermute | solution.py:21
  89.2 30.1 %collective-permute-start.14 = (bf16[256,384]{1,0:T(8,128)(2,1)}, bf16[256,384]{1,0:T(8,128)(2,1)S(1)}, u32[]{:S(2)}, u32[]{:S(2)}) collective-permute-start(bf16[256,384]{1,0:T(8,128)(2,1)} %get-tuple-element.9.refs_4_.payload), channel_id=1, source_target_pairs={{0,8},{4,12},{8,0},{12,4},{1,9},{5,13},{9,1},{13,5},{2,10},{6,14},... | collective-permute-start | bytes 589832 | tf_op jit(solution)/shard_map/ppermute | solution.py:21
  90.6 12.1 %collective-permute-start.12 = (bf16[256,384]{1,0:T(8,128)(2,1)}, bf16[256,384]{1,0:T(8,128)(2,1)S(1)}, u32[]{:S(2)}, u32[]{:S(2)}) collective-permute-start(bf16[256,384]{1,0:T(8,128)(2,1)} %get-tuple-element.9.refs_4_.payload), channel_id=1, source_target_pairs={{0,4},{4,8},{8,12},{12,0},{1,5},{5,9},{9,13},{13,1},{2,6},{6,10},{... | collective-permute-start | bytes 589832 | tf_op jit(solution)/shard_map/ppermute | solution.py:21
  102.7 62.9 %collective-permute-start.6 = (bf16[256,1024]{1,0:T(8,128)(2,1)}, bf16[256,1024]{1,0:T(8,128)(2,1)}, u32[]{:S(2)}, u32[]{:S(2)}) collective-permute-start(bf16[256,1024]{1,0:T(8,128)(2,1)} %fusion.5), channel_id=1, source_target_pairs={{0,8},{4,12},{8,0},{12,4},{1,9},{5,13},{9,1},{13,5},{2,10},{6,14},... | collective-permute-start | bytes 1572872 | tf_op jit(solution)/shard_map/ppermute | solution.py:21
  113.7 52.0 %collective-permute-start.9 = (bf16[256,1024]{1,0:T(8,128)(2,1)}, bf16[256,1024]{1,0:T(8,128)(2,1)}, u32[]{:S(2)}, u32[]{:S(2)}) collective-permute-start(bf16[256,1024]{1,0:T(8,128)(2,1)} %fusion.6), channel_id=1, source_target_pairs={{0,4},{4,8},{8,12},{12,0},{1,5},{5,9},{9,13},{13,1},{2,6},{6,10},{... | collective-permute-start | bytes 1572872 | tf_op jit(solution)/shard_map/ppermute | solution.py:21
  119.3 51.5 %collective-permute-start.17 = (bf16[256,1024]{1,0:T(8,128)(2,1)}, bf16[256,1024]{1,0:T(8,128)(2,1)}, u32[]{:S(2)}, u32[]{:S(2)}) collective-permute-start(bf16[256,1024]{1,0:T(8,128)(2,1)} %shard_map.127), channel_id=1, source_target_pairs={{0,4},{4,8},{8,12},{12,0},{1,5},{5,9},{9,13},{13,1},{2,6},{6,10},{... | collective-permute-start | bytes 1572872 | tf_op jit(solution)/shard_map/ppermute | solution.py:21
  124.9 51.9 %collective-permute-start.15 = (bf16[256,1024]{1,0:T(8,128)(2,1)}, bf16[256,1024]{1,0:T(8,128)(2,1)}, u32[]{:S(2)}, u32[]{:S(2)}) collective-permute-start(bf16[256,1024]{1,0:T(8,128)(2,1)} %shard_map.126), channel_id=1, source_target_pairs={{0,8},{4,12},{8,0},{12,4},{1,9},{5,13},{9,1},{13,5},{2,10},{6,14},... | collective-permute-start | bytes 1572872 | tf_op jit(solution)/shard_map/ppermute | solution.py:21
  128.0 48.9 %collective-permute-start.13 = (bf16[256,1024]{1,0:T(8,128)(2,1)}, bf16[256,1024]{1,0:T(8,128)(2,1)}, u32[]{:S(2)}, u32[]{:S(2)}) collective-permute-start(bf16[256,1024]{1,0:T(8,128)(2,1)} %shard_map.125), channel_id=1, source_target_pairs={{0,12},{4,0},{8,4},{12,8},{1,13},{5,1},{9,5},{13,9},{2,14},{6,2},{... | collective-permute-start | bytes 1572872 | tf_op jit(solution)/shard_map/ppermute | solution.py:21
  179.3 24.7 %collective-permute-start.24 = (bf16[256,1024]{1,0:T(8,128)(2,1)S(1)}, bf16[256,1024]{1,0:T(8,128)(2,1)S(1)}, u32[]{:S(2)}, u32[]{:S(2)}) collective-permute-start(bf16[256,1024]{1,0:T(8,128)(2,1)S(1)} %add_convert_fusion.1), channel_id=1, source_target_pairs={{0,4},{4,8},{8,12},{12,0},{1,5},{5,9},{9,13},{13,1},{2,6},{6,10},{... | collective-permute-start | bytes 1572872 | tf_op jit(solution)/shard_map/ppermute | solution.py:21
  190.9 33.4 %collective-permute-start.21 = (bf16[256,1024]{1,0:T(8,128)(2,1)S(1)}, bf16[256,1024]{1,0:T(8,128)(2,1)S(1)}, u32[]{:S(2)}, u32[]{:S(2)}) collective-permute-start(bf16[256,1024]{1,0:T(8,128)(2,1)S(1)} %add_convert_fusion.1), channel_id=1, source_target_pairs={{0,8},{4,12},{8,0},{12,4},{1,9},{5,13},{9,1},{13,5},{2,10},{6,14},... | collective-permute-start | bytes 1572872 | tf_op jit(solution)/shard_map/ppermute | solution.py:21
  191.6 33.7 %collective-permute-start.18 = (bf16[256,1024]{1,0:T(8,128)(2,1)S(1)}, bf16[256,1024]{1,0:T(8,128)(2,1)S(1)}, u32[]{:S(2)}, u32[]{:S(2)}) collective-permute-start(bf16[256,1024]{1,0:T(8,128)(2,1)S(1)} %add_convert_fusion.1), channel_id=1, source_target_pairs={{0,12},{4,0},{8,4},{12,8},{1,13},{5,1},{9,5},{13,9},{2,14},{6,2},{... | collective-permute-start | bytes 1572872 | tf_op jit(solution)/shard_map/ppermute | solution.py:21
  195.1 49.2 %collective-permute-start.27 = (bf16[128,1280]{1,0:T(8,128)(2,1)}, bf16[128,1280]{1,0:T(8,128)(2,1)}, u32[]{:S(2)}, u32[]{:S(2)}) collective-permute-start(bf16[128,1280]{1,0:T(8,128)(2,1)} %constant_dynamic-slice_fusion), channel_id=1, source_target_pairs={{0,1},{1,0},{2,3},{3,2},{4,5},{5,4},{6,7},{7,6},{8,9},{9,8},{10,11... | collective-permute-start | bytes 983048 | tf_op jit(solution)/shard_map/ppermute | solution.py:26
  205.0 21.8 %collective-permute-start.25 = (bf16[128,1280]{1,0:T(8,128)(2,1)S(1)}, bf16[128,1280]{1,0:T(8,128)(2,1)S(1)}, u32[]{:S(2)}, u32[]{:S(2)}) collective-permute-start(bf16[128,1280]{1,0:T(8,128)(2,1)S(1)} %constant_dynamic-slice_fusion.1), channel_id=1, source_target_pairs={{0,1},{1,0},{2,3},{3,2},{4,5},{5,4},{6,7},{7,6},{8,9},{9,8},{10,11... | collective-permute-start | bytes 983048 | tf_op jit(solution)/shard_map/ppermute | solution.py:26
  225.3 16.8 %collective-permute-start.22 = (bf16[128,1280]{1,0:T(8,128)(2,1)S(1)}, bf16[128,1280]{1,0:T(8,128)(2,1)S(1)}, u32[]{:S(2)}, u32[]{:S(2)}) collective-permute-start(bf16[128,1280]{1,0:T(8,128)(2,1)S(1)} %constant_dynamic-slice_fusion.2), channel_id=1, source_target_pairs={{0,1},{1,0},{2,3},{3,2},{4,5},{5,4},{6,7},{7,6},{8,9},{9,8},{10,11... | collective-permute-start | bytes 983048 | tf_op jit(solution)/shard_map/ppermute | solution.py:26
  226.3 16.6 %collective-permute-start.19 = (bf16[128,1280]{1,0:T(8,128)(2,1)S(1)}, bf16[128,1280]{1,0:T(8,128)(2,1)S(1)}, u32[]{:S(2)}, u32[]{:S(2)}) collective-permute-start(bf16[128,1280]{1,0:T(8,128)(2,1)S(1)} %constant_dynamic-slice_fusion.3), channel_id=1, source_target_pairs={{0,1},{1,0},{2,3},{3,2},{4,5},{5,4},{6,7},{7,6},{8,9},{9,8},{10,11... | collective-permute-start | bytes 983048 | tf_op jit(solution)/shard_map/ppermute | solution.py:26
  227.6 22.9 %collective-permute-start.26 = (bf16[128,1280]{1,0:T(8,128)(2,1)}, bf16[128,1280]{1,0:T(8,128)(2,1)S(1)}, u32[]{:S(2)}, u32[]{:S(2)}) collective-permute-start(bf16[128,1280]{1,0:T(8,128)(2,1)} %add_convert_fusion.3), channel_id=1, source_target_pairs={{0,12},{4,0},{8,4},{12,8},{1,13},{5,1},{9,5},{13,9},{2,14},{6,2},{... | collective-permute-start | bytes 983048 | tf_op jit(solution)/shard_map/ppermute | solution.py:21
  242.9 26.7 %collective-permute-start.23 = (bf16[128,1280]{1,0:T(8,128)(2,1)}, bf16[128,1280]{1,0:T(8,128)(2,1)S(1)}, u32[]{:S(2)}, u32[]{:S(2)}) collective-permute-start(bf16[128,1280]{1,0:T(8,128)(2,1)} %add_convert_fusion.4), channel_id=1, source_target_pairs={{0,8},{4,12},{8,0},{12,4},{1,9},{5,13},{9,1},{13,5},{2,10},{6,14},... | collective-permute-start | bytes 983048 | tf_op jit(solution)/shard_map/ppermute | solution.py:21
  243.7 25.9 %collective-permute-start.20 = (bf16[128,1280]{1,0:T(8,128)(2,1)}, bf16[128,1280]{1,0:T(8,128)(2,1)}, u32[]{:S(2)}, u32[]{:S(2)}) collective-permute-start(bf16[128,1280]{1,0:T(8,128)(2,1)} %add_convert_fusion.5), channel_id=1, source_target_pairs={{0,4},{4,8},{8,12},{12,0},{1,5},{5,9},{9,13},{13,1},{2,6},{6,10},{... | collective-permute-start | bytes 983048 | tf_op jit(solution)/shard_map/ppermute | solution.py:21
  273.5 16.0 %collective-permute-start.28 = (bf16[2,128,1280]{2,1,0:T(8,128)(2,1)S(1)}, bf16[2,128,1280]{2,1,0:T(8,128)(2,1)}, u32[]{:S(2)}, u32[]{:S(2)}) collective-permute-start(bf16[2,128,1280]{2,1,0:T(8,128)(2,1)S(1)} %pad_maximum_fusion), channel_id=1, source_target_pairs={{0,2},{1,3},{2,0},{3,1},{4,6},{5,7},{6,4},{7,5},{8,10},{9,11},{10,... | collective-permute-start | bytes 1966088 | tf_op jit(solution)/shard_map/ppermute | solution.py:31
  275.0 17.4 %collective-permute-start.32 = (bf16[1024,256]{1,0:T(8,128)(2,1)}, bf16[1024,256]{1,0:T(8,128)(2,1)}, u32[]{:S(2)}, u32[]{:S(2)}) collective-permute-start(bf16[1024,256]{1,0:T(8,128)(2,1)} %get-tuple-element.15.refs_0_), channel_id=1, source_target_pairs={{0,12},{4,0},{8,4},{12,8},{1,13},{5,1},{9,5},{13,9},{2,14},{6,2},{... | collective-permute-start | bytes 1572872 | tf_op jit(solution)/shard_map/ppermute | solution.py:21
  275.0 50.1 %collective-permute-start.31 = (bf16[1024,256]{1,0:T(8,128)(2,1)}, bf16[1024,256]{1,0:T(8,128)(2,1)}, u32[]{:S(2)}, u32[]{:S(2)}) collective-permute-start(bf16[1024,256]{1,0:T(8,128)(2,1)} %get-tuple-element.15.refs_0_), channel_id=1, source_target_pairs={{0,8},{4,12},{8,0},{12,4},{1,9},{5,13},{9,1},{13,5},{2,10},{6,14},... | collective-permute-start | bytes 1572872 | tf_op jit(solution)/shard_map/ppermute | solution.py:21
  279.4 45.8 %collective-permute-start.30 = (bf16[1024,256]{1,0:T(8,128)(2,1)}, bf16[1024,256]{1,0:T(8,128)(2,1)}, u32[]{:S(2)}, u32[]{:S(2)}) collective-permute-start(bf16[1024,256]{1,0:T(8,128)(2,1)} %get-tuple-element.15.refs_0_), channel_id=1, source_target_pairs={{0,4},{4,8},{8,12},{12,0},{1,5},{5,9},{9,13},{13,1},{2,6},{6,10},{... | collective-permute-start | bytes 1572872 | tf_op jit(solution)/shard_map/ppermute | solution.py:21
  291.6 46.2 %collective-permute-start.29 = (bf16[128,1280]{1,0:T(8,128)(2,1)}, bf16[128,1280]{1,0:T(8,128)(2,1)}, u32[]{:S(2)}, u32[]{:S(2)}) collective-permute-start(bf16[128,1280]{1,0:T(8,128)(2,1)} %dynamic-slice_bitcast_fusion), channel_id=1, source_target_pairs={{0,1},{1,0},{2,3},{3,2},{4,5},{5,4},{6,7},{7,6},{8,9},{9,8},{10,11... | collective-permute-start | bytes 983048 | tf_op jit(solution)/shard_map/ppermute | solution.py:26
  (13 other events, 214.7 us)

commit v3 on v2

--- a/solution.py
+++ b/solution.py
@@ -21,6 +21,36 @@
     return lax.ppermute(x, "req", [(i, (i + turn) % count) for i in range(count)])
 
 
+def step_up(x, first, last):
+    return lax.ppermute(x, "req", [(i, i + 1) for i in range(first, last)])
+
+
+def step_down(x, first, last):
+    top = lax.axis_size("req") - 1
+    return lax.ppermute(x, "req", [(top - i, top - i - 1) for i in range(first, last)])
+
+
+def line_gather(x):
+    count = lax.axis_size("req")
+    below, above = [], []
+    low = high = x
+    for hop in range(count - 1):
+        low, high = step_up(low, hop, count - 1), step_down(high, hop, count - 1)
+        below.append(low)
+        above.append(high)
+    return below, above
+
+
+def line_sum(blocks):
+    count = lax.axis_size("req")
+    low, high = blocks[1], blocks[count - 1]
+    for hop in range(1, count):
+        if hop > 1:
+            low, high = low + blocks[hop], high + blocks[count - hop]
+        low, high = step_up(low, 0, hop), step_down(high, 0, hop)
+    return blocks[0], low, high
+
+
 def swap_core(x):
     count = lax.axis_size("tensor")
     return lax.ppermute(x, "tensor", [(i, i ^ 1) for i in range(count)])
@@ -53,7 +83,7 @@
     return lax.dot_general(a, b, dims, preferred_element_type=F32)
 
 
-def prep_kernel(maps, raw, bias, rate, seg_row, seg_col, payload, run, run_t, step_t):
+def prep_kernel(maps, raw, bias, rate, seg_row, seg_col, payload, b_part, run, run_t, step_t):
     num_tok, heads = raw.shape
     dim = maps.shape[1] // 2
     z = raw[...] + bias[...]
@@ -73,7 +103,7 @@
     high = grown.astype(BF)
     low = (grown - high.astype(F32)).astype(BF)
     payload[:, :dim] = maps[:, dim:].astype(BF)
-    payload[:, dim : 2 * dim] = maps[:, :dim].astype(BF)
+    b_part[...] = maps[:, :dim].astype(BF)
     head = lax.broadcasted_iota(jnp.int32, (heads, LANES), 0)
     lane = lax.broadcasted_iota(jnp.int32, (heads, LANES), 1)
     tail = jnp.zeros((num_tok, LANES), F32)
@@ -81,7 +111,7 @@
         tail += dot16(part, (lane == head + i * heads).astype(BF), NN)
     seg_lane = lax.broadcasted_iota(jnp.int32, (num_tok, LANES), 1) == 3 * heads
     tail = jnp.where(seg_lane, seg_row[...].astype(F32), tail)
-    payload[:, 2 * dim :] = tail.astype(BF)
+    payload[:, dim:] = tail.astype(BF)
 
 
 def prep(maps, raw, bias, rate, seg):
@@ -89,7 +119,8 @@
     return pl.pallas_call(
         prep_kernel,
         out_shape=[
-            jax.ShapeDtypeStruct((num_tok, maps.shape[1] + LANES), BF),
+            jax.ShapeDtypeStruct((num_tok, maps.shape[1] // 2 + LANES), BF),
+            jax.ShapeDtypeStruct((num_tok, maps.shape[1] // 2), BF),
             jax.ShapeDtypeStruct((num_tok, heads), F32),
             jax.ShapeDtypeStruct((heads, num_tok), F32),
             jax.ShapeDtypeStruct((heads, num_tok), F32),
@@ -118,24 +149,23 @@
 def carried_part(slot, member, payload, cache):
     num_tok = payload.shape[0]
     _, heads, width, dim = cache.shape
-    chunk = min(heads, 4)
     ranks = slot.shape[0]
 
     def state_map(rank, i, slot, member):
-        return (slot[rank], i, 0, 0)
+        return (slot[rank], 0, 0, 0)
 
     return pl.pallas_call(
         carried_kernel,
         out_shape=jax.ShapeDtypeStruct((num_tok, heads * width), BF),
         grid_spec=pltpu.PrefetchScalarGridSpec(
             num_scalar_prefetch=2,
-            grid=(heads // chunk,),
+            grid=(1,),
             in_specs=[pl.BlockSpec(payload.shape, lambda i, *_: (0, 0))]
             + [
-                pl.BlockSpec((1, chunk, width, dim), functools.partial(state_map, rank))
+                pl.BlockSpec((1, heads, width, dim), functools.partial(state_map, rank))
                 for rank in range(ranks)
             ],
-            out_specs=pl.BlockSpec((num_tok, chunk * width), lambda i, *_: (0, i)),
+            out_specs=pl.BlockSpec((num_tok, heads * width), lambda i, *_: (0, 0)),
         ),
         cost_estimate=pl.CostEstimate(
             flops=2 * num_tok * dim * heads * width * ranks,
@@ -145,28 +175,22 @@
     )(slot, member, payload, *([cache] * ranks))
 
 
-def within_kernel(owners, *refs):
-    parts = refs[:owners]
-    payload, seg_row, seg_col, run, run_t, step_t, gain, base, grown, x_t = refs[owners:]
+def within_kernel(x, payload, b_part, seg_row, seg_col, run, run_t, step_t, gain, base, grown):
     num_tok, columns = base.shape
     heads = run.shape[1]
     width = columns // heads
-    dim = (payload.shape[1] - LANES) // 2
+    dim = b_part.shape[1]
     down = lax.broadcasted_iota(jnp.int32, (num_tok, num_tok), 0)
     along = lax.broadcasted_iota(jnp.int32, (num_tok, num_tok), 1)
     keep = (seg_row[...] == seg_col[...]) & (down >= along)
-    raw = dot16(payload[:, :dim], payload[:, dim : 2 * dim], NT)
+    raw = dot16(payload[:, :dim], b_part[...], NT)
     scores = jnp.where(keep, raw, 0.0)
     pair = LANES // width
     lane = lax.broadcasted_iota(jnp.int32, (num_tok, LANES), 1) // width
     for first in range(0, heads, pair):
         at = slice(first * width, (first + pair) * width)
-        values = parts[0][:, at].astype(F32)
-        for part in parts[1:]:
-            values += part[:, at].astype(F32)
-        values = values.astype(BF)
+        values = x[:, at]
         exact = values.astype(F32)
-        x_t[at, :] = exact.T.astype(BF)
         total = jnp.zeros((num_tok, LANES), F32)
         rise = jnp.zeros((num_tok, LANES), F32)
         for i in range(pair):
@@ -181,62 +205,61 @@
         grown[:, at] = rise
 
 
-def within_part(parts, payload, seg, run, run_t, step_t, gain):
-    num_tok, columns = parts[0].shape
+def within_part(x, payload, b_part, seg, run, run_t, step_t, gain):
+    num_tok, columns = x.shape
     heads = run.shape[1]
     return pl.pallas_call(
-        functools.partial(within_kernel, len(parts)),
-        out_shape=[
-            jax.ShapeDtypeStruct((num_tok, columns), F32),
-            jax.ShapeDtypeStruct((num_tok, columns), F32),
-            jax.ShapeDtypeStruct((columns, num_tok), BF),
-        ],
+        within_kernel,
+        out_shape=[jax.ShapeDtypeStruct((num_tok, columns), F32)] * 2,
         cost_estimate=pl.CostEstimate(
             flops=2 * num_tok * num_tok * columns * 2,
-            bytes_accessed=num_tok * columns * (2 * len(parts) + 10),
+            bytes_accessed=num_tok * columns * 10,
             transcendentals=num_tok * num_tok * heads,
         ),
-    )(*parts, payload, seg[:, None], seg[None, :], run, run_t, step_t, gain[None])
+    )(x, payload, b_part, seg[:, None], seg[None, :], run, run_t, step_t, gain[None])
 
 
 def states_kernel(owners, which, member, state, *refs):
-    x_refs, payloads, out = refs[:owners], refs[owners:-1], refs[-1]
+    sources = 2 * owners - 1
+    x_refs, refs, out = refs[:sources], refs[sources:-1], refs[-1]
+    payloads, b_parts = refs[:owners], refs[owners:]
     heads, width, dim = state.shape[1:]
     at = pl.program_id(0)
 
-    def update(x_ref, payload):
-        tail = payload[:, 2 * dim :].astype(F32).T
+    def update(x_ref, payload, b_part):
+        tail = payload[:, dim:].astype(F32).T
         inside = tail[3 * heads : 3 * heads + 1] == member[at].astype(F32)
         weights = jnp.where(inside, tail[:heads], 0.0)
         rise = tail[heads : 2 * heads] + tail[2 * heads : 3 * heads]
         rise = jnp.max(jnp.where(inside, rise, 0.0), axis=1, keepdims=True)
-        b_part = payload[:, dim : 2 * dim]
         for h in range(heads):
             rows = slice(h * width, (h + 1) * width)
             scaled = (x_ref[rows, :].astype(F32) * weights[h : h + 1]).astype(BF)
-            out[0, h] = state[0, h] * rise[h : h + 1] + dot16(scaled, b_part, NN)
-
-    for i in range(owners):
-        pl.when(which[at] == i)(functools.partial(update, x_refs[i], payloads[i]))
+            out[0, h] = state[0, h] * rise[h : h + 1] + dot16(scaled, b_part[...], NN)
+
+    for i in range(sources):
+        away = i if i < owners else 2 * owners - 1 - i
+        pl.when(which[at] == i)(
+            functools.partial(update, x_refs[i], payloads[away], b_parts[away])
+        )
 
     @pl.when(which[at] < 0)
     def _():
         out[...] = state[...]
 
 
-def states_part(which, member, cache, x_all, payloads):
+def states_part(which, member, cache, x_all, payloads, b_parts):
     slots, heads, width, dim = cache.shape
     columns, num_tok = x_all[0].shape
     slab = pl.BlockSpec((1, heads, width, dim), lambda s, *_: (s, 0, 0, 0))
+    fixed = [*x_all, *payloads, *b_parts]
     return pl.pallas_call(
-        functools.partial(states_kernel, len(x_all)),
+        functools.partial(states_kernel, len(payloads)),
         out_shape=jax.ShapeDtypeStruct(cache.shape, cache.dtype),
         grid_spec=pltpu.PrefetchScalarGridSpec(
             num_scalar_prefetch=2,
             grid=(slots,),
-            in_specs=[slab]
-            + [pl.BlockSpec(x.shape, lambda s, *_: (0, 0)) for x in x_all]
-            + [pl.BlockSpec(p.shape, lambda s, *_: (0, 0)) for p in payloads],
+            in_specs=[slab] + [pl.BlockSpec(x.shape, lambda s, *_: (0, 0)) for x in fixed],
             out_specs=slab,
         ),
         cost_estimate=pl.CostEstimate(
@@ -244,7 +267,7 @@
             bytes_accessed=cache.size * 8 + len(x_all) * num_tok * columns * 2,
             transcendentals=0,
         ),
-    )(which, member, cache, *x_all, *payloads)
+    )(which, member, cache, *fixed)
 
 
 def body(
@@ -272,13 +295,18 @@
     slots_dev, heads, width, state_dim = cache.shape
     columns = heads * width
     half = depth // 2
-
-    def token_block(req, start, size):
-        return lax.dynamic_slice(tokens, (0, req * depth + start), (num_tok, size))
-
-    near = [token_block(own_req, core * half, half)]
+    piece = num_tok // chips
+
+    def chip_rows(x, place):
+        return lax.dynamic_slice_in_dim(x, ((own_chip - place) % chips) * piece, piece)
+
+    near = []
     for k in range(1, reqs):
-        near.append(turn_req(token_block((own_req + k) % reqs, core * half, half), k))
+        start = ((own_req + k) % reqs) * depth + core * half
+        block = lax.dynamic_slice(tokens, (own_chip * piece, start), (piece, half))
+        block = turn_req(block, k)
+        pieces = [block] + [turn_chip(block, turn) for turn in range(1, chips)]
+        near.append(jnp.concatenate(pieces, axis=0))
 
     share = depth // tensors
     bc_share = lax.dynamic_slice_in_dim(w_bc, own_tensor * share, share)
@@ -302,8 +330,9 @@
     places = jnp.arange(num_tok, dtype=jnp.int32)
     ends = jnp.cumsum(suffix_lengths[0])
     seg = jnp.sum((places[:, None] >= ends[None, :]).astype(jnp.int32), axis=1)
-    payload, run, run_t, step_t = prep(state_maps, raw_step, dt_bias, decay_rate, seg)
+    payload, b_part, run, run_t, step_t = prep(state_maps, raw_step, dt_bias, decay_rate, seg)
     payloads = [payload] + [turn_req(payload, k) for k in range(1, reqs)]
+    b_parts = [b_part] + [turn_req(b_part, k) for k in range(1, reqs)]
 
     per_pair = (slots_dev + reqs - 1) // reqs
     total_reqs = checkpoint_slot.shape[0]
@@ -334,34 +363,42 @@
 
     w_near = lax.dynamic_slice_in_dim(w_x, core * half, half)
     w_far = lax.dynamic_slice_in_dim(w_x, (1 - core) * half, half)
-    parts = []
-    for k in range(reqs):
-        partial = jnp.dot(near[k], w_near, preferred_element_type=F32) + jnp.dot(
-            swap_core(near[k]), w_far, preferred_element_type=F32
+    own_block = lax.dynamic_slice(tokens, (0, own_req * depth), (num_tok, depth))
+    own_block = jnp.concatenate([chip_rows(own_block, place) for place in range(chips)], axis=0)
+    total = jnp.dot(own_block, w_x, preferred_element_type=F32)
+    for k in range(1, reqs):
+        partial = jnp.dot(near[k - 1], w_near, preferred_element_type=F32) + jnp.dot(
+            swap_core(near[k - 1]), w_far, preferred_element_type=F32
         )
-        parts.append(partial.astype(BF))
-    parts = [parts[0]] + [turn_req(parts[k], -k) for k in range(1, reqs)]
-
-    carried = [
-        carried_part(pair_slot[k], pair_member[k], payloads[k], cache) for k in range(reqs)
-    ]
-    carried = [carried[0]] + [turn_req(carried[k], -k) for k in range(1, reqs)]
-
-    base, grown, x_t = within_part(parts, payload, seg, run, run_t, step_t, skip_gain)
-    held = carried[0].astype(F32)
-    for k in range(1, reqs):
-        held = held + carried[k].astype(F32)
+        total = total + turn_req(partial.astype(BF), -k).astype(F32)
+    values = total.astype(BF)
+    values = jnp.concatenate([chip_rows(values, place) for place in range(chips)], axis=0)
+
+    carried = line_sum(
+        [carried_part(pair_slot[k], pair_member[k], payloads[k], cache) for k in range(reqs)]
+    )
+
+    base, grown = within_part(values, payload, b_part, seg, run, run_t, step_t, skip_gain)
+    held = sum(block.astype(F32) for block in carried)
     outputs = (base + grown * held).astype(BF)
 
     rows_half = num_tok // 2
-    arrived = []
-    for k in range(reqs):
-        block = outputs if k == 0 else turn_req(outputs, k)
+
+    def project(block):
         product = jnp.dot(block, w_out, preferred_element_type=F32).astype(BF)
         kept = lax.dynamic_slice_in_dim(product, core * rows_half, rows_half)
         given = lax.dynamic_slice_in_dim(product, (1 - core) * rows_half, rows_half)
-        summed = (kept.astype(F32) + swap_core(given).astype(F32)).astype(BF)
-        arrived.append(summed if k == 0 else turn_req(summed, -k))
+        return (kept.astype(F32) + swap_core(given).astype(F32)).astype(BF)
+
+    below, above = line_gather(outputs)
+    arrived = [project(outputs)]
+    from_above, from_below = [], []
+    for k in range(1, reqs):
+        down = [(i, i - k) for i in range(k, reqs)]
+        up = [(i, i + k) for i in range(reqs - k)]
+        from_above.append(lax.ppermute(project(below[k - 1]), "req", down))
+        from_below.append(lax.ppermute(project(above[k - 1]), "req", up))
+    arrived += [from_above[k] + from_below[reqs - 2 - k] for k in range(reqs - 1)]
 
     def column_block(req):
         chosen = arrived[0]
@@ -383,11 +420,18 @@
         [jnp.where(core == 0, kept, other), jnp.where(core == 0, other, kept)], axis=0
     )
 
-    x_all = [x_t] + [turn_req(x_t, k) for k in range(1, reqs)]
+    x_t = values.T
+    x_below, x_above = line_gather(x_t)
+    which = jnp.where(owner <= own_req, own_req - owner, reqs - 1 + owner - own_req)
     slot_ids = own_req * slots_dev + jnp.arange(slots_dev, dtype=jnp.int32)
     match_slot = checkpoint_slot[None, :] == slot_ids[:, None]
     new_cache = states_part(
-        pick(match_slot, away, -1), pick(match_slot, index % req_dev, -1), cache, x_all, payloads
+        pick(match_slot, which, -1),
+        pick(match_slot, index % req_dev, -1),
+        cache,
+        [x_t, *x_below, *x_above],
+        payloads,
+        b_parts,
     )
     return (layer_out, new_cache)
 

time: 340 us -> 315 us (0.926); the launches traced: 340 us -> 311 us
  waiting for transfers between devices: 174 us -> 95.2 us
  starting transfers between devices: 65.1 us -> 98.7 us
  local copies, waits for them, and re-layouts: 17.8 us -> 29.3 us
  other arithmetic: 15.5 us -> 23.1 us
  Pallas kernels: 40.1 us -> 34.3 us
    ppermute x21 -> x12, waiting for transfers between devices: 163 us -> 35 us  [turn_req(): lax.ppermute(x, 'req', [(i, (i + turn) % count) for i in range(count)])]
    ppermute x0 -> x24, starting transfers between devices: none -> 60 us  [the longest x9 26.9 us: step_up(): return lax.ppermute(x, 'req', [(i, i + 1) for i in range(first, last)])]
    ppermute x0 -> x24, waiting for transfers between devices: none -> 51.4 us  [the longest x9 28.2 us: step_down(): lax.ppermute(x, 'req', [(top - i, top - i - 1) for i in range(first, last)])]
    ppermute x21 -> x12, starting transfers between devices: 53.9 us -> 25.8 us  [turn_req(): lax.ppermute(x, 'req', [(i, (i + turn) % count) for i in range(count)])]
    unnamed x23 -> x54, local copies, waits for them, and re-layouts: 5.05 us -> 12.6 us
    pallas_call x4, Pallas kernels: 19.6 us -> 14.2 us  [carried_part(): pl.pallas_call(carried_kernel, out_shape=jax.ShapeDtypeStruct((num_tok, h...]
    ppermute x2 -> x5, starting transfers between devices: 3.11 us -> 7.86 us  [turn_chip(): lax.ppermute(x, 'tensor', [(i, (i + 2 * turn) % count) for i in range(cou...]
    ppermute x2 -> x5, waiting for transfers between devices: 11.6 us -> 7.37 us  [turn_chip(): lax.ppermute(x, 'tensor', [(i, (i + 2 * turn) % count) for i in range(cou...]
  transfers between devices with their start and end apart: 34 -> 54, of which waited for: 11 -> 19; matrix products, arithmetic and copies ran while one was open for 14% -> 23% of each run, Pallas kernels for 12% -> 11%
where the time goes in v3:
time: 315 us; the launch traced here: 311 us
  starting transfers between devices  98.7 us (31%)
  waiting for transfers between devices  95.2 us (30%)
  Pallas kernels  34.3 us (11%)
  local copies, waits for them, and re-layouts  29.3 us (9%)
  matrix products  28.8 us (9%)
  other arithmetic  23.1 us (7%)
    ppermute x12, waiting for transfers between devices, turn_req(): lax.ppermute(x, 'req', [(i, (i + turn) % count) for i in range(count)])  35 us
    ppermute x9, waiting for transfers between devices, step_down(): lax.ppermute(x, 'req', [(top - i, top - i - 1) for i in range(first, last)])  28.2 us
    ppermute x9, starting transfers between devices, step_up(): return lax.ppermute(x, 'req', [(i, i + 1) for i in range(first, last)])  26.9 us
    ppermute x12, starting transfers between devices, turn_req(): lax.ppermute(x, 'req', [(i, (i + turn) % count) for i in range(count)])  25.8 us
    ppermute x3, starting transfers between devices, body(): from_below.append(lax.ppermute(project(above[k - 1]), 'req', up))  18.3 us
    ppermute x9, waiting for transfers between devices, step_up(): return lax.ppermute(x, 'req', [(i, i + 1) for i in range(first, last)])  16.6 us
    pallas_call x4, Pallas kernels, carried_part(): pl.pallas_call(carried_kernel, out_shape=jax.ShapeDtypeStruct((num_tok, h...  14.2 us
    pallas_call x1, Pallas kernels, states_part(): pl.pallas_call(functools.partial(states_kernel, len(payloads)), out_shape...  13.2 us
  transfers between devices with their start and end apart: 54, of which 19 were waited for; matrix products, arithmetic and copies ran while one was open for 23% of the time, Pallas kernels for 11%

profile of v3, /device:TPU:0, one launch (start us, length us, event | category | flops | bytes accessed | tf_op | source)
XLA Modules:
  0.0 311.0 jit_solution(8597418428343907926)
XLA Ops:
  2.7 3.0 collective-permute-start
  11.6 3.5 %all-to-all-start = ((bf16[4,400,256]{2,1,0:T(8,128)(2,1)}), bf16[4,400,256]{2,1,0:T(8,128)(2,1)S(1)}, u32[]{:S(2)}, u32[]{:S(2)}) async-start(bf16[4,400,256]{2,1,0:T(8,128)(2,1)} %broadcast_in_dim.77), calls=%async_computation | async-start | bytes 1638400 | tf_op jit(solution)/shard_map/all_to_all | solution.py:67
  15.1 4.4 %copy.43 = bf16[256,5120]{0,1:T(8,128)(2,1)} copy(bf16[256,5120]{1,0:T(8,128)(2,1)} %param.11) | data formatting | bytes 5242880 | tf_op args[0]
  24.4 3.4 %collective-permute-done.4 = bf16[128,640]{1,0:T(8,128)(2,1)} collective-permute-done((bf16[128,640]{1,0:T(8,128)(2,1)}, bf16[128,640]{1,0:T(8,128)(2,1)}, u32[]{:S(2)}, u32[]{:S(2)}) %collective-permute-start.4) | collective-permute-done | bytes 163872 | tf_op jit(solution)/shard_map/ppermute | solution.py:21
  57.3 3.2 %fusion.6.raw = f32[256,16]{1,0:T(8,128)} fusion(bf16[4,16,1280]{2,1,0:T(8,128)(2,1)S(1)} %reshape.120, bf16[32,4,8,1280]{3,2,1,0:T(8,128)(2,1)} %bitcast.68), kind=kOutput, calls=%fused_computation.17 | convolution fusion | flops 41943040 | bytes 2801664 | tf_op jit(solution)/shard_map/trk,rhk->th/dot_general | solution.py:324
  60.5 3.5 %collective-permute-done.13 = f32[256,256]{1,0:T(8,128)S(1)} collective-permute-done((f32[256,256]{1,0:T(8,128)S(1)}, f32[256,256]{1,0:T(8,128)S(1)}, u32[]{:S(2)}, u32[]{:S(2)}) %collective-permute-start.13) | collective-permute-done | bytes 262176 | tf_op jit(solution)/shard_map/ppermute | solution.py:61
  67.5 3.3 %collective-permute-start.18 = (bf16[256,256]{1,0:T(8,128)(2,1)}, bf16[256,256]{1,0:T(8,128)(2,1)S(1)}, u32[]{:S(2)}, u32[]{:S(2)}) collective-permute-start(bf16[256,256]{1,0:T(8,128)(2,1)} %get-tuple-element.9.payload.refs_7_), channel_id=1, source_target_pairs={{0,12},{4,0},{8,4},{12,8},{1,13},{5,1},{9,5},{13,9},{2,14},{6,2},{... | collective-permute-start | bytes 393224 | tf_op jit(solution)/shard_map/ppermute | solution.py:21
  71.1 3.2 %fusion.5 = bf16[256,1024]{0,1:T(8,128)(2,1)} fusion(f32[256,1024]{0,1:T(8,128)} %fusion.9, bf16[256,640]{1,0:T(8,128)(2,1)} %constant_dynamic-update-slice_fusion.4, bf16[1280,1024]{1,0:T(8,128)(2,1)} %param.12, s32[]{:T(128)S(6)} %select_n.330), kind=kOutput, calls=%fused_computation.16 | convolution fusion | flops 336068608 | bytes 3211268 | tf_op jit(solution)/shard_map/dot_general | solution.py:370
  76.3 17.0 %collective-permute-done.18.payload.refs_10_ = bf16[256,256]{1,0:T(8,128)(2,1)S(1)} collective-permute-done((bf16[256,256]{1,0:T(8,128)(2,1)}, bf16[256,256]{1,0:T(8,128)(2,1)S(1)}, u32[]{:S(2)}, u32[]{:S(2)}) %collective-permute-start.18) | collective-permute-done | bytes 131104 | tf_op jit(solution)/shard_map/ppermute | solution.py:21
  94.0 3.5 %shard_map.127 = bf16[256,1024]{1,0:T(8,128)(2,1)} custom-call(s32[3]{0:T(128)} %get-tuple-element.52.slot, s32[4]{0:T(128)} %get-tuple-element.48.member, bf16[256,256]{1,0:T(8,128)(2,1)} %copy-done.11, f32[12,16,64,128]{3,2,1,0:T(8,128)} %state.1, f32[12,16,64,128]{3,2,1,0:T(8,128)} %state.1, f32[12,16,64,128]{3,2,1,0:T(8,128)} %state.1), custom_call_target="tpu_custom_call" | custom-call | flops 201326592 | bytes 2097152 | tf_op jit(solution)/shard_map/pallas_call | solution.py:157
  98.9 3.6 %shard_map.125 = bf16[256,1024]{1,0:T(8,128)(2,1)} custom-call(s32[3]{0:T(128)} %get-tuple-element.54.slot, s32[4]{0:T(128)} %get-tuple-element.46.member, bf16[256,256]{1,0:T(8,128)(2,1)} %copy-done.12, f32[12,16,64,128]{3,2,1,0:T(8,128)} %state.1, f32[12,16,64,128]{3,2,1,0:T(8,128)} %state.1, f32[12,16,64,128]{3,2,1,0:T(8,128)} %state.1), custom_call_target="tpu_custom_call" | custom-call | flops 201326592 | bytes 2097152 | tf_op jit(solution)/shard_map/pallas_call | solution.py:157
  102.5 3.6 %collective-permute-start.15 = (bf16[256,1024]{1,0:T(8,128)(2,1)}, bf16[256,1024]{1,0:T(8,128)(2,1)}, u32[]{:S(2)}, u32[]{:S(2)}) collective-permute-start(bf16[256,1024]{1,0:T(8,128)(2,1)} %shard_map.125), channel_id=1, source_target_pairs={{0,4},{1,5},{2,6},{3,7},{16,20},{17,21},{18,22},{19,23}} | collective-permute-start | bytes 1572872 | tf_op jit(solution)/shard_map/ppermute | solution.py:25
  110.8 9.1 %collective-permute-done.16.payload.refs_9_ = bf16[256,256]{1,0:T(8,128)(2,1)S(1)} collective-permute-done((bf16[256,256]{1,0:T(8,128)(2,1)S(1)}, bf16[256,256]{1,0:T(8,128)(2,1)S(1)}, u32[]{:S(2)}, u32[]{:S(2)}) %collective-permute-start.16) | collective-permute-done | bytes 131104 | tf_op jit(solution)/shard_map/ppermute | solution.py:21
  120.5 3.5 %shard_map.126 = bf16[256,1024]{1,0:T(8,128)(2,1)} custom-call(s32[3]{0:T(128)} %get-tuple-element.53.slot, s32[4]{0:T(128)} %get-tuple-element.47.member, bf16[256,256]{1,0:T(8,128)(2,1)} %copy-done.13, f32[12,16,64,128]{3,2,1,0:T(8,128)} %state.1, f32[12,16,64,128]{3,2,1,0:T(8,128)} %state.1, f32[12,16,64,128]{3,2,1,0:T(8,128)} %state.1), custom_call_target="tpu_custom_call" | custom-call | flops 201326592 | bytes 2097152 | tf_op jit(solution)/shard_map/pallas_call | solution.py:157
  125.5 3.3 %collective-permute-start.17 = (bf16[256,1024]{1,0:T(8,128)(2,1)S(1)}, bf16[256,1024]{1,0:T(8,128)(2,1)S(1)}, u32[]{:S(2)}, u32[]{:S(2)}) collective-permute-start(bf16[256,1024]{1,0:T(8,128)(2,1)S(1)} %get-tuple-element.41), channel_id=1, source_target_pairs={{0,4},{4,8},{1,5},{5,9},{2,6},{6,10},{3,7},{7,11},{16,20},{20,24},... | collective-permute-start | bytes 1572872 | tf_op jit(solution)/shard_map/ppermute | solution.py:25
  132.5 9.0 %collective-permute-done.17 = bf16[256,1024]{1,0:T(8,128)(2,1)S(1)} collective-permute-done((bf16[256,1024]{1,0:T(8,128)(2,1)S(1)}, bf16[256,1024]{1,0:T(8,128)(2,1)S(1)}, u32[]{:S(2)}, u32[]{:S(2)}) %collective-permute-start.17) | collective-permute-done | bytes 524320 | tf_op jit(solution)/shard_map/ppermute | solution.py:25
  142.5 5.2 %collective-permute-start.19 = (bf16[256,1024]{1,0:T(8,128)(2,1)}, bf16[256,1024]{1,0:T(8,128)(2,1)}, u32[]{:S(2)}, u32[]{:S(2)}) collective-permute-start(bf16[256,1024]{1,0:T(8,128)(2,1)} %add.325), channel_id=1, source_target_pairs={{0,4},{4,8},{8,12},{1,5},{5,9},{9,13},{2,6},{6,10},{10,14},{3,7},{... | collective-permute-start | bytes 1572872 | tf_op jit(solution)/shard_map/ppermute | solution.py:25
  154.8 3.5 %shard_map.124 = bf16[256,1024]{1,0:T(8,128)(2,1)} custom-call(s32[3]{0:T(128)} %get-tuple-element.51.slot, s32[4]{0:T(128)} %get-tuple-element.45.member, bf16[256,256]{1,0:T(8,128)(2,1)} %get-tuple-element.9.payload.refs_7_, f32[12,16,64,128]{3,2,1,0:T(8,128)} %state.1, f32[12,16,64,128]{3,2,1,0:T(8,128)} %state.1, f32[12,16,64,128]{3,2,1,0:T(8,128)} %state.1), custom_call_target="tpu_custom_call" | custom-call | flops 201326592 | bytes 2097152 | tf_op jit(solution)/shard_map/pallas_call | solution.py:157
  158.3 4.1 %shard_map.123 = (f32[256,1024]{1,0:T(8,128)}, f32[256,1024]{1,0:T(8,128)}) custom-call(bf16[256,1024]{1,0:T(8,128)(2,1)} %copy.47.x, bf16[256,256]{1,0:T(8,128)(2,1)} %get-tuple-element.9.payload.refs_7_, bf16[256,128]{1,0:T(8,128)(2,1)} %get-tuple-element.10.b_part.refs_11_, s32[256,1]{1,0:T(8,128)} %copy.46.seg_row, s32[1,256]{1,0:T(1,128)} %bitcast.75, ...), custom_call_target="tpu_custom_call" | custom-call | flops 268435456 | bytes 2621440 | tf_op jit(solution)/shard_map/pallas_call | solution.py:211
  166.1 5.2 %collective-permute-start.23 = (bf16[256,1024]{1,0:T(8,128)(2,1)S(1)}, bf16[256,1024]{1,0:T(8,128)(2,1)S(1)}, u32[]{:S(2)}, u32[]{:S(2)}) collective-permute-start(bf16[256,1024]{1,0:T(8,128)(2,1)S(1)} %add_convert_fusion.1), channel_id=1, source_target_pairs={{0,4},{4,8},{8,12},{1,5},{5,9},{9,13},{2,6},{6,10},{10,14},{3,7},{... | collective-permute-start | bytes 1572872 | tf_op jit(solution)/shard_map/ppermute | solution.py:25
  172.4 7.6 %collective-permute-done.23 = bf16[256,1024]{1,0:T(8,128)(2,1)S(1)} collective-permute-done((bf16[256,1024]{1,0:T(8,128)(2,1)S(1)}, bf16[256,1024]{1,0:T(8,128)(2,1)S(1)}, u32[]{:S(2)}, u32[]{:S(2)}) %collective-permute-start.23) | collective-permute-done | bytes 524320 | tf_op jit(solution)/shard_map/ppermute | solution.py:25
  185.9 9.7 %collective-permute-start.30 = (bf16[128,1280]{1,0:T(8,128)(2,1)S(1)}, bf16[128,1280]{1,0:T(8,128)(2,1)}, u32[]{:S(2)}, u32[]{:S(2)}) collective-permute-start(bf16[128,1280]{1,0:T(8,128)(2,1)S(1)} %add_convert_fusion.8), channel_id=1, source_target_pairs={{0,4},{4,8},{8,12},{1,5},{5,9},{9,13},{2,6},{6,10},{10,14},{3,7},{... | collective-permute-start | bytes 983048 | tf_op jit(solution)/shard_map/ppermute | solution.py:400
  204.2 15.0 %collective-permute-done.38 = bf16[256,1024]{1,0:T(8,128)(2,1)S(1)} collective-permute-done((bf16[256,1024]{1,0:T(8,128)(2,1)S(1)}, bf16[256,1024]{1,0:T(8,128)(2,1)S(1)}, u32[]{:S(2)}, u32[]{:S(2)}) %collective-permute-start.38) | collective-permute-done | bytes 524320 | tf_op jit(solution)/shard_map/ppermute | solution.py:30
  224.9 6.7 %collective-permute-start.35 = (bf16[128,1280]{1,0:T(8,128)(2,1)}, bf16[128,1280]{1,0:T(8,128)(2,1)}, u32[]{:S(2)}, u32[]{:S(2)}) collective-permute-start(bf16[128,1280]{1,0:T(8,128)(2,1)} %add_convert_fusion.6), channel_id=1, source_target_pairs={{0,8},{4,12},{1,9},{5,13},{2,10},{6,14},{3,11},{7,15},{16,24},{20,... | collective-permute-start | bytes 983048 | tf_op jit(solution)/shard_map/ppermute | solution.py:400
  237.9 5.3 %collective-permute-start.44 = (bf16[1024,256]{1,0:T(8,128)(2,1)S(1)}, bf16[1024,256]{1,0:T(8,128)(2,1)}, u32[]{:S(2)}, u32[]{:S(2)}) collective-permute-start(bf16[1024,256]{1,0:T(8,128)(2,1)S(1)} %get-tuple-element.39.refs_0_), channel_id=1, source_target_pairs={{0,4},{4,8},{8,12},{1,5},{5,9},{9,13},{2,6},{6,10},{10,14},{3,7},{... | collective-permute-start | bytes 1572872 | tf_op jit(solution)/shard_map/ppermute | solution.py:25
  243.2 3.1 collective-permute-done.40
  246.3 3.5 %collective-permute-done.27 = bf16[128,1280]{1,0:T(8,128)(2,1)} collective-permute-done((bf16[128,1280]{1,0:T(8,128)(2,1)}, bf16[128,1280]{1,0:T(8,128)(2,1)}, u32[]{:S(2)}, u32[]{:S(2)}) %collective-permute-start.27) | collective-permute-done | bytes 327712 | tf_op jit(solution)/shard_map/ppermute | solution.py:399
  262.0 5.4 %collective-permute-start.52 = (bf16[256,128]{1,0:T(8,128)(2,1)S(1)}, bf16[256,128]{1,0:T(8,128)(2,1)S(1)}, u32[]{:S(2)}, u32[]{:S(2)}) collective-permute-start(bf16[256,128]{1,0:T(8,128)(2,1)S(1)} %copy-done.16), channel_id=1, source_target_pairs={{0,12},{4,0},{8,4},{12,8},{1,13},{5,1},{9,5},{13,9},{2,14},{6,2},{... | collective-permute-start | bytes 196616 | tf_op jit(solution)/shard_map/ppermute | solution.py:21
  267.4 8.0 %collective-permute-done.48.refs_5_ = bf16[1024,256]{1,0:T(8,128)(2,1)} collective-permute-done((bf16[1024,256]{1,0:T(8,128)(2,1)}, bf16[1024,256]{1,0:T(8,128)(2,1)}, u32[]{:S(2)}, u32[]{:S(2)}) %collective-permute-start.48) | collective-permute-done | bytes 524320 | tf_op jit(solution)/shard_map/ppermute | solution.py:30
  280.5 8.7 %collective-permute-start.51 = (bf16[256,128]{1,0:T(8,128)(2,1)S(1)}, bf16[256,128]{1,0:T(8,128)(2,1)S(1)}, u32[]{:S(2)}, u32[]{:S(2)}) collective-permute-start(bf16[256,128]{1,0:T(8,128)(2,1)S(1)} %copy-done.16), channel_id=1, source_target_pairs={{0,8},{4,12},{8,0},{12,4},{1,9},{5,13},{9,1},{13,5},{2,10},{6,14},... | collective-permute-start | bytes 196616 | tf_op jit(solution)/shard_map/ppermute | solution.py:21
  292.0 3.3 %collective-permute-done.50.refs_12_ = bf16[256,128]{1,0:T(8,128)(2,1)S(1)} collective-permute-done((bf16[256,128]{1,0:T(8,128)(2,1)S(1)}, bf16[256,128]{1,0:T(8,128)(2,1)S(1)}, u32[]{:S(2)}, u32[]{:S(2)}) %collective-permute-start.50) | collective-permute-done | bytes 65568 | tf_op jit(solution)/shard_map/ppermute | solution.py:21
  295.9 13.2 %shard_map.128 = f32[12,16,64,128]{3,2,1,0:T(8,128)} custom-call(s32[12]{0:T(128)} %get-tuple-element.50.which, s32[12]{0:T(128)} %get-tuple-element.49.member, f32[12,16,64,128]{3,2,1,0:T(8,128)} %state.1, bf16[1024,256]{1,0:T(8,128)(2,1)} %copy-done.4, bf16[1024,256]{1,0:T(8,128)(2,1)} %collective-permute-done.44.refs_1_, ...), custom_call_target="tpu_custom_call" | custom-call | flops 805306368 | bytes 16252928 | tf_op jit(solution)/shard_map/pallas_call | solution.py:256
  (213 shorter events, 121.8 us)
Async XLA Ops:
  2.7 27.6 %collective-permute-start = (bf16[128,640]{1,0:T(8,128)(2,1)}, bf16[128,640]{1,0:T(8,128)(2,1)}, u32[]{:S(2)}, u32[]{:S(2)}) collective-permute-start(bf16[128,640]{1,0:T(8,128)(2,1)} %get-tuple-element.29), channel_id=1, source_target_pairs={{0,4},{4,8},{8,12},{12,0},{1,5},{5,9},{9,13},{13,1},{2,6},{6,10},{... | collective-permute-start | bytes 491528 | tf_op jit(solution)/shard_map/ppermute | solution.py:21
  5.8 25.2 %collective-permute-start.8 = (bf16[128,640]{1,0:T(8,128)(2,1)}, bf16[128,640]{1,0:T(8,128)(2,1)}, u32[]{:S(2)}, u32[]{:S(2)}) collective-permute-start(bf16[128,640]{1,0:T(8,128)(2,1)} %get-tuple-element.30), channel_id=1, source_target_pairs={{0,12},{4,0},{8,4},{12,8},{1,13},{5,1},{9,5},{13,9},{2,14},{6,2},{... | collective-permute-start | bytes 491528 | tf_op jit(solution)/shard_map/ppermute | solution.py:21
  7.8 20.1 %collective-permute-start.4 = (bf16[128,640]{1,0:T(8,128)(2,1)}, bf16[128,640]{1,0:T(8,128)(2,1)}, u32[]{:S(2)}, u32[]{:S(2)}) collective-permute-start(bf16[128,640]{1,0:T(8,128)(2,1)} %get-tuple-element.31), channel_id=1, source_target_pairs={{0,8},{4,12},{8,0},{12,4},{1,9},{5,13},{9,1},{13,5},{2,10},{6,14},... | collective-permute-start | bytes 491528 | tf_op jit(solution)/shard_map/ppermute | solution.py:21
  11.6 33.0 %all-to-all-start = ((bf16[4,400,256]{2,1,0:T(8,128)(2,1)}), bf16[4,400,256]{2,1,0:T(8,128)(2,1)S(1)}, u32[]{:S(2)}, u32[]{:S(2)}) async-start(bf16[4,400,256]{2,1,0:T(8,128)(2,1)} %broadcast_in_dim.77), calls=%async_computation | async-start | bytes 1638400 | tf_op jit(solution)/shard_map/all_to_all | solution.py:67
  39.4 66.7 %collective-permute-start.2 = (bf16[256,640]{1,0:T(8,128)(2,1)}, bf16[256,640]{1,0:T(8,128)(2,1)}, u32[]{:S(2)}, u32[]{:S(2)}) collective-permute-start(bf16[256,640]{1,0:T(8,128)(2,1)} %constant_dynamic-update-slice_fusion), channel_id=1, source_target_pairs={{0,1},{1,0},{2,3},{3,2},{4,5},{5,4},{6,7},{7,6},{8,9},{9,8},{10,11... | collective-permute-start | bytes 983048 | tf_op jit(solution)/shard_map/ppermute | solution.py:56
  50.3 99.7 %collective-permute-start.7 = (bf16[256,1024]{0,1:T(8,128)(2,1)}, bf16[256,1024]{0,1:T(8,128)(2,1)}, u32[]{:S(2)}, u32[]{:S(2)}) collective-permute-start(bf16[256,1024]{0,1:T(8,128)(2,1)} %fusion.4), channel_id=1, source_target_pairs={{0,8},{4,12},{8,0},{12,4},{1,9},{5,13},{9,1},{13,5},{2,10},{6,14},... | collective-permute-start | bytes 1572872 | tf_op jit(solution)/shard_map/ppermute | solution.py:21
  67.5 25.8 %collective-permute-start.18 = (bf16[256,256]{1,0:T(8,128)(2,1)}, bf16[256,256]{1,0:T(8,128)(2,1)S(1)}, u32[]{:S(2)}, u32[]{:S(2)}) collective-permute-start(bf16[256,256]{1,0:T(8,128)(2,1)} %get-tuple-element.9.payload.refs_7_), channel_id=1, source_target_pairs={{0,12},{4,0},{8,4},{12,8},{1,13},{5,1},{9,5},{13,9},{2,14},{6,2},{... | collective-permute-start | bytes 393224 | tf_op jit(solution)/shard_map/ppermute | solution.py:21
  70.8 27.4 %collective-permute-start.14 = (bf16[256,256]{1,0:T(8,128)(2,1)}, bf16[256,256]{1,0:T(8,128)(2,1)S(1)}, u32[]{:S(2)}, u32[]{:S(2)}) collective-permute-start(bf16[256,256]{1,0:T(8,128)(2,1)} %get-tuple-element.9.payload.refs_7_), channel_id=1, source_target_pairs={{0,4},{4,8},{8,12},{12,0},{1,5},{5,9},{9,13},{13,1},{2,6},{6,10},{... | collective-permute-start | bytes 393224 | tf_op jit(solution)/shard_map/ppermute | solution.py:21
  74.3 75.7 %collective-permute-start.11 = (bf16[256,1024]{0,1:T(8,128)(2,1)}, bf16[256,1024]{0,1:T(8,128)(2,1)}, u32[]{:S(2)}, u32[]{:S(2)}) collective-permute-start(bf16[256,1024]{0,1:T(8,128)(2,1)} %fusion.5), channel_id=1, source_target_pairs={{0,4},{4,8},{8,12},{12,0},{1,5},{5,9},{9,13},{13,1},{2,6},{6,10},{... | collective-permute-start | bytes 1572872 | tf_op jit(solution)/shard_map/ppermute | solution.py:21
  97.5 26.5 %collective-permute-start.20 = (bf16[256,1024]{1,0:T(8,128)(2,1)}, bf16[256,1024]{1,0:T(8,128)(2,1)S(1)}, u32[]{:S(2)}, u32[]{:S(2)}) collective-permute-start(bf16[256,1024]{1,0:T(8,128)(2,1)} %shard_map.127), channel_id=1, source_target_pairs={{12,8},{13,9},{14,10},{15,11},{28,24},{29,25},{30,26},{31,27}} | collective-permute-start | bytes 1572872 | tf_op jit(solution)/shard_map/ppermute | solution.py:30
  102.5 21.5 %collective-permute-start.15 = (bf16[256,1024]{1,0:T(8,128)(2,1)}, bf16[256,1024]{1,0:T(8,128)(2,1)}, u32[]{:S(2)}, u32[]{:S(2)}) collective-permute-start(bf16[256,1024]{1,0:T(8,128)(2,1)} %shard_map.125), channel_id=1, source_target_pairs={{0,4},{1,5},{2,6},{3,7},{16,20},{17,21},{18,22},{19,23}} | collective-permute-start | bytes 1572872 | tf_op jit(solution)/shard_map/ppermute | solution.py:25
  119.9 30.1 %collective-permute-start.3 = (bf16[256,1024]{0,1:T(8,128)(2,1)}, bf16[256,1024]{0,1:T(8,128)(2,1)}, u32[]{:S(2)}, u32[]{:S(2)}) collective-permute-start(bf16[256,1024]{0,1:T(8,128)(2,1)} %fusion.3), channel_id=1, source_target_pairs={{0,12},{4,0},{8,4},{12,8},{1,13},{5,1},{9,5},{13,9},{2,14},{6,2},{... | collective-permute-start | bytes 1572872 | tf_op jit(solution)/shard_map/ppermute | solution.py:21
  128.8 18.8 %collective-permute-start.21 = (bf16[256,1024]{1,0:T(8,128)(2,1)S(1)}, bf16[256,1024]{1,0:T(8,128)(2,1)S(1)}, u32[]{:S(2)}, u32[]{:S(2)}) collective-permute-start(bf16[256,1024]{1,0:T(8,128)(2,1)S(1)} %get-tuple-element.42), channel_id=1, source_target_pairs={{12,8},{8,4},{13,9},{9,5},{14,10},{10,6},{15,11},{11,7},{28,24},{2... | collective-permute-start | bytes 1572872 | tf_op jit(solution)/shard_map/ppermute | solution.py:30
  142.5 20.0 %collective-permute-start.19 = (bf16[256,1024]{1,0:T(8,128)(2,1)}, bf16[256,1024]{1,0:T(8,128)(2,1)}, u32[]{:S(2)}, u32[]{:S(2)}) collective-permute-start(bf16[256,1024]{1,0:T(8,128)(2,1)} %add.325), channel_id=1, source_target_pairs={{0,4},{4,8},{8,12},{1,5},{5,9},{9,13},{2,6},{6,10},{10,14},{3,7},{... | collective-permute-start | bytes 1572872 | tf_op jit(solution)/shard_map/ppermute | solution.py:25
  164.8 16.1 %collective-permute-start.28 = (bf16[256,1024]{1,0:T(8,128)(2,1)S(1)}, bf16[256,1024]{1,0:T(8,128)(2,1)S(1)}, u32[]{:S(2)}, u32[]{:S(2)}) collective-permute-start(bf16[256,1024]{1,0:T(8,128)(2,1)S(1)} %add_convert_fusion.1), channel_id=1, source_target_pairs={{12,8},{8,4},{4,0},{13,9},{9,5},{5,1},{14,10},{10,6},{6,2},{15,11}... | collective-permute-start | bytes 1572872 | tf_op jit(solution)/shard_map/ppermute | solution.py:30
  172.3 60.1 %collective-permute-start.41 = (bf16[128,1280]{1,0:T(8,128)(2,1)S(1)}, bf16[128,1280]{1,0:T(8,128)(2,1)S(1)}, u32[]{:S(2)}, u32[]{:S(2)}) collective-permute-start(bf16[128,1280]{1,0:T(8,128)(2,1)S(1)} %constant_dynamic-slice_fusion), channel_id=1, source_target_pairs={{0,1},{1,0},{2,3},{3,2},{4,5},{5,4},{6,7},{7,6},{8,9},{9,8},{10,11... | collective-permute-start | bytes 983048 | tf_op jit(solution)/shard_map/ppermute | solution.py:56
  182.4 17.1 %collective-permute-start.33 = (bf16[256,1024]{1,0:T(8,128)(2,1)S(1)}, bf16[256,1024]{1,0:T(8,128)(2,1)S(1)}, u32[]{:S(2)}, u32[]{:S(2)}) collective-permute-start(bf16[256,1024]{1,0:T(8,128)(2,1)S(1)} %collective-permute-done.28), channel_id=1, source_target_pairs={{8,4},{4,0},{9,5},{5,1},{10,6},{6,2},{11,7},{7,3},{24,20},{20,16},... | collective-permute-start | bytes 1572872 | tf_op jit(solution)/shard_map/ppermute | solution.py:30
  184.5 49.9 %collective-permute-start.37 = (bf16[128,1280]{1,0:T(8,128)(2,1)S(1)}, bf16[128,1280]{1,0:T(8,128)(2,1)S(1)}, u32[]{:S(2)}, u32[]{:S(2)}) collective-permute-start(bf16[128,1280]{1,0:T(8,128)(2,1)S(1)} %add_convert_fusion.5), channel_id=1, source_target_pairs={{4,0},{8,4},{12,8},{5,1},{9,5},{13,9},{6,2},{10,6},{14,10},{7,3},{... | collective-permute-start | bytes 983048 | tf_op jit(solution)/shard_map/ppermute | solution.py:399
  185.9 50.6 %collective-permute-start.30 = (bf16[128,1280]{1,0:T(8,128)(2,1)S(1)}, bf16[128,1280]{1,0:T(8,128)(2,1)}, u32[]{:S(2)}, u32[]{:S(2)}) collective-permute-start(bf16[128,1280]{1,0:T(8,128)(2,1)S(1)} %add_convert_fusion.8), channel_id=1, source_target_pairs={{0,4},{4,8},{8,12},{1,5},{5,9},{9,13},{2,6},{6,10},{10,14},{3,7},{... | collective-permute-start | bytes 983048 | tf_op jit(solution)/shard_map/ppermute | solution.py:400
  200.5 18.7 %collective-permute-start.38 = (bf16[256,1024]{1,0:T(8,128)(2,1)S(1)}, bf16[256,1024]{1,0:T(8,128)(2,1)S(1)}, u32[]{:S(2)}, u32[]{:S(2)}) collective-permute-start(bf16[256,1024]{1,0:T(8,128)(2,1)S(1)} %collective-permute-done.33), channel_id=1, source_target_pairs={{4,0},{5,1},{6,2},{7,3},{20,16},{21,17},{22,18},{23,19}} | collective-permute-start | bytes 1572872 | tf_op jit(solution)/shard_map/ppermute | solution.py:30
  202.6 19.0 %collective-permute-start.25 = (bf16[256,1024]{1,0:T(8,128)(2,1)S(1)}, bf16[256,1024]{1,0:T(8,128)(2,1)S(1)}, u32[]{:S(2)}, u32[]{:S(2)}) collective-permute-start(bf16[256,1024]{1,0:T(8,128)(2,1)S(1)} %collective-permute-done.24), channel_id=1, source_target_pairs={{8,12},{9,13},{10,14},{11,15},{24,28},{25,29},{26,30},{27,31}} | collective-permute-start | bytes 1572872 | tf_op jit(solution)/shard_map/ppermute | solution.py:25
  219.2 18.7 %collective-permute-start.32 = (bf16[128,1280]{1,0:T(8,128)(2,1)}, bf16[128,1280]{1,0:T(8,128)(2,1)}, u32[]{:S(2)}, u32[]{:S(2)}) collective-permute-start(bf16[128,1280]{1,0:T(8,128)(2,1)} %add_convert_fusion.7), channel_id=1, source_target_pairs={{8,0},{12,4},{9,1},{13,5},{10,2},{14,6},{11,3},{15,7},{24,16},{28,... | collective-permute-start | bytes 983048 | tf_op jit(solution)/shard_map/ppermute | solution.py:399
  224.9 18.3 %collective-permute-start.35 = (bf16[128,1280]{1,0:T(8,128)(2,1)}, bf16[128,1280]{1,0:T(8,128)(2,1)}, u32[]{:S(2)}, u32[]{:S(2)}) collective-permute-start(bf16[128,1280]{1,0:T(8,128)(2,1)} %add_convert_fusion.6), channel_id=1, source_target_pairs={{0,8},{4,12},{1,9},{5,13},{2,10},{6,14},{3,11},{7,15},{16,24},{20,... | collective-permute-start | bytes 983048 | tf_op jit(solution)/shard_map/ppermute | solution.py:400
  236.6 22.7 %collective-permute-start.47 = (bf16[1024,256]{1,0:T(8,128)(2,1)S(1)}, bf16[1024,256]{1,0:T(8,128)(2,1)}, u32[]{:S(2)}, u32[]{:S(2)}) collective-permute-start(bf16[1024,256]{1,0:T(8,128)(2,1)S(1)} %get-tuple-element.39.refs_0_), channel_id=1, source_target_pairs={{12,8},{8,4},{4,0},{13,9},{9,5},{5,1},{14,10},{10,6},{6,2},{15,11}... | collective-permute-start | bytes 1572872 | tf_op jit(solution)/shard_map/ppermute | solution.py:30
  237.9 22.7 %collective-permute-start.44 = (bf16[1024,256]{1,0:T(8,128)(2,1)S(1)}, bf16[1024,256]{1,0:T(8,128)(2,1)}, u32[]{:S(2)}, u32[]{:S(2)}) collective-permute-start(bf16[1024,256]{1,0:T(8,128)(2,1)S(1)} %get-tuple-element.39.refs_0_), channel_id=1, source_target_pairs={{0,4},{4,8},{8,12},{1,5},{5,9},{9,13},{2,6},{6,10},{10,14},{3,7},{... | collective-permute-start | bytes 1572872 | tf_op jit(solution)/shard_map/ppermute | solution.py:25
  254.3 23.9 %collective-permute-start.42 = (bf16[2,128,1280]{2,1,0:T(8,128)(2,1)}, bf16[2,128,1280]{2,1,0:T(8,128)(2,1)}, u32[]{:S(2)}, u32[]{:S(2)}) collective-permute-start(bf16[2,128,1280]{2,1,0:T(8,128)(2,1)} %pad_maximum_fusion), channel_id=1, source_target_pairs={{0,2},{1,3},{2,0},{3,1},{4,6},{5,7},{6,4},{7,5},{8,10},{9,11},{10,... | collective-permute-start | bytes 1966088 | tf_op jit(solution)/shard_map/ppermute | solution.py:61
  259.3 16.1 %collective-permute-start.48 = (bf16[1024,256]{1,0:T(8,128)(2,1)}, bf16[1024,256]{1,0:T(8,128)(2,1)}, u32[]{:S(2)}, u32[]{:S(2)}) collective-permute-start(bf16[1024,256]{1,0:T(8,128)(2,1)} %collective-permute-done.47.refs_4_), channel_id=1, source_target_pairs={{8,4},{4,0},{9,5},{5,1},{10,6},{6,2},{11,7},{7,3},{24,20},{20,16},... | collective-permute-start | bytes 1572872 | tf_op jit(solution)/shard_map/ppermute | solution.py:30
  260.6 16.1 %collective-permute-start.45 = (bf16[1024,256]{1,0:T(8,128)(2,1)}, bf16[1024,256]{1,0:T(8,128)(2,1)}, u32[]{:S(2)}, u32[]{:S(2)}) collective-permute-start(bf16[1024,256]{1,0:T(8,128)(2,1)} %collective-permute-done.44.refs_1_), channel_id=1, source_target_pairs={{4,8},{8,12},{5,9},{9,13},{6,10},{10,14},{7,11},{11,15},{20,24},{2... | collective-permute-start | bytes 1572872 | tf_op jit(solution)/shard_map/ppermute | solution.py:25
  262.0 27.2 %collective-permute-start.52 = (bf16[256,128]{1,0:T(8,128)(2,1)S(1)}, bf16[256,128]{1,0:T(8,128)(2,1)S(1)}, u32[]{:S(2)}, u32[]{:S(2)}) collective-permute-start(bf16[256,128]{1,0:T(8,128)(2,1)S(1)} %copy-done.16), channel_id=1, source_target_pairs={{0,12},{4,0},{8,4},{12,8},{1,13},{5,1},{9,5},{13,9},{2,14},{6,2},{... | collective-permute-start | bytes 196616 | tf_op jit(solution)/shard_map/ppermute | solution.py:21
  275.4 19.9 %collective-permute-start.49 = (bf16[1024,256]{1,0:T(8,128)(2,1)}, bf16[1024,256]{1,0:T(8,128)(2,1)}, u32[]{:S(2)}, u32[]{:S(2)}) collective-permute-start(bf16[1024,256]{1,0:T(8,128)(2,1)} %collective-permute-done.48.refs_5_), channel_id=1, source_target_pairs={{4,0},{5,1},{6,2},{7,3},{20,16},{21,17},{22,18},{23,19}} | collective-permute-start | bytes 1572872 | tf_op jit(solution)/shard_map/ppermute | solution.py:30
  276.7 18.6 %collective-permute-start.46 = (bf16[1024,256]{1,0:T(8,128)(2,1)}, bf16[1024,256]{1,0:T(8,128)(2,1)}, u32[]{:S(2)}, u32[]{:S(2)}) collective-permute-start(bf16[1024,256]{1,0:T(8,128)(2,1)} %collective-permute-done.45.refs_2_), channel_id=1, source_target_pairs={{8,12},{9,13},{10,14},{11,15},{24,28},{25,29},{26,30},{27,31}} | collective-permute-start | bytes 1572872 | tf_op jit(solution)/shard_map/ppermute | solution.py:25
  280.3 28.8 %collective-permute-start.43 = (bf16[128,1280]{1,0:T(8,128)(2,1)}, bf16[128,1280]{1,0:T(8,128)(2,1)}, u32[]{:S(2)}, u32[]{:S(2)}) collective-permute-start(bf16[128,1280]{1,0:T(8,128)(2,1)} %dynamic-slice_bitcast_fusion), channel_id=1, source_target_pairs={{0,1},{1,0},{2,3},{3,2},{4,5},{5,4},{6,7},{7,6},{8,9},{9,8},{10,11... | collective-permute-start | bytes 983048 | tf_op jit(solution)/shard_map/ppermute | solution.py:56
  (47 other events, 619.6 us)

commit v4 on v2

v4 whole, which is shorter than its diff:
```python
import functools

import jax
import jax.numpy as jnp
from jax import lax
from jax.experimental import pallas as pl
from jax.experimental.pallas import tpu as pltpu
from jax.sharding import PartitionSpec as P

HIGH = lax.Precision.HIGHEST
BF = jnp.bfloat16
F32 = jnp.float32
NN = (((1,), (0,)), ((), ()))
NT = (((1,), (1,)), ((), ()))
TN = (((0,), (0,)), ((), ()))
TT = (((0,), (1,)), ((), ()))
LANES = 128


def turn_req(x, turn):
    count = lax.axis_size("req")
    return lax.ppermute(x, "req", [(i, (i + turn) % count) for i in range(count)])


def swap_core(x):
    count = lax.axis_size("tensor")
    return lax.ppermute(x, "tensor", [(i, i ^ 1) for i in range(count)])


def turn_chip(x, turn):
    count = lax.axis_size("tensor")
    return lax.ppermute(x, "tensor", [(i, (i + 2 * turn) % count) for i in range(count)])


def spread_out(x):
    count = lax.axis_size("req")
    wide = jnp.broadcast_to(x[None], (count,) + x.shape)
    return lax.all_to_all(wide, "req", split_axis=0, concat_axis=0, tiled=True)


def sum_tensor(x):
    x = x + swap_core(x)
    total = x
    for turn in range(1, lax.axis_size("tensor") // 2):
        total = total + turn_chip(x, turn)
    return total


def dot32(a, b, dims):
    return lax.dot_general(a, b, dims, precision=HIGH, preferred_element_type=F32)


def dot16(a, b, dims):
    return lax.dot_general(a, b, dims, preferred_element_type=F32)


def prep_kernel(maps, raw, bias, rate, seg_row, seg_col, c_seg, tail_t, c_part, b_part, run, run_t, step_t):
    num_tok, heads = raw.shape
    dim = maps.shape[1] // 2
    z = raw[...] + bias[...]
    step = jnp.maximum(z, 0.0) + jnp.log1p(jnp.exp(-jnp.abs(z)))
    log_decay = -step * rate[...]
    down = lax.broadcasted_iota(jnp.int32, (num_tok, num_tok), 0)
    along = lax.broadcasted_iota(jnp.int32, (num_tok, num_tok), 1)
    same = seg_row[...] == seg_col[...]
    causal = (same & (down >= along)).astype(F32)
    run[...] = dot32(causal, log_decay, NN)
    flat_t = dot32(log_decay, causal, TT)
    run_t[...] = flat_t
    totals_t = dot32(log_decay, same.astype(F32), TN)
    flat_step = dot32(step, (down == along).astype(F32), TN)
    step_t[...] = flat_step
    grown = jnp.exp(totals_t)
    high = grown.astype(BF)
    tail_t[...] = jnp.zeros_like(tail_t)
    tail_t[:heads, :] = (jnp.exp(jnp.minimum(totals_t - flat_t, 0.0)) * flat_step).astype(BF)
    tail_t[16 : 16 + heads, :] = high
    tail_t[32 : 32 + heads, :] = (grown - high.astype(F32)).astype(BF)
    seg_rows = jnp.broadcast_to(seg_col[...].astype(F32), (16, num_tok)).astype(BF)
    tail_t[48:64, :] = seg_rows
    c_seg[:dim, :] = maps[:, dim:].T.astype(BF)
    c_seg[dim:, :] = seg_rows
    c_part[...] = maps[:, dim:].astype(BF)
    b_part[...] = maps[:, :dim].astype(BF)


def prep(maps, raw, bias, rate, seg):
    num_tok, heads = raw.shape
    dim = maps.shape[1] // 2
    return pl.pallas_call(
        prep_kernel,
        out_shape=[
            jax.ShapeDtypeStruct((dim + 16, num_tok), BF),
            jax.ShapeDtypeStruct((64, num_tok), BF),
            jax.ShapeDtypeStruct((num_tok, dim), BF),
            jax.ShapeDtypeStruct((num_tok, dim), BF),
            jax.ShapeDtypeStruct((num_tok, heads), F32),
            jax.ShapeDtypeStruct((heads, num_tok), F32),
            jax.ShapeDtypeStruct((heads, num_tok), F32),
        ],
        cost_estimate=pl.CostEstimate(flops=1 << 28, bytes_accessed=1 << 20, transcendentals=1 << 14),
    )(maps, raw, bias[None], rate[None], seg[:, None], seg[None, :])


def carried_kernel(owners, slot, member, *refs):
    c_segs, states, outs = refs[:owners], refs[owners:-owners], refs[-owners:]
    heads, width, dim = states[0].shape[1:]
    at = pl.program_id(0)
    ranks = len(states)
    flat = [state[0].reshape(heads * width, dim).astype(BF) for state in states]

    def fill(c_seg, out):
        c_rows = c_seg[:dim, :].astype(F32)
        seg = c_seg[dim : dim + 1, :].astype(F32)
        total = jnp.zeros(out.shape, F32)
        for rank in range(ranks):
            inside = seg == member[at * ranks + rank].astype(F32)
            mine = jnp.where(inside, c_rows, 0.0).T.astype(BF)
            total += dot16(mine, flat[rank], NT)
        out[...] = total.astype(BF)

    for i in range(owners):
        pl.when(at == i)(functools.partial(fill, c_segs[i], outs[i]))


def carried_part(slot, member, c_segs, cache):
    num_tok = c_segs[0].shape[1]
    _, heads, width, dim = cache.shape
    owners = len(c_segs)
    ranks = slot.shape[0] // owners

    def state_map(rank, i, slot, member):
        return (slot[i * ranks + rank], 0, 0, 0)

    return pl.pallas_call(
        functools.partial(carried_kernel, owners),
        out_shape=[jax.ShapeDtypeStruct((num_tok, heads * width), BF)] * owners,
        grid_spec=pltpu.PrefetchScalarGridSpec(
            num_scalar_prefetch=2,
            grid=(owners,),
            in_specs=[pl.BlockSpec(c_seg.shape, lambda i, *_: (0, 0)) for c_seg in c_segs]
            + [
                pl.BlockSpec((1, heads, width, dim), functools.partial(state_map, rank))
                for rank in range(ranks)
            ],
            out_specs=[pl.BlockSpec((num_tok, heads * width), lambda i, *_: (0, 0))] * owners,
        ),
        cost_estimate=pl.CostEstimate(
            flops=2 * owners * num_tok * dim * heads * width * ranks,
            bytes_accessed=owners * (ranks * dim * 4 + num_tok * 2) * heads * width,
            transcendentals=0,
        ),
    )(slot, member, *c_segs, *([cache] * ranks))


def gather_kernel(count, chips, chip, *refs):
    parts = refs[:count]
    b_part, tail_t, x, bundle = refs[count:]
    num_tok, columns = x.shape
    dim = b_part.shape[1]
    piece = num_tok // chips
    for place in range(chips):
        rows = pl.ds(pl.multiple_of(lax.rem(chip[0] - place + chips, chips) * piece, piece), piece)
        at = slice(place * piece, (place + 1) * piece)
        total = parts[0][at, :].astype(F32)
        for part in parts[1:]:
            total += part[at, :].astype(F32)
        x[rows, :] = total.astype(BF)
    for first in range(0, columns, LANES):
        at = slice(first, first + LANES)
        bundle[at, :] = x[:, at].astype(F32).T.astype(BF)
    bundle[columns : columns + dim, :] = b_part[...].astype(F32).T.astype(BF)
    bundle[columns + dim :, :] = tail_t[...]


def gather_part(parts, b_part, tail_t, chip, chips):
    num_tok, columns = parts[0].shape
    rows = columns + b_part.shape[1] + tail_t.shape[0]
    vmem = pl.BlockSpec(memory_space=pltpu.VMEM)
    return pl.pallas_call(
        functools.partial(gather_kernel, len(parts), chips),
        out_shape=[
            jax.ShapeDtypeStruct((num_tok, columns), BF),
            jax.ShapeDtypeStruct((rows, num_tok), BF),
        ],
        in_specs=[pl.BlockSpec(memory_space=pltpu.SMEM)] + [vmem] * (len(parts) + 2),
        cost_estimate=pl.CostEstimate(
            flops=num_tok * columns * len(parts),
            bytes_accessed=num_tok * columns * 2 * (len(parts) + 2),
            transcendentals=0,
        ),
    )(chip.reshape(1).astype(jnp.int32), *parts, b_part, tail_t)


def within_kernel(x, c_part, b_part, seg_row, seg_col, run, run_t, step_t, gain, base, grown):
    num_tok, columns = base.shape
    heads = run.shape[1]
    width = columns // heads
    down = lax.broadcasted_iota(jnp.int32, (num_tok, num_tok), 0)
    along = lax.broadcasted_iota(jnp.int32, (num_tok, num_tok), 1)
    keep = (seg_row[...] == seg_col[...]) & (down >= along)
    raw = dot16(c_part[...], b_part[...], NT)
    scores = jnp.where(keep, raw, 0.0)
    pair = LANES // width
    lane = lax.broadcasted_iota(jnp.int32, (num_tok, LANES), 1) // width
    for first in range(0, heads, pair):
        at = slice(first * width, (first + pair) * width)
        values = x[:, at]
        exact = values.astype(F32)
        total = jnp.zeros((num_tok, LANES), F32)
        rise = jnp.zeros((num_tok, LANES), F32)
        for i in range(pair):
            h = first + i
            run_col = run[:, h : h + 1]
            decay = jnp.exp(jnp.minimum(run_col - run_t[h : h + 1, :], 0.0))
            mixing = (decay * scores * step_t[h : h + 1, :]).astype(BF)
            inner = dot16(mixing, values, NN) + gain[:, h : h + 1] * exact
            total = jnp.where(lane == i, inner, total)
            rise = jnp.where(lane == i, jnp.exp(run_col), rise)
        base[:, at] = total
        grown[:, at] = rise


def within_part(x, c_part, b_part, seg, run, run_t, step_t, gain):
    num_tok, columns = x.shape
    heads = run.shape[1]
    return pl.pallas_call(
        within_kernel,
        out_shape=[jax.ShapeDtypeStruct((num_tok, columns), F32)] * 2,
        cost_estimate=pl.CostEstimate(
            flops=2 * num_tok * num_tok * columns * 2,
            bytes_accessed=num_tok * columns * 10,
            transcendentals=num_tok * num_tok * heads,
        ),
    )(x, c_part, b_part, seg[:, None], seg[None, :], run, run_t, step_t, gain[None])


def states_kernel(owner, member, state, bundle, out):
    heads, width, dim = state.shape[1:]
    columns = heads * width
    at = pl.program_id(0)

    @pl.when(member[at] >= 0)
    def _():
        b_rows = bundle[0, columns : columns + dim, :]
        tail = bundle[0, columns + dim :, :].astype(F32)
        inside = tail[48:49] == member[at].astype(F32)
        weights = jnp.where(inside, tail[:heads], 0.0)
        rise = tail[16 : 16 + heads] + tail[32 : 32 + heads]
        rise = jnp.max(jnp.where(inside, rise, 0.0), axis=1, keepdims=True)
        for h in range(heads):
            rows = slice(h * width, (h + 1) * width)
            scaled = (bundle[0, rows, :].astype(F32) * weights[h : h + 1]).astype(BF)
            out[0, h] = state[0, h] * rise[h : h + 1] + dot16(scaled, b_rows, NT)

    @pl.when(member[at] < 0)
    def _():
        out[...] = state[...]


def states_part(owner, member, cache, bundles):
    slots, heads, width, dim = cache.shape
    _, rows, num_tok = bundles.shape
    slab = pl.BlockSpec((1, heads, width, dim), lambda s, *_: (s, 0, 0, 0))
    return pl.pallas_call(
        states_kernel,
        out_shape=jax.ShapeDtypeStruct(cache.shape, cache.dtype),
        grid_spec=pltpu.PrefetchScalarGridSpec(
            num_scalar_prefetch=2,
            grid=(slots,),
            in_specs=[
                slab,
                pl.BlockSpec((1, rows, num_tok), lambda s, owner, member: (owner[s], 0, 0)),
            ],
            out_specs=slab,
        ),
        cost_estimate=pl.CostEstimate(
            flops=2 * slots * num_tok * heads * width * dim,
            bytes_accessed=cache.size * 8 + slots * rows * num_tok * 2,
            transcendentals=0,
        ),
    )(owner, member, cache, bundles)


def body(
    tokens,
    w_x,
    w_bc,
    w_dt,
    dt_bias,
    decay_rate,
    skip_gain,
    w_out,
    suffix_lengths,
    checkpoint_slot,
    cache,
):
    reqs = lax.axis_size("req")
    tensors = lax.axis_size("tensor")
    chips = tensors // 2
    own_req = lax.axis_index("req")
    own_tensor = lax.axis_index("tensor")
    own_chip = own_tensor // 2
    core = own_tensor % 2
    num_tok = tokens.shape[0]
    depth = w_x.shape[0]
    slots_dev, heads, width, state_dim = cache.shape
    columns = heads * width
    half = depth // 2
    piece = num_tok // chips
    piece = num_tok // chips

    share = depth // tensors
    bc_share = lax.dynamic_slice_in_dim(w_bc, own_tensor * share, share)
    small = spread_out(jnp.concatenate([bc_share, w_dt.T.reshape(-1, w_bc.shape[1])], axis=0))
    bc_tokens = lax.dynamic_index_in_dim(
        tokens.reshape(num_tok, reqs, tensors, share), own_tensor, axis=2, keepdims=False
    )
    state_maps = sum_tensor(
        jnp.dot(
            bc_tokens.reshape(num_tok, reqs * share),
            small[:, :share].reshape(reqs * share, -1),
            preferred_element_type=F32,
        )
    )
    raw_step = jnp.einsum(
        "trk,rhk->th",
        tokens.reshape(num_tok, reqs, depth),
        small[:, share:].reshape(reqs, heads, depth),
        preferred_element_type=F32,
    )
    places = jnp.arange(num_tok, dtype=jnp.int32)
    ends = jnp.cumsum(suffix_lengths[0])
    seg = jnp.sum((places[:, None] >= ends[None, :]).astype(jnp.int32), axis=1)
    c_seg, tail_t, c_part, b_part, run, run_t, step_t = prep(
        state_maps, raw_step, dt_bias, decay_rate, seg
    )
    c_segs = [c_seg] + [turn_req(c_seg, k) for k in range(1, reqs)]

    per_pair = (slots_dev + reqs - 1) // reqs
    total_reqs = checkpoint_slot.shape[0]
    req_dev = total_reqs // reqs
    holder = checkpoint_slot // slots_dev
    index = jnp.arange(total_reqs, dtype=jnp.int32)
    owner = index // req_dev
    pair_key = holder * reqs + owner
    rank_in_pair = jnp.sum(
        (pair_key[:, None] == pair_key[None, :])
        & (checkpoint_slot[None, :] < checkpoint_slot[:, None]),
        axis=1,
    )
    away = (own_req - owner) % reqs
    pairs = jnp.arange(reqs * per_pair, dtype=jnp.int32)
    match = (holder == own_req)[None, :] & (
        (away * per_pair + rank_in_pair)[None, :] == pairs[:, None]
    )

    def pick(match, values, missing):
        found = jnp.sum(jnp.where(match, values[None, :], 0), axis=1)
        return jnp.where(jnp.any(match, axis=1), found, missing).astype(jnp.int32)

    pair_slot = pick(match, checkpoint_slot % slots_dev, 0)
    pair_member = pick(match, index % req_dev, -1)

    def chip_rows(x, place):
        return lax.dynamic_slice_in_dim(x, ((own_chip - place) % chips) * piece, piece)

    own_block = lax.dynamic_slice(tokens, (0, own_req * depth), (num_tok, depth))
    own_block = jnp.concatenate([chip_rows(own_block, place) for place in range(chips)], axis=0)
    parts = [jnp.dot(own_block, w_x, preferred_element_type=F32).astype(BF)]
    w_near = lax.dynamic_slice_in_dim(w_x, core * half, half)
    w_far = lax.dynamic_slice_in_dim(w_x, (1 - core) * half, half)
    w_turned = jnp.concatenate([w_near, w_far], axis=0)
    for k in range(1, reqs):
        start = ((own_req + k) % reqs) * depth + core * half
        block = lax.dynamic_slice(tokens, (own_chip * piece, start), (piece, half))
        block = turn_req(block, k)
        pieces = [block] + [turn_chip(block, turn) for turn in range(1, chips)]
        near = jnp.concatenate(pieces, axis=0)
        both = jnp.concatenate([near, swap_core(near)], axis=1)
        partial = jnp.dot(both, w_turned, preferred_element_type=F32).astype(BF)
        parts.append(turn_req(partial, -k))
    x, bundle = gather_part(parts, b_part, tail_t, own_chip, chips)
    bundles = lax.all_gather(bundle, "req", axis=0)

    carried = carried_part(pair_slot, pair_member, c_segs, cache)
    carried = [carried[0]] + [turn_req(carried[k], -k) for k in range(1, reqs)]

    base, grown = within_part(x, c_part, b_part, seg, run, run_t, step_t, skip_gain)
    held = sum(block.astype(F32) for block in carried)
    outputs = (base + grown * held).astype(BF)

    rows_half = num_tok // 2
    rows_share = rows_half // chips

    def project(block):
        product = jnp.dot(block, w_out, preferred_element_type=F32).astype(BF)
        kept = lax.dynamic_slice_in_dim(product, core * rows_half, rows_half)
        given = lax.dynamic_slice_in_dim(product, (1 - core) * rows_half, rows_half)
        summed = (kept.astype(F32) + swap_core(given).astype(F32)).astype(BF)
        total = lax.dynamic_slice_in_dim(summed, own_chip * rows_share, rows_share).astype(F32)
        for turn in range(1, chips):
            to_chip = (own_chip + turn) % chips
            given = lax.dynamic_slice_in_dim(summed, to_chip * rows_share, rows_share)
            total = total + turn_chip(given, turn).astype(F32)
        return total.astype(BF)

    arrived = [project(outputs)]
    for k in range(1, reqs):
        arrived.append(turn_req(project(turn_req(outputs, k)), -k))

    def column_blocks(chip):
        def one(req):
            chosen = arrived[0]
            for k in range(1, reqs):
                chosen = jnp.where((req - own_req) % reqs == k, arrived[k], chosen)
            return chosen

        return jnp.stack([one(2 * chip + c) for c in range(2)])

    shares = [column_blocks(own_chip)]
    for turn in range(1, chips):
        shares.append(turn_chip(column_blocks((own_chip + turn) % chips), turn))
    ordered = []
    for chip in range(chips):
        chosen = shares[0]
        for turn in range(1, chips):
            chosen = jnp.where((own_chip - chip) % chips == turn, shares[turn], chosen)
        ordered.append(chosen)
    ordered = jnp.concatenate(ordered, axis=1)
    kept = lax.dynamic_index_in_dim(ordered, core, axis=0, keepdims=False)
    other = swap_core(lax.dynamic_index_in_dim(ordered, 1 - core, axis=0, keepdims=False))
    layer_out = jnp.concatenate(
        [jnp.where(core == 0, kept, other), jnp.where(core == 0, other, kept)], axis=0
    )

    slot_ids = own_req * slots_dev + jnp.arange(slots_dev, dtype=jnp.int32)
    match_slot = checkpoint_slot[None, :] == slot_ids[:, None]
    new_cache = states_part(
        pick(match_slot, owner, 0), pick(match_slot, index % req_dev, -1), cache, bundles
    )
    return (layer_out, new_cache)


def solution(mesh):
    placed = (
        P(("groups", "req"), None),
        P("req", "tensor"),
        P("req", None),
        P("req", "tensor"),
        P("tensor"),
        P("tensor"),
        P("tensor"),
        P("tensor", "req"),
        P(("groups", "req"), None),
        P("groups"),
        P(("groups", "req"), "tensor", None, None),
    )
    return jax.shard_map(
        body,
        mesh=mesh,
        in_specs=placed,
        out_specs=(P(("groups", "req"), "tensor"), P(("groups", "req"), "tensor", None, None)),
        check_vma=False,
    )
```

time: 340 us -> 309 us (0.909)
  waiting for transfers between devices: 174 us -> 127 us
  between operations: 0.92 us -> 14.5 us
  local copies, waits for them, and re-layouts: 17.8 us -> 27.9 us
  Pallas kernels: 40.1 us -> 30.6 us
  starting transfers between devices: 65.1 us -> 73.2 us
  matrix products: 25.8 us -> 21.4 us
    ppermute x21 -> x18, waiting for transfers between devices: 163 us -> 109 us  [turn_req(): lax.ppermute(x, 'req', [(i, (i + turn) % count) for i in range(count)])]
    pallas_call x7 -> x5, Pallas kernels: 40.1 us -> 30.6 us  [the longest x1 13.8 us: states_part(): pl.pallas_call(states_kernel, out_shape=jax.ShapeDtypeStruct(cache.shape,...]
    ppermute x2 -> x9, starting transfers between devices: 3.11 us -> 11.9 us  [turn_chip(): lax.ppermute(x, 'tensor', [(i, (i + 2 * turn) % count) for i in range(cou...]
    unnamed x23 -> x26, local copies, waits for them, and re-layouts: 5.05 us -> 10.7 us
    ppermute x2 -> x9, waiting for transfers between devices: 11.6 us -> 17 us  [turn_chip(): lax.ppermute(x, 'tensor', [(i, (i + 2 * turn) % count) for i in range(cou...]
    dynamic_slice x5 -> x11, local copies, waits for them, and re-layouts: 3.32 us -> 7.87 us  [the longest x1 3.48 us: body(): w_near = lax.dynamic_slice_in_dim(w_x, core * half, half)]
    dot_general x12 -> x8, matrix products: 20.4 us -> 15.8 us  [the longest x3 9.08 us: body(): partial = jnp.dot(both, w_turned, preferred_element_type=F32).astype(BF)]
    ppermute x21 -> x18, starting transfers between devices: 53.9 us -> 55.9 us  [turn_req(): lax.ppermute(x, 'req', [(i, (i + turn) % count) for i in range(count)])]
  transfers between devices with their start and end apart: 34 -> 38, of which waited for: 11 -> 11; matrix products, arithmetic and copies ran while one was open for 14% -> 18% of each run, Pallas kernels for 12% -> 5%
where the time goes in v4:
time: 309 us; the launch traced here: 308 us
  waiting for transfers between devices  127 us (41%)
  starting transfers between devices  73.2 us (24%)
  Pallas kernels  30.6 us (10%)
  local copies, waits for them, and re-layouts  27.9 us (9%)
  matrix products  21.4 us (7%)
  between operations  14.5 us (5%)
  other arithmetic  13.6 us (4%)
    ppermute x18, waiting for transfers between devices, turn_req(): lax.ppermute(x, 'req', [(i, (i + turn) % count) for i in range(count)])  109 us
    ppermute x18, starting transfers between devices, turn_req(): lax.ppermute(x, 'req', [(i, (i + turn) % count) for i in range(count)])  55.9 us
    ppermute x9, waiting for transfers between devices, turn_chip(): lax.ppermute(x, 'tensor', [(i, (i + 2 * turn) % count) for i in range(cou...  17 us
    pallas_call x1, Pallas kernels, states_part(): pl.pallas_call(states_kernel, out_shape=jax.ShapeDtypeStruct(cache.shape,...  13.8 us
    ppermute x9, starting transfers between devices, turn_chip(): lax.ppermute(x, 'tensor', [(i, (i + 2 * turn) % count) for i in range(cou...  11.9 us
    unnamed x26, local copies, waits for them, and re-layouts  10.7 us
    dot_general x3, matrix products, body(): partial = jnp.dot(both, w_turned, preferred_element_type=F32).astype(BF)  9.08 us
    pallas_call x1, Pallas kernels, carried_part(): pl.pallas_call(functools.partial(carried_kernel, owners), out_shape=[jax....  7.15 us
  transfers between devices with their start and end apart: 38, of which 11 were waited for; matrix products, arithmetic and copies ran while one was open for 18% of the time, Pallas kernels for 5%

profile of v4, /device:TPU:0, one launch (start us, length us, event | category | flops | bytes accessed | tf_op | source)
XLA Modules:
  0.0 308.2 jit_solution(264339749950399462)
XLA Ops:
  9.3 5.0 %collective-permute-start.8 = (bf16[128,640]{1,0:T(8,128)(2,1)}, bf16[128,640]{1,0:T(8,128)(2,1)}, u32[]{:S(2)}, u32[]{:S(2)}) collective-permute-start(bf16[128,640]{1,0:T(8,128)(2,1)} %get-tuple-element.42), channel_id=1, source_target_pairs={{0,12},{4,0},{8,4},{12,8},{1,13},{5,1},{9,5},{13,9},{2,14},{6,2},{... | collective-permute-start | bytes 491528 | tf_op jit(solution)/shard_map/ppermute | solution.py:22
  18.1 4.1 %all-to-all-start = ((bf16[4,400,256]{2,1,0:T(8,128)(2,1)}), bf16[4,400,256]{2,1,0:T(8,128)(2,1)S(1)}, u32[]{:S(2)}, u32[]{:S(2)}) async-start(bf16[4,400,256]{2,1,0:T(8,128)(2,1)} %broadcast_in_dim.77), calls=%async_computation | async-start | bytes 1638400 | tf_op jit(solution)/shard_map/all_to_all | solution.py:38
  22.3 4.4 %copy.20 = bf16[256,5120]{0,1:T(8,128)(2,1)} copy(bf16[256,5120]{1,0:T(8,128)(2,1)} %param.11) | data formatting | bytes 5242880 | tf_op args[0]
  30.8 3.5 %constant_dynamic-slice_fusion.11 = (bf16[640,1024]{1,0:T(8,128)(2,1)}, bf16[640,1024]{1,0:T(8,128)(2,1)}) fusion(bf16[1280,1024]{1,0:T(8,128)(2,1)} %param.12, s32[]{:T(128)S(6)} %select_n.341, s32[]{:T(128)S(6)} %select_n.342), kind=kLoop, calls=%fused_computation.84 | loop fusion | bytes 5242888 | tf_op jit(solution)/shard_map/dynamic_slice | solution.py:371
  43.3 3.3 %collective-permute-done.1 = bf16[128,640]{1,0:T(8,128)(2,1)S(1)} collective-permute-done((bf16[128,640]{1,0:T(8,128)(2,1)}, bf16[128,640]{1,0:T(8,128)(2,1)S(1)}, u32[]{:S(2)}, u32[]{:S(2)}) %collective-permute-start.1) | collective-permute-done | bytes 163872 | tf_op jit(solution)/shard_map/ppermute | solution.py:32
  48.6 2.3 fusion.35
  50.9 2.8 convolution_convert_fusion.6
  53.7 3.5 %collective-permute-start.3 = (bf16[256,1024]{1,0:T(8,128)(2,1)}, bf16[256,1024]{1,0:T(8,128)(2,1)}, u32[]{:S(2)}, u32[]{:S(2)}) collective-permute-start(bf16[256,1024]{1,0:T(8,128)(2,1)} %convolution_convert_fusion.6), channel_id=1, source_target_pairs={{0,12},{4,0},{8,4},{12,8},{1,13},{5,1},{9,5},{13,9},{2,14},{6,2},{... | collective-permute-start | bytes 1572872 | tf_op jit(solution)/shard_map/ppermute | solution.py:22
  57.2 2.8 convolution_convert_fusion.4
  64.3 3.2 %fusion.3.raw = f32[256,16]{1,0:T(8,128)} fusion(bf16[4,16,1280]{2,1,0:T(8,128)(2,1)S(1)} %reshape.106, bf16[32,4,8,1280]{3,2,1,0:T(8,128)(2,1)} %bitcast.51), kind=kOutput, calls=%fused_computation.12 | convolution fusion | flops 41943040 | bytes 2801664 | tf_op jit(solution)/shard_map/trk,rhk->th/dot_general | solution.py:326
  67.6 3.7 %collective-permute-done.13 = f32[256,256]{1,0:T(8,128)S(1)} collective-permute-done((f32[256,256]{1,0:T(8,128)S(1)}, f32[256,256]{1,0:T(8,128)S(1)}, u32[]{:S(2)}, u32[]{:S(2)}) %collective-permute-start.13) | collective-permute-done | bytes 262176 | tf_op jit(solution)/shard_map/ppermute | solution.py:32
  72.0 2.6 shard_map.122
  74.7 3.5 %collective-permute-start.16 = (bf16[144,256]{1,0:T(8,128)(2,1)}, bf16[144,256]{1,0:T(8,128)(2,1)S(1)}, u32[]{:S(2)}, u32[]{:S(2)}) collective-permute-start(bf16[144,256]{1,0:T(8,128)(2,1)} %get-tuple-element.26.refs_0_), channel_id=1, source_target_pairs={{0,12},{4,0},{8,4},{12,8},{1,13},{5,1},{9,5},{13,9},{2,14},{6,2},{... | collective-permute-start | bytes 221192 | tf_op jit(solution)/shard_map/ppermute | solution.py:22
  78.8 3.6 %convolution_convert_fusion.5 = bf16[256,1024]{1,0:T(8,128)(2,1)} fusion(bf16[640,1024]{1,0:T(8,128)(2,1)} %get-tuple-element.46, bf16[640,1024]{1,0:T(8,128)(2,1)} %get-tuple-element.45, bf16[256,640]{1,0:T(8,128)(2,1)} %collective-permute-done.6, bf16[256,640]{1,0:T(8,128)(2,1)} %constant_dynamic-update-slice_fusion.2), kind=kOutput, calls=%fused_computation.9 | convolution fusion | flops 677904384 | bytes 3801088 | tf_op jit(solution)/shard_map/dot_general | solution.py:381
  84.7 14.5 %collective-permute-done.15.refs_2_ = bf16[144,256]{1,0:T(8,128)(2,1)S(1)} collective-permute-done((bf16[144,256]{1,0:T(8,128)(2,1)}, bf16[144,256]{1,0:T(8,128)(2,1)S(1)}, u32[]{:S(2)}, u32[]{:S(2)}) %collective-permute-start.15) | collective-permute-done | bytes 73760 | tf_op jit(solution)/shard_map/ppermute | solution.py:22
  99.9 7.2 %shard_map.125 = (bf16[256,1024]{1,0:T(8,128)(2,1)}, bf16[256,1024]{1,0:T(8,128)(2,1)}, bf16[256,1024]{1,0:T(8,128)(2,1)}, bf16[256,1024]{1,0:T(8,128)(2,1)}) custom-call(s32[12]{0:T(128)} %get-tuple-element.59.slot, s32[12]{0:T(128)} %get-tuple-element.58.member, bf16[144,256]{1,0:T(8,128)(2,1)} %get-tuple-element.26.refs_0_, bf16[144,256]{1,0:T(8,128)(2,1)} %copy-done.7, ...), custom_call_target="tpu_custom_call" | custom-call | flops 805306368 | bytes 8388608 | tf_op jit(solution)/shard_map/pallas_call | solution.py:135
  107.0 2.3 collective-permute-start.18
  112.7 3.4 %convolution_convert_fusion.7.refs_0_ = bf16[256,1024]{1,0:T(8,128)(2,1)} fusion(bf16[1280,1024]{1,0:T(8,128)(2,1)} %param.12, bf16[128,1280]{1,0:T(8,128)(2,1)S(1)} %get-tuple-element.48, bf16[128,1280]{1,0:T(8,128)(2,1)S(1)} %get-tuple-element.47), kind=kOutput, calls=%fused_computation.11 | convolution fusion | flops 672661504 | bytes 3801088 | tf_op jit(solution)/shard_map/dot_general | solution.py:370
  116.2 2.9 shard_map.123
  119.1 4.1 %shard_map.124 = (f32[256,1024]{1,0:T(8,128)}, f32[256,1024]{1,0:T(8,128)}) custom-call(bf16[256,1024]{1,0:T(8,128)(2,1)} %get-tuple-element.19.x, bf16[256,128]{1,0:T(8,128)(2,1)} %get-tuple-element.20.c_part, bf16[256,128]{1,0:T(8,128)(2,1)} %get-tuple-element.17.refs_4_.b_part, s32[256,1]{1,0:T(8,128)} %copy.23.seg_row, s32[1,256]{1,0:T(1,128)} %bitcast.59, ...), custom_call_target="tpu_custom_call" | custom-call | flops 268435456 | bytes 2621440 | tf_op jit(solution)/shard_map/pallas_call | solution.py:227
  123.2 32.2 %collective-permute-done.18 = bf16[256,1024]{1,0:T(8,128)(2,1)} collective-permute-done((bf16[256,1024]{1,0:T(8,128)(2,1)}, bf16[256,1024]{1,0:T(8,128)(2,1)}, u32[]{:S(2)}, u32[]{:S(2)}) %collective-permute-start.18) | collective-permute-done | bytes 524320 | tf_op jit(solution)/shard_map/ppermute | solution.py:22
  155.4 2.6 add_convert_fusion
  162.4 2.8 collective-permute-start.20
  168.6 11.8 %collective-permute-done.28 = bf16[256,1024]{1,0:T(8,128)(2,1)S(1)} collective-permute-done((bf16[256,1024]{1,0:T(8,128)(2,1)S(1)}, bf16[256,1024]{1,0:T(8,128)(2,1)S(1)}, u32[]{:S(2)}, u32[]{:S(2)}) %collective-permute-start.28) | collective-permute-done | bytes 524320 | tf_op jit(solution)/shard_map/ppermute | solution.py:22
  181.4 41.7 %collective-permute-done.24 = bf16[256,1024]{1,0:T(8,128)(2,1)S(1)} collective-permute-done((bf16[256,1024]{1,0:T(8,128)(2,1)S(1)}, bf16[256,1024]{1,0:T(8,128)(2,1)S(1)}, u32[]{:S(2)}, u32[]{:S(2)}) %collective-permute-start.24) | collective-permute-done | bytes 524320 | tf_op jit(solution)/shard_map/ppermute | solution.py:22
  229.6 3.1 %collective-permute-done.30 = bf16[64,1280]{1,0:T(8,128)(2,1)S(1)} collective-permute-done((bf16[64,1280]{1,0:T(8,128)(2,1)S(1)}, bf16[64,1280]{1,0:T(8,128)(2,1)S(1)}, u32[]{:S(2)}, u32[]{:S(2)}) %collective-permute-start.30) | collective-permute-done | bytes 163872 | tf_op jit(solution)/shard_map/ppermute | solution.py:32
  232.8 24.1 %collective-permute-start.31 = (bf16[64,1280]{1,0:T(8,128)(2,1)S(1)}, bf16[64,1280]{1,0:T(8,128)(2,1)S(1)}, u32[]{:S(2)}, u32[]{:S(2)}) collective-permute-start(bf16[64,1280]{1,0:T(8,128)(2,1)S(1)} %add_convert_fusion.6), channel_id=1, source_target_pairs={{0,12},{4,0},{8,4},{12,8},{1,13},{5,1},{9,5},{13,9},{2,14},{6,2},{... | collective-permute-start | bytes 491528 | tf_op jit(solution)/shard_map/ppermute | solution.py:22
  257.6 3.4 %collective-permute-start.27 = (bf16[64,1280]{1,0:T(8,128)(2,1)}, bf16[64,1280]{1,0:T(8,128)(2,1)S(1)}, u32[]{:S(2)}, u32[]{:S(2)}) collective-permute-start(bf16[64,1280]{1,0:T(8,128)(2,1)} %add_convert_fusion.7), channel_id=1, source_target_pairs={{0,8},{4,12},{8,0},{12,4},{1,9},{5,13},{9,1},{13,5},{2,10},{6,14},... | collective-permute-start | bytes 491528 | tf_op jit(solution)/shard_map/ppermute | solution.py:22
  261.7 3.4 %collective-permute-start.23 = (bf16[64,1280]{1,0:T(8,128)(2,1)}, bf16[64,1280]{1,0:T(8,128)(2,1)}, u32[]{:S(2)}, u32[]{:S(2)}) collective-permute-start(bf16[64,1280]{1,0:T(8,128)(2,1)} %add_convert_fusion.8), channel_id=1, source_target_pairs={{0,4},{4,8},{8,12},{12,0},{1,5},{5,9},{9,13},{13,1},{2,6},{6,10},{... | collective-permute-start | bytes 491528 | tf_op jit(solution)/shard_map/ppermute | solution.py:22
  265.1 8.1 %collective-permute-done.27 = bf16[64,1280]{1,0:T(8,128)(2,1)S(1)} collective-permute-done((bf16[64,1280]{1,0:T(8,128)(2,1)}, bf16[64,1280]{1,0:T(8,128)(2,1)S(1)}, u32[]{:S(2)}, u32[]{:S(2)}) %collective-permute-start.27) | collective-permute-done | bytes 163872 | tf_op jit(solution)/shard_map/ppermute | solution.py:22
  276.9 6.9 %collective-permute-done.34 = bf16[2,64,1280]{2,1,0:T(8,128)(2,1)} collective-permute-done((bf16[2,64,1280]{2,1,0:T(8,128)(2,1)S(1)}, bf16[2,64,1280]{2,1,0:T(8,128)(2,1)}, u32[]{:S(2)}, u32[]{:S(2)}) %collective-permute-start.34) | collective-permute-done | bytes 327712 | tf_op jit(solution)/shard_map/ppermute | solution.py:32
  287.5 13.8 %shard_map.126 = f32[12,16,64,128]{3,2,1,0:T(8,128)} custom-call(s32[12]{0:T(128)} %get-tuple-element.57.owner, s32[12]{0:T(128)} %get-tuple-element.56.member, f32[12,16,64,128]{3,2,1,0:T(8,128)} %state.1, bf16[4,1216,256]{2,1,0:T(8,128)(2,1)} %bitcast.53), custom_call_target="tpu_custom_call" | custom-call | flops 805306368 | bytes 20054016 | tf_op jit(solution)/shard_map/pallas_call | solution.py:265
  (139 shorter events, 57.0 us)
Async XLA Ops:
  9.3 25.0 %collective-permute-start.8 = (bf16[128,640]{1,0:T(8,128)(2,1)}, bf16[128,640]{1,0:T(8,128)(2,1)}, u32[]{:S(2)}, u32[]{:S(2)}) collective-permute-start(bf16[128,640]{1,0:T(8,128)(2,1)} %get-tuple-element.42), channel_id=1, source_target_pairs={{0,12},{4,0},{8,4},{12,8},{1,13},{5,1},{9,5},{13,9},{2,14},{6,2},{... | collective-permute-start | bytes 491528 | tf_op jit(solution)/shard_map/ppermute | solution.py:22
  14.4 21.4 %collective-permute-start.4 = (bf16[128,640]{1,0:T(8,128)(2,1)}, bf16[128,640]{1,0:T(8,128)(2,1)}, u32[]{:S(2)}, u32[]{:S(2)}) collective-permute-start(bf16[128,640]{1,0:T(8,128)(2,1)} %get-tuple-element.43), channel_id=1, source_target_pairs={{0,8},{4,12},{8,0},{12,4},{1,9},{5,13},{9,1},{13,5},{2,10},{6,14},... | collective-permute-start | bytes 491528 | tf_op jit(solution)/shard_map/ppermute | solution.py:22
  14.4 21.9 %collective-permute-start = (bf16[128,640]{1,0:T(8,128)(2,1)}, bf16[128,640]{1,0:T(8,128)(2,1)}, u32[]{:S(2)}, u32[]{:S(2)}) collective-permute-start(bf16[128,640]{1,0:T(8,128)(2,1)} %get-tuple-element.44), channel_id=1, source_target_pairs={{0,4},{4,8},{8,12},{12,0},{1,5},{5,9},{9,13},{13,1},{2,6},{6,10},{... | collective-permute-start | bytes 491528 | tf_op jit(solution)/shard_map/ppermute | solution.py:22
  18.1 30.4 %all-to-all-start = ((bf16[4,400,256]{2,1,0:T(8,128)(2,1)}), bf16[4,400,256]{2,1,0:T(8,128)(2,1)S(1)}, u32[]{:S(2)}, u32[]{:S(2)}) async-start(bf16[4,400,256]{2,1,0:T(8,128)(2,1)} %broadcast_in_dim.77), calls=%async_computation | async-start | bytes 1638400 | tf_op jit(solution)/shard_map/all_to_all | solution.py:38
  22.2 265.3 %all-gather.3.cloned.1.call-start = ((), (), s32[]{:S(2)}) async-start(), calls=%async_computation.1 | async-start | bytes 3112960 | tf_op jit(solution)/shard_map/all_gather | solution.py:384
  34.3 8.3 %collective-permute-start.9 = (bf16[128,640]{1,0:T(8,128)(2,1)}, bf16[128,640]{1,0:T(8,128)(2,1)S(1)}, u32[]{:S(2)}, u32[]{:S(2)}) collective-permute-start(bf16[128,640]{1,0:T(8,128)(2,1)} %collective-permute-done.8), channel_id=1, source_target_pairs={{0,2},{1,3},{2,0},{3,1},{4,6},{5,7},{6,4},{7,5},{8,10},{9,11},{10,... | collective-permute-start | bytes 491528 | tf_op jit(solution)/shard_map/ppermute | solution.py:32
  35.8 11.5 %collective-permute-start.5 = (bf16[128,640]{1,0:T(8,128)(2,1)}, bf16[128,640]{1,0:T(8,128)(2,1)S(1)}, u32[]{:S(2)}, u32[]{:S(2)}) collective-permute-start(bf16[128,640]{1,0:T(8,128)(2,1)} %collective-permute-done.4), channel_id=1, source_target_pairs={{0,2},{1,3},{2,0},{3,1},{4,6},{5,7},{6,4},{7,5},{8,10},{9,11},{10,... | collective-permute-start | bytes 491528 | tf_op jit(solution)/shard_map/ppermute | solution.py:32
  36.3 10.3 %collective-permute-start.1 = (bf16[128,640]{1,0:T(8,128)(2,1)}, bf16[128,640]{1,0:T(8,128)(2,1)S(1)}, u32[]{:S(2)}, u32[]{:S(2)}) collective-permute-start(bf16[128,640]{1,0:T(8,128)(2,1)} %collective-permute-done), channel_id=1, source_target_pairs={{0,2},{1,3},{2,0},{3,1},{4,6},{5,7},{6,4},{7,5},{8,10},{9,11},{10,... | collective-permute-start | bytes 491528 | tf_op jit(solution)/shard_map/ppermute | solution.py:32
  43.3 13.9 %collective-permute-start.10 = (bf16[256,640]{1,0:T(8,128)(2,1)}, bf16[256,640]{1,0:T(8,128)(2,1)}, u32[]{:S(2)}, u32[]{:S(2)}) collective-permute-start(bf16[256,640]{1,0:T(8,128)(2,1)} %constant_dynamic-update-slice_fusion.4), channel_id=1, source_target_pairs={{0,1},{1,0},{2,3},{3,2},{4,5},{5,4},{6,7},{7,6},{8,9},{9,8},{10,11... | collective-permute-start | bytes 983048 | tf_op jit(solution)/shard_map/ppermute | solution.py:27
  48.0 30.2 %collective-permute-start.6 = (bf16[256,640]{1,0:T(8,128)(2,1)}, bf16[256,640]{1,0:T(8,128)(2,1)}, u32[]{:S(2)}, u32[]{:S(2)}) collective-permute-start(bf16[256,640]{1,0:T(8,128)(2,1)} %constant_dynamic-update-slice_fusion.2), channel_id=1, source_target_pairs={{0,1},{1,0},{2,3},{3,2},{4,5},{5,4},{6,7},{7,6},{8,9},{9,8},{10,11... | collective-permute-start | bytes 983048 | tf_op jit(solution)/shard_map/ppermute | solution.py:27
  50.9 10.8 %collective-permute-start.12 = (f32[256,256]{1,0:T(8,128)}, f32[256,256]{1,0:T(8,128)}, u32[]{:S(2)}, u32[]{:S(2)}) collective-permute-start(f32[256,256]{1,0:T(8,128)} %fusion.35), channel_id=1, source_target_pairs={{0,1},{1,0},{2,3},{3,2},{4,5},{5,4},{6,7},{7,6},{8,9},{9,8},{10,11... | collective-permute-start | bytes 786440 | tf_op jit(solution)/shard_map/ppermute | solution.py:27
  53.7 55.6 %collective-permute-start.3 = (bf16[256,1024]{1,0:T(8,128)(2,1)}, bf16[256,1024]{1,0:T(8,128)(2,1)}, u32[]{:S(2)}, u32[]{:S(2)}) collective-permute-start(bf16[256,1024]{1,0:T(8,128)(2,1)} %convolution_convert_fusion.6), channel_id=1, source_target_pairs={{0,12},{4,0},{8,4},{12,8},{1,13},{5,1},{9,5},{13,9},{2,14},{6,2},{... | collective-permute-start | bytes 1572872 | tf_op jit(solution)/shard_map/ppermute | solution.py:22
  60.0 56.2 %collective-permute-start.11 = (bf16[256,1024]{1,0:T(8,128)(2,1)}, bf16[256,1024]{1,0:T(8,128)(2,1)}, u32[]{:S(2)}, u32[]{:S(2)}) collective-permute-start(bf16[256,1024]{1,0:T(8,128)(2,1)} %convolution_convert_fusion.4), channel_id=1, source_target_pairs={{0,4},{4,8},{8,12},{12,0},{1,5},{5,9},{9,13},{13,1},{2,6},{6,10},{... | collective-permute-start | bytes 1572872 | tf_op jit(solution)/shard_map/ppermute | solution.py:22
  62.8 8.5 %collective-permute-start.13 = (f32[256,256]{1,0:T(8,128)S(1)}, f32[256,256]{1,0:T(8,128)S(1)}, u32[]{:S(2)}, u32[]{:S(2)}) collective-permute-start(f32[256,256]{1,0:T(8,128)S(1)} %add.276), channel_id=1, source_target_pairs={{0,2},{1,3},{2,0},{3,1},{4,6},{5,7},{6,4},{7,5},{8,10},{9,11},{10,... | collective-permute-start | bytes 786440 | tf_op jit(solution)/shard_map/ppermute | solution.py:32
  74.7 8.5 %collective-permute-start.16 = (bf16[144,256]{1,0:T(8,128)(2,1)}, bf16[144,256]{1,0:T(8,128)(2,1)S(1)}, u32[]{:S(2)}, u32[]{:S(2)}) collective-permute-start(bf16[144,256]{1,0:T(8,128)(2,1)} %get-tuple-element.26.refs_0_), channel_id=1, source_target_pairs={{0,12},{4,0},{8,4},{12,8},{1,13},{5,1},{9,5},{13,9},{2,14},{6,2},{... | collective-permute-start | bytes 221192 | tf_op jit(solution)/shard_map/ppermute | solution.py:22
  78.2 21.0 %collective-permute-start.15 = (bf16[144,256]{1,0:T(8,128)(2,1)}, bf16[144,256]{1,0:T(8,128)(2,1)S(1)}, u32[]{:S(2)}, u32[]{:S(2)}) collective-permute-start(bf16[144,256]{1,0:T(8,128)(2,1)} %get-tuple-element.26.refs_0_), channel_id=1, source_target_pairs={{0,8},{4,12},{8,0},{12,4},{1,9},{5,13},{9,1},{13,5},{2,10},{6,14},... | collective-permute-start | bytes 221192 | tf_op jit(solution)/shard_map/ppermute | solution.py:22
  78.2 21.0 %collective-permute-start.14 = (bf16[144,256]{1,0:T(8,128)(2,1)}, bf16[144,256]{1,0:T(8,128)(2,1)S(1)}, u32[]{:S(2)}, u32[]{:S(2)}) collective-permute-start(bf16[144,256]{1,0:T(8,128)(2,1)} %get-tuple-element.26.refs_0_), channel_id=1, source_target_pairs={{0,4},{4,8},{8,12},{12,0},{1,5},{5,9},{9,13},{13,1},{2,6},{6,10},{... | collective-permute-start | bytes 221192 | tf_op jit(solution)/shard_map/ppermute | solution.py:22
  83.2 33.0 %collective-permute-start.7 = (bf16[256,1024]{1,0:T(8,128)(2,1)}, bf16[256,1024]{1,0:T(8,128)(2,1)}, u32[]{:S(2)}, u32[]{:S(2)}) collective-permute-start(bf16[256,1024]{1,0:T(8,128)(2,1)} %convolution_convert_fusion.5), channel_id=1, source_target_pairs={{0,8},{4,12},{8,0},{12,4},{1,9},{5,13},{9,1},{13,5},{2,10},{6,14},... | collective-permute-start | bytes 1572872 | tf_op jit(solution)/shard_map/ppermute | solution.py:22
  107.0 16.2 %collective-permute-start.17 = (bf16[256,1024]{1,0:T(8,128)(2,1)}, bf16[256,1024]{1,0:T(8,128)(2,1)S(1)}, u32[]{:S(2)}, u32[]{:S(2)}) collective-permute-start(bf16[256,1024]{1,0:T(8,128)(2,1)} %get-tuple-element.28), channel_id=1, source_target_pairs={{0,12},{4,0},{8,4},{12,8},{1,13},{5,1},{9,5},{13,9},{2,14},{6,2},{... | collective-permute-start | bytes 1572872 | tf_op jit(solution)/shard_map/ppermute | solution.py:22
  107.0 48.4 %collective-permute-start.18 = (bf16[256,1024]{1,0:T(8,128)(2,1)}, bf16[256,1024]{1,0:T(8,128)(2,1)}, u32[]{:S(2)}, u32[]{:S(2)}) collective-permute-start(bf16[256,1024]{1,0:T(8,128)(2,1)} %get-tuple-element.29), channel_id=1, source_target_pairs={{0,8},{4,12},{8,0},{12,4},{1,9},{5,13},{9,1},{13,5},{2,10},{6,14},... | collective-permute-start | bytes 1572872 | tf_op jit(solution)/shard_map/ppermute | solution.py:22
  109.3 46.0 %collective-permute-start.19 = (bf16[256,1024]{1,0:T(8,128)(2,1)}, bf16[256,1024]{1,0:T(8,128)(2,1)}, u32[]{:S(2)}, u32[]{:S(2)}) collective-permute-start(bf16[256,1024]{1,0:T(8,128)(2,1)} %get-tuple-element.30), channel_id=1, source_target_pairs={{0,4},{4,8},{8,12},{12,0},{1,5},{5,9},{9,13},{13,1},{2,6},{6,10},{... | collective-permute-start | bytes 1572872 | tf_op jit(solution)/shard_map/ppermute | solution.py:22
  159.9 20.6 %collective-permute-start.28 = (bf16[256,1024]{1,0:T(8,128)(2,1)S(1)}, bf16[256,1024]{1,0:T(8,128)(2,1)S(1)}, u32[]{:S(2)}, u32[]{:S(2)}) collective-permute-start(bf16[256,1024]{1,0:T(8,128)(2,1)S(1)} %add_convert_fusion), channel_id=1, source_target_pairs={{0,4},{4,8},{8,12},{12,0},{1,5},{5,9},{9,13},{13,1},{2,6},{6,10},{... | collective-permute-start | bytes 1572872 | tf_op jit(solution)/shard_map/ppermute | solution.py:22
  160.4 62.7 %collective-permute-start.24 = (bf16[256,1024]{1,0:T(8,128)(2,1)S(1)}, bf16[256,1024]{1,0:T(8,128)(2,1)S(1)}, u32[]{:S(2)}, u32[]{:S(2)}) collective-permute-start(bf16[256,1024]{1,0:T(8,128)(2,1)S(1)} %add_convert_fusion), channel_id=1, source_target_pairs={{0,8},{4,12},{8,0},{12,4},{1,9},{5,13},{9,1},{13,5},{2,10},{6,14},... | collective-permute-start | bytes 1572872 | tf_op jit(solution)/shard_map/ppermute | solution.py:22
  162.4 61.7 %collective-permute-start.20 = (bf16[256,1024]{1,0:T(8,128)(2,1)S(1)}, bf16[256,1024]{1,0:T(8,128)(2,1)S(1)}, u32[]{:S(2)}, u32[]{:S(2)}) collective-permute-start(bf16[256,1024]{1,0:T(8,128)(2,1)S(1)} %add_convert_fusion), channel_id=1, source_target_pairs={{0,12},{4,0},{8,4},{12,8},{1,13},{5,1},{9,5},{13,9},{2,14},{6,2},{... | collective-permute-start | bytes 1572872 | tf_op jit(solution)/shard_map/ppermute | solution.py:22
  167.1 98.0 %collective-permute-start.33 = (bf16[64,1280]{1,0:T(8,128)(2,1)}, bf16[64,1280]{1,0:T(8,128)(2,1)}, u32[]{:S(2)}, u32[]{:S(2)}) collective-permute-start(bf16[64,1280]{1,0:T(8,128)(2,1)} %constant_dynamic-slice_fusion), channel_id=1, source_target_pairs={{0,2},{1,3},{2,0},{3,1},{4,6},{5,7},{6,4},{7,5},{8,10},{9,11},{10,... | collective-permute-start | bytes 491528 | tf_op jit(solution)/shard_map/ppermute | solution.py:32
  181.3 44.2 %collective-permute-start.29 = (bf16[128,1280]{1,0:T(8,128)(2,1)S(1)}, bf16[128,1280]{1,0:T(8,128)(2,1)S(1)}, u32[]{:S(2)}, u32[]{:S(2)}) collective-permute-start(bf16[128,1280]{1,0:T(8,128)(2,1)S(1)} %constant_dynamic-slice_fusion.3), channel_id=1, source_target_pairs={{0,1},{1,0},{2,3},{3,2},{4,5},{5,4},{6,7},{7,6},{8,9},{9,8},{10,11... | collective-permute-start | bytes 983048 | tf_op jit(solution)/shard_map/ppermute | solution.py:27
  227.3 29.5 %collective-permute-start.26 = (bf16[64,1280]{1,0:T(8,128)(2,1)S(1)}, bf16[64,1280]{1,0:T(8,128)(2,1)S(1)}, u32[]{:S(2)}, u32[]{:S(2)}) collective-permute-start(bf16[64,1280]{1,0:T(8,128)(2,1)S(1)} %constant_dynamic-slice_fusion.4), channel_id=1, source_target_pairs={{0,2},{1,3},{2,0},{3,1},{4,6},{5,7},{6,4},{7,5},{8,10},{9,11},{10,... | collective-permute-start | bytes 491528 | tf_op jit(solution)/shard_map/ppermute | solution.py:32
  228.0 33.0 %collective-permute-start.22 = (bf16[64,1280]{1,0:T(8,128)(2,1)S(1)}, bf16[64,1280]{1,0:T(8,128)(2,1)S(1)}, u32[]{:S(2)}, u32[]{:S(2)}) collective-permute-start(bf16[64,1280]{1,0:T(8,128)(2,1)S(1)} %constant_dynamic-slice_fusion.6), channel_id=1, source_target_pairs={{0,2},{1,3},{2,0},{3,1},{4,6},{5,7},{6,4},{7,5},{8,10},{9,11},{10,... | collective-permute-start | bytes 491528 | tf_op jit(solution)/shard_map/ppermute | solution.py:32
  232.8 32.3 %collective-permute-start.31 = (bf16[64,1280]{1,0:T(8,128)(2,1)S(1)}, bf16[64,1280]{1,0:T(8,128)(2,1)S(1)}, u32[]{:S(2)}, u32[]{:S(2)}) collective-permute-start(bf16[64,1280]{1,0:T(8,128)(2,1)S(1)} %add_convert_fusion.6), channel_id=1, source_target_pairs={{0,12},{4,0},{8,4},{12,8},{1,13},{5,1},{9,5},{13,9},{2,14},{6,2},{... | collective-permute-start | bytes 491528 | tf_op jit(solution)/shard_map/ppermute | solution.py:22
  257.6 15.7 %collective-permute-start.27 = (bf16[64,1280]{1,0:T(8,128)(2,1)}, bf16[64,1280]{1,0:T(8,128)(2,1)S(1)}, u32[]{:S(2)}, u32[]{:S(2)}) collective-permute-start(bf16[64,1280]{1,0:T(8,128)(2,1)} %add_convert_fusion.7), channel_id=1, source_target_pairs={{0,8},{4,12},{8,0},{12,4},{1,9},{5,13},{9,1},{13,5},{2,10},{6,14},... | collective-permute-start | bytes 491528 | tf_op jit(solution)/shard_map/ppermute | solution.py:22
  261.7 11.6 %collective-permute-start.23 = (bf16[64,1280]{1,0:T(8,128)(2,1)}, bf16[64,1280]{1,0:T(8,128)(2,1)}, u32[]{:S(2)}, u32[]{:S(2)}) collective-permute-start(bf16[64,1280]{1,0:T(8,128)(2,1)} %add_convert_fusion.8), channel_id=1, source_target_pairs={{0,4},{4,8},{8,12},{12,0},{1,5},{5,9},{9,13},{13,1},{2,6},{6,10},{... | collective-permute-start | bytes 491528 | tf_op jit(solution)/shard_map/ppermute | solution.py:22
  275.3 8.4 %collective-permute-start.34 = (bf16[2,64,1280]{2,1,0:T(8,128)(2,1)S(1)}, bf16[2,64,1280]{2,1,0:T(8,128)(2,1)}, u32[]{:S(2)}, u32[]{:S(2)}) collective-permute-start(bf16[2,64,1280]{2,1,0:T(8,128)(2,1)S(1)} %pad_maximum_fusion.5), channel_id=1, source_target_pairs={{0,2},{1,3},{2,0},{3,1},{4,6},{5,7},{6,4},{7,5},{8,10},{9,11},{10,... | collective-permute-start | bytes 983048 | tf_op jit(solution)/shard_map/ppermute | solution.py:32
  (17 other events, 256.9 us)
Sparse Core Ops, SparseCore 0:
  160.0 87.7 all-gather.2

commit v5 on v4

v5 whole, which is shorter than its diff:
```python
import functools

import jax
import jax.numpy as jnp
from jax import lax
from jax.experimental import pallas as pl
from jax.experimental.pallas import tpu as pltpu
from jax.sharding import PartitionSpec as P

HIGH = lax.Precision.HIGHEST
BF = jnp.bfloat16
F32 = jnp.float32
NN = (((1,), (0,)), ((), ()))
NT = (((1,), (1,)), ((), ()))
TN = (((0,), (0,)), ((), ()))
TT = (((0,), (1,)), ((), ()))
LANES = 128
PARAMS = pltpu.CompilerParams(vmem_limit_bytes=24 * 1024 * 1024)
COST = pl.CostEstimate(flops=1, bytes_accessed=1, transcendentals=0)


def turn_req(x, turn):
    count = lax.axis_size("req")
    return lax.ppermute(x, "req", [(i, (i + turn) % count) for i in range(count)])


def step_up(x, first, last):
    return lax.ppermute(x, "req", [(i, i + 1) for i in range(first, last)])


def step_down(x, first, last):
    top = lax.axis_size("req") - 1
    return lax.ppermute(x, "req", [(top - i, top - i - 1) for i in range(first, last)])


def line_gather(x):
    count = lax.axis_size("req")
    below, above = [], []
    low = high = x
    for hop in range(count - 1):
        low, high = step_up(low, hop, count - 1), step_down(high, hop, count - 1)
        below.append(low)
        above.append(high)
    return below, above


def line_sum(blocks):
    count = lax.axis_size("req")
    low, high = blocks[1], blocks[count - 1]
    for hop in range(1, count):
        if hop > 1:
            low, high = low + blocks[hop], high + blocks[count - hop]
        low, high = step_up(low, 0, hop), step_down(high, 0, hop)
    return blocks[0], low, high


def swap_core(x):
    count = lax.axis_size("tensor")
    return lax.ppermute(x, "tensor", [(i, i ^ 1) for i in range(count)])


def turn_chip(x, turn):
    count = lax.axis_size("tensor")
    return lax.ppermute(x, "tensor", [(i, (i + 2 * turn) % count) for i in range(count)])


def turn_tensor(x, turn):
    count = lax.axis_size("tensor")
    return lax.ppermute(x, "tensor", [(i, (i + turn) % count) for i in range(count)])


def dot32(a, b, dims):
    return lax.dot_general(a, b, dims, precision=HIGH, preferred_element_type=F32)


def dot16(a, b, dims):
    return lax.dot_general(a, b, dims, preferred_element_type=F32)


def block_kernel(chips, place, w_small, *refs):
    near, far, (block, small) = refs[:chips], refs[chips:-2], refs[-2:]
    piece, half = near[0].shape

    def fill(core):
        own, other = slice(core * half, (core + 1) * half), slice((1 - core) * half, (2 - core) * half)
        for i in range(chips):
            at = lax.rem(place[0] - i + chips, chips) * piece
            rows = pl.ds(pl.multiple_of(at, piece), piece)
            block[rows, own] = near[i][...]
            block[rows, other] = far[i][...]

    for core in range(2):
        pl.when(place[1] == core)(functools.partial(fill, core))
    sums = dot16(block[...], w_small[...], NN)
    lane = lax.broadcasted_iota(jnp.int32, sums.shape, 1)
    low = (lane >= place[2]) & (lane < place[3])
    high = sums.astype(BF)
    small[...] = jnp.where(low, sums - high.astype(F32), sums).astype(BF)


def block_part(place, w_small, near, far):
    chips = len(near)
    num_tok = near[0].shape[0] * chips
    vmem = pl.BlockSpec(memory_space=pltpu.VMEM)
    return pl.pallas_call(
        functools.partial(block_kernel, chips),
        out_shape=[
            jax.ShapeDtypeStruct((num_tok, w_small.shape[0]), BF),
            jax.ShapeDtypeStruct((num_tok, LANES), BF),
        ],
        in_specs=[pl.BlockSpec(memory_space=pltpu.SMEM)] + [vmem] * (1 + 2 * chips),
        compiler_params=PARAMS,
        cost_estimate=COST,
    )(place, w_small, *near, *far)


def product_kernel(block, weights, *refs):
    refs[-1][...] = dot16(block[...], weights[...], NN).astype(BF)


def product_part(block, weights, before):
    vmem = pl.BlockSpec(memory_space=pltpu.VMEM)
    return pl.pallas_call(
        product_kernel,
        out_shape=jax.ShapeDtypeStruct((block.shape[0], weights.shape[1]), BF),
        in_specs=[vmem, vmem] + [pl.BlockSpec(memory_space=pl.ANY)] * len(before),
        compiler_params=PARAMS,
        cost_estimate=COST,
    )(block, weights, *before)


def fold_kernel(share, heads, count, own, *refs):
    parts, (bc_t, raw_t) = refs[:count], refs[-2:]
    lane = lax.broadcasted_iota(jnp.int32, own.shape, 1)
    total = jnp.where(lane < share + heads, own[...], 0.0)
    for part in parts:
        total += part[...].astype(F32)
    total = total.T
    bc_t[...] = total[:share].astype(BF)
    raw_t[...] = total[share : share + heads] + total[share + heads : share + 2 * heads]


def fold_part(own, parts, share, heads, before):
    num_tok = own.shape[0]
    vmem = pl.BlockSpec(memory_space=pltpu.VMEM)
    rest = pl.BlockSpec(memory_space=pl.ANY)
    return pl.pallas_call(
        functools.partial(fold_kernel, share, heads, len(parts)),
        out_shape=[
            jax.ShapeDtypeStruct((share, num_tok), BF),
            jax.ShapeDtypeStruct((heads, num_tok), F32),
        ],
        in_specs=[vmem] * (1 + len(parts)) + [rest] * len(before),
        compiler_params=PARAMS,
        cost_estimate=COST,
    )(own, *parts, *before)


def prep_kernel(count, place, raw_t, bias, rate, seg_row, seg_col, *refs):
    quarters, (bc_t, c_seg, tail_t, run, run_t, step_t) = refs[:count], refs[-6:]
    heads, num_tok = raw_t.shape
    share = quarters[0].shape[0]
    dim = bc_t.shape[0] // 2
    for k, quarter in enumerate(quarters):
        at = lax.rem(place[4] - k + count, count) * share
        bc_t[pl.ds(pl.multiple_of(at, share), share), :] = quarter[...]
    z = raw_t[...] + bias[...]
    step = jnp.maximum(z, 0.0) + jnp.log1p(jnp.exp(-jnp.abs(z)))
    log_decay = -step * rate[...]
    down = lax.broadcasted_iota(jnp.int32, (num_tok, num_tok), 0)
    along = lax.broadcasted_iota(jnp.int32, (num_tok, num_tok), 1)
    same = seg_row[...] == seg_col[...]
    causal = (same & (down >= along)).astype(F32)
    run[...] = dot32(causal, log_decay, NT)
    running = dot32(log_decay, causal, NT)
    totals = dot32(log_decay, same.astype(F32), NT)
    run_t[...] = running
    step_t[...] = step
    grown = jnp.exp(totals)
    high = grown.astype(BF)
    tail_t[...] = jnp.zeros_like(tail_t)
    tail_t[:heads, :] = (jnp.exp(jnp.minimum(totals - running, 0.0)) * step).astype(BF)
    tail_t[16 : 16 + heads, :] = high
    tail_t[32 : 32 + heads, :] = (grown - high.astype(F32)).astype(BF)
    seg_rows = jnp.broadcast_to(seg_col[...].astype(F32), (16, num_tok)).astype(BF)
    tail_t[48:64, :] = seg_rows
    c_seg[:dim, :] = bc_t[dim:, :]
    c_seg[dim:, :] = seg_rows


def prep(place, raw_t, bias, rate, seg, quarters, before):
    heads, num_tok = raw_t.shape
    rows = quarters[0].shape[0] * len(quarters)
    vmem = pl.BlockSpec(memory_space=pltpu.VMEM)
    return pl.pallas_call(
        functools.partial(prep_kernel, len(quarters)),
        out_shape=[
            jax.ShapeDtypeStruct((rows, num_tok), BF),
            jax.ShapeDtypeStruct((rows // 2 + 16, num_tok), BF),
            jax.ShapeDtypeStruct((64, num_tok), BF),
            jax.ShapeDtypeStruct((num_tok, heads), F32),
            jax.ShapeDtypeStruct((heads, num_tok), F32),
            jax.ShapeDtypeStruct((heads, num_tok), F32),
        ],
        in_specs=[pl.BlockSpec(memory_space=pltpu.SMEM)]
        + [vmem] * (5 + len(quarters))
        + [pl.BlockSpec(memory_space=pl.ANY)] * len(before),
        compiler_params=PARAMS,
        cost_estimate=COST,
    )(place, raw_t, bias[:, None], rate[:, None], seg[:, None], seg[None, :], *quarters, *before)


def carried_kernel(owners, ranks, slot, member, *refs):
    c_segs, outs = refs[:owners], refs[-owners:]
    states = refs[owners : owners + ranks]
    heads, width, dim = states[0].shape[1:]
    at = pl.program_id(0)
    flat = [state[0].reshape(heads * width, dim).astype(BF) for state in states]

    def fill(c_seg, out):
        c_rows = c_seg[:dim, :].astype(F32)
        seg = c_seg[dim : dim + 1, :].astype(F32)
        total = jnp.zeros(out.shape, F32)
        for rank in range(ranks):
            inside = seg == member[at * ranks + rank].astype(F32)
            mine = jnp.where(inside, c_rows, 0.0).T.astype(BF)
            total += dot16(mine, flat[rank], NT)
        out[...] = total.astype(BF)

    for i in range(owners):
        pl.when(at == i)(functools.partial(fill, c_segs[i], outs[i]))


def carried_part(slot, member, c_segs, cache, before):
    num_tok = c_segs[0].shape[1]
    _, heads, width, dim = cache.shape
    owners = len(c_segs)
    ranks = slot.shape[0] // owners

    def state_map(rank, i, slot, member):
        return (slot[i * ranks + rank], 0, 0, 0)

    return pl.pallas_call(
        functools.partial(carried_kernel, owners, ranks),
        out_shape=[jax.ShapeDtypeStruct((num_tok, heads * width), BF)] * owners,
        grid_spec=pltpu.PrefetchScalarGridSpec(
            num_scalar_prefetch=2,
            grid=(owners,),
            in_specs=[pl.BlockSpec(c_seg.shape, lambda i, *_: (0, 0)) for c_seg in c_segs]
            + [
                pl.BlockSpec((1, heads, width, dim), functools.partial(state_map, rank))
                for rank in range(ranks)
            ]
            + [pl.BlockSpec(memory_space=pl.ANY)] * len(before),
            out_specs=[pl.BlockSpec((num_tok, heads * width), lambda i, *_: (0, 0))] * owners,
        ),
        compiler_params=PARAMS,
        cost_estimate=COST,
    )(slot, member, *c_segs, *([cache] * ranks), *before)


def gather_kernel(count, *refs):
    parts = refs[:count]
    bc_t, tail_t = refs[count : count + 2]
    x, bundle = refs[-2:]
    columns = x.shape[1]
    dim = bc_t.shape[0] // 2
    for first in range(0, columns, LANES):
        at = slice(first, first + LANES)
        total = parts[0][:, at].astype(F32)
        for part in parts[1:]:
            total += part[:, at].astype(F32)
        x[:, at] = total.astype(BF)
        bundle[at, :] = total.T.astype(BF)
    bundle[columns : columns + dim, :] = bc_t[:dim, :]
    bundle[columns + dim :, :] = tail_t[...]


def gather_part(parts, bc_t, tail_t, before):
    num_tok, columns = parts[0].shape
    rows = columns + bc_t.shape[0] // 2 + tail_t.shape[0]
    vmem = pl.BlockSpec(memory_space=pltpu.VMEM)
    return pl.pallas_call(
        functools.partial(gather_kernel, len(parts)),
        out_shape=[
            jax.ShapeDtypeStruct((num_tok, columns), BF),
            jax.ShapeDtypeStruct((rows, num_tok), BF),
        ],
        in_specs=[vmem] * (len(parts) + 2) + [pl.BlockSpec(memory_space=pl.ANY)] * len(before),
        compiler_params=PARAMS,
        cost_estimate=COST,
    )(*parts, bc_t, tail_t, *before)


def within_kernel(x, bc_t, seg_row, seg_col, run, run_t, step_t, gain, base, grown):
    num_tok, columns = base.shape
    heads = run.shape[1]
    width = columns // heads
    down = lax.broadcasted_iota(jnp.int32, (num_tok, num_tok), 0)
    along = lax.broadcasted_iota(jnp.int32, (num_tok, num_tok), 1)
    keep = (seg_row[...] == seg_col[...]) & (down >= along)
    dim = bc_t.shape[0] // 2
    raw = dot16(bc_t[dim:, :], bc_t[:dim, :], TN)
    scores = jnp.where(keep, raw, 0.0)
    pair = LANES // width
    lane = lax.broadcasted_iota(jnp.int32, (num_tok, LANES), 1) // width
    for first in range(0, heads, pair):
        at = slice(first * width, (first + pair) * width)
        values = x[:, at]
        exact = values.astype(F32)
        total = jnp.zeros((num_tok, LANES), F32)
        rise = jnp.zeros((num_tok, LANES), F32)
        for i in range(pair):
            h = first + i
            run_col = run[:, h : h + 1]
            decay = jnp.exp(jnp.minimum(run_col - run_t[h : h + 1, :], 0.0))
            mixing = (decay * scores * step_t[h : h + 1, :]).astype(BF)
            inner = dot16(mixing, values, NN) + gain[:, h : h + 1] * exact
            total = jnp.where(lane == i, inner, total)
            rise = jnp.where(lane == i, jnp.exp(run_col), rise)
        base[:, at] = total
        grown[:, at] = rise


def within_part(x, bc_t, seg, run, run_t, step_t, gain):
    num_tok, columns = x.shape
    heads = run.shape[1]
    return pl.pallas_call(
        within_kernel,
        out_shape=[jax.ShapeDtypeStruct((num_tok, columns), F32)] * 2,
        compiler_params=PARAMS,
        cost_estimate=COST,
    )(x, bc_t, seg[:, None], seg[None, :], run, run_t, step_t, gain[None])


def outputs_kernel(count, base, grown, *refs):
    held = refs[0][...].astype(F32)
    for block in refs[1:count]:
        held += block[...].astype(F32)
    refs[-1][...] = (base[...] + grown[...] * held).astype(BF)


def outputs_part(base, grown, carried, before):
    vmem = pl.BlockSpec(memory_space=pltpu.VMEM)
    rest = pl.BlockSpec(memory_space=pl.ANY)
    return pl.pallas_call(
        functools.partial(outputs_kernel, len(carried)),
        out_shape=jax.ShapeDtypeStruct(base.shape, BF),
        in_specs=[vmem] * (2 + len(carried)) + [rest] * len(before),
        compiler_params=PARAMS,
        cost_estimate=COST,
    )(base, grown, *carried, *before)


def states_kernel(sources, which, member, state, *refs):
    bundles, (out, done) = refs[:sources], refs[-2:]
    heads, width, dim = state.shape[1:]
    columns = heads * width
    at = pl.program_id(0)
    done[...] = jnp.zeros_like(done)

    def update(bundle):
        b_rows = bundle[columns : columns + dim, :]
        tail = bundle[columns + dim :, :].astype(F32)
        inside = tail[48:49] == member[at].astype(F32)
        weights = jnp.where(inside, tail[:heads], 0.0)
        rise = tail[16 : 16 + heads] + tail[32 : 32 + heads]
        rise = jnp.max(jnp.where(inside, rise, 0.0), axis=1, keepdims=True)
        for h in range(heads):
            rows = slice(h * width, (h + 1) * width)
            scaled = (bundle[rows, :].astype(F32) * weights[h : h + 1]).astype(BF)
            out[0, h] = state[0, h] * rise[h : h + 1] + dot16(scaled, b_rows, NT)

    for i in range(sources):
        pl.when(which[at] == i)(functools.partial(update, bundles[i]))

    @pl.when(which[at] < 0)
    def _():
        out[...] = state[...]


def states_part(which, member, cache, bundles, before):
    slots, heads, width, dim = cache.shape
    rows, num_tok = bundles[0].shape
    slab = pl.BlockSpec((1, heads, width, dim), lambda s, *_: (s, 0, 0, 0))
    fixed = pl.BlockSpec((rows, num_tok), lambda s, *_: (0, 0))
    return pl.pallas_call(
        functools.partial(states_kernel, len(bundles)),
        out_shape=[
            jax.ShapeDtypeStruct(cache.shape, cache.dtype),
            jax.ShapeDtypeStruct((8, LANES), jnp.int32),
        ],
        grid_spec=pltpu.PrefetchScalarGridSpec(
            num_scalar_prefetch=2,
            grid=(slots,),
            in_specs=[slab]
            + [fixed] * len(bundles)
            + [pl.BlockSpec(memory_space=pl.ANY)] * len(before),
            out_specs=[slab, pl.BlockSpec((8, LANES), lambda s, *_: (0, 0))],
        ),
        compiler_params=PARAMS,
        cost_estimate=COST,
    )(which, member, cache, *bundles, *before)


def output_kernel(count, place, w_out, *refs):
    blocks, (kept, given, product) = refs[:count], refs[-3:]
    half = product.shape[0] // 2
    for i, block in enumerate(blocks):
        product[...] = dot16(block[...], w_out[...], NN).astype(BF)
        rows = slice(i * half, (i + 1) * half)
        kept[rows, :] = product[pl.ds(pl.multiple_of(place[1] * half, half), half), :]
        given[rows, :] = product[pl.ds(pl.multiple_of((1 - place[1]) * half, half), half), :]


def output_part(place, w_out, blocks, before):
    vmem = pl.BlockSpec(memory_space=pltpu.VMEM)
    num_tok, columns = blocks[0].shape[0], w_out.shape[1]
    half = jax.ShapeDtypeStruct((len(blocks) * num_tok // 2, columns), BF)
    return pl.pallas_call(
        functools.partial(output_kernel, len(blocks)),
        out_shape=[half, half],
        in_specs=[pl.BlockSpec(memory_space=pltpu.SMEM)]
        + [vmem] * (1 + len(blocks))
        + [pl.BlockSpec(memory_space=pl.ANY)] * len(before),
        scratch_shapes=[pltpu.VMEM((num_tok, columns), BF)],
        compiler_params=PARAMS,
        cost_estimate=COST,
    )(place, w_out, *blocks, *before)


def core_kernel(count, half, place, kept, got, *refs):
    mine, *theirs, total = refs
    chips = 1 + len(theirs)
    share = half // chips
    total[...] = (kept[...].astype(F32) + got[...].astype(F32)).astype(BF)
    for turn, out in enumerate((mine, *theirs)):
        at = lax.rem(place[0] + turn, chips) * share
        for i in range(count):
            rows = pl.ds(pl.multiple_of(i * half + at, share), share)
            out[i * share : (i + 1) * share, :] = total[rows, :]


def core_part(place, kept, got, chips, half):
    vmem = pl.BlockSpec(memory_space=pltpu.VMEM)
    rows, columns = kept.shape
    share = jax.ShapeDtypeStruct((rows // chips, columns), BF)
    mine, *theirs = pl.pallas_call(
        functools.partial(core_kernel, rows // half, half),
        out_shape=[share] * chips,
        in_specs=[pl.BlockSpec(memory_space=pltpu.SMEM), vmem, vmem],
        scratch_shapes=[pltpu.VMEM((rows, columns), BF)],
        compiler_params=PARAMS,
        cost_estimate=COST,
    )(place, kept, got)
    return mine, theirs


def chip_kernel(count, others, mine, *refs):
    theirs, outs = refs[:others], refs[-count:]
    share = mine.shape[0] // count
    for i, out in enumerate(outs):
        rows = slice(i * share, (i + 1) * share)
        total = mine[rows, :].astype(F32)
        for block in theirs:
            total += block[rows, :].astype(F32)
        out[...] = total.astype(BF)


def chip_part(mine, theirs, count, before):
    rows, columns = mine.shape
    vmem = pl.BlockSpec(memory_space=pltpu.VMEM)
    return pl.pallas_call(
        functools.partial(chip_kernel, count, len(theirs)),
        out_shape=[jax.ShapeDtypeStruct((rows // count, columns), BF)] * count,
        in_specs=[vmem] * (1 + len(theirs)) + [pl.BlockSpec(memory_space=pl.ANY)] * len(before),
        compiler_params=PARAMS,
        cost_estimate=COST,
    )(mine, *theirs, *before)


def order_kernel(count, place, *refs):
    out = refs[-1]
    rows = refs[0].shape[0]
    for k in range(count):
        source = lax.rem(place[4] - k + count, count)
        at = (lax.rem(source, 2) * (count // 2) + lax.div(source, 2)) * rows
        out[pl.ds(pl.multiple_of(at, rows), rows), :] = refs[k][...]


def order_part(place, shares):
    vmem = pl.BlockSpec(memory_space=pltpu.VMEM)
    rows, columns = shares[0].shape
    return pl.pallas_call(
        functools.partial(order_kernel, len(shares)),
        out_shape=jax.ShapeDtypeStruct((rows * len(shares), columns), BF),
        in_specs=[pl.BlockSpec(memory_space=pltpu.SMEM)] + [vmem] * len(shares),
        compiler_params=PARAMS,
        cost_estimate=COST,
    )(place, *shares)


def body(
    tokens,
    w_x,
    w_bc,
    w_dt,
    dt_bias,
    decay_rate,
    skip_gain,
    w_out,
    suffix_lengths,
    checkpoint_slot,
    cache,
):
    reqs = lax.axis_size("req")
    tensors = lax.axis_size("tensor")
    chips = tensors // 2
    own_req = lax.axis_index("req")
    own_tensor = lax.axis_index("tensor")
    own_chip = own_tensor // 2
    core = own_tensor % 2
    num_tok = tokens.shape[0]
    depth = w_x.shape[0]
    slots_dev, heads, width, state_dim = cache.shape
    columns = heads * width
    half = depth // 2
    piece = num_tok // chips
    piece = num_tok // chips

    places = jnp.arange(num_tok, dtype=jnp.int32)
    ends = jnp.cumsum(suffix_lengths[0])
    seg = jnp.sum((places[:, None] >= ends[None, :]).astype(jnp.int32), axis=1)

    share = w_bc.shape[1] // tensors
    bc_share = lax.dynamic_slice_in_dim(w_bc, own_tensor * share, share, axis=1)
    w_small = jnp.concatenate(
        [bc_share, w_dt, w_dt, jnp.zeros((depth, LANES - share - 2 * heads), BF)], axis=1
    )
    place = jnp.stack(
        [own_chip, core, 0 * core + share + heads, 0 * core + share + 2 * heads, own_tensor]
    ).astype(jnp.int32)
    own_block = lax.dynamic_slice(tokens, (0, own_req * depth), (num_tok, depth))
    parts = [jnp.dot(own_block, w_x, preferred_element_type=F32).astype(BF)]
    smalls = [jnp.dot(own_block, w_small, preferred_element_type=F32)]
    order = sorted(range(1, reqs), key=lambda k: min(k, reqs - k))
    blocks, own_smalls = [], []
    for k in order:
        start = ((own_req + k) % reqs) * depth + core * half
        block = lax.dynamic_slice(tokens, (own_chip * piece, start), (piece, half))
        block = turn_req(block, k)
        near = [block] + [turn_chip(block, turn) for turn in range(1, chips)]
        block, small = block_part(place, w_small, near, [swap_core(b) for b in near])
        blocks.append(block)
        own_smalls.append(small)
        smalls.append(turn_req(small, -k))
    products = [product_part(blocks[0], w_x, [])]
    for i, block in enumerate(blocks[1:], 1):
        before = [smalls[1], own_smalls[-1]] if i < len(blocks) - 1 else smalls[2:]
        products.append(product_part(block, w_x, before))
    parts += [turn_req(product, -k) for k, product in zip(order, products)]

    bc_share, raw_t = fold_part(smalls[0], smalls[1:], share, heads, [])
    quarters = [bc_share] + [turn_tensor(bc_share, k) for k in range(1, tensors)]
    bc_t, c_seg, tail_t, run, run_t, step_t = prep(
        place, raw_t, dt_bias, decay_rate, seg, quarters, [parts[1], *products[1:]]
    )
    c_segs = [c_seg] + [turn_req(c_seg, k) for k in range(1, reqs)]
    x, bundle = gather_part(parts, bc_t, tail_t, [])
    below, above = line_gather(bundle)

    per_pair = (slots_dev + reqs - 1) // reqs
    total_reqs = checkpoint_slot.shape[0]
    req_dev = total_reqs // reqs
    holder = checkpoint_slot // slots_dev
    index = jnp.arange(total_reqs, dtype=jnp.int32)
    owner = index // req_dev
    pair_key = holder * reqs + owner
    rank_in_pair = jnp.sum(
        (pair_key[:, None] == pair_key[None, :])
        & (checkpoint_slot[None, :] < checkpoint_slot[:, None]),
        axis=1,
    )
    away = (own_req - owner) % reqs
    pairs = jnp.arange(reqs * per_pair, dtype=jnp.int32)
    match = (holder == own_req)[None, :] & (
        (away * per_pair + rank_in_pair)[None, :] == pairs[:, None]
    )

    def pick(match, values, missing):
        found = jnp.sum(jnp.where(match, values[None, :], 0), axis=1)
        return jnp.where(jnp.any(match, axis=1), found, missing).astype(jnp.int32)

    pair_slot = pick(match, checkpoint_slot % slots_dev, 0)
    pair_member = pick(match, index % req_dev, -1)

    carried = carried_part(pair_slot, pair_member, c_segs, cache, [])

    base, grown = within_part(x, bc_t, seg, run, run_t, step_t, skip_gain)
    outputs = outputs_part(base, grown, line_sum(carried), [below[-1], above[-1]])

    slot_ids = own_req * slots_dev + jnp.arange(slots_dev, dtype=jnp.int32)
    match_slot = checkpoint_slot[None, :] == slot_ids[:, None]
    which = jnp.where(owner <= own_req, own_req - owner, reqs - 1 + owner - own_req)

    def sum_cores(kept, given):
        mine, theirs = core_part(place, kept, swap_core(given), chips, num_tok // 2)
        return mine, [turn_chip(block, turn + 1) for turn, block in enumerate(theirs)]

    far = order[-1]
    came = {k: turn_req(outputs, k) for k in order}
    kept, given = output_part(place, w_out, [outputs, came[far]], [])
    new_cache, zero = states_part(
        pick(match_slot, which, -1),
        pick(match_slot, index % req_dev, -1),
        cache,
        [bundle, *below, *above],
        [kept],
    )
    arrived = {}
    arrived[0], block = chip_part(*sum_cores(kept, given), 2, [])
    arrived[far] = turn_req(block, -far)
    kept, given = output_part(place, w_out, [came[k] for k in order[:-1]], [zero, block])
    blocks = chip_part(*sum_cores(kept, given), reqs - 2, [arrived[far]])
    for k, block in zip(order, blocks):
        arrived[k] = turn_req(block, -k)

    def column_block(req):
        chosen = arrived[0]
        for k in range(1, reqs):
            chosen = jnp.where((req - own_req) % reqs == k, arrived[k], chosen)
        return chosen

    shares = [column_block(own_tensor)]
    for k in range(1, tensors):
        block = column_block((own_tensor + k) % tensors)
        shares.append(
            lax.ppermute(block, "tensor", [(i, (i + k) % tensors) for i in range(tensors)])
        )
    layer_out = order_part(place, shares)
    return (layer_out, new_cache)


def solution(mesh):
    placed = (
        P(("groups", "req"), None),
        P("req", "tensor"),
        P("req", None),
        P("req", "tensor"),
        P("tensor"),
        P("tensor"),
        P("tensor"),
        P("tensor", "req"),
        P(("groups", "req"), None),
        P("groups"),
        P(("groups", "req"), "tensor", None, None),
    )
    return jax.shard_map(
        body,
        mesh=mesh,
        in_specs=placed,
        out_specs=(P(("groups", "req"), "tensor"), P(("groups", "req"), "tensor", None, None)),
        check_vma=False,
    )
```

time: 309 us -> 254 us (0.82)
  waiting for transfers between devices: 127 us -> 91.8 us
  starting transfers between devices: 73.2 us -> 99 us
  matrix products: 21.4 us -> 4.14 us
  local copies, waits for them, and re-layouts: 27.9 us -> 13.2 us
  between operations: 14.5 us -> 1.24 us
  other arithmetic: 13.6 us -> 7.88 us
  Pallas kernels: 30.6 us -> 34.7 us
    ppermute x18, waiting for transfers between devices: 109 us -> 52.3 us  [turn_req(): lax.ppermute(x, 'req', [(i, (i + turn) % count) for i in range(count)])]
    ppermute x0 -> x18, starting transfers between devices: none -> 34.4 us  [the longest x6 24.3 us: step_up(): return lax.ppermute(x, 'req', [(i, i + 1) for i in range(first, last)])]
    ppermute x0 -> x18, waiting for transfers between devices: none -> 30.7 us  [the longest x6 15.1 us: step_down(): lax.ppermute(x, 'req', [(top - i, top - i - 1) for i in range(first, last)])]
    dot_general x9 -> x1, matrix products: 18 us -> 1.41 us  [body(): smalls = [jnp.dot(own_block, w_small, preferred_element_type=F32)]]
    ppermute x9 -> x5, waiting for transfers between devices: 17 us -> 6.64 us  [turn_chip(): lax.ppermute(x, 'tensor', [(i, (i + 2 * turn) % count) for i in range(cou...]
    dynamic_slice x12 -> x1, local copies, waits for them, and re-layouts: 8.71 us -> 0.88 us  [body(): bc_share = lax.dynamic_slice_in_dim(w_bc, own_tensor * share, share, axis=1)]
    pallas_call x4 -> x19, Pallas kernels: 26.5 us -> 33 us  [the longest x1 8.92 us: states_part(): pl.pallas_call(functools.partial(states_kernel, len(bundles)), out_shape=...]
    convert_element_type x8 -> x0, other arithmetic: 5.48 us -> none  [the longest x1 2.62 us: body(): outputs = (base + grown * held).astype(BF)]
  transfers between devices with their start and end apart: 38 -> 49, of which waited for: 11 -> 22; matrix products, arithmetic and copies ran while one was open for 18% -> 6% of each run, Pallas kernels for 5% -> 11%
where the time goes in v5:
time: 254 us; the launch traced here: 252 us
  starting transfers between devices  99 us (39%)
  waiting for transfers between devices  91.8 us (36%)
  Pallas kernels  34.7 us (14%)
  local copies, waits for them, and re-layouts  13.2 us (5%)
  other arithmetic  7.88 us (3%)
  matrix products  4.14 us (2%)
    ppermute x18, starting transfers between devices, turn_req(): lax.ppermute(x, 'req', [(i, (i + turn) % count) for i in range(count)])  57.2 us
    ppermute x18, waiting for transfers between devices, turn_req(): lax.ppermute(x, 'req', [(i, (i + turn) % count) for i in range(count)])  52.3 us
    ppermute x6, starting transfers between devices, step_up(): return lax.ppermute(x, 'req', [(i, i + 1) for i in range(first, last)])  24.3 us
    ppermute x6, waiting for transfers between devices, step_down(): lax.ppermute(x, 'req', [(top - i, top - i - 1) for i in range(first, last)])  15.1 us
    pallas_call x1, Pallas kernels, states_part(): pl.pallas_call(functools.partial(states_kernel, len(bundles)), out_shape=...  8.92 us
    unnamed x43, local copies, waits for them, and re-layouts  8.63 us
    ppermute x6, waiting for transfers between devices, step_up(): return lax.ppermute(x, 'req', [(i, i + 1) for i in range(first, last)])  7.77 us
    ppermute x5, starting transfers between devices, turn_chip(): lax.ppermute(x, 'tensor', [(i, (i + 2 * turn) % count) for i in range(cou...  6.69 us
  transfers between devices with their start and end apart: 49, of which 22 were waited for; matrix products, arithmetic and copies ran while one was open for 6% of the time, Pallas kernels for 11%

profile of v5, /device:TPU:0, one launch (start us, length us, event | category | flops | bytes accessed | tf_op | source)
XLA Modules:
  0.0 252.0 jit_solution(5741810571455774513)
XLA Ops:
  2.7 4.0 %collective-permute-start.10 = (bf16[128,640]{1,0:T(8,128)(2,1)}, bf16[128,640]{1,0:T(8,128)(2,1)}, u32[]{:S(2)}, u32[]{:S(2)}) collective-permute-start(bf16[128,640]{1,0:T(8,128)(2,1)} %get-tuple-element.82), channel_id=1, source_target_pairs={{0,8},{4,12},{8,0},{12,4},{1,9},{5,13},{9,1},{13,5},{2,10},{6,14},... | collective-permute-start | bytes 491528 | tf_op jit(solution)/shard_map/ppermute | solution.py:24
  24.6 2.2 collective-permute-done.6.refs_1_
  26.8 2.5 collective-permute-done.1.refs_1_
  36.5 5.0 %collective-permute-start.15 = (bf16[256,128]{1,0:T(8,128)(2,1)S(1)}, bf16[256,128]{1,0:T(8,128)(2,1)S(1)}, u32[]{:S(2)}, u32[]{:S(2)}) collective-permute-start(bf16[256,128]{1,0:T(8,128)(2,1)S(1)} %get-tuple-element.43), channel_id=1, source_target_pairs={{0,4},{4,8},{8,12},{12,0},{1,5},{5,9},{9,13},{13,1},{2,6},{6,10},{... | collective-permute-start | bytes 196616 | tf_op jit(solution)/shard_map/ppermute | solution.py:24
  49.3 2.0 collective-permute-start.17
  53.0 2.7 %convolution_convert_fusion.refs_0_ = bf16[256,1024]{1,0:T(8,128)(2,1)} fusion(bf16[1280,1024]{1,0:T(8,128)(2,1)S(1)} %copy-done.2, bf16[256,5120]{1,0:T(8,128)(2,1)} %param.11, s32[]{:T(128)S(6)} %select_n.245), kind=kOutput, calls=%fused_computation | convolution fusion | flops 671350784 | bytes 3801092 | tf_op jit(solution)/shard_map/dot_general | solution.py:544
  64.7 25.0 %collective-permute-start.21 = (bf16[144,256]{1,0:T(8,128)(2,1)S(1)}, bf16[144,256]{1,0:T(8,128)(2,1)S(1)}, u32[]{:S(2)}, u32[]{:S(2)}) collective-permute-start(bf16[144,256]{1,0:T(8,128)(2,1)S(1)} %get-tuple-element.54.refs_0_), channel_id=1, source_target_pairs={{0,4},{4,8},{8,12},{12,0},{1,5},{5,9},{9,13},{13,1},{2,6},{6,10},{... | collective-permute-start | bytes 221192 | tf_op jit(solution)/shard_map/ppermute | solution.py:24
  89.7 2.4 collective-permute-start.23
  92.1 7.6 %collective-permute-done.17.refs_3_ = bf16[256,1024]{1,0:T(8,128)(2,1)} collective-permute-done((bf16[256,1024]{1,0:T(8,128)(2,1)}, bf16[256,1024]{1,0:T(8,128)(2,1)}, u32[]{:S(2)}, u32[]{:S(2)}) %collective-permute-start.17) | collective-permute-done | bytes 524320 | tf_op jit(solution)/shard_map/ppermute | solution.py:24
  104.2 2.8 %copy-done.1 = f32[12,16,64,128]{3,2,1,0:T(8,128)S(1)} copy-done((f32[12,16,64,128]{3,2,1,0:T(8,128)S(1)}, f32[12,16,64,128]{3,2,1,0:T(8,128)}, u32[]{:S(2)}) %copy-start.1) | copy-done | bytes 6291480
  107.0 3.4 %shard_map.132 = (bf16[256,1024]{1,0:T(8,128)(2,1)S(1)}, bf16[256,1024]{1,0:T(8,128)(2,1)S(1)}, bf16[256,1024]{1,0:T(8,128)(2,1)S(1)}, bf16[256,1024]{1,0:T(8,128)(2,1)S(1)}) custom-call(s32[12]{0:T(128)S(1)} %get-tuple-element.94.slot, s32[12]{0:T(128)S(1)} %get-tuple-element.93.member, bf16[144,256]{1,0:T(8,128)(2,1)S(1)} %get-tuple-element.54.refs_0_, ...), custom_call_target="tpu_custom_call" | custom-call | flops 1 | bytes 1 | tf_op jit(solution)/shard_map/pallas_call | solution.py:243
  110.4 4.6 %collective-permute-start.24 = (bf16[256,1024]{1,0:T(8,128)(2,1)S(1)}, bf16[256,1024]{1,0:T(8,128)(2,1)S(1)}, u32[]{:S(2)}, u32[]{:S(2)}) collective-permute-start(bf16[256,1024]{1,0:T(8,128)(2,1)S(1)} %get-tuple-element.56), channel_id=1, source_target_pairs={{0,4},{1,5},{2,6},{3,7},{16,20},{17,21},{18,22},{19,23}} | collective-permute-start | bytes 1572872 | tf_op jit(solution)/shard_map/ppermute | solution.py:28
  116.5 3.2 %collective-permute-done.33.refs_4_ = bf16[1216,256]{1,0:T(8,128)(2,1)S(1)} collective-permute-done((bf16[1216,256]{1,0:T(8,128)(2,1)S(1)}, bf16[1216,256]{1,0:T(8,128)(2,1)S(1)}, u32[]{:S(2)}, u32[]{:S(2)}) %collective-permute-start.33) | collective-permute-done | bytes 622624 | tf_op jit(solution)/shard_map/ppermute | solution.py:33
  121.0 5.1 %collective-permute-done.24 = bf16[256,1024]{1,0:T(8,128)(2,1)S(1)} collective-permute-done((bf16[256,1024]{1,0:T(8,128)(2,1)S(1)}, bf16[256,1024]{1,0:T(8,128)(2,1)S(1)}, u32[]{:S(2)}, u32[]{:S(2)}) %collective-permute-start.24) | collective-permute-done | bytes 524320 | tf_op jit(solution)/shard_map/ppermute | solution.py:28
  126.9 5.0 %collective-permute-start.25 = (bf16[256,1024]{1,0:T(8,128)(2,1)S(1)}, bf16[256,1024]{1,0:T(8,128)(2,1)S(1)}, u32[]{:S(2)}, u32[]{:S(2)}) collective-permute-start(bf16[256,1024]{1,0:T(8,128)(2,1)S(1)} %get-tuple-element.90), channel_id=1, source_target_pairs={{0,4},{4,8},{1,5},{5,9},{2,6},{6,10},{3,7},{7,11},{16,20},{20,24},... | collective-permute-start | bytes 1572872 | tf_op jit(solution)/shard_map/ppermute | solution.py:28
  132.6 4.0 %collective-permute-done.34.refs_5_ = bf16[1216,256]{1,0:T(8,128)(2,1)S(1)} collective-permute-done((bf16[1216,256]{1,0:T(8,128)(2,1)S(1)}, bf16[1216,256]{1,0:T(8,128)(2,1)S(1)}, u32[]{:S(2)}, u32[]{:S(2)}) %collective-permute-start.34) | collective-permute-done | bytes 622624 | tf_op jit(solution)/shard_map/ppermute | solution.py:33
  139.4 2.6 %collective-permute-done.25 = bf16[256,1024]{1,0:T(8,128)(2,1)S(1)} collective-permute-done((bf16[256,1024]{1,0:T(8,128)(2,1)S(1)}, bf16[256,1024]{1,0:T(8,128)(2,1)S(1)}, u32[]{:S(2)}, u32[]{:S(2)}) %collective-permute-start.25) | collective-permute-done | bytes 524320 | tf_op jit(solution)/shard_map/ppermute | solution.py:28
  142.2 12.0 %collective-permute-start.26 = (bf16[256,1024]{1,0:T(8,128)(2,1)S(1)}, bf16[256,1024]{1,0:T(8,128)(2,1)S(1)}, u32[]{:S(2)}, u32[]{:S(2)}) collective-permute-start(bf16[256,1024]{1,0:T(8,128)(2,1)S(1)} %add.187), channel_id=1, source_target_pairs={{0,4},{4,8},{8,12},{1,5},{5,9},{9,13},{2,6},{6,10},{10,14},{3,7},{... | collective-permute-start | bytes 1572872 | tf_op jit(solution)/shard_map/ppermute | solution.py:28
  155.9 7.9 %collective-permute-done.29.refs_2_ = bf16[256,1024]{1,0:T(8,128)(2,1)S(1)} collective-permute-done((bf16[256,1024]{1,0:T(8,128)(2,1)S(1)}, bf16[256,1024]{1,0:T(8,128)(2,1)S(1)}, u32[]{:S(2)}, u32[]{:S(2)}) %collective-permute-start.29) | collective-permute-done | bytes 524320 | tf_op jit(solution)/shard_map/ppermute | solution.py:33
  164.1 3.4 %collective-permute-start.38 = (bf16[256,1024]{1,0:T(8,128)(2,1)S(1)}, bf16[256,1024]{1,0:T(8,128)(2,1)S(1)}, u32[]{:S(2)}, u32[]{:S(2)}) collective-permute-start(bf16[256,1024]{1,0:T(8,128)(2,1)S(1)} %shard_map.133.refs_0_), channel_id=1, source_target_pairs={{0,8},{4,12},{8,0},{12,4},{1,9},{5,13},{9,1},{13,5},{2,10},{6,14},... | collective-permute-start | bytes 1572872 | tf_op jit(solution)/shard_map/ppermute | solution.py:24
  167.5 20.6 %collective-permute-done.38.refs_1_ = bf16[256,1024]{1,0:T(8,128)(2,1)S(1)} collective-permute-done((bf16[256,1024]{1,0:T(8,128)(2,1)S(1)}, bf16[256,1024]{1,0:T(8,128)(2,1)S(1)}, u32[]{:S(2)}, u32[]{:S(2)}) %collective-permute-start.38) | collective-permute-done | bytes 524320 | tf_op jit(solution)/shard_map/ppermute | solution.py:24
  188.2 2.1 shard_map.134
  190.4 3.8 %collective-permute-start.37 = (bf16[256,1024]{1,0:T(8,128)(2,1)S(1)}, bf16[256,1024]{1,0:T(8,128)(2,1)S(1)}, u32[]{:S(2)}, u32[]{:S(2)}) collective-permute-start(bf16[256,1024]{1,0:T(8,128)(2,1)S(1)} %shard_map.133.refs_0_), channel_id=1, source_target_pairs={{0,12},{4,0},{8,4},{12,8},{1,13},{5,1},{9,5},{13,9},{2,14},{6,2},{... | collective-permute-start | bytes 1572872 | tf_op jit(solution)/shard_map/ppermute | solution.py:24
  197.0 8.9 %shard_map.135 = (f32[12,16,64,128]{3,2,1,0:T(8,128)}, s32[8,128]{1,0:T(8,128)S(1)}) custom-call(s32[12]{0:T(128)S(1)} %get-tuple-element.92.which, s32[12]{0:T(128)S(1)} %get-tuple-element.91.member, f32[12,16,64,128]{3,2,1,0:T(8,128)S(1)} %bitcast.13, bf16[1216,256]{1,0:T(8,128)(2,1)S(1)} %get-tuple-element.59.refs_0_, ...), custom_call_target="tpu_custom_call" | custom-call | flops 1 | bytes 1 | tf_op jit(solution)/shard_map/pallas_call | solution.py:387
  207.0 8.9 %collective-permute-done.37.refs_1_ = bf16[256,1024]{1,0:T(8,128)(2,1)S(1)} collective-permute-done((bf16[256,1024]{1,0:T(8,128)(2,1)S(1)}, bf16[256,1024]{1,0:T(8,128)(2,1)S(1)}, u32[]{:S(2)}, u32[]{:S(2)}) %collective-permute-start.37) | collective-permute-done | bytes 524320 | tf_op jit(solution)/shard_map/ppermute | solution.py:24
  215.9 2.1 shard_map.138
  218.2 2.1 collective-permute-done.41.got
  222.7 2.4 collective-permute-start.43
  225.2 8.0 %collective-permute-done.43.refs_1_ = bf16[64,1280]{1,0:T(8,128)(2,1)S(1)} collective-permute-done((bf16[64,1280]{1,0:T(8,128)(2,1)S(1)}, bf16[64,1280]{1,0:T(8,128)(2,1)S(1)}, u32[]{:S(2)}, u32[]{:S(2)}) %collective-permute-start.43) | collective-permute-done | bytes 163872 | tf_op jit(solution)/shard_map/ppermute | solution.py:24
  233.3 3.8 %collective-permute-start.45 = (bf16[64,1280]{1,0:T(8,128)(2,1)S(1)}, bf16[64,1280]{1,0:T(8,128)(2,1)S(1)}, u32[]{:S(2)}, u32[]{:S(2)}) collective-permute-start(bf16[64,1280]{1,0:T(8,128)(2,1)S(1)} %get-tuple-element.71), channel_id=1, source_target_pairs={{0,12},{4,0},{8,4},{12,8},{1,13},{5,1},{9,5},{13,9},{2,14},{6,2},{... | collective-permute-start | bytes 491528 | tf_op jit(solution)/shard_map/ppermute | solution.py:24
  237.1 5.1 %collective-permute-done.44 = bf16[64,1280]{1,0:T(8,128)(2,1)S(1)} collective-permute-done((bf16[64,1280]{1,0:T(8,128)(2,1)S(1)}, bf16[64,1280]{1,0:T(8,128)(2,1)S(1)}, u32[]{:S(2)}, u32[]{:S(2)}) %collective-permute-start.44) | collective-permute-done | bytes 163872 | tf_op jit(solution)/shard_map/ppermute | solution.py:24
  244.5 3.9 %collective-permute-done.46.refs_1_ = bf16[64,1280]{1,0:T(8,128)(2,1)S(1)} collective-permute-done((bf16[64,1280]{1,0:T(8,128)(2,1)S(1)}, bf16[64,1280]{1,0:T(8,128)(2,1)S(1)}, u32[]{:S(2)}, u32[]{:S(2)}) %collective-permute-start.46) | collective-permute-done | bytes 163872 | tf_op jit(solution)/shard_map/ppermute | solution.py:638
  (158 shorter events, 71.4 us)
Async XLA Ops:
  2.7 13.9 %collective-permute-start.10 = (bf16[128,640]{1,0:T(8,128)(2,1)}, bf16[128,640]{1,0:T(8,128)(2,1)}, u32[]{:S(2)}, u32[]{:S(2)}) collective-permute-start(bf16[128,640]{1,0:T(8,128)(2,1)} %get-tuple-element.82), channel_id=1, source_target_pairs={{0,8},{4,12},{8,0},{12,4},{1,9},{5,13},{9,1},{13,5},{2,10},{6,14},... | collective-permute-start | bytes 491528 | tf_op jit(solution)/shard_map/ppermute | solution.py:24
  6.7 11.8 %collective-permute-start.5 = (bf16[128,640]{1,0:T(8,128)(2,1)}, bf16[128,640]{1,0:T(8,128)(2,1)}, u32[]{:S(2)}, u32[]{:S(2)}) collective-permute-start(bf16[128,640]{1,0:T(8,128)(2,1)} %get-tuple-element.84), channel_id=1, source_target_pairs={{0,12},{4,0},{8,4},{12,8},{1,13},{5,1},{9,5},{13,9},{2,14},{6,2},{... | collective-permute-start | bytes 491528 | tf_op jit(solution)/shard_map/ppermute | solution.py:24
  8.1 11.4 %collective-permute-start = (bf16[128,640]{1,0:T(8,128)(2,1)}, bf16[128,640]{1,0:T(8,128)(2,1)}, u32[]{:S(2)}, u32[]{:S(2)}) collective-permute-start(bf16[128,640]{1,0:T(8,128)(2,1)} %get-tuple-element.83), channel_id=1, source_target_pairs={{0,4},{4,8},{8,12},{12,0},{1,5},{5,9},{9,13},{13,1},{2,6},{6,10},{... | collective-permute-start | bytes 491528 | tf_op jit(solution)/shard_map/ppermute | solution.py:24
  21.4 13.5 %collective-permute-start.7 = (bf16[128,640]{1,0:T(8,128)(2,1)}, bf16[128,640]{1,0:T(8,128)(2,1)}, u32[]{:S(2)}, u32[]{:S(2)}) collective-permute-start(bf16[128,640]{1,0:T(8,128)(2,1)} %collective-permute-done.5.refs_0_), channel_id=1, source_target_pairs={{0,1},{1,0},{2,3},{3,2},{4,5},{5,4},{6,7},{7,6},{8,9},{9,8},{10,11... | collective-permute-start | bytes 491528 | tf_op jit(solution)/shard_map/ppermute | solution.py:59
  23.4 18.1 %collective-permute-start.2 = (bf16[128,640]{1,0:T(8,128)(2,1)}, bf16[128,640]{1,0:T(8,128)(2,1)}, u32[]{:S(2)}, u32[]{:S(2)}) collective-permute-start(bf16[128,640]{1,0:T(8,128)(2,1)} %collective-permute-done.refs_0_), channel_id=1, source_target_pairs={{0,1},{1,0},{2,3},{3,2},{4,5},{5,4},{6,7},{7,6},{8,9},{9,8},{10,11... | collective-permute-start | bytes 491528 | tf_op jit(solution)/shard_map/ppermute | solution.py:59
  29.3 12.3 %collective-permute-start.3 = (bf16[128,640]{1,0:T(8,128)(2,1)}, bf16[128,640]{1,0:T(8,128)(2,1)}, u32[]{:S(2)}, u32[]{:S(2)}) collective-permute-start(bf16[128,640]{1,0:T(8,128)(2,1)} %collective-permute-done.1.refs_1_), channel_id=1, source_target_pairs={{0,1},{1,0},{2,3},{3,2},{4,5},{5,4},{6,7},{7,6},{8,9},{9,8},{10,11... | collective-permute-start | bytes 491528 | tf_op jit(solution)/shard_map/ppermute | solution.py:59
  33.3 14.4 %collective-permute-start.16 = (bf16[256,128]{1,0:T(8,128)(2,1)S(1)}, bf16[256,128]{1,0:T(8,128)(2,1)S(1)}, u32[]{:S(2)}, u32[]{:S(2)}) collective-permute-start(bf16[256,128]{1,0:T(8,128)(2,1)S(1)} %get-tuple-element.41.refs_1_), channel_id=1, source_target_pairs={{0,8},{4,12},{8,0},{12,4},{1,9},{5,13},{9,1},{13,5},{2,10},{6,14},... | collective-permute-start | bytes 196616 | tf_op jit(solution)/shard_map/ppermute | solution.py:24
  36.5 11.2 %collective-permute-start.15 = (bf16[256,128]{1,0:T(8,128)(2,1)S(1)}, bf16[256,128]{1,0:T(8,128)(2,1)S(1)}, u32[]{:S(2)}, u32[]{:S(2)}) collective-permute-start(bf16[256,128]{1,0:T(8,128)(2,1)S(1)} %get-tuple-element.43), channel_id=1, source_target_pairs={{0,4},{4,8},{8,12},{12,0},{1,5},{5,9},{9,13},{13,1},{2,6},{6,10},{... | collective-permute-start | bytes 196616 | tf_op jit(solution)/shard_map/ppermute | solution.py:24
  46.2 17.1 %collective-permute-start.4 = (bf16[256,1024]{1,0:T(8,128)(2,1)}, bf16[256,1024]{1,0:T(8,128)(2,1)}, u32[]{:S(2)}, u32[]{:S(2)}) collective-permute-start(bf16[256,1024]{1,0:T(8,128)(2,1)} %shard_map.123), channel_id=1, source_target_pairs={{0,12},{4,0},{8,4},{12,8},{1,13},{5,1},{9,5},{13,9},{2,14},{6,2},{... | collective-permute-start | bytes 1572872 | tf_op jit(solution)/shard_map/ppermute | solution.py:24
  49.3 50.4 %collective-permute-start.17 = (bf16[256,1024]{1,0:T(8,128)(2,1)}, bf16[256,1024]{1,0:T(8,128)(2,1)}, u32[]{:S(2)}, u32[]{:S(2)}) collective-permute-start(bf16[256,1024]{1,0:T(8,128)(2,1)} %shard_map.127.refs_6_), channel_id=1, source_target_pairs={{0,8},{4,12},{8,0},{12,4},{1,9},{5,13},{9,1},{13,5},{2,10},{6,14},... | collective-permute-start | bytes 1572872 | tf_op jit(solution)/shard_map/ppermute | solution.py:24
  53.0 46.7 %collective-permute-start.14 = (bf16[256,1024]{1,0:T(8,128)(2,1)}, bf16[256,1024]{1,0:T(8,128)(2,1)}, u32[]{:S(2)}, u32[]{:S(2)}) collective-permute-start(bf16[256,1024]{1,0:T(8,128)(2,1)} %shard_map.126.refs_5_), channel_id=1, source_target_pairs={{0,4},{4,8},{8,12},{12,0},{1,5},{5,9},{9,13},{13,1},{2,6},{6,10},{... | collective-permute-start | bytes 1572872 | tf_op jit(solution)/shard_map/ppermute | solution.py:24
  64.7 39.5 %collective-permute-start.21 = (bf16[144,256]{1,0:T(8,128)(2,1)S(1)}, bf16[144,256]{1,0:T(8,128)(2,1)S(1)}, u32[]{:S(2)}, u32[]{:S(2)}) collective-permute-start(bf16[144,256]{1,0:T(8,128)(2,1)S(1)} %get-tuple-element.54.refs_0_), channel_id=1, source_target_pairs={{0,4},{4,8},{8,12},{12,0},{1,5},{5,9},{9,13},{13,1},{2,6},{6,10},{... | collective-permute-start | bytes 221192 | tf_op jit(solution)/shard_map/ppermute | solution.py:24
  89.7 14.5 %collective-permute-start.22 = (bf16[144,256]{1,0:T(8,128)(2,1)S(1)}, bf16[144,256]{1,0:T(8,128)(2,1)S(1)}, u32[]{:S(2)}, u32[]{:S(2)}) collective-permute-start(bf16[144,256]{1,0:T(8,128)(2,1)S(1)} %get-tuple-element.54.refs_0_), channel_id=1, source_target_pairs={{0,8},{4,12},{8,0},{12,4},{1,9},{5,13},{9,1},{13,5},{2,10},{6,14},... | collective-permute-start | bytes 221192 | tf_op jit(solution)/shard_map/ppermute | solution.py:24
  89.7 14.5 %collective-permute-start.23 = (bf16[144,256]{1,0:T(8,128)(2,1)S(1)}, bf16[144,256]{1,0:T(8,128)(2,1)S(1)}, u32[]{:S(2)}, u32[]{:S(2)}) collective-permute-start(bf16[144,256]{1,0:T(8,128)(2,1)S(1)} %get-tuple-element.54.refs_0_), channel_id=1, source_target_pairs={{0,12},{4,0},{8,4},{12,8},{1,13},{5,1},{9,5},{13,9},{2,14},{6,2},{... | collective-permute-start | bytes 221192 | tf_op jit(solution)/shard_map/ppermute | solution.py:24
  101.5 14.3 %collective-permute-start.30 = (bf16[1216,256]{1,0:T(8,128)(2,1)S(1)}, bf16[1216,256]{1,0:T(8,128)(2,1)S(1)}, u32[]{:S(2)}, u32[]{:S(2)}) collective-permute-start(bf16[1216,256]{1,0:T(8,128)(2,1)S(1)} %get-tuple-element.59.refs_0_), channel_id=1, source_target_pairs={{0,4},{4,8},{8,12},{1,5},{5,9},{9,13},{2,6},{6,10},{10,14},{3,7},{... | collective-permute-start | bytes 1867784 | tf_op jit(solution)/shard_map/ppermute | solution.py:28
  102.8 16.9 %collective-permute-start.33 = (bf16[1216,256]{1,0:T(8,128)(2,1)S(1)}, bf16[1216,256]{1,0:T(8,128)(2,1)S(1)}, u32[]{:S(2)}, u32[]{:S(2)}) collective-permute-start(bf16[1216,256]{1,0:T(8,128)(2,1)S(1)} %get-tuple-element.59.refs_0_), channel_id=1, source_target_pairs={{12,8},{8,4},{4,0},{13,9},{9,5},{5,1},{14,10},{10,6},{6,2},{15,11}... | collective-permute-start | bytes 1867784 | tf_op jit(solution)/shard_map/ppermute | solution.py:33
  110.4 15.7 %collective-permute-start.24 = (bf16[256,1024]{1,0:T(8,128)(2,1)S(1)}, bf16[256,1024]{1,0:T(8,128)(2,1)S(1)}, u32[]{:S(2)}, u32[]{:S(2)}) collective-permute-start(bf16[256,1024]{1,0:T(8,128)(2,1)S(1)} %get-tuple-element.56), channel_id=1, source_target_pairs={{0,4},{1,5},{2,6},{3,7},{16,20},{17,21},{18,22},{19,23}} | collective-permute-start | bytes 1572872 | tf_op jit(solution)/shard_map/ppermute | solution.py:28
  115.0 11.1 %collective-permute-start.27 = (bf16[256,1024]{1,0:T(8,128)(2,1)S(1)}, bf16[256,1024]{1,0:T(8,128)(2,1)S(1)}, u32[]{:S(2)}, u32[]{:S(2)}) collective-permute-start(bf16[256,1024]{1,0:T(8,128)(2,1)S(1)} %get-tuple-element.58), channel_id=1, source_target_pairs={{12,8},{13,9},{14,10},{15,11},{28,24},{29,25},{30,26},{31,27}} | collective-permute-start | bytes 1572872 | tf_op jit(solution)/shard_map/ppermute | solution.py:33
  115.8 16.1 %collective-permute-start.31 = (bf16[1216,256]{1,0:T(8,128)(2,1)S(1)}, bf16[1216,256]{1,0:T(8,128)(2,1)S(1)}, u32[]{:S(2)}, u32[]{:S(2)}) collective-permute-start(bf16[1216,256]{1,0:T(8,128)(2,1)S(1)} %collective-permute-done.30.refs_1_), channel_id=1, source_target_pairs={{4,8},{8,12},{5,9},{9,13},{6,10},{10,14},{7,11},{11,15},{20,24},{2... | collective-permute-start | bytes 1867784 | tf_op jit(solution)/shard_map/ppermute | solution.py:28
  119.7 16.9 %collective-permute-start.34 = (bf16[1216,256]{1,0:T(8,128)(2,1)S(1)}, bf16[1216,256]{1,0:T(8,128)(2,1)S(1)}, u32[]{:S(2)}, u32[]{:S(2)}) collective-permute-start(bf16[1216,256]{1,0:T(8,128)(2,1)S(1)} %collective-permute-done.33.refs_4_), channel_id=1, source_target_pairs={{8,4},{4,0},{9,5},{5,1},{10,6},{6,2},{11,7},{7,3},{24,20},{20,16},... | collective-permute-start | bytes 1867784 | tf_op jit(solution)/shard_map/ppermute | solution.py:33
  126.2 11.7 %collective-permute-start.28 = (bf16[256,1024]{1,0:T(8,128)(2,1)S(1)}, bf16[256,1024]{1,0:T(8,128)(2,1)S(1)}, u32[]{:S(2)}, u32[]{:S(2)}) collective-permute-start(bf16[256,1024]{1,0:T(8,128)(2,1)S(1)} %get-tuple-element.89), channel_id=1, source_target_pairs={{12,8},{8,4},{13,9},{9,5},{14,10},{10,6},{15,11},{11,7},{28,24},{2... | collective-permute-start | bytes 1572872 | tf_op jit(solution)/shard_map/ppermute | solution.py:33
  126.9 15.2 %collective-permute-start.25 = (bf16[256,1024]{1,0:T(8,128)(2,1)S(1)}, bf16[256,1024]{1,0:T(8,128)(2,1)S(1)}, u32[]{:S(2)}, u32[]{:S(2)}) collective-permute-start(bf16[256,1024]{1,0:T(8,128)(2,1)S(1)} %get-tuple-element.90), channel_id=1, source_target_pairs={{0,4},{4,8},{1,5},{5,9},{2,6},{6,10},{3,7},{7,11},{16,20},{20,24},... | collective-permute-start | bytes 1572872 | tf_op jit(solution)/shard_map/ppermute | solution.py:28
  131.9 31.9 %collective-permute-start.32 = (bf16[1216,256]{1,0:T(8,128)(2,1)S(1)}, bf16[1216,256]{1,0:T(8,128)(2,1)S(1)}, u32[]{:S(2)}, u32[]{:S(2)}) collective-permute-start(bf16[1216,256]{1,0:T(8,128)(2,1)S(1)} %collective-permute-done.31.refs_2_), channel_id=1, source_target_pairs={{8,12},{9,13},{10,14},{11,15},{24,28},{25,29},{26,30},{27,31}} | collective-permute-start | bytes 1867784 | tf_op jit(solution)/shard_map/ppermute | solution.py:28
  136.6 27.2 %collective-permute-start.35 = (bf16[1216,256]{1,0:T(8,128)(2,1)S(1)}, bf16[1216,256]{1,0:T(8,128)(2,1)S(1)}, u32[]{:S(2)}, u32[]{:S(2)}) collective-permute-start(bf16[1216,256]{1,0:T(8,128)(2,1)S(1)} %collective-permute-done.34.refs_5_), channel_id=1, source_target_pairs={{4,0},{5,1},{6,2},{7,3},{20,16},{21,17},{22,18},{23,19}} | collective-permute-start | bytes 1867784 | tf_op jit(solution)/shard_map/ppermute | solution.py:33
  138.1 25.7 %collective-permute-start.29 = (bf16[256,1024]{1,0:T(8,128)(2,1)S(1)}, bf16[256,1024]{1,0:T(8,128)(2,1)S(1)}, u32[]{:S(2)}, u32[]{:S(2)}) collective-permute-start(bf16[256,1024]{1,0:T(8,128)(2,1)S(1)} %add.189), channel_id=1, source_target_pairs={{12,8},{8,4},{4,0},{13,9},{9,5},{5,1},{14,10},{10,6},{6,2},{15,11}... | collective-permute-start | bytes 1572872 | tf_op jit(solution)/shard_map/ppermute | solution.py:33
  142.2 21.6 %collective-permute-start.26 = (bf16[256,1024]{1,0:T(8,128)(2,1)S(1)}, bf16[256,1024]{1,0:T(8,128)(2,1)S(1)}, u32[]{:S(2)}, u32[]{:S(2)}) collective-permute-start(bf16[256,1024]{1,0:T(8,128)(2,1)S(1)} %add.187), channel_id=1, source_target_pairs={{0,4},{4,8},{8,12},{1,5},{5,9},{9,13},{2,6},{6,10},{10,14},{3,7},{... | collective-permute-start | bytes 1572872 | tf_op jit(solution)/shard_map/ppermute | solution.py:28
  164.1 24.0 %collective-permute-start.38 = (bf16[256,1024]{1,0:T(8,128)(2,1)S(1)}, bf16[256,1024]{1,0:T(8,128)(2,1)S(1)}, u32[]{:S(2)}, u32[]{:S(2)}) collective-permute-start(bf16[256,1024]{1,0:T(8,128)(2,1)S(1)} %shard_map.133.refs_0_), channel_id=1, source_target_pairs={{0,8},{4,12},{8,0},{12,4},{1,9},{5,13},{9,1},{13,5},{2,10},{6,14},... | collective-permute-start | bytes 1572872 | tf_op jit(solution)/shard_map/ppermute | solution.py:24
  190.4 16.6 %collective-permute-start.36 = (bf16[256,1024]{1,0:T(8,128)(2,1)S(1)}, bf16[256,1024]{1,0:T(8,128)(2,1)S(1)}, u32[]{:S(2)}, u32[]{:S(2)}) collective-permute-start(bf16[256,1024]{1,0:T(8,128)(2,1)S(1)} %shard_map.133.refs_0_), channel_id=1, source_target_pairs={{0,4},{4,8},{8,12},{12,0},{1,5},{5,9},{9,13},{13,1},{2,6},{6,10},{... | collective-permute-start | bytes 1572872 | tf_op jit(solution)/shard_map/ppermute | solution.py:24
  190.4 25.5 %collective-permute-start.37 = (bf16[256,1024]{1,0:T(8,128)(2,1)S(1)}, bf16[256,1024]{1,0:T(8,128)(2,1)S(1)}, u32[]{:S(2)}, u32[]{:S(2)}) collective-permute-start(bf16[256,1024]{1,0:T(8,128)(2,1)S(1)} %shard_map.133.refs_0_), channel_id=1, source_target_pairs={{0,12},{4,0},{8,4},{12,8},{1,13},{5,1},{9,5},{13,9},{2,14},{6,2},{... | collective-permute-start | bytes 1572872 | tf_op jit(solution)/shard_map/ppermute | solution.py:24
  195.2 10.7 %collective-permute-start.40 = (bf16[128,1280]{1,0:T(8,128)(2,1)S(1)}, bf16[128,1280]{1,0:T(8,128)(2,1)S(1)}, u32[]{:S(2)}, u32[]{:S(2)}) collective-permute-start(bf16[128,1280]{1,0:T(8,128)(2,1)S(1)} %get-tuple-element.64), channel_id=1, source_target_pairs={{0,2},{1,3},{2,0},{3,1},{4,6},{5,7},{6,4},{7,5},{8,10},{9,11},{10,... | collective-permute-start | bytes 983048 | tf_op jit(solution)/shard_map/ppermute | solution.py:64
  221.2 11.9 %collective-permute-start.42 = (bf16[128,1280]{1,0:T(8,128)(2,1)S(1)}, bf16[128,1280]{1,0:T(8,128)(2,1)S(1)}, u32[]{:S(2)}, u32[]{:S(2)}) collective-permute-start(bf16[128,1280]{1,0:T(8,128)(2,1)S(1)} %get-tuple-element.69), channel_id=1, source_target_pairs={{0,2},{1,3},{2,0},{3,1},{4,6},{5,7},{6,4},{7,5},{8,10},{9,11},{10,... | collective-permute-start | bytes 983048 | tf_op jit(solution)/shard_map/ppermute | solution.py:64
  222.7 10.4 %collective-permute-start.43 = (bf16[64,1280]{1,0:T(8,128)(2,1)S(1)}, bf16[64,1280]{1,0:T(8,128)(2,1)S(1)}, u32[]{:S(2)}, u32[]{:S(2)}) collective-permute-start(bf16[64,1280]{1,0:T(8,128)(2,1)S(1)} %get-tuple-element.65.refs_3_), channel_id=1, source_target_pairs={{0,8},{4,12},{8,0},{12,4},{1,9},{5,13},{9,1},{13,5},{2,10},{6,14},... | collective-permute-start | bytes 491528 | tf_op jit(solution)/shard_map/ppermute | solution.py:24
  (38 other events, 532.4 us)

commit v6 on v5

--- a/solution.py
+++ b/solution.py
@@ -78,7 +78,7 @@
 
 
 def block_kernel(chips, place, w_small, *refs):
-    near, far, (block, small) = refs[:chips], refs[chips:-2], refs[-2:]
+    near, far, (block, small) = refs[:chips], refs[chips : 2 * chips], refs[-2:]
     piece, half = near[0].shape
 
     def fill(core):
@@ -98,7 +98,7 @@
     small[...] = jnp.where(low, sums - high.astype(F32), sums).astype(BF)
 
 
-def block_part(place, w_small, near, far):
+def block_part(place, w_small, near, far, before):
     chips = len(near)
     num_tok = near[0].shape[0] * chips
     vmem = pl.BlockSpec(memory_space=pltpu.VMEM)
@@ -108,10 +108,12 @@
             jax.ShapeDtypeStruct((num_tok, w_small.shape[0]), BF),
             jax.ShapeDtypeStruct((num_tok, LANES), BF),
         ],
-        in_specs=[pl.BlockSpec(memory_space=pltpu.SMEM)] + [vmem] * (1 + 2 * chips),
-        compiler_params=PARAMS,
-        cost_estimate=COST,
-    )(place, w_small, *near, *far)
+        in_specs=[pl.BlockSpec(memory_space=pltpu.SMEM)]
+        + [vmem] * (1 + 2 * chips)
+        + [pl.BlockSpec(memory_space=pl.ANY)] * len(before),
+        compiler_params=PARAMS,
+        cost_estimate=COST,
+    )(place, w_small, *near, *far, *before)
 
 
 def product_kernel(block, weights, *refs):
@@ -479,6 +481,22 @@
     )(mine, *theirs, *before)
 
 
+def hold_kernel(count, *refs):
+    for source, out in zip(refs[:count], refs[-count:]):
+        out[...] = source[...]
+
+
+def hold_part(arrays, before):
+    vmem = pl.BlockSpec(memory_space=pltpu.VMEM)
+    return pl.pallas_call(
+        functools.partial(hold_kernel, len(arrays)),
+        out_shape=[jax.ShapeDtypeStruct(x.shape, x.dtype) for x in arrays],
+        in_specs=[vmem] * len(arrays) + [pl.BlockSpec(memory_space=pl.ANY)] * len(before),
+        compiler_params=PARAMS,
+        cost_estimate=COST,
+    )(*arrays, *before)
+
+
 def order_kernel(count, place, *refs):
     out = refs[-1]
     rows = refs[0].shape[0]
@@ -544,26 +562,30 @@
     parts = [jnp.dot(own_block, w_x, preferred_element_type=F32).astype(BF)]
     smalls = [jnp.dot(own_block, w_small, preferred_element_type=F32)]
     order = sorted(range(1, reqs), key=lambda k: min(k, reqs - k))
-    blocks, own_smalls = [], []
-    for k in order:
+    def token_block(k, first, rows):
         start = ((own_req + k) % reqs) * depth + core * half
-        block = lax.dynamic_slice(tokens, (own_chip * piece, start), (piece, half))
-        block = turn_req(block, k)
-        near = [block] + [turn_chip(block, turn) for turn in range(1, chips)]
-        block, small = block_part(place, w_small, near, [swap_core(b) for b in near])
-        blocks.append(block)
-        own_smalls.append(small)
+        return lax.dynamic_slice(tokens, (first, start), (rows, half))
+
+    arrived = [turn_req(token_block(k, 0, num_tok), k) for k in order[:-1]]
+    products = []
+    for k, near in zip(order, arrived):
+        block, small = block_part(place, w_small, [near], [swap_core(near)], [])
         smalls.append(turn_req(small, -k))
-    products = [product_part(blocks[0], w_x, [])]
-    for i, block in enumerate(blocks[1:], 1):
-        before = [smalls[1], own_smalls[-1]] if i < len(blocks) - 1 else smalls[2:]
-        products.append(product_part(block, w_x, before))
-    parts += [turn_req(product, -k) for k, product in zip(order, products)]
-
-    bc_share, raw_t = fold_part(smalls[0], smalls[1:], share, heads, [])
+        products.append(product_part(block, w_x, []))
+        parts.append(turn_req(products[-1], -k))
+    (near,) = hold_part([token_block(order[-1], own_chip * piece, piece)], arrived[-1:])
+    near = turn_req(near, order[-1])
+    near = [near] + [turn_chip(near, turn) for turn in range(1, chips)]
+    far = [swap_core(block) for block in near]
+    block, small = block_part(place, w_small, near, far, smalls[1:] + parts[1:2])
+    smalls.append(turn_req(small, -order[-1]))
+    products.append(product_part(block, w_x, smalls[-1:]))
+    parts.append(turn_req(products[-1], -order[-1]))
+
+    bc_share, raw_t = fold_part(smalls[0], smalls[1:], share, heads, [*parts[1:-1], products[-1]])
     quarters = [bc_share] + [turn_tensor(bc_share, k) for k in range(1, tensors)]
     bc_t, c_seg, tail_t, run, run_t, step_t = prep(
-        place, raw_t, dt_bias, decay_rate, seg, quarters, [parts[1], *products[1:]]
+        place, raw_t, dt_bias, decay_rate, seg, quarters, []
     )
     c_segs = [c_seg] + [turn_req(c_seg, k) for k in range(1, reqs)]
     x, bundle = gather_part(parts, bc_t, tail_t, [])
@@ -609,7 +631,7 @@
 
     far = order[-1]
     came = {k: turn_req(outputs, k) for k in order}
-    kept, given = output_part(place, w_out, [outputs, came[far]], [])
+    kept, given = output_part(place, w_out, [outputs, came[far]], [below[-1],above[-1]])
     new_cache, zero = states_part(
         pick(match_slot, which, -1),
         pick(match_slot, index % req_dev, -1),
@@ -620,10 +642,13 @@
     arrived = {}
     arrived[0], block = chip_part(*sum_cores(kept, given), 2, [])
     arrived[far] = turn_req(block, -far)
-    kept, given = output_part(place, w_out, [came[k] for k in order[:-1]], [zero, block])
-    blocks = chip_part(*sum_cores(kept, given), reqs - 2, [arrived[far]])
-    for k, block in zip(order, blocks):
+    before = [zero, block]
+    for k in order[:-1]:
+        kept, given = output_part(place, w_out, [came[k]], before)
+        returned = [arrived[j] for j in order if j in arrived] if k == order[-2] else []
+        (block,) = chip_part(*sum_cores(kept, given), 1, returned)
         arrived[k] = turn_req(block, -k)
+        before = [block]
 
     def column_block(req):
         chosen = arrived[0]

time: 254 us -> 247 us (0.972)
  waiting for transfers between devices: 91.8 us -> 114 us
  starting transfers between devices: 99 us -> 78.1 us
  other arithmetic: 7.88 us -> 3.68 us
    ppermute x18, starting transfers between devices: 57.2 us -> 37.4 us  [turn_req(): lax.ppermute(x, 'req', [(i, (i + turn) % count) for i in range(count)])]
    ppermute x18, waiting for transfers between devices: 52.3 us -> 67.4 us  [turn_req(): lax.ppermute(x, 'req', [(i, (i + turn) % count) for i in range(count)])]
    ppermute x6, waiting for transfers between devices: 7.77 us -> 11.2 us  [step_up(): return lax.ppermute(x, 'req', [(i, i + 1) for i in range(first, last)])]
    ppermute x6, starting transfers between devices: 24.3 us -> 21.7 us  [step_up(): return lax.ppermute(x, 'req', [(i, i + 1) for i in range(first, last)])]
    ppermute x5 -> x4, waiting for transfers between devices: 6.64 us -> 8.94 us  [turn_chip(): lax.ppermute(x, 'tensor', [(i, (i + 2 * turn) % count) for i in range(cou...]
    ppermute x5 -> x4, starting transfers between devices: 6.69 us -> 6.14 us  [turn_chip(): lax.ppermute(x, 'tensor', [(i, (i + 2 * turn) % count) for i in range(cou...]
    unnamed x43 -> x35, local copies, waits for them, and re-layouts: 8.63 us -> 8.29 us
  transfers between devices with their start and end apart: 49 -> 47, of which waited for: 22 -> 25; matrix products, arithmetic and copies ran while one was open for 6% -> 5% of each run, Pallas kernels for 11% -> 11%
where the time goes in v6:
time: 247 us; the launch traced here: 246 us
  waiting for transfers between devices  114 us (46%)
  starting transfers between devices  78.1 us (32%)
  Pallas kernels  33.5 us (14%)
  local copies, waits for them, and re-layouts  11.9 us (5%)
  matrix products  4.26 us (2%)
  other arithmetic  3.68 us (1%)
    ppermute x18, waiting for transfers between devices, turn_req(): lax.ppermute(x, 'req', [(i, (i + turn) % count) for i in range(count)])  67.4 us
    ppermute x18, starting transfers between devices, turn_req(): lax.ppermute(x, 'req', [(i, (i + turn) % count) for i in range(count)])  37.4 us
    ppermute x6, starting transfers between devices, step_up(): return lax.ppermute(x, 'req', [(i, i + 1) for i in range(first, last)])  21.7 us
    ppermute x6, waiting for transfers between devices, step_down(): lax.ppermute(x, 'req', [(top - i, top - i - 1) for i in range(first, last)])  15.1 us
    ppermute x6, waiting for transfers between devices, step_up(): return lax.ppermute(x, 'req', [(i, i + 1) for i in range(first, last)])  11.2 us
    ppermute x4, waiting for transfers between devices, turn_chip(): lax.ppermute(x, 'tensor', [(i, (i + 2 * turn) % count) for i in range(cou...  8.94 us
    unnamed x35, local copies, waits for them, and re-layouts  8.29 us
    pallas_call x1, Pallas kernels, states_part(): pl.pallas_call(functools.partial(states_kernel, len(bundles)), out_shape=...  6.66 us
  transfers between devices with their start and end apart: 47, of which 25 were waited for; matrix products, arithmetic and copies ran while one was open for 5% of the time, Pallas kernels for 11%

profile of v6, /device:TPU:0, one launch (start us, length us, event | category | flops | bytes accessed | tf_op | source)
XLA Modules:
  0.0 246.2 jit_solution(9629971578764276908)
XLA Ops:
  2.7 5.0 %collective-permute-start.3 = (bf16[256,640]{1,0:T(8,128)(2,1)}, bf16[256,640]{1,0:T(8,128)(2,1)}, u32[]{:S(2)}, u32[]{:S(2)}) collective-permute-start(bf16[256,640]{1,0:T(8,128)(2,1)} %get-tuple-element.86), channel_id=1, source_target_pairs={{0,12},{4,0},{8,4},{12,8},{1,13},{5,1},{9,5},{13,9},{2,14},{6,2},{... | collective-permute-start | bytes 983048 | tf_op jit(solution)/shard_map/ppermute | solution.py:24
  13.3 9.7 %collective-permute-done.refs_0_ = bf16[256,640]{1,0:T(8,128)(2,1)} collective-permute-done((bf16[256,640]{1,0:T(8,128)(2,1)}, bf16[256,640]{1,0:T(8,128)(2,1)}, u32[]{:S(2)}, u32[]{:S(2)}) %collective-permute-start) | collective-permute-done | bytes 327712 | tf_op jit(solution)/shard_map/ppermute | solution.py:24
  29.6 3.3 %collective-permute-start.2 = (bf16[256,1024]{1,0:T(8,128)(2,1)}, bf16[256,1024]{1,0:T(8,128)(2,1)}, u32[]{:S(2)}, u32[]{:S(2)}) collective-permute-start(bf16[256,1024]{1,0:T(8,128)(2,1)} %shard_map.123), channel_id=1, source_target_pairs={{0,12},{4,0},{8,4},{12,8},{1,13},{5,1},{9,5},{13,9},{2,14},{6,2},{... | collective-permute-start | bytes 1572872 | tf_op jit(solution)/shard_map/ppermute | solution.py:24
  33.1 3.3 %collective-permute-done.6.refs_0_ = bf16[128,640]{1,0:T(8,128)(2,1)} collective-permute-done((bf16[128,640]{1,0:T(8,128)(2,1)}, bf16[128,640]{1,0:T(8,128)(2,1)}, u32[]{:S(2)}, u32[]{:S(2)}) %collective-permute-start.6) | collective-permute-done | bytes 163872 | tf_op jit(solution)/shard_map/ppermute | solution.py:24
  38.0 4.2 %collective-permute-done.7.refs_1_ = bf16[128,640]{1,0:T(8,128)(2,1)} collective-permute-done((bf16[128,640]{1,0:T(8,128)(2,1)}, bf16[128,640]{1,0:T(8,128)(2,1)}, u32[]{:S(2)}, u32[]{:S(2)}) %collective-permute-start.7) | collective-permute-done | bytes 163872 | tf_op jit(solution)/shard_map/ppermute | solution.py:64
  45.0 3.8 %collective-permute-start.10 = (bf16[256,128]{1,0:T(8,128)(2,1)S(1)}, bf16[256,128]{1,0:T(8,128)(2,1)S(1)}, u32[]{:S(2)}, u32[]{:S(2)}) collective-permute-start(bf16[256,128]{1,0:T(8,128)(2,1)S(1)} %get-tuple-element.42), channel_id=1, source_target_pairs={{0,12},{4,0},{8,4},{12,8},{1,13},{5,1},{9,5},{13,9},{2,14},{6,2},{... | collective-permute-start | bytes 196616 | tf_op jit(solution)/shard_map/ppermute | solution.py:24
  55.1 13.0 %collective-permute-done.12.refs_0_.refs_2_ = bf16[256,128]{1,0:T(8,128)(2,1)S(1)} collective-permute-done((bf16[256,128]{1,0:T(8,128)(2,1)S(1)}, bf16[256,128]{1,0:T(8,128)(2,1)S(1)}, u32[]{:S(2)}, u32[]{:S(2)}) %collective-permute-start.12) | collective-permute-done | bytes 65568 | tf_op jit(solution)/shard_map/ppermute | solution.py:24
  69.8 2.8 %convolution_convert_fusion.refs_0_ = bf16[256,1024]{1,0:T(8,128)(2,1)} fusion(bf16[1280,1024]{1,0:T(8,128)(2,1)S(1)} %copy-done.3, bf16[256,5120]{1,0:T(8,128)(2,1)} %param.11, s32[]{:T(128)S(6)} %select_n.243), kind=kOutput, calls=%fused_computation | convolution fusion | flops 671350784 | bytes 3801092 | tf_op jit(solution)/shard_map/dot_general | solution.py:562
  79.5 3.0 %collective-permute-start.18 = (bf16[144,256]{1,0:T(8,128)(2,1)S(1)}, bf16[144,256]{1,0:T(8,128)(2,1)S(1)}, u32[]{:S(2)}, u32[]{:S(2)}) collective-permute-start(bf16[144,256]{1,0:T(8,128)(2,1)S(1)} %get-tuple-element.56.refs_0_), channel_id=1, source_target_pairs={{0,8},{4,12},{8,0},{12,4},{1,9},{5,13},{9,1},{13,5},{2,10},{6,14},... | collective-permute-start | bytes 221192 | tf_op jit(solution)/shard_map/ppermute | solution.py:24
  82.5 2.8 %collective-permute-start.19 = (bf16[144,256]{1,0:T(8,128)(2,1)S(1)}, bf16[144,256]{1,0:T(8,128)(2,1)S(1)}, u32[]{:S(2)}, u32[]{:S(2)}) collective-permute-start(bf16[144,256]{1,0:T(8,128)(2,1)S(1)} %get-tuple-element.56.refs_0_), channel_id=1, source_target_pairs={{0,12},{4,0},{8,4},{12,8},{1,13},{5,1},{9,5},{13,9},{2,14},{6,2},{... | collective-permute-start | bytes 221192 | tf_op jit(solution)/shard_map/ppermute | solution.py:24
  85.3 11.4 %collective-permute-done.13.refs_3_ = bf16[256,1024]{1,0:T(8,128)(2,1)} collective-permute-done((bf16[256,1024]{1,0:T(8,128)(2,1)}, bf16[256,1024]{1,0:T(8,128)(2,1)}, u32[]{:S(2)}, u32[]{:S(2)}) %collective-permute-start.13) | collective-permute-done | bytes 524320 | tf_op jit(solution)/shard_map/ppermute | solution.py:24
  102.1 2.8 %copy-done.1 = f32[12,16,64,128]{3,2,1,0:T(8,128)S(1)} copy-done((f32[12,16,64,128]{3,2,1,0:T(8,128)S(1)}, f32[12,16,64,128]{3,2,1,0:T(8,128)}, u32[]{:S(2)}) %copy-start.1) | copy-done | bytes 6291480
  104.9 3.4 %shard_map.133 = (bf16[256,1024]{1,0:T(8,128)(2,1)S(1)}, bf16[256,1024]{1,0:T(8,128)(2,1)S(1)}, bf16[256,1024]{1,0:T(8,128)(2,1)S(1)}, bf16[256,1024]{1,0:T(8,128)(2,1)S(1)}) custom-call(s32[12]{0:T(128)S(1)} %get-tuple-element.97.slot, s32[12]{0:T(128)S(1)} %get-tuple-element.96.member, bf16[144,256]{1,0:T(8,128)(2,1)S(1)} %get-tuple-element.56.refs_0_, ...), custom_call_target="tpu_custom_call" | custom-call | flops 1 | bytes 1 | tf_op jit(solution)/shard_map/pallas_call | solution.py:245
  108.3 4.6 %collective-permute-start.20 = (bf16[256,1024]{1,0:T(8,128)(2,1)S(1)}, bf16[256,1024]{1,0:T(8,128)(2,1)S(1)}, u32[]{:S(2)}, u32[]{:S(2)}) collective-permute-start(bf16[256,1024]{1,0:T(8,128)(2,1)S(1)} %get-tuple-element.58), channel_id=1, source_target_pairs={{0,4},{1,5},{2,6},{3,7},{16,20},{17,21},{18,22},{19,23}} | collective-permute-start | bytes 1572872 | tf_op jit(solution)/shard_map/ppermute | solution.py:28
  115.8 2.7 %collective-permute-done.29.refs_4_ = bf16[1216,256]{1,0:T(8,128)(2,1)S(1)} collective-permute-done((bf16[1216,256]{1,0:T(8,128)(2,1)S(1)}, bf16[1216,256]{1,0:T(8,128)(2,1)S(1)}, u32[]{:S(2)}, u32[]{:S(2)}) %collective-permute-start.29) | collective-permute-done | bytes 622624 | tf_op jit(solution)/shard_map/ppermute | solution.py:33
  119.8 5.8 %collective-permute-done.20 = bf16[256,1024]{1,0:T(8,128)(2,1)S(1)} collective-permute-done((bf16[256,1024]{1,0:T(8,128)(2,1)S(1)}, bf16[256,1024]{1,0:T(8,128)(2,1)S(1)}, u32[]{:S(2)}, u32[]{:S(2)}) %collective-permute-start.20) | collective-permute-done | bytes 524320 | tf_op jit(solution)/shard_map/ppermute | solution.py:28
  126.4 5.0 %collective-permute-start.21 = (bf16[256,1024]{1,0:T(8,128)(2,1)S(1)}, bf16[256,1024]{1,0:T(8,128)(2,1)S(1)}, u32[]{:S(2)}, u32[]{:S(2)}) collective-permute-start(bf16[256,1024]{1,0:T(8,128)(2,1)S(1)} %get-tuple-element.93), channel_id=1, source_target_pairs={{0,4},{4,8},{1,5},{5,9},{2,6},{6,10},{3,7},{7,11},{16,20},{20,24},... | collective-permute-start | bytes 1572872 | tf_op jit(solution)/shard_map/ppermute | solution.py:28
  132.2 3.3 %collective-permute-done.30.refs_5_ = bf16[1216,256]{1,0:T(8,128)(2,1)S(1)} collective-permute-done((bf16[1216,256]{1,0:T(8,128)(2,1)S(1)}, bf16[1216,256]{1,0:T(8,128)(2,1)S(1)}, u32[]{:S(2)}, u32[]{:S(2)}) %collective-permute-start.30) | collective-permute-done | bytes 622624 | tf_op jit(solution)/shard_map/ppermute | solution.py:33
  138.2 3.9 %collective-permute-done.21 = bf16[256,1024]{1,0:T(8,128)(2,1)S(1)} collective-permute-done((bf16[256,1024]{1,0:T(8,128)(2,1)S(1)}, bf16[256,1024]{1,0:T(8,128)(2,1)S(1)}, u32[]{:S(2)}, u32[]{:S(2)}) %collective-permute-start.21) | collective-permute-done | bytes 524320 | tf_op jit(solution)/shard_map/ppermute | solution.py:28
  142.3 9.4 %collective-permute-start.22 = (bf16[256,1024]{1,0:T(8,128)(2,1)S(1)}, bf16[256,1024]{1,0:T(8,128)(2,1)S(1)}, u32[]{:S(2)}, u32[]{:S(2)}) collective-permute-start(bf16[256,1024]{1,0:T(8,128)(2,1)S(1)} %add.185), channel_id=1, source_target_pairs={{0,4},{4,8},{8,12},{1,5},{5,9},{9,13},{2,6},{6,10},{10,14},{3,7},{... | collective-permute-start | bytes 1572872 | tf_op jit(solution)/shard_map/ppermute | solution.py:28
  153.5 9.1 %collective-permute-done.25.refs_2_ = bf16[256,1024]{1,0:T(8,128)(2,1)S(1)} collective-permute-done((bf16[256,1024]{1,0:T(8,128)(2,1)S(1)}, bf16[256,1024]{1,0:T(8,128)(2,1)S(1)}, u32[]{:S(2)}, u32[]{:S(2)}) %collective-permute-start.25) | collective-permute-done | bytes 524320 | tf_op jit(solution)/shard_map/ppermute | solution.py:33
  162.9 7.7 %collective-permute-start.34 = (bf16[256,1024]{1,0:T(8,128)(2,1)S(1)}, bf16[256,1024]{1,0:T(8,128)(2,1)S(1)}, u32[]{:S(2)}, u32[]{:S(2)}) collective-permute-start(bf16[256,1024]{1,0:T(8,128)(2,1)S(1)} %shard_map.134.refs_0_), channel_id=1, source_target_pairs={{0,8},{4,12},{8,0},{12,4},{1,9},{5,13},{9,1},{13,5},{2,10},{6,14},... | collective-permute-start | bytes 1572872 | tf_op jit(solution)/shard_map/ppermute | solution.py:24
  170.7 14.7 %collective-permute-done.34.refs_1_ = bf16[256,1024]{1,0:T(8,128)(2,1)S(1)} collective-permute-done((bf16[256,1024]{1,0:T(8,128)(2,1)S(1)}, bf16[256,1024]{1,0:T(8,128)(2,1)S(1)}, u32[]{:S(2)}, u32[]{:S(2)}) %collective-permute-start.34) | collective-permute-done | bytes 524320 | tf_op jit(solution)/shard_map/ppermute | solution.py:24
  185.4 2.1 shard_map.135
  194.6 6.7 %shard_map.136 = (f32[12,16,64,128]{3,2,1,0:T(8,128)}, s32[8,128]{1,0:T(8,128)S(1)}) custom-call(s32[12]{0:T(128)S(1)} %get-tuple-element.95.which, s32[12]{0:T(128)S(1)} %get-tuple-element.94.member, f32[12,16,64,128]{3,2,1,0:T(8,128)S(1)} %bitcast.13, bf16[1216,256]{1,0:T(8,128)(2,1)S(1)} %get-tuple-element.61.refs_0_, ...), custom_call_target="tpu_custom_call" | custom-call | flops 1 | bytes 1 | tf_op jit(solution)/shard_map/pallas_call | solution.py:389
  201.3 3.0 %collective-permute-done.33.refs_0_ = bf16[256,1024]{1,0:T(8,128)(2,1)S(1)} collective-permute-done((bf16[256,1024]{1,0:T(8,128)(2,1)S(1)}, bf16[256,1024]{1,0:T(8,128)(2,1)S(1)}, u32[]{:S(2)}, u32[]{:S(2)}) %collective-permute-start.33) | collective-permute-done | bytes 524320 | tf_op jit(solution)/shard_map/ppermute | solution.py:24
  209.7 4.8 %collective-permute-done.38.refs_0_ = bf16[64,1280]{1,0:T(8,128)(2,1)S(1)} collective-permute-done((bf16[64,1280]{1,0:T(8,128)(2,1)S(1)}, bf16[64,1280]{1,0:T(8,128)(2,1)S(1)}, u32[]{:S(2)}, u32[]{:S(2)}) %collective-permute-start.38) | collective-permute-done | bytes 163872 | tf_op jit(solution)/shard_map/ppermute | solution.py:64
  217.2 2.3 collective-permute-start.41
  221.8 5.8 %collective-permute-done.42.refs_2_ = bf16[64,1280]{1,0:T(8,128)(2,1)S(1)} collective-permute-done((bf16[64,1280]{1,0:T(8,128)(2,1)S(1)}, bf16[64,1280]{1,0:T(8,128)(2,1)S(1)}, u32[]{:S(2)}, u32[]{:S(2)}) %collective-permute-start.42) | collective-permute-done | bytes 163872 | tf_op jit(solution)/shard_map/ppermute | solution.py:24
  227.6 4.1 %collective-permute-start.43 = (bf16[64,1280]{1,0:T(8,128)(2,1)S(1)}, bf16[64,1280]{1,0:T(8,128)(2,1)S(1)}, u32[]{:S(2)}, u32[]{:S(2)}) collective-permute-start(bf16[64,1280]{1,0:T(8,128)(2,1)S(1)} %shard_map.144), channel_id=1, source_target_pairs={{0,4},{4,8},{8,12},{12,0},{1,5},{5,9},{9,13},{13,1},{2,6},{6,10},{... | collective-permute-start | bytes 491528 | tf_op jit(solution)/shard_map/ppermute | solution.py:24
  231.7 3.9 %collective-permute-done.43 = bf16[64,1280]{1,0:T(8,128)(2,1)S(1)} collective-permute-done((bf16[64,1280]{1,0:T(8,128)(2,1)S(1)}, bf16[64,1280]{1,0:T(8,128)(2,1)S(1)}, u32[]{:S(2)}, u32[]{:S(2)}) %collective-permute-start.43) | collective-permute-done | bytes 163872 | tf_op jit(solution)/shard_map/ppermute | solution.py:24
  238.7 2.9 %collective-permute-done.44.refs_1_ = bf16[64,1280]{1,0:T(8,128)(2,1)S(1)} collective-permute-done((bf16[64,1280]{1,0:T(8,128)(2,1)S(1)}, bf16[64,1280]{1,0:T(8,128)(2,1)S(1)}, u32[]{:S(2)}, u32[]{:S(2)}) %collective-permute-start.44) | collective-permute-done | bytes 163872 | tf_op jit(solution)/shard_map/ppermute | solution.py:663
  (151 shorter events, 74.6 us)
Async XLA Ops:
  2.7 21.3 %collective-permute-start.3 = (bf16[256,640]{1,0:T(8,128)(2,1)}, bf16[256,640]{1,0:T(8,128)(2,1)}, u32[]{:S(2)}, u32[]{:S(2)}) collective-permute-start(bf16[256,640]{1,0:T(8,128)(2,1)} %get-tuple-element.86), channel_id=1, source_target_pairs={{0,12},{4,0},{8,4},{12,8},{1,13},{5,1},{9,5},{13,9},{2,14},{6,2},{... | collective-permute-start | bytes 983048 | tf_op jit(solution)/shard_map/ppermute | solution.py:24
  7.8 15.2 %collective-permute-start = (bf16[256,640]{1,0:T(8,128)(2,1)}, bf16[256,640]{1,0:T(8,128)(2,1)}, u32[]{:S(2)}, u32[]{:S(2)}) collective-permute-start(bf16[256,640]{1,0:T(8,128)(2,1)} %get-tuple-element.87), channel_id=1, source_target_pairs={{0,4},{4,8},{8,12},{12,0},{1,5},{5,9},{9,13},{13,1},{2,6},{6,10},{... | collective-permute-start | bytes 983048 | tf_op jit(solution)/shard_map/ppermute | solution.py:24
  24.7 11.8 %collective-permute-start.6 = (bf16[128,640]{1,0:T(8,128)(2,1)}, bf16[128,640]{1,0:T(8,128)(2,1)}, u32[]{:S(2)}, u32[]{:S(2)}) collective-permute-start(bf16[128,640]{1,0:T(8,128)(2,1)} %shard_map.126), channel_id=1, source_target_pairs={{0,8},{4,12},{8,0},{12,4},{1,9},{5,13},{9,1},{13,5},{2,10},{6,14},... | collective-permute-start | bytes 491528 | tf_op jit(solution)/shard_map/ppermute | solution.py:24
  29.6 22.1 %collective-permute-start.2 = (bf16[256,1024]{1,0:T(8,128)(2,1)}, bf16[256,1024]{1,0:T(8,128)(2,1)}, u32[]{:S(2)}, u32[]{:S(2)}) collective-permute-start(bf16[256,1024]{1,0:T(8,128)(2,1)} %shard_map.123), channel_id=1, source_target_pairs={{0,12},{4,0},{8,4},{12,8},{1,13},{5,1},{9,5},{13,9},{2,14},{6,2},{... | collective-permute-start | bytes 1572872 | tf_op jit(solution)/shard_map/ppermute | solution.py:24
  33.0 9.4 %collective-permute-start.4 = (bf16[256,640]{1,0:T(8,128)(2,1)}, bf16[256,640]{1,0:T(8,128)(2,1)}, u32[]{:S(2)}, u32[]{:S(2)}) collective-permute-start(bf16[256,640]{1,0:T(8,128)(2,1)} %collective-permute-done.3.refs_0_.refs_1_), channel_id=1, source_target_pairs={{0,1},{1,0},{2,3},{3,2},{4,5},{5,4},{6,7},{7,6},{8,9},{9,8},{10,11... | collective-permute-start | bytes 983048 | tf_op jit(solution)/shard_map/ppermute | solution.py:59
  38.0 11.7 %collective-permute-start.8 = (bf16[128,640]{1,0:T(8,128)(2,1)}, bf16[128,640]{1,0:T(8,128)(2,1)}, u32[]{:S(2)}, u32[]{:S(2)}) collective-permute-start(bf16[128,640]{1,0:T(8,128)(2,1)} %collective-permute-done.6.refs_0_), channel_id=1, source_target_pairs={{0,1},{1,0},{2,3},{3,2},{4,5},{5,4},{6,7},{7,6},{8,9},{9,8},{10,11... | collective-permute-start | bytes 491528 | tf_op jit(solution)/shard_map/ppermute | solution.py:59
  42.2 9.5 %collective-permute-start.9 = (bf16[128,640]{1,0:T(8,128)(2,1)}, bf16[128,640]{1,0:T(8,128)(2,1)}, u32[]{:S(2)}, u32[]{:S(2)}) collective-permute-start(bf16[128,640]{1,0:T(8,128)(2,1)} %collective-permute-done.7.refs_1_), channel_id=1, source_target_pairs={{0,1},{1,0},{2,3},{3,2},{4,5},{5,4},{6,7},{7,6},{8,9},{9,8},{10,11... | collective-permute-start | bytes 491528 | tf_op jit(solution)/shard_map/ppermute | solution.py:59
  49.7 22.9 %collective-permute-start.5 = (bf16[256,1024]{1,0:T(8,128)(2,1)S(1)}, bf16[256,1024]{1,0:T(8,128)(2,1)S(1)}, u32[]{:S(2)}, u32[]{:S(2)}) collective-permute-start(bf16[256,1024]{1,0:T(8,128)(2,1)S(1)} %shard_map.125), channel_id=1, source_target_pairs={{0,4},{4,8},{8,12},{12,0},{1,5},{5,9},{9,13},{13,1},{2,6},{6,10},{... | collective-permute-start | bytes 1572872 | tf_op jit(solution)/shard_map/ppermute | solution.py:24
  53.3 14.8 %collective-permute-start.12 = (bf16[256,128]{1,0:T(8,128)(2,1)S(1)}, bf16[256,128]{1,0:T(8,128)(2,1)S(1)}, u32[]{:S(2)}, u32[]{:S(2)}) collective-permute-start(bf16[256,128]{1,0:T(8,128)(2,1)S(1)} %get-tuple-element.45), channel_id=1, source_target_pairs={{0,8},{4,12},{8,0},{12,4},{1,9},{5,13},{9,1},{13,5},{2,10},{6,14},... | collective-permute-start | bytes 196616 | tf_op jit(solution)/shard_map/ppermute | solution.py:24
  69.7 27.0 %collective-permute-start.13 = (bf16[256,1024]{1,0:T(8,128)(2,1)}, bf16[256,1024]{1,0:T(8,128)(2,1)}, u32[]{:S(2)}, u32[]{:S(2)}) collective-permute-start(bf16[256,1024]{1,0:T(8,128)(2,1)} %shard_map.128.refs_5_), channel_id=1, source_target_pairs={{0,8},{4,12},{8,0},{12,4},{1,9},{5,13},{9,1},{13,5},{2,10},{6,14},... | collective-permute-start | bytes 1572872 | tf_op jit(solution)/shard_map/ppermute | solution.py:24
  79.4 22.7 %collective-permute-start.17 = (bf16[144,256]{1,0:T(8,128)(2,1)S(1)}, bf16[144,256]{1,0:T(8,128)(2,1)S(1)}, u32[]{:S(2)}, u32[]{:S(2)}) collective-permute-start(bf16[144,256]{1,0:T(8,128)(2,1)S(1)} %get-tuple-element.56.refs_0_), channel_id=1, source_target_pairs={{0,4},{4,8},{8,12},{12,0},{1,5},{5,9},{9,13},{13,1},{2,6},{6,10},{... | collective-permute-start | bytes 221192 | tf_op jit(solution)/shard_map/ppermute | solution.py:24
  79.5 22.6 %collective-permute-start.18 = (bf16[144,256]{1,0:T(8,128)(2,1)S(1)}, bf16[144,256]{1,0:T(8,128)(2,1)S(1)}, u32[]{:S(2)}, u32[]{:S(2)}) collective-permute-start(bf16[144,256]{1,0:T(8,128)(2,1)S(1)} %get-tuple-element.56.refs_0_), channel_id=1, source_target_pairs={{0,8},{4,12},{8,0},{12,4},{1,9},{5,13},{9,1},{13,5},{2,10},{6,14},... | collective-permute-start | bytes 221192 | tf_op jit(solution)/shard_map/ppermute | solution.py:24
  82.5 19.7 %collective-permute-start.19 = (bf16[144,256]{1,0:T(8,128)(2,1)S(1)}, bf16[144,256]{1,0:T(8,128)(2,1)S(1)}, u32[]{:S(2)}, u32[]{:S(2)}) collective-permute-start(bf16[144,256]{1,0:T(8,128)(2,1)S(1)} %get-tuple-element.56.refs_0_), channel_id=1, source_target_pairs={{0,12},{4,0},{8,4},{12,8},{1,13},{5,1},{9,5},{13,9},{2,14},{6,2},{... | collective-permute-start | bytes 221192 | tf_op jit(solution)/shard_map/ppermute | solution.py:24
  99.4 15.7 %collective-permute-start.26 = (bf16[1216,256]{1,0:T(8,128)(2,1)S(1)}, bf16[1216,256]{1,0:T(8,128)(2,1)S(1)}, u32[]{:S(2)}, u32[]{:S(2)}) collective-permute-start(bf16[1216,256]{1,0:T(8,128)(2,1)S(1)} %get-tuple-element.61.refs_0_), channel_id=1, source_target_pairs={{0,4},{4,8},{8,12},{1,5},{5,9},{9,13},{2,6},{6,10},{10,14},{3,7},{... | collective-permute-start | bytes 1867784 | tf_op jit(solution)/shard_map/ppermute | solution.py:28
  100.8 17.8 %collective-permute-start.29 = (bf16[1216,256]{1,0:T(8,128)(2,1)S(1)}, bf16[1216,256]{1,0:T(8,128)(2,1)S(1)}, u32[]{:S(2)}, u32[]{:S(2)}) collective-permute-start(bf16[1216,256]{1,0:T(8,128)(2,1)S(1)} %get-tuple-element.61.refs_0_), channel_id=1, source_target_pairs={{12,8},{8,4},{4,0},{13,9},{9,5},{5,1},{14,10},{10,6},{6,2},{15,11}... | collective-permute-start | bytes 1867784 | tf_op jit(solution)/shard_map/ppermute | solution.py:33
  108.3 17.3 %collective-permute-start.20 = (bf16[256,1024]{1,0:T(8,128)(2,1)S(1)}, bf16[256,1024]{1,0:T(8,128)(2,1)S(1)}, u32[]{:S(2)}, u32[]{:S(2)}) collective-permute-start(bf16[256,1024]{1,0:T(8,128)(2,1)S(1)} %get-tuple-element.58), channel_id=1, source_target_pairs={{0,4},{1,5},{2,6},{3,7},{16,20},{17,21},{18,22},{19,23}} | collective-permute-start | bytes 1572872 | tf_op jit(solution)/shard_map/ppermute | solution.py:28
  112.9 12.7 %collective-permute-start.23 = (bf16[256,1024]{1,0:T(8,128)(2,1)S(1)}, bf16[256,1024]{1,0:T(8,128)(2,1)S(1)}, u32[]{:S(2)}, u32[]{:S(2)}) collective-permute-start(bf16[256,1024]{1,0:T(8,128)(2,1)S(1)} %get-tuple-element.60), channel_id=1, source_target_pairs={{12,8},{13,9},{14,10},{15,11},{28,24},{29,25},{30,26},{31,27}} | collective-permute-start | bytes 1572872 | tf_op jit(solution)/shard_map/ppermute | solution.py:33
  115.1 16.3 %collective-permute-start.27 = (bf16[1216,256]{1,0:T(8,128)(2,1)S(1)}, bf16[1216,256]{1,0:T(8,128)(2,1)S(1)}, u32[]{:S(2)}, u32[]{:S(2)}) collective-permute-start(bf16[1216,256]{1,0:T(8,128)(2,1)S(1)} %collective-permute-done.26.refs_1_), channel_id=1, source_target_pairs={{4,8},{8,12},{5,9},{9,13},{6,10},{10,14},{7,11},{11,15},{20,24},{2... | collective-permute-start | bytes 1867784 | tf_op jit(solution)/shard_map/ppermute | solution.py:28
  118.5 16.9 %collective-permute-start.30 = (bf16[1216,256]{1,0:T(8,128)(2,1)S(1)}, bf16[1216,256]{1,0:T(8,128)(2,1)S(1)}, u32[]{:S(2)}, u32[]{:S(2)}) collective-permute-start(bf16[1216,256]{1,0:T(8,128)(2,1)S(1)} %collective-permute-done.29.refs_4_), channel_id=1, source_target_pairs={{8,4},{4,0},{9,5},{5,1},{10,6},{6,2},{11,7},{7,3},{24,20},{20,16},... | collective-permute-start | bytes 1867784 | tf_op jit(solution)/shard_map/ppermute | solution.py:33
  125.7 11.0 %collective-permute-start.24 = (bf16[256,1024]{1,0:T(8,128)(2,1)S(1)}, bf16[256,1024]{1,0:T(8,128)(2,1)S(1)}, u32[]{:S(2)}, u32[]{:S(2)}) collective-permute-start(bf16[256,1024]{1,0:T(8,128)(2,1)S(1)} %get-tuple-element.92), channel_id=1, source_target_pairs={{12,8},{8,4},{13,9},{9,5},{14,10},{10,6},{15,11},{11,7},{28,24},{2... | collective-permute-start | bytes 1572872 | tf_op jit(solution)/shard_map/ppermute | solution.py:33
  126.4 15.7 %collective-permute-start.21 = (bf16[256,1024]{1,0:T(8,128)(2,1)S(1)}, bf16[256,1024]{1,0:T(8,128)(2,1)S(1)}, u32[]{:S(2)}, u32[]{:S(2)}) collective-permute-start(bf16[256,1024]{1,0:T(8,128)(2,1)S(1)} %get-tuple-element.93), channel_id=1, source_target_pairs={{0,4},{4,8},{1,5},{5,9},{2,6},{6,10},{3,7},{7,11},{16,20},{20,24},... | collective-permute-start | bytes 1572872 | tf_op jit(solution)/shard_map/ppermute | solution.py:28
  131.5 31.2 %collective-permute-start.28 = (bf16[1216,256]{1,0:T(8,128)(2,1)S(1)}, bf16[1216,256]{1,0:T(8,128)(2,1)S(1)}, u32[]{:S(2)}, u32[]{:S(2)}) collective-permute-start(bf16[1216,256]{1,0:T(8,128)(2,1)S(1)} %collective-permute-done.27.refs_2_), channel_id=1, source_target_pairs={{8,12},{9,13},{10,14},{11,15},{24,28},{25,29},{26,30},{27,31}} | collective-permute-start | bytes 1867784 | tf_op jit(solution)/shard_map/ppermute | solution.py:28
  135.4 27.2 %collective-permute-start.31 = (bf16[1216,256]{1,0:T(8,128)(2,1)S(1)}, bf16[1216,256]{1,0:T(8,128)(2,1)S(1)}, u32[]{:S(2)}, u32[]{:S(2)}) collective-permute-start(bf16[1216,256]{1,0:T(8,128)(2,1)S(1)} %collective-permute-done.30.refs_5_), channel_id=1, source_target_pairs={{4,0},{5,1},{6,2},{7,3},{20,16},{21,17},{22,18},{23,19}} | collective-permute-start | bytes 1867784 | tf_op jit(solution)/shard_map/ppermute | solution.py:33
  136.9 25.7 %collective-permute-start.25 = (bf16[256,1024]{1,0:T(8,128)(2,1)S(1)}, bf16[256,1024]{1,0:T(8,128)(2,1)S(1)}, u32[]{:S(2)}, u32[]{:S(2)}) collective-permute-start(bf16[256,1024]{1,0:T(8,128)(2,1)S(1)} %add.187), channel_id=1, source_target_pairs={{12,8},{8,4},{4,0},{13,9},{9,5},{5,1},{14,10},{10,6},{6,2},{15,11}... | collective-permute-start | bytes 1572872 | tf_op jit(solution)/shard_map/ppermute | solution.py:33
  142.3 20.3 %collective-permute-start.22 = (bf16[256,1024]{1,0:T(8,128)(2,1)S(1)}, bf16[256,1024]{1,0:T(8,128)(2,1)S(1)}, u32[]{:S(2)}, u32[]{:S(2)}) collective-permute-start(bf16[256,1024]{1,0:T(8,128)(2,1)S(1)} %add.185), channel_id=1, source_target_pairs={{0,4},{4,8},{8,12},{1,5},{5,9},{9,13},{2,6},{6,10},{10,14},{3,7},{... | collective-permute-start | bytes 1572872 | tf_op jit(solution)/shard_map/ppermute | solution.py:28
  162.9 22.4 %collective-permute-start.34 = (bf16[256,1024]{1,0:T(8,128)(2,1)S(1)}, bf16[256,1024]{1,0:T(8,128)(2,1)S(1)}, u32[]{:S(2)}, u32[]{:S(2)}) collective-permute-start(bf16[256,1024]{1,0:T(8,128)(2,1)S(1)} %shard_map.134.refs_0_), channel_id=1, source_target_pairs={{0,8},{4,12},{8,0},{12,4},{1,9},{5,13},{9,1},{13,5},{2,10},{6,14},... | collective-permute-start | bytes 1572872 | tf_op jit(solution)/shard_map/ppermute | solution.py:24
  187.6 16.7 %collective-permute-start.33 = (bf16[256,1024]{1,0:T(8,128)(2,1)S(1)}, bf16[256,1024]{1,0:T(8,128)(2,1)S(1)}, u32[]{:S(2)}, u32[]{:S(2)}) collective-permute-start(bf16[256,1024]{1,0:T(8,128)(2,1)S(1)} %shard_map.134.refs_0_), channel_id=1, source_target_pairs={{0,4},{4,8},{8,12},{12,0},{1,5},{5,9},{9,13},{13,1},{2,6},{6,10},{... | collective-permute-start | bytes 1572872 | tf_op jit(solution)/shard_map/ppermute | solution.py:24
  190.7 10.6 %collective-permute-start.36 = (bf16[128,1280]{1,0:T(8,128)(2,1)S(1)}, bf16[128,1280]{1,0:T(8,128)(2,1)S(1)}, u32[]{:S(2)}, u32[]{:S(2)}) collective-permute-start(bf16[128,1280]{1,0:T(8,128)(2,1)S(1)} %get-tuple-element.66), channel_id=1, source_target_pairs={{0,2},{1,3},{2,0},{3,1},{4,6},{5,7},{6,4},{7,5},{8,10},{9,11},{10,... | collective-permute-start | bytes 983048 | tf_op jit(solution)/shard_map/ppermute | solution.py:64
  192.4 22.7 %collective-permute-start.32 = (bf16[256,1024]{1,0:T(8,128)(2,1)S(1)}, bf16[256,1024]{1,0:T(8,128)(2,1)S(1)}, u32[]{:S(2)}, u32[]{:S(2)}) collective-permute-start(bf16[256,1024]{1,0:T(8,128)(2,1)S(1)} %shard_map.134.refs_0_), channel_id=1, source_target_pairs={{0,12},{4,0},{8,4},{12,8},{1,13},{5,1},{9,5},{13,9},{2,14},{6,2},{... | collective-permute-start | bytes 1572872 | tf_op jit(solution)/shard_map/ppermute | solution.py:24
  216.6 11.0 %collective-permute-start.42 = (bf16[64,1280]{1,0:T(8,128)(2,1)S(1)}, bf16[64,1280]{1,0:T(8,128)(2,1)S(1)}, u32[]{:S(2)}, u32[]{:S(2)}) collective-permute-start(bf16[64,1280]{1,0:T(8,128)(2,1)S(1)} %get-tuple-element.67.refs_2_), channel_id=1, source_target_pairs={{0,8},{4,12},{8,0},{12,4},{1,9},{5,13},{9,1},{13,5},{2,10},{6,14},... | collective-permute-start | bytes 491528 | tf_op jit(solution)/shard_map/ppermute | solution.py:24
  217.2 10.4 %collective-permute-start.41 = (bf16[64,1280]{1,0:T(8,128)(2,1)S(1)}, bf16[64,1280]{1,0:T(8,128)(2,1)S(1)}, u32[]{:S(2)}, u32[]{:S(2)}) collective-permute-start(bf16[64,1280]{1,0:T(8,128)(2,1)S(1)} %shard_map.141.refs_1_), channel_id=1, source_target_pairs={{0,12},{4,0},{8,4},{12,8},{1,13},{5,1},{9,5},{13,9},{2,14},{6,2},{... | collective-permute-start | bytes 491528 | tf_op jit(solution)/shard_map/ppermute | solution.py:24
  227.6 8.0 %collective-permute-start.43 = (bf16[64,1280]{1,0:T(8,128)(2,1)S(1)}, bf16[64,1280]{1,0:T(8,128)(2,1)S(1)}, u32[]{:S(2)}, u32[]{:S(2)}) collective-permute-start(bf16[64,1280]{1,0:T(8,128)(2,1)S(1)} %shard_map.144), channel_id=1, source_target_pairs={{0,4},{4,8},{8,12},{12,0},{1,5},{5,9},{9,13},{13,1},{2,6},{6,10},{... | collective-permute-start | bytes 491528 | tf_op jit(solution)/shard_map/ppermute | solution.py:24
  (32 other events, 344.7 us)

commit v7 on v6

--- a/solution.py
+++ b/solution.py
@@ -566,19 +566,26 @@
         start = ((own_req + k) % reqs) * depth + core * half
         return lax.dynamic_slice(tokens, (first, start), (rows, half))
 
-    arrived = [turn_req(token_block(k, 0, num_tok), k) for k in order[:-1]]
-    products = []
-    for k, near in zip(order, arrived):
+    arrived = [token_block(k, 0, num_tok) for k in order[:-1]]
+    for i in range(1, len(arrived)):
+        (arrived[i],) = hold_part(arrived[i : i + 1], [arrived[i - 1]])
+    arrived = [turn_req(block, k) for k, block in zip(order, arrived)]
+    blocks = []
+    for i, (k, near) in enumerate(zip(order, arrived)):
         block, small = block_part(place, w_small, [near], [swap_core(near)], [])
         smalls.append(turn_req(small, -k))
-        products.append(product_part(block, w_x, []))
-        parts.append(turn_req(products[-1], -k))
-    (near,) = hold_part([token_block(order[-1], own_chip * piece, piece)], arrived[-1:])
-    near = turn_req(near, order[-1])
+        blocks.append(block)
+        if i == 0:
+            products = [product_part(block, w_x, [])]
+            parts.append(turn_req(products[0], -k))
+    near = turn_req(token_block(order[-1], own_chip * piece, piece), order[-1])
     near = [near] + [turn_chip(near, turn) for turn in range(1, chips)]
     far = [swap_core(block) for block in near]
     block, small = block_part(place, w_small, near, far, smalls[1:] + parts[1:2])
     smalls.append(turn_req(small, -order[-1]))
+    for k, near in zip(order[1:-1], blocks[1:]):
+        products.append(product_part(near, w_x, [small]))
+        parts.append(turn_req(products[-1], -k))
     products.append(product_part(block, w_x, smalls[-1:]))
     parts.append(turn_req(products[-1], -order[-1]))
 
@@ -631,7 +638,7 @@
 
     far = order[-1]
     came = {k: turn_req(outputs, k) for k in order}
-    kept, given = output_part(place, w_out, [outputs, came[far]], [below[-1],above[-1]])
+    kept, given = output_part(place, w_out, [outputs, came[far]], [below[-1], above[-1]])
     new_cache, zero = states_part(
         pick(match_slot, which, -1),
         pick(match_slot, index % req_dev, -1),

time: 247 us -> 244 us (0.988)
  waiting for transfers between devices: 114 us -> 92.4 us
  starting transfers between devices: 78.1 us -> 95.2 us
    ppermute x18, waiting for transfers between devices: 67.4 us -> 44.7 us  [turn_req(): lax.ppermute(x, 'req', [(i, (i + turn) % count) for i in range(count)])]
    ppermute x18, starting transfers between devices: 37.4 us -> 54 us  [turn_req(): lax.ppermute(x, 'req', [(i, (i + turn) % count) for i in range(count)])]
    unnamed x35 -> x37, local copies, waits for them, and re-layouts: 8.29 us -> 8.49 us
  transfers between devices with their start and end apart: 47 -> 47, of which waited for: 25 -> 26; matrix products, arithmetic and copies ran while one was open for 5% -> 5% of each run, Pallas kernels for 11% -> 11%
where the time goes in v7:
time: 244 us; the launch traced here: 243 us
  starting transfers between devices  95.2 us (39%)
  waiting for transfers between devices  92.4 us (38%)
  Pallas kernels  33.1 us (14%)
  local copies, waits for them, and re-layouts  12.6 us (5%)
  matrix products  4.26 us (2%)
  other arithmetic  3.68 us (2%)
    ppermute x18, starting transfers between devices, turn_req(): lax.ppermute(x, 'req', [(i, (i + turn) % count) for i in range(count)])  54 us
    ppermute x18, waiting for transfers between devices, turn_req(): lax.ppermute(x, 'req', [(i, (i + turn) % count) for i in range(count)])  44.7 us
    ppermute x6, starting transfers between devices, step_up(): return lax.ppermute(x, 'req', [(i, i + 1) for i in range(first, last)])  21.6 us
    ppermute x6, waiting for transfers between devices, step_down(): lax.ppermute(x, 'req', [(top - i, top - i - 1) for i in range(first, last)])  14.9 us
    ppermute x6, waiting for transfers between devices, step_up(): return lax.ppermute(x, 'req', [(i, i + 1) for i in range(first, last)])  11.2 us
    ppermute x4, waiting for transfers between devices, turn_chip(): lax.ppermute(x, 'tensor', [(i, (i + 2 * turn) % count) for i in range(cou...  8.92 us
    unnamed x37, local copies, waits for them, and re-layouts  8.49 us
    ppermute x6, starting transfers between devices, step_down(): lax.ppermute(x, 'req', [(top - i, top - i - 1) for i in range(first, last)])  6.53 us
  transfers between devices with their start and end apart: 47, of which 26 were waited for; matrix products, arithmetic and copies ran while one was open for 5% of the time, Pallas kernels for 11%

profile of v7, /device:TPU:0, one launch (start us, length us, event | category | flops | bytes accessed | tf_op | source)
XLA Modules:
  0.0 242.5 jit_solution(12491780746060957072)
XLA Ops:
  2.6 3.0 %collective-permute-start = (bf16[256,640]{1,0:T(8,128)(2,1)}, bf16[256,640]{1,0:T(8,128)(2,1)}, u32[]{:S(2)}, u32[]{:S(2)}) collective-permute-start(bf16[256,640]{1,0:T(8,128)(2,1)} %get-tuple-element.87.refs_1_), channel_id=1, source_target_pairs={{0,4},{4,8},{8,12},{12,0},{1,5},{5,9},{9,13},{13,1},{2,6},{6,10},{... | collective-permute-start | bytes 983048 | tf_op jit(solution)/shard_map/ppermute | solution.py:24
  12.2 2.1 maximum_maximum_fusion.w_small
  22.6 8.0 %collective-permute-start.2 = (bf16[256,1024]{1,0:T(8,128)(2,1)}, bf16[256,1024]{1,0:T(8,128)(2,1)}, u32[]{:S(2)}, u32[]{:S(2)}) collective-permute-start(bf16[256,1024]{1,0:T(8,128)(2,1)} %shard_map.123), channel_id=1, source_target_pairs={{0,12},{4,0},{8,4},{12,8},{1,13},{5,1},{9,5},{13,9},{2,14},{6,2},{... | collective-permute-start | bytes 1572872 | tf_op jit(solution)/shard_map/ppermute | solution.py:24
  33.0 4.2 %collective-permute-done.6.refs_1_ = bf16[128,640]{1,0:T(8,128)(2,1)} collective-permute-done((bf16[128,640]{1,0:T(8,128)(2,1)}, bf16[128,640]{1,0:T(8,128)(2,1)}, u32[]{:S(2)}, u32[]{:S(2)}) %collective-permute-start.6) | collective-permute-done | bytes 163872 | tf_op jit(solution)/shard_map/ppermute | solution.py:64
  41.8 3.2 %collective-permute-start.9 = (bf16[256,128]{1,0:T(8,128)(2,1)S(1)}, bf16[256,128]{1,0:T(8,128)(2,1)S(1)}, u32[]{:S(2)}, u32[]{:S(2)}) collective-permute-start(bf16[256,128]{1,0:T(8,128)(2,1)S(1)} %get-tuple-element.42), channel_id=1, source_target_pairs={{0,12},{4,0},{8,4},{12,8},{1,13},{5,1},{9,5},{13,9},{2,14},{6,2},{... | collective-permute-start | bytes 196616 | tf_op jit(solution)/shard_map/ppermute | solution.py:24
  44.9 4.9 %collective-permute-done.10.refs_5_.refs_1_ = bf16[256,128]{1,0:T(8,128)(2,1)S(1)} collective-permute-done((bf16[256,128]{1,0:T(8,128)(2,1)S(1)}, bf16[256,128]{1,0:T(8,128)(2,1)S(1)}, u32[]{:S(2)}, u32[]{:S(2)}) %collective-permute-start.10) | collective-permute-done | bytes 65568 | tf_op jit(solution)/shard_map/ppermute | solution.py:24
  55.5 2.2 collective-permute-done.12.refs_0_.refs_2_
  61.3 2.8 %convolution_convert_fusion.refs_0_ = bf16[256,1024]{1,0:T(8,128)(2,1)} fusion(bf16[1280,1024]{1,0:T(8,128)(2,1)S(1)} %copy-done.3, bf16[256,5120]{1,0:T(8,128)(2,1)} %param.11, s32[]{:T(128)S(6)} %select_n.243), kind=kOutput, calls=%fused_computation | convolution fusion | flops 671350784 | bytes 3801092 | tf_op jit(solution)/shard_map/dot_general | solution.py:562
  64.1 7.3 %collective-permute-done.11.refs_4_.refs_2_ = bf16[256,1024]{1,0:T(8,128)(2,1)S(1)} collective-permute-done((bf16[256,1024]{1,0:T(8,128)(2,1)S(1)}, bf16[256,1024]{1,0:T(8,128)(2,1)S(1)}, u32[]{:S(2)}, u32[]{:S(2)}) %collective-permute-start.11) | collective-permute-done | bytes 524320 | tf_op jit(solution)/shard_map/ppermute | solution.py:24
  78.2 9.1 %collective-permute-start.17 = (bf16[144,256]{1,0:T(8,128)(2,1)S(1)}, bf16[144,256]{1,0:T(8,128)(2,1)S(1)}, u32[]{:S(2)}, u32[]{:S(2)}) collective-permute-start(bf16[144,256]{1,0:T(8,128)(2,1)S(1)} %get-tuple-element.56.refs_0_), channel_id=1, source_target_pairs={{0,4},{4,8},{8,12},{12,0},{1,5},{5,9},{9,13},{13,1},{2,6},{6,10},{... | collective-permute-start | bytes 221192 | tf_op jit(solution)/shard_map/ppermute | solution.py:24
  89.4 2.9 %collective-permute-start.19 = (bf16[144,256]{1,0:T(8,128)(2,1)S(1)}, bf16[144,256]{1,0:T(8,128)(2,1)S(1)}, u32[]{:S(2)}, u32[]{:S(2)}) collective-permute-start(bf16[144,256]{1,0:T(8,128)(2,1)S(1)} %get-tuple-element.56.refs_0_), channel_id=1, source_target_pairs={{0,12},{4,0},{8,4},{12,8},{1,13},{5,1},{9,5},{13,9},{2,14},{6,2},{... | collective-permute-start | bytes 221192 | tf_op jit(solution)/shard_map/ppermute | solution.py:24
  98.7 2.8 %copy-done.1 = f32[12,16,64,128]{3,2,1,0:T(8,128)S(1)} copy-done((f32[12,16,64,128]{3,2,1,0:T(8,128)S(1)}, f32[12,16,64,128]{3,2,1,0:T(8,128)}, u32[]{:S(2)}) %copy-start.1) | copy-done | bytes 6291480
  101.5 3.4 %shard_map.133 = (bf16[256,1024]{1,0:T(8,128)(2,1)S(1)}, bf16[256,1024]{1,0:T(8,128)(2,1)S(1)}, bf16[256,1024]{1,0:T(8,128)(2,1)S(1)}, bf16[256,1024]{1,0:T(8,128)(2,1)S(1)}) custom-call(s32[12]{0:T(128)S(1)} %get-tuple-element.97.slot, s32[12]{0:T(128)S(1)} %get-tuple-element.96.member, bf16[144,256]{1,0:T(8,128)(2,1)S(1)} %get-tuple-element.56.refs_0_, ...), custom_call_target="tpu_custom_call" | custom-call | flops 1 | bytes 1 | tf_op jit(solution)/shard_map/pallas_call | solution.py:245
  105.0 4.6 %collective-permute-start.20 = (bf16[256,1024]{1,0:T(8,128)(2,1)S(1)}, bf16[256,1024]{1,0:T(8,128)(2,1)S(1)}, u32[]{:S(2)}, u32[]{:S(2)}) collective-permute-start(bf16[256,1024]{1,0:T(8,128)(2,1)S(1)} %get-tuple-element.58), channel_id=1, source_target_pairs={{0,4},{1,5},{2,6},{3,7},{16,20},{17,21},{18,22},{19,23}} | collective-permute-start | bytes 1572872 | tf_op jit(solution)/shard_map/ppermute | solution.py:28
  112.4 2.6 %collective-permute-done.29.refs_4_ = bf16[1216,256]{1,0:T(8,128)(2,1)S(1)} collective-permute-done((bf16[1216,256]{1,0:T(8,128)(2,1)S(1)}, bf16[1216,256]{1,0:T(8,128)(2,1)S(1)}, u32[]{:S(2)}, u32[]{:S(2)}) %collective-permute-start.29) | collective-permute-done | bytes 622624 | tf_op jit(solution)/shard_map/ppermute | solution.py:33
  116.3 5.8 %collective-permute-done.20 = bf16[256,1024]{1,0:T(8,128)(2,1)S(1)} collective-permute-done((bf16[256,1024]{1,0:T(8,128)(2,1)S(1)}, bf16[256,1024]{1,0:T(8,128)(2,1)S(1)}, u32[]{:S(2)}, u32[]{:S(2)}) %collective-permute-start.20) | collective-permute-done | bytes 524320 | tf_op jit(solution)/shard_map/ppermute | solution.py:28
  122.9 5.0 %collective-permute-start.21 = (bf16[256,1024]{1,0:T(8,128)(2,1)S(1)}, bf16[256,1024]{1,0:T(8,128)(2,1)S(1)}, u32[]{:S(2)}, u32[]{:S(2)}) collective-permute-start(bf16[256,1024]{1,0:T(8,128)(2,1)S(1)} %get-tuple-element.93), channel_id=1, source_target_pairs={{0,4},{4,8},{1,5},{5,9},{2,6},{6,10},{3,7},{7,11},{16,20},{20,24},... | collective-permute-start | bytes 1572872 | tf_op jit(solution)/shard_map/ppermute | solution.py:28
  128.7 3.2 %collective-permute-done.30.refs_5_ = bf16[1216,256]{1,0:T(8,128)(2,1)S(1)} collective-permute-done((bf16[1216,256]{1,0:T(8,128)(2,1)S(1)}, bf16[1216,256]{1,0:T(8,128)(2,1)S(1)}, u32[]{:S(2)}, u32[]{:S(2)}) %collective-permute-start.30) | collective-permute-done | bytes 622624 | tf_op jit(solution)/shard_map/ppermute | solution.py:33
  134.6 3.9 %collective-permute-done.21 = bf16[256,1024]{1,0:T(8,128)(2,1)S(1)} collective-permute-done((bf16[256,1024]{1,0:T(8,128)(2,1)S(1)}, bf16[256,1024]{1,0:T(8,128)(2,1)S(1)}, u32[]{:S(2)}, u32[]{:S(2)}) %collective-permute-start.21) | collective-permute-done | bytes 524320 | tf_op jit(solution)/shard_map/ppermute | solution.py:28
  138.7 9.3 %collective-permute-start.22 = (bf16[256,1024]{1,0:T(8,128)(2,1)S(1)}, bf16[256,1024]{1,0:T(8,128)(2,1)S(1)}, u32[]{:S(2)}, u32[]{:S(2)}) collective-permute-start(bf16[256,1024]{1,0:T(8,128)(2,1)S(1)} %add.185), channel_id=1, source_target_pairs={{0,4},{4,8},{8,12},{1,5},{5,9},{9,13},{2,6},{6,10},{10,14},{3,7},{... | collective-permute-start | bytes 1572872 | tf_op jit(solution)/shard_map/ppermute | solution.py:28
  149.8 9.1 %collective-permute-done.25.refs_2_ = bf16[256,1024]{1,0:T(8,128)(2,1)S(1)} collective-permute-done((bf16[256,1024]{1,0:T(8,128)(2,1)S(1)}, bf16[256,1024]{1,0:T(8,128)(2,1)S(1)}, u32[]{:S(2)}, u32[]{:S(2)}) %collective-permute-start.25) | collective-permute-done | bytes 524320 | tf_op jit(solution)/shard_map/ppermute | solution.py:33
  159.2 7.7 %collective-permute-start.34 = (bf16[256,1024]{1,0:T(8,128)(2,1)S(1)}, bf16[256,1024]{1,0:T(8,128)(2,1)S(1)}, u32[]{:S(2)}, u32[]{:S(2)}) collective-permute-start(bf16[256,1024]{1,0:T(8,128)(2,1)S(1)} %shard_map.134.refs_0_), channel_id=1, source_target_pairs={{0,8},{4,12},{8,0},{12,4},{1,9},{5,13},{9,1},{13,5},{2,10},{6,14},... | collective-permute-start | bytes 1572872 | tf_op jit(solution)/shard_map/ppermute | solution.py:24
  166.9 14.8 %collective-permute-done.34.refs_1_ = bf16[256,1024]{1,0:T(8,128)(2,1)S(1)} collective-permute-done((bf16[256,1024]{1,0:T(8,128)(2,1)S(1)}, bf16[256,1024]{1,0:T(8,128)(2,1)S(1)}, u32[]{:S(2)}, u32[]{:S(2)}) %collective-permute-start.34) | collective-permute-done | bytes 524320 | tf_op jit(solution)/shard_map/ppermute | solution.py:24
  181.7 2.2 shard_map.135
  190.9 6.2 %shard_map.136 = (f32[12,16,64,128]{3,2,1,0:T(8,128)}, s32[8,128]{1,0:T(8,128)S(1)}) custom-call(s32[12]{0:T(128)S(1)} %get-tuple-element.95.which, s32[12]{0:T(128)S(1)} %get-tuple-element.94.member, f32[12,16,64,128]{3,2,1,0:T(8,128)S(1)} %bitcast.13, bf16[1216,256]{1,0:T(8,128)(2,1)S(1)} %get-tuple-element.61.refs_0_, ...), custom_call_target="tpu_custom_call" | custom-call | flops 1 | bytes 1 | tf_op jit(solution)/shard_map/pallas_call | solution.py:389
  197.2 3.4 %collective-permute-done.33.refs_0_ = bf16[256,1024]{1,0:T(8,128)(2,1)S(1)} collective-permute-done((bf16[256,1024]{1,0:T(8,128)(2,1)S(1)}, bf16[256,1024]{1,0:T(8,128)(2,1)S(1)}, u32[]{:S(2)}, u32[]{:S(2)}) %collective-permute-start.33) | collective-permute-done | bytes 524320 | tf_op jit(solution)/shard_map/ppermute | solution.py:24
  206.0 4.7 %collective-permute-done.38.refs_0_ = bf16[64,1280]{1,0:T(8,128)(2,1)S(1)} collective-permute-done((bf16[64,1280]{1,0:T(8,128)(2,1)S(1)}, bf16[64,1280]{1,0:T(8,128)(2,1)S(1)}, u32[]{:S(2)}, u32[]{:S(2)}) %collective-permute-start.38) | collective-permute-done | bytes 163872 | tf_op jit(solution)/shard_map/ppermute | solution.py:64
  213.5 2.3 collective-permute-start.41
  218.1 5.8 %collective-permute-done.42.refs_2_ = bf16[64,1280]{1,0:T(8,128)(2,1)S(1)} collective-permute-done((bf16[64,1280]{1,0:T(8,128)(2,1)S(1)}, bf16[64,1280]{1,0:T(8,128)(2,1)S(1)}, u32[]{:S(2)}, u32[]{:S(2)}) %collective-permute-start.42) | collective-permute-done | bytes 163872 | tf_op jit(solution)/shard_map/ppermute | solution.py:24
  223.9 4.1 %collective-permute-start.43 = (bf16[64,1280]{1,0:T(8,128)(2,1)S(1)}, bf16[64,1280]{1,0:T(8,128)(2,1)S(1)}, u32[]{:S(2)}, u32[]{:S(2)}) collective-permute-start(bf16[64,1280]{1,0:T(8,128)(2,1)S(1)} %shard_map.144), channel_id=1, source_target_pairs={{0,4},{4,8},{8,12},{12,0},{1,5},{5,9},{9,13},{13,1},{2,6},{6,10},{... | collective-permute-start | bytes 491528 | tf_op jit(solution)/shard_map/ppermute | solution.py:24
  228.0 3.9 %collective-permute-done.43 = bf16[64,1280]{1,0:T(8,128)(2,1)S(1)} collective-permute-done((bf16[64,1280]{1,0:T(8,128)(2,1)S(1)}, bf16[64,1280]{1,0:T(8,128)(2,1)S(1)}, u32[]{:S(2)}, u32[]{:S(2)}) %collective-permute-start.43) | collective-permute-done | bytes 163872 | tf_op jit(solution)/shard_map/ppermute | solution.py:24
  235.0 2.9 %collective-permute-done.44.refs_1_ = bf16[64,1280]{1,0:T(8,128)(2,1)S(1)} collective-permute-done((bf16[64,1280]{1,0:T(8,128)(2,1)S(1)}, bf16[64,1280]{1,0:T(8,128)(2,1)S(1)}, u32[]{:S(2)}, u32[]{:S(2)}) %collective-permute-start.44) | collective-permute-done | bytes 163872 | tf_op jit(solution)/shard_map/ppermute | solution.py:670
  (153 shorter events, 84.1 us)
Async XLA Ops:
  2.6 13.9 %collective-permute-start = (bf16[256,640]{1,0:T(8,128)(2,1)}, bf16[256,640]{1,0:T(8,128)(2,1)}, u32[]{:S(2)}, u32[]{:S(2)}) collective-permute-start(bf16[256,640]{1,0:T(8,128)(2,1)} %get-tuple-element.87.refs_1_), channel_id=1, source_target_pairs={{0,4},{4,8},{8,12},{12,0},{1,5},{5,9},{9,13},{13,1},{2,6},{6,10},{... | collective-permute-start | bytes 983048 | tf_op jit(solution)/shard_map/ppermute | solution.py:24
  6.4 26.0 %collective-permute-start.3 = (bf16[256,640]{1,0:T(8,128)(2,1)}, bf16[256,640]{1,0:T(8,128)(2,1)}, u32[]{:S(2)}, u32[]{:S(2)}) collective-permute-start(bf16[256,640]{1,0:T(8,128)(2,1)} %shard_map.124), channel_id=1, source_target_pairs={{0,12},{4,0},{8,4},{12,8},{1,13},{5,1},{9,5},{13,9},{2,14},{6,2},{... | collective-permute-start | bytes 983048 | tf_op jit(solution)/shard_map/ppermute | solution.py:24
  10.0 20.8 %collective-permute-start.5 = (bf16[128,640]{1,0:T(8,128)(2,1)}, bf16[128,640]{1,0:T(8,128)(2,1)}, u32[]{:S(2)}, u32[]{:S(2)}) collective-permute-start(bf16[128,640]{1,0:T(8,128)(2,1)} %dynamic_slice.19), channel_id=1, source_target_pairs={{0,8},{4,12},{8,0},{12,4},{1,9},{5,13},{9,1},{13,5},{2,10},{6,14},... | collective-permute-start | bytes 491528 | tf_op jit(solution)/shard_map/ppermute | solution.py:24
  22.6 27.3 %collective-permute-start.2 = (bf16[256,1024]{1,0:T(8,128)(2,1)}, bf16[256,1024]{1,0:T(8,128)(2,1)}, u32[]{:S(2)}, u32[]{:S(2)}) collective-permute-start(bf16[256,1024]{1,0:T(8,128)(2,1)} %shard_map.123), channel_id=1, source_target_pairs={{0,12},{4,0},{8,4},{12,8},{1,13},{5,1},{9,5},{13,9},{2,14},{6,2},{... | collective-permute-start | bytes 1572872 | tf_op jit(solution)/shard_map/ppermute | solution.py:24
  32.4 12.5 %collective-permute-start.7 = (bf16[128,640]{1,0:T(8,128)(2,1)}, bf16[128,640]{1,0:T(8,128)(2,1)}, u32[]{:S(2)}, u32[]{:S(2)}) collective-permute-start(bf16[128,640]{1,0:T(8,128)(2,1)} %collective-permute-done.5.refs_0_), channel_id=1, source_target_pairs={{0,1},{1,0},{2,3},{3,2},{4,5},{5,4},{6,7},{7,6},{8,9},{9,8},{10,11... | collective-permute-start | bytes 491528 | tf_op jit(solution)/shard_map/ppermute | solution.py:59
  37.2 7.8 %collective-permute-start.8 = (bf16[128,640]{1,0:T(8,128)(2,1)}, bf16[128,640]{1,0:T(8,128)(2,1)}, u32[]{:S(2)}, u32[]{:S(2)}) collective-permute-start(bf16[128,640]{1,0:T(8,128)(2,1)} %collective-permute-done.6.refs_1_), channel_id=1, source_target_pairs={{0,1},{1,0},{2,3},{3,2},{4,5},{5,4},{6,7},{7,6},{8,9},{9,8},{10,11... | collective-permute-start | bytes 491528 | tf_op jit(solution)/shard_map/ppermute | solution.py:59
  39.8 10.1 %collective-permute-start.10 = (bf16[256,128]{1,0:T(8,128)(2,1)S(1)}, bf16[256,128]{1,0:T(8,128)(2,1)S(1)}, u32[]{:S(2)}, u32[]{:S(2)}) collective-permute-start(bf16[256,128]{1,0:T(8,128)(2,1)S(1)} %get-tuple-element.43), channel_id=1, source_target_pairs={{0,4},{4,8},{8,12},{12,0},{1,5},{5,9},{9,13},{13,1},{2,6},{6,10},{... | collective-permute-start | bytes 196616 | tf_op jit(solution)/shard_map/ppermute | solution.py:24
  41.8 8.1 %collective-permute-start.9 = (bf16[256,128]{1,0:T(8,128)(2,1)S(1)}, bf16[256,128]{1,0:T(8,128)(2,1)S(1)}, u32[]{:S(2)}, u32[]{:S(2)}) collective-permute-start(bf16[256,128]{1,0:T(8,128)(2,1)S(1)} %get-tuple-element.42), channel_id=1, source_target_pairs={{0,12},{4,0},{8,4},{12,8},{1,13},{5,1},{9,5},{13,9},{2,14},{6,2},{... | collective-permute-start | bytes 196616 | tf_op jit(solution)/shard_map/ppermute | solution.py:24
  54.6 16.8 %collective-permute-start.11 = (bf16[256,1024]{1,0:T(8,128)(2,1)S(1)}, bf16[256,1024]{1,0:T(8,128)(2,1)S(1)}, u32[]{:S(2)}, u32[]{:S(2)}) collective-permute-start(bf16[256,1024]{1,0:T(8,128)(2,1)S(1)} %shard_map.127), channel_id=1, source_target_pairs={{0,4},{4,8},{8,12},{12,0},{1,5},{5,9},{9,13},{13,1},{2,6},{6,10},{... | collective-permute-start | bytes 1572872 | tf_op jit(solution)/shard_map/ppermute | solution.py:24
  59.3 34.0 %collective-permute-start.13 = (bf16[256,1024]{1,0:T(8,128)(2,1)}, bf16[256,1024]{1,0:T(8,128)(2,1)}, u32[]{:S(2)}, u32[]{:S(2)}) collective-permute-start(bf16[256,1024]{1,0:T(8,128)(2,1)} %shard_map.128.refs_5_), channel_id=1, source_target_pairs={{0,8},{4,12},{8,0},{12,4},{1,9},{5,13},{9,1},{13,5},{2,10},{6,14},... | collective-permute-start | bytes 1572872 | tf_op jit(solution)/shard_map/ppermute | solution.py:24
  78.2 20.5 %collective-permute-start.17 = (bf16[144,256]{1,0:T(8,128)(2,1)S(1)}, bf16[144,256]{1,0:T(8,128)(2,1)S(1)}, u32[]{:S(2)}, u32[]{:S(2)}) collective-permute-start(bf16[144,256]{1,0:T(8,128)(2,1)S(1)} %get-tuple-element.56.refs_0_), channel_id=1, source_target_pairs={{0,4},{4,8},{8,12},{12,0},{1,5},{5,9},{9,13},{13,1},{2,6},{6,10},{... | collective-permute-start | bytes 221192 | tf_op jit(solution)/shard_map/ppermute | solution.py:24
  87.4 11.4 %collective-permute-start.18 = (bf16[144,256]{1,0:T(8,128)(2,1)S(1)}, bf16[144,256]{1,0:T(8,128)(2,1)S(1)}, u32[]{:S(2)}, u32[]{:S(2)}) collective-permute-start(bf16[144,256]{1,0:T(8,128)(2,1)S(1)} %get-tuple-element.56.refs_0_), channel_id=1, source_target_pairs={{0,8},{4,12},{8,0},{12,4},{1,9},{5,13},{9,1},{13,5},{2,10},{6,14},... | collective-permute-start | bytes 221192 | tf_op jit(solution)/shard_map/ppermute | solution.py:24
  89.4 9.4 %collective-permute-start.19 = (bf16[144,256]{1,0:T(8,128)(2,1)S(1)}, bf16[144,256]{1,0:T(8,128)(2,1)S(1)}, u32[]{:S(2)}, u32[]{:S(2)}) collective-permute-start(bf16[144,256]{1,0:T(8,128)(2,1)S(1)} %get-tuple-element.56.refs_0_), channel_id=1, source_target_pairs={{0,12},{4,0},{8,4},{12,8},{1,13},{5,1},{9,5},{13,9},{2,14},{6,2},{... | collective-permute-start | bytes 221192 | tf_op jit(solution)/shard_map/ppermute | solution.py:24
  96.0 15.7 %collective-permute-start.26 = (bf16[1216,256]{1,0:T(8,128)(2,1)S(1)}, bf16[1216,256]{1,0:T(8,128)(2,1)S(1)}, u32[]{:S(2)}, u32[]{:S(2)}) collective-permute-start(bf16[1216,256]{1,0:T(8,128)(2,1)S(1)} %get-tuple-element.61.refs_0_), channel_id=1, source_target_pairs={{0,4},{4,8},{8,12},{1,5},{5,9},{9,13},{2,6},{6,10},{10,14},{3,7},{... | collective-permute-start | bytes 1867784 | tf_op jit(solution)/shard_map/ppermute | solution.py:28
  97.4 17.7 %collective-permute-start.29 = (bf16[1216,256]{1,0:T(8,128)(2,1)S(1)}, bf16[1216,256]{1,0:T(8,128)(2,1)S(1)}, u32[]{:S(2)}, u32[]{:S(2)}) collective-permute-start(bf16[1216,256]{1,0:T(8,128)(2,1)S(1)} %get-tuple-element.61.refs_0_), channel_id=1, source_target_pairs={{12,8},{8,4},{4,0},{13,9},{9,5},{5,1},{14,10},{10,6},{6,2},{15,11}... | collective-permute-start | bytes 1867784 | tf_op jit(solution)/shard_map/ppermute | solution.py:33
  105.0 17.2 %collective-permute-start.20 = (bf16[256,1024]{1,0:T(8,128)(2,1)S(1)}, bf16[256,1024]{1,0:T(8,128)(2,1)S(1)}, u32[]{:S(2)}, u32[]{:S(2)}) collective-permute-start(bf16[256,1024]{1,0:T(8,128)(2,1)S(1)} %get-tuple-element.58), channel_id=1, source_target_pairs={{0,4},{1,5},{2,6},{3,7},{16,20},{17,21},{18,22},{19,23}} | collective-permute-start | bytes 1572872 | tf_op jit(solution)/shard_map/ppermute | solution.py:28
  109.5 12.6 %collective-permute-start.23 = (bf16[256,1024]{1,0:T(8,128)(2,1)S(1)}, bf16[256,1024]{1,0:T(8,128)(2,1)S(1)}, u32[]{:S(2)}, u32[]{:S(2)}) collective-permute-start(bf16[256,1024]{1,0:T(8,128)(2,1)S(1)} %get-tuple-element.60), channel_id=1, source_target_pairs={{12,8},{13,9},{14,10},{15,11},{28,24},{29,25},{30,26},{31,27}} | collective-permute-start | bytes 1572872 | tf_op jit(solution)/shard_map/ppermute | solution.py:33
  111.7 16.2 %collective-permute-start.27 = (bf16[1216,256]{1,0:T(8,128)(2,1)S(1)}, bf16[1216,256]{1,0:T(8,128)(2,1)S(1)}, u32[]{:S(2)}, u32[]{:S(2)}) collective-permute-start(bf16[1216,256]{1,0:T(8,128)(2,1)S(1)} %collective-permute-done.26.refs_1_), channel_id=1, source_target_pairs={{4,8},{8,12},{5,9},{9,13},{6,10},{10,14},{7,11},{11,15},{20,24},{2... | collective-permute-start | bytes 1867784 | tf_op jit(solution)/shard_map/ppermute | solution.py:28
  115.0 16.8 %collective-permute-start.30 = (bf16[1216,256]{1,0:T(8,128)(2,1)S(1)}, bf16[1216,256]{1,0:T(8,128)(2,1)S(1)}, u32[]{:S(2)}, u32[]{:S(2)}) collective-permute-start(bf16[1216,256]{1,0:T(8,128)(2,1)S(1)} %collective-permute-done.29.refs_4_), channel_id=1, source_target_pairs={{8,4},{4,0},{9,5},{5,1},{10,6},{6,2},{11,7},{7,3},{24,20},{20,16},... | collective-permute-start | bytes 1867784 | tf_op jit(solution)/shard_map/ppermute | solution.py:33
  122.2 10.9 %collective-permute-start.24 = (bf16[256,1024]{1,0:T(8,128)(2,1)S(1)}, bf16[256,1024]{1,0:T(8,128)(2,1)S(1)}, u32[]{:S(2)}, u32[]{:S(2)}) collective-permute-start(bf16[256,1024]{1,0:T(8,128)(2,1)S(1)} %get-tuple-element.92), channel_id=1, source_target_pairs={{12,8},{8,4},{13,9},{9,5},{14,10},{10,6},{15,11},{11,7},{28,24},{2... | collective-permute-start | bytes 1572872 | tf_op jit(solution)/shard_map/ppermute | solution.py:33
  122.9 15.6 %collective-permute-start.21 = (bf16[256,1024]{1,0:T(8,128)(2,1)S(1)}, bf16[256,1024]{1,0:T(8,128)(2,1)S(1)}, u32[]{:S(2)}, u32[]{:S(2)}) collective-permute-start(bf16[256,1024]{1,0:T(8,128)(2,1)S(1)} %get-tuple-element.93), channel_id=1, source_target_pairs={{0,4},{4,8},{1,5},{5,9},{2,6},{6,10},{3,7},{7,11},{16,20},{20,24},... | collective-permute-start | bytes 1572872 | tf_op jit(solution)/shard_map/ppermute | solution.py:28
  128.0 31.0 %collective-permute-start.28 = (bf16[1216,256]{1,0:T(8,128)(2,1)S(1)}, bf16[1216,256]{1,0:T(8,128)(2,1)S(1)}, u32[]{:S(2)}, u32[]{:S(2)}) collective-permute-start(bf16[1216,256]{1,0:T(8,128)(2,1)S(1)} %collective-permute-done.27.refs_2_), channel_id=1, source_target_pairs={{8,12},{9,13},{10,14},{11,15},{24,28},{25,29},{26,30},{27,31}} | collective-permute-start | bytes 1867784 | tf_op jit(solution)/shard_map/ppermute | solution.py:28
  131.8 27.1 %collective-permute-start.31 = (bf16[1216,256]{1,0:T(8,128)(2,1)S(1)}, bf16[1216,256]{1,0:T(8,128)(2,1)S(1)}, u32[]{:S(2)}, u32[]{:S(2)}) collective-permute-start(bf16[1216,256]{1,0:T(8,128)(2,1)S(1)} %collective-permute-done.30.refs_5_), channel_id=1, source_target_pairs={{4,0},{5,1},{6,2},{7,3},{20,16},{21,17},{22,18},{23,19}} | collective-permute-start | bytes 1867784 | tf_op jit(solution)/shard_map/ppermute | solution.py:33
  133.3 25.6 %collective-permute-start.25 = (bf16[256,1024]{1,0:T(8,128)(2,1)S(1)}, bf16[256,1024]{1,0:T(8,128)(2,1)S(1)}, u32[]{:S(2)}, u32[]{:S(2)}) collective-permute-start(bf16[256,1024]{1,0:T(8,128)(2,1)S(1)} %add.187), channel_id=1, source_target_pairs={{12,8},{8,4},{4,0},{13,9},{9,5},{5,1},{14,10},{10,6},{6,2},{15,11}... | collective-permute-start | bytes 1572872 | tf_op jit(solution)/shard_map/ppermute | solution.py:33
  138.7 20.2 %collective-permute-start.22 = (bf16[256,1024]{1,0:T(8,128)(2,1)S(1)}, bf16[256,1024]{1,0:T(8,128)(2,1)S(1)}, u32[]{:S(2)}, u32[]{:S(2)}) collective-permute-start(bf16[256,1024]{1,0:T(8,128)(2,1)S(1)} %add.185), channel_id=1, source_target_pairs={{0,4},{4,8},{8,12},{1,5},{5,9},{9,13},{2,6},{6,10},{10,14},{3,7},{... | collective-permute-start | bytes 1572872 | tf_op jit(solution)/shard_map/ppermute | solution.py:28
  159.2 22.5 %collective-permute-start.34 = (bf16[256,1024]{1,0:T(8,128)(2,1)S(1)}, bf16[256,1024]{1,0:T(8,128)(2,1)S(1)}, u32[]{:S(2)}, u32[]{:S(2)}) collective-permute-start(bf16[256,1024]{1,0:T(8,128)(2,1)S(1)} %shard_map.134.refs_0_), channel_id=1, source_target_pairs={{0,8},{4,12},{8,0},{12,4},{1,9},{5,13},{9,1},{13,5},{2,10},{6,14},... | collective-permute-start | bytes 1572872 | tf_op jit(solution)/shard_map/ppermute | solution.py:24
  183.9 16.7 %collective-permute-start.33 = (bf16[256,1024]{1,0:T(8,128)(2,1)S(1)}, bf16[256,1024]{1,0:T(8,128)(2,1)S(1)}, u32[]{:S(2)}, u32[]{:S(2)}) collective-permute-start(bf16[256,1024]{1,0:T(8,128)(2,1)S(1)} %shard_map.134.refs_0_), channel_id=1, source_target_pairs={{0,4},{4,8},{8,12},{12,0},{1,5},{5,9},{9,13},{13,1},{2,6},{6,10},{... | collective-permute-start | bytes 1572872 | tf_op jit(solution)/shard_map/ppermute | solution.py:24
  187.0 10.1 %collective-permute-start.36 = (bf16[128,1280]{1,0:T(8,128)(2,1)S(1)}, bf16[128,1280]{1,0:T(8,128)(2,1)S(1)}, u32[]{:S(2)}, u32[]{:S(2)}) collective-permute-start(bf16[128,1280]{1,0:T(8,128)(2,1)S(1)} %get-tuple-element.66), channel_id=1, source_target_pairs={{0,2},{1,3},{2,0},{3,1},{4,6},{5,7},{6,4},{7,5},{8,10},{9,11},{10,... | collective-permute-start | bytes 983048 | tf_op jit(solution)/shard_map/ppermute | solution.py:64
  188.7 22.7 %collective-permute-start.32 = (bf16[256,1024]{1,0:T(8,128)(2,1)S(1)}, bf16[256,1024]{1,0:T(8,128)(2,1)S(1)}, u32[]{:S(2)}, u32[]{:S(2)}) collective-permute-start(bf16[256,1024]{1,0:T(8,128)(2,1)S(1)} %shard_map.134.refs_0_), channel_id=1, source_target_pairs={{0,12},{4,0},{8,4},{12,8},{1,13},{5,1},{9,5},{13,9},{2,14},{6,2},{... | collective-permute-start | bytes 1572872 | tf_op jit(solution)/shard_map/ppermute | solution.py:24
  212.9 11.0 %collective-permute-start.42 = (bf16[64,1280]{1,0:T(8,128)(2,1)S(1)}, bf16[64,1280]{1,0:T(8,128)(2,1)S(1)}, u32[]{:S(2)}, u32[]{:S(2)}) collective-permute-start(bf16[64,1280]{1,0:T(8,128)(2,1)S(1)} %get-tuple-element.67.refs_2_), channel_id=1, source_target_pairs={{0,8},{4,12},{8,0},{12,4},{1,9},{5,13},{9,1},{13,5},{2,10},{6,14},... | collective-permute-start | bytes 491528 | tf_op jit(solution)/shard_map/ppermute | solution.py:24
  213.5 10.4 %collective-permute-start.41 = (bf16[64,1280]{1,0:T(8,128)(2,1)S(1)}, bf16[64,1280]{1,0:T(8,128)(2,1)S(1)}, u32[]{:S(2)}, u32[]{:S(2)}) collective-permute-start(bf16[64,1280]{1,0:T(8,128)(2,1)S(1)} %shard_map.141.refs_1_), channel_id=1, source_target_pairs={{0,12},{4,0},{8,4},{12,8},{1,13},{5,1},{9,5},{13,9},{2,14},{6,2},{... | collective-permute-start | bytes 491528 | tf_op jit(solution)/shard_map/ppermute | solution.py:24
  223.9 8.0 %collective-permute-start.43 = (bf16[64,1280]{1,0:T(8,128)(2,1)S(1)}, bf16[64,1280]{1,0:T(8,128)(2,1)S(1)}, u32[]{:S(2)}, u32[]{:S(2)}) collective-permute-start(bf16[64,1280]{1,0:T(8,128)(2,1)S(1)} %shard_map.144), channel_id=1, source_target_pairs={{0,4},{4,8},{8,12},{12,0},{1,5},{5,9},{9,13},{13,1},{2,6},{6,10},{... | collective-permute-start | bytes 491528 | tf_op jit(solution)/shard_map/ppermute | solution.py:24
  (33 other events, 353.2 us)

commit v8 on v7

--- a/solution.py
+++ b/solution.py
@@ -650,9 +650,9 @@
     arrived[0], block = chip_part(*sum_cores(kept, given), 2, [])
     arrived[far] = turn_req(block, -far)
     before = [zero, block]
-    for k in order[:-1]:
+    for k in order[-2::-1]:
         kept, given = output_part(place, w_out, [came[k]], before)
-        returned = [arrived[j] for j in order if j in arrived] if k == order[-2] else []
+        returned = [arrived[j] for j in order if j in arrived] if k == order[0] else []
         (block,) = chip_part(*sum_cores(kept, given), 1, returned)
         arrived[k] = turn_req(block, -k)
         before = [block]

time: 244 us -> 243 us (level)
  waiting for transfers between devices: 92.4 us -> 95.3 us
  starting transfers between devices: 95.2 us -> 92.6 us
    ppermute x18, waiting for transfers between devices: 44.7 us -> 47.3 us  [turn_req(): lax.ppermute(x, 'req', [(i, (i + turn) % count) for i in range(count)])]
    ppermute x18, starting transfers between devices: 54 us -> 51.4 us  [turn_req(): lax.ppermute(x, 'req', [(i, (i + turn) % count) for i in range(count)])]
where the time goes in v8:
time: 243 us; the launch traced here: 242 us
  waiting for transfers between devices  95.3 us (39%)
  starting transfers between devices  92.6 us (38%)
  Pallas kernels  32.6 us (13%)
  local copies, waits for them, and re-layouts  12.6 us (5%)
  matrix products  4.26 us (2%)
  other arithmetic  3.68 us (2%)
    ppermute x18, starting transfers between devices, turn_req(): lax.ppermute(x, 'req', [(i, (i + turn) % count) for i in range(count)])  51.4 us
    ppermute x18, waiting for transfers between devices, turn_req(): lax.ppermute(x, 'req', [(i, (i + turn) % count) for i in range(count)])  47.3 us
    ppermute x6, starting transfers between devices, step_up(): return lax.ppermute(x, 'req', [(i, i + 1) for i in range(first, last)])  21.6 us
    ppermute x6, waiting for transfers between devices, step_down(): lax.ppermute(x, 'req', [(top - i, top - i - 1) for i in range(first, last)])  14.9 us
    ppermute x6, waiting for transfers between devices, step_up(): return lax.ppermute(x, 'req', [(i, i + 1) for i in range(first, last)])  11.2 us
    ppermute x4, waiting for transfers between devices, turn_chip(): lax.ppermute(x, 'tensor', [(i, (i + 2 * turn) % count) for i in range(cou...  11.1 us
    unnamed x37, local copies, waits for them, and re-layouts  8.49 us
    ppermute x6, starting transfers between devices, step_down(): lax.ppermute(x, 'req', [(top - i, top - i - 1) for i in range(first, last)])  6.53 us
  transfers between devices with their start and end apart: 47, of which 26 were waited for; matrix products, arithmetic and copies ran while one was open for 5% of the time, Pallas kernels for 11%

profile of v8, /device:TPU:0, one launch (start us, length us, event | category | flops | bytes accessed | tf_op | source)
XLA Modules:
  0.0 242.4 jit_solution(5899169322454867354)
XLA Ops:
  2.6 3.0 %collective-permute-start = (bf16[256,640]{1,0:T(8,128)(2,1)}, bf16[256,640]{1,0:T(8,128)(2,1)}, u32[]{:S(2)}, u32[]{:S(2)}) collective-permute-start(bf16[256,640]{1,0:T(8,128)(2,1)} %get-tuple-element.87.refs_1_), channel_id=1, source_target_pairs={{0,4},{4,8},{8,12},{12,0},{1,5},{5,9},{9,13},{13,1},{2,6},{6,10},{... | collective-permute-start | bytes 983048 | tf_op jit(solution)/shard_map/ppermute | solution.py:24
  12.2 2.1 maximum_maximum_fusion.w_small
  22.6 8.0 %collective-permute-start.2 = (bf16[256,1024]{1,0:T(8,128)(2,1)}, bf16[256,1024]{1,0:T(8,128)(2,1)}, u32[]{:S(2)}, u32[]{:S(2)}) collective-permute-start(bf16[256,1024]{1,0:T(8,128)(2,1)} %shard_map.123), channel_id=1, source_target_pairs={{0,12},{4,0},{8,4},{12,8},{1,13},{5,1},{9,5},{13,9},{2,14},{6,2},{... | collective-permute-start | bytes 1572872 | tf_op jit(solution)/shard_map/ppermute | solution.py:24
  33.0 4.2 %collective-permute-done.6.refs_1_ = bf16[128,640]{1,0:T(8,128)(2,1)} collective-permute-done((bf16[128,640]{1,0:T(8,128)(2,1)}, bf16[128,640]{1,0:T(8,128)(2,1)}, u32[]{:S(2)}, u32[]{:S(2)}) %collective-permute-start.6) | collective-permute-done | bytes 163872 | tf_op jit(solution)/shard_map/ppermute | solution.py:64
  41.8 3.2 %collective-permute-start.9 = (bf16[256,128]{1,0:T(8,128)(2,1)S(1)}, bf16[256,128]{1,0:T(8,128)(2,1)S(1)}, u32[]{:S(2)}, u32[]{:S(2)}) collective-permute-start(bf16[256,128]{1,0:T(8,128)(2,1)S(1)} %get-tuple-element.42), channel_id=1, source_target_pairs={{0,12},{4,0},{8,4},{12,8},{1,13},{5,1},{9,5},{13,9},{2,14},{6,2},{... | collective-permute-start | bytes 196616 | tf_op jit(solution)/shard_map/ppermute | solution.py:24
  44.9 4.9 %collective-permute-done.10.refs_5_.refs_1_ = bf16[256,128]{1,0:T(8,128)(2,1)S(1)} collective-permute-done((bf16[256,128]{1,0:T(8,128)(2,1)S(1)}, bf16[256,128]{1,0:T(8,128)(2,1)S(1)}, u32[]{:S(2)}, u32[]{:S(2)}) %collective-permute-start.10) | collective-permute-done | bytes 65568 | tf_op jit(solution)/shard_map/ppermute | solution.py:24
  55.5 2.2 collective-permute-done.12.refs_0_.refs_2_
  61.3 2.8 %convolution_convert_fusion.refs_0_ = bf16[256,1024]{1,0:T(8,128)(2,1)} fusion(bf16[1280,1024]{1,0:T(8,128)(2,1)S(1)} %copy-done.3, bf16[256,5120]{1,0:T(8,128)(2,1)} %param.11, s32[]{:T(128)S(6)} %select_n.243), kind=kOutput, calls=%fused_computation | convolution fusion | flops 671350784 | bytes 3801092 | tf_op jit(solution)/shard_map/dot_general | solution.py:562
  64.1 7.3 %collective-permute-done.11.refs_4_.refs_2_ = bf16[256,1024]{1,0:T(8,128)(2,1)S(1)} collective-permute-done((bf16[256,1024]{1,0:T(8,128)(2,1)S(1)}, bf16[256,1024]{1,0:T(8,128)(2,1)S(1)}, u32[]{:S(2)}, u32[]{:S(2)}) %collective-permute-start.11) | collective-permute-done | bytes 524320 | tf_op jit(solution)/shard_map/ppermute | solution.py:24
  78.2 9.1 %collective-permute-start.17 = (bf16[144,256]{1,0:T(8,128)(2,1)S(1)}, bf16[144,256]{1,0:T(8,128)(2,1)S(1)}, u32[]{:S(2)}, u32[]{:S(2)}) collective-permute-start(bf16[144,256]{1,0:T(8,128)(2,1)S(1)} %get-tuple-element.56.refs_0_), channel_id=1, source_target_pairs={{0,4},{4,8},{8,12},{12,0},{1,5},{5,9},{9,13},{13,1},{2,6},{6,10},{... | collective-permute-start | bytes 221192 | tf_op jit(solution)/shard_map/ppermute | solution.py:24
  89.4 2.9 %collective-permute-start.19 = (bf16[144,256]{1,0:T(8,128)(2,1)S(1)}, bf16[144,256]{1,0:T(8,128)(2,1)S(1)}, u32[]{:S(2)}, u32[]{:S(2)}) collective-permute-start(bf16[144,256]{1,0:T(8,128)(2,1)S(1)} %get-tuple-element.56.refs_0_), channel_id=1, source_target_pairs={{0,12},{4,0},{8,4},{12,8},{1,13},{5,1},{9,5},{13,9},{2,14},{6,2},{... | collective-permute-start | bytes 221192 | tf_op jit(solution)/shard_map/ppermute | solution.py:24
  98.7 2.8 %copy-done.1 = f32[12,16,64,128]{3,2,1,0:T(8,128)S(1)} copy-done((f32[12,16,64,128]{3,2,1,0:T(8,128)S(1)}, f32[12,16,64,128]{3,2,1,0:T(8,128)}, u32[]{:S(2)}) %copy-start.1) | copy-done | bytes 6291480
  101.5 3.4 %shard_map.133 = (bf16[256,1024]{1,0:T(8,128)(2,1)S(1)}, bf16[256,1024]{1,0:T(8,128)(2,1)S(1)}, bf16[256,1024]{1,0:T(8,128)(2,1)S(1)}, bf16[256,1024]{1,0:T(8,128)(2,1)S(1)}) custom-call(s32[12]{0:T(128)S(1)} %get-tuple-element.97.slot, s32[12]{0:T(128)S(1)} %get-tuple-element.96.member, bf16[144,256]{1,0:T(8,128)(2,1)S(1)} %get-tuple-element.56.refs_0_, ...), custom_call_target="tpu_custom_call" | custom-call | flops 1 | bytes 1 | tf_op jit(solution)/shard_map/pallas_call | solution.py:245
  105.0 4.6 %collective-permute-start.20 = (bf16[256,1024]{1,0:T(8,128)(2,1)S(1)}, bf16[256,1024]{1,0:T(8,128)(2,1)S(1)}, u32[]{:S(2)}, u32[]{:S(2)}) collective-permute-start(bf16[256,1024]{1,0:T(8,128)(2,1)S(1)} %get-tuple-element.58), channel_id=1, source_target_pairs={{0,4},{1,5},{2,6},{3,7},{16,20},{17,21},{18,22},{19,23}} | collective-permute-start | bytes 1572872 | tf_op jit(solution)/shard_map/ppermute | solution.py:28
  112.4 2.6 %collective-permute-done.29.refs_4_ = bf16[1216,256]{1,0:T(8,128)(2,1)S(1)} collective-permute-done((bf16[1216,256]{1,0:T(8,128)(2,1)S(1)}, bf16[1216,256]{1,0:T(8,128)(2,1)S(1)}, u32[]{:S(2)}, u32[]{:S(2)}) %collective-permute-start.29) | collective-permute-done | bytes 622624 | tf_op jit(solution)/shard_map/ppermute | solution.py:33
  116.3 5.8 %collective-permute-done.20 = bf16[256,1024]{1,0:T(8,128)(2,1)S(1)} collective-permute-done((bf16[256,1024]{1,0:T(8,128)(2,1)S(1)}, bf16[256,1024]{1,0:T(8,128)(2,1)S(1)}, u32[]{:S(2)}, u32[]{:S(2)}) %collective-permute-start.20) | collective-permute-done | bytes 524320 | tf_op jit(solution)/shard_map/ppermute | solution.py:28
  122.9 5.0 %collective-permute-start.21 = (bf16[256,1024]{1,0:T(8,128)(2,1)S(1)}, bf16[256,1024]{1,0:T(8,128)(2,1)S(1)}, u32[]{:S(2)}, u32[]{:S(2)}) collective-permute-start(bf16[256,1024]{1,0:T(8,128)(2,1)S(1)} %get-tuple-element.93), channel_id=1, source_target_pairs={{0,4},{4,8},{1,5},{5,9},{2,6},{6,10},{3,7},{7,11},{16,20},{20,24},... | collective-permute-start | bytes 1572872 | tf_op jit(solution)/shard_map/ppermute | solution.py:28
  128.7 3.2 %collective-permute-done.30.refs_5_ = bf16[1216,256]{1,0:T(8,128)(2,1)S(1)} collective-permute-done((bf16[1216,256]{1,0:T(8,128)(2,1)S(1)}, bf16[1216,256]{1,0:T(8,128)(2,1)S(1)}, u32[]{:S(2)}, u32[]{:S(2)}) %collective-permute-start.30) | collective-permute-done | bytes 622624 | tf_op jit(solution)/shard_map/ppermute | solution.py:33
  134.6 3.9 %collective-permute-done.21 = bf16[256,1024]{1,0:T(8,128)(2,1)S(1)} collective-permute-done((bf16[256,1024]{1,0:T(8,128)(2,1)S(1)}, bf16[256,1024]{1,0:T(8,128)(2,1)S(1)}, u32[]{:S(2)}, u32[]{:S(2)}) %collective-permute-start.21) | collective-permute-done | bytes 524320 | tf_op jit(solution)/shard_map/ppermute | solution.py:28
  138.7 9.3 %collective-permute-start.22 = (bf16[256,1024]{1,0:T(8,128)(2,1)S(1)}, bf16[256,1024]{1,0:T(8,128)(2,1)S(1)}, u32[]{:S(2)}, u32[]{:S(2)}) collective-permute-start(bf16[256,1024]{1,0:T(8,128)(2,1)S(1)} %add.185), channel_id=1, source_target_pairs={{0,4},{4,8},{8,12},{1,5},{5,9},{9,13},{2,6},{6,10},{10,14},{3,7},{... | collective-permute-start | bytes 1572872 | tf_op jit(solution)/shard_map/ppermute | solution.py:28
  149.8 9.1 %collective-permute-done.25.refs_2_ = bf16[256,1024]{1,0:T(8,128)(2,1)S(1)} collective-permute-done((bf16[256,1024]{1,0:T(8,128)(2,1)S(1)}, bf16[256,1024]{1,0:T(8,128)(2,1)S(1)}, u32[]{:S(2)}, u32[]{:S(2)}) %collective-permute-start.25) | collective-permute-done | bytes 524320 | tf_op jit(solution)/shard_map/ppermute | solution.py:33
  159.2 7.7 %collective-permute-start.33 = (bf16[256,1024]{1,0:T(8,128)(2,1)S(1)}, bf16[256,1024]{1,0:T(8,128)(2,1)S(1)}, u32[]{:S(2)}, u32[]{:S(2)}) collective-permute-start(bf16[256,1024]{1,0:T(8,128)(2,1)S(1)} %shard_map.134.refs_0_), channel_id=1, source_target_pairs={{0,8},{4,12},{8,0},{12,4},{1,9},{5,13},{9,1},{13,5},{2,10},{6,14},... | collective-permute-start | bytes 1572872 | tf_op jit(solution)/shard_map/ppermute | solution.py:24
  166.9 14.8 %collective-permute-done.33.refs_1_ = bf16[256,1024]{1,0:T(8,128)(2,1)S(1)} collective-permute-done((bf16[256,1024]{1,0:T(8,128)(2,1)S(1)}, bf16[256,1024]{1,0:T(8,128)(2,1)S(1)}, u32[]{:S(2)}, u32[]{:S(2)}) %collective-permute-start.33) | collective-permute-done | bytes 524320 | tf_op jit(solution)/shard_map/ppermute | solution.py:24
  181.7 2.2 shard_map.135
  183.9 2.1 collective-permute-start.32
  188.9 5.8 %shard_map.136 = (f32[12,16,64,128]{3,2,1,0:T(8,128)}, s32[8,128]{1,0:T(8,128)S(1)}) custom-call(s32[12]{0:T(128)S(1)} %get-tuple-element.95.which, s32[12]{0:T(128)S(1)} %get-tuple-element.94.member, f32[12,16,64,128]{3,2,1,0:T(8,128)S(1)} %bitcast.13, bf16[1216,256]{1,0:T(8,128)(2,1)S(1)} %get-tuple-element.61.refs_0_, ...), custom_call_target="tpu_custom_call" | custom-call | flops 1 | bytes 1 | tf_op jit(solution)/shard_map/pallas_call | solution.py:389
  194.6 2.2 collective-permute-done.35.refs_0_
  203.8 4.7 %collective-permute-done.37.refs_0_ = bf16[64,1280]{1,0:T(8,128)(2,1)S(1)} collective-permute-done((bf16[64,1280]{1,0:T(8,128)(2,1)S(1)}, bf16[64,1280]{1,0:T(8,128)(2,1)S(1)}, u32[]{:S(2)}, u32[]{:S(2)}) %collective-permute-start.37) | collective-permute-done | bytes 163872 | tf_op jit(solution)/shard_map/ppermute | solution.py:64
  211.3 2.7 %collective-permute-start.39 = (bf16[64,1280]{1,0:T(8,128)(2,1)S(1)}, bf16[64,1280]{1,0:T(8,128)(2,1)S(1)}, u32[]{:S(2)}, u32[]{:S(2)}) collective-permute-start(bf16[64,1280]{1,0:T(8,128)(2,1)S(1)} %get-tuple-element.67.refs_2_), channel_id=1, source_target_pairs={{0,8},{4,12},{8,0},{12,4},{1,9},{5,13},{9,1},{13,5},{2,10},{6,14},... | collective-permute-start | bytes 491528 | tf_op jit(solution)/shard_map/ppermute | solution.py:24
  217.9 8.0 %collective-permute-done.39.refs_2_ = bf16[64,1280]{1,0:T(8,128)(2,1)S(1)} collective-permute-done((bf16[64,1280]{1,0:T(8,128)(2,1)S(1)}, bf16[64,1280]{1,0:T(8,128)(2,1)S(1)}, u32[]{:S(2)}, u32[]{:S(2)}) %collective-permute-start.39) | collective-permute-done | bytes 163872 | tf_op jit(solution)/shard_map/ppermute | solution.py:24
  226.1 5.6 %collective-permute-done.43 = bf16[64,1280]{1,0:T(8,128)(2,1)S(1)} collective-permute-done((bf16[64,1280]{1,0:T(8,128)(2,1)S(1)}, bf16[64,1280]{1,0:T(8,128)(2,1)S(1)}, u32[]{:S(2)}, u32[]{:S(2)}) %collective-permute-start.43) | collective-permute-done | bytes 163872 | tf_op jit(solution)/shard_map/ppermute | solution.py:24
  234.9 2.9 %collective-permute-done.44.refs_1_ = bf16[64,1280]{1,0:T(8,128)(2,1)S(1)} collective-permute-done((bf16[64,1280]{1,0:T(8,128)(2,1)S(1)}, bf16[64,1280]{1,0:T(8,128)(2,1)S(1)}, u32[]{:S(2)}, u32[]{:S(2)}) %collective-permute-start.44) | collective-permute-done | bytes 163872 | tf_op jit(solution)/shard_map/ppermute | solution.py:670
  (153 shorter events, 83.1 us)
Async XLA Ops:
  2.6 13.9 %collective-permute-start = (bf16[256,640]{1,0:T(8,128)(2,1)}, bf16[256,640]{1,0:T(8,128)(2,1)}, u32[]{:S(2)}, u32[]{:S(2)}) collective-permute-start(bf16[256,640]{1,0:T(8,128)(2,1)} %get-tuple-element.87.refs_1_), channel_id=1, source_target_pairs={{0,4},{4,8},{8,12},{12,0},{1,5},{5,9},{9,13},{13,1},{2,6},{6,10},{... | collective-permute-start | bytes 983048 | tf_op jit(solution)/shard_map/ppermute | solution.py:24
  6.4 26.0 %collective-permute-start.3 = (bf16[256,640]{1,0:T(8,128)(2,1)}, bf16[256,640]{1,0:T(8,128)(2,1)}, u32[]{:S(2)}, u32[]{:S(2)}) collective-permute-start(bf16[256,640]{1,0:T(8,128)(2,1)} %shard_map.124), channel_id=1, source_target_pairs={{0,12},{4,0},{8,4},{12,8},{1,13},{5,1},{9,5},{13,9},{2,14},{6,2},{... | collective-permute-start | bytes 983048 | tf_op jit(solution)/shard_map/ppermute | solution.py:24
  10.0 20.8 %collective-permute-start.5 = (bf16[128,640]{1,0:T(8,128)(2,1)}, bf16[128,640]{1,0:T(8,128)(2,1)}, u32[]{:S(2)}, u32[]{:S(2)}) collective-permute-start(bf16[128,640]{1,0:T(8,128)(2,1)} %dynamic_slice.19), channel_id=1, source_target_pairs={{0,8},{4,12},{8,0},{12,4},{1,9},{5,13},{9,1},{13,5},{2,10},{6,14},... | collective-permute-start | bytes 491528 | tf_op jit(solution)/shard_map/ppermute | solution.py:24
  22.6 27.3 %collective-permute-start.2 = (bf16[256,1024]{1,0:T(8,128)(2,1)}, bf16[256,1024]{1,0:T(8,128)(2,1)}, u32[]{:S(2)}, u32[]{:S(2)}) collective-permute-start(bf16[256,1024]{1,0:T(8,128)(2,1)} %shard_map.123), channel_id=1, source_target_pairs={{0,12},{4,0},{8,4},{12,8},{1,13},{5,1},{9,5},{13,9},{2,14},{6,2},{... | collective-permute-start | bytes 1572872 | tf_op jit(solution)/shard_map/ppermute | solution.py:24
  32.4 12.5 %collective-permute-start.7 = (bf16[128,640]{1,0:T(8,128)(2,1)}, bf16[128,640]{1,0:T(8,128)(2,1)}, u32[]{:S(2)}, u32[]{:S(2)}) collective-permute-start(bf16[128,640]{1,0:T(8,128)(2,1)} %collective-permute-done.5.refs_0_), channel_id=1, source_target_pairs={{0,1},{1,0},{2,3},{3,2},{4,5},{5,4},{6,7},{7,6},{8,9},{9,8},{10,11... | collective-permute-start | bytes 491528 | tf_op jit(solution)/shard_map/ppermute | solution.py:59
  37.2 7.8 %collective-permute-start.8 = (bf16[128,640]{1,0:T(8,128)(2,1)}, bf16[128,640]{1,0:T(8,128)(2,1)}, u32[]{:S(2)}, u32[]{:S(2)}) collective-permute-start(bf16[128,640]{1,0:T(8,128)(2,1)} %collective-permute-done.6.refs_1_), channel_id=1, source_target_pairs={{0,1},{1,0},{2,3},{3,2},{4,5},{5,4},{6,7},{7,6},{8,9},{9,8},{10,11... | collective-permute-start | bytes 491528 | tf_op jit(solution)/shard_map/ppermute | solution.py:59
  39.8 10.1 %collective-permute-start.10 = (bf16[256,128]{1,0:T(8,128)(2,1)S(1)}, bf16[256,128]{1,0:T(8,128)(2,1)S(1)}, u32[]{:S(2)}, u32[]{:S(2)}) collective-permute-start(bf16[256,128]{1,0:T(8,128)(2,1)S(1)} %get-tuple-element.43), channel_id=1, source_target_pairs={{0,4},{4,8},{8,12},{12,0},{1,5},{5,9},{9,13},{13,1},{2,6},{6,10},{... | collective-permute-start | bytes 196616 | tf_op jit(solution)/shard_map/ppermute | solution.py:24
  41.8 8.1 %collective-permute-start.9 = (bf16[256,128]{1,0:T(8,128)(2,1)S(1)}, bf16[256,128]{1,0:T(8,128)(2,1)S(1)}, u32[]{:S(2)}, u32[]{:S(2)}) collective-permute-start(bf16[256,128]{1,0:T(8,128)(2,1)S(1)} %get-tuple-element.42), channel_id=1, source_target_pairs={{0,12},{4,0},{8,4},{12,8},{1,13},{5,1},{9,5},{13,9},{2,14},{6,2},{... | collective-permute-start | bytes 196616 | tf_op jit(solution)/shard_map/ppermute | solution.py:24
  54.6 16.8 %collective-permute-start.11 = (bf16[256,1024]{1,0:T(8,128)(2,1)S(1)}, bf16[256,1024]{1,0:T(8,128)(2,1)S(1)}, u32[]{:S(2)}, u32[]{:S(2)}) collective-permute-start(bf16[256,1024]{1,0:T(8,128)(2,1)S(1)} %shard_map.127), channel_id=1, source_target_pairs={{0,4},{4,8},{8,12},{12,0},{1,5},{5,9},{9,13},{13,1},{2,6},{6,10},{... | collective-permute-start | bytes 1572872 | tf_op jit(solution)/shard_map/ppermute | solution.py:24
  59.3 34.0 %collective-permute-start.13 = (bf16[256,1024]{1,0:T(8,128)(2,1)}, bf16[256,1024]{1,0:T(8,128)(2,1)}, u32[]{:S(2)}, u32[]{:S(2)}) collective-permute-start(bf16[256,1024]{1,0:T(8,128)(2,1)} %shard_map.128.refs_5_), channel_id=1, source_target_pairs={{0,8},{4,12},{8,0},{12,4},{1,9},{5,13},{9,1},{13,5},{2,10},{6,14},... | collective-permute-start | bytes 1572872 | tf_op jit(solution)/shard_map/ppermute | solution.py:24
  78.2 20.5 %collective-permute-start.17 = (bf16[144,256]{1,0:T(8,128)(2,1)S(1)}, bf16[144,256]{1,0:T(8,128)(2,1)S(1)}, u32[]{:S(2)}, u32[]{:S(2)}) collective-permute-start(bf16[144,256]{1,0:T(8,128)(2,1)S(1)} %get-tuple-element.56.refs_0_), channel_id=1, source_target_pairs={{0,4},{4,8},{8,12},{12,0},{1,5},{5,9},{9,13},{13,1},{2,6},{6,10},{... | collective-permute-start | bytes 221192 | tf_op jit(solution)/shard_map/ppermute | solution.py:24
  87.4 11.4 %collective-permute-start.18 = (bf16[144,256]{1,0:T(8,128)(2,1)S(1)}, bf16[144,256]{1,0:T(8,128)(2,1)S(1)}, u32[]{:S(2)}, u32[]{:S(2)}) collective-permute-start(bf16[144,256]{1,0:T(8,128)(2,1)S(1)} %get-tuple-element.56.refs_0_), channel_id=1, source_target_pairs={{0,8},{4,12},{8,0},{12,4},{1,9},{5,13},{9,1},{13,5},{2,10},{6,14},... | collective-permute-start | bytes 221192 | tf_op jit(solution)/shard_map/ppermute | solution.py:24
  89.4 9.4 %collective-permute-start.19 = (bf16[144,256]{1,0:T(8,128)(2,1)S(1)}, bf16[144,256]{1,0:T(8,128)(2,1)S(1)}, u32[]{:S(2)}, u32[]{:S(2)}) collective-permute-start(bf16[144,256]{1,0:T(8,128)(2,1)S(1)} %get-tuple-element.56.refs_0_), channel_id=1, source_target_pairs={{0,12},{4,0},{8,4},{12,8},{1,13},{5,1},{9,5},{13,9},{2,14},{6,2},{... | collective-permute-start | bytes 221192 | tf_op jit(solution)/shard_map/ppermute | solution.py:24
  96.0 15.7 %collective-permute-start.26 = (bf16[1216,256]{1,0:T(8,128)(2,1)S(1)}, bf16[1216,256]{1,0:T(8,128)(2,1)S(1)}, u32[]{:S(2)}, u32[]{:S(2)}) collective-permute-start(bf16[1216,256]{1,0:T(8,128)(2,1)S(1)} %get-tuple-element.61.refs_0_), channel_id=1, source_target_pairs={{0,4},{4,8},{8,12},{1,5},{5,9},{9,13},{2,6},{6,10},{10,14},{3,7},{... | collective-permute-start | bytes 1867784 | tf_op jit(solution)/shard_map/ppermute | solution.py:28
  97.4 17.7 %collective-permute-start.29 = (bf16[1216,256]{1,0:T(8,128)(2,1)S(1)}, bf16[1216,256]{1,0:T(8,128)(2,1)S(1)}, u32[]{:S(2)}, u32[]{:S(2)}) collective-permute-start(bf16[1216,256]{1,0:T(8,128)(2,1)S(1)} %get-tuple-element.61.refs_0_), channel_id=1, source_target_pairs={{12,8},{8,4},{4,0},{13,9},{9,5},{5,1},{14,10},{10,6},{6,2},{15,11}... | collective-permute-start | bytes 1867784 | tf_op jit(solution)/shard_map/ppermute | solution.py:33
  105.0 17.2 %collective-permute-start.20 = (bf16[256,1024]{1,0:T(8,128)(2,1)S(1)}, bf16[256,1024]{1,0:T(8,128)(2,1)S(1)}, u32[]{:S(2)}, u32[]{:S(2)}) collective-permute-start(bf16[256,1024]{1,0:T(8,128)(2,1)S(1)} %get-tuple-element.58), channel_id=1, source_target_pairs={{0,4},{1,5},{2,6},{3,7},{16,20},{17,21},{18,22},{19,23}} | collective-permute-start | bytes 1572872 | tf_op jit(solution)/shard_map/ppermute | solution.py:28
  109.5 12.6 %collective-permute-start.23 = (bf16[256,1024]{1,0:T(8,128)(2,1)S(1)}, bf16[256,1024]{1,0:T(8,128)(2,1)S(1)}, u32[]{:S(2)}, u32[]{:S(2)}) collective-permute-start(bf16[256,1024]{1,0:T(8,128)(2,1)S(1)} %get-tuple-element.60), channel_id=1, source_target_pairs={{12,8},{13,9},{14,10},{15,11},{28,24},{29,25},{30,26},{31,27}} | collective-permute-start | bytes 1572872 | tf_op jit(solution)/shard_map/ppermute | solution.py:33
  111.7 16.2 %collective-permute-start.27 = (bf16[1216,256]{1,0:T(8,128)(2,1)S(1)}, bf16[1216,256]{1,0:T(8,128)(2,1)S(1)}, u32[]{:S(2)}, u32[]{:S(2)}) collective-permute-start(bf16[1216,256]{1,0:T(8,128)(2,1)S(1)} %collective-permute-done.26.refs_1_), channel_id=1, source_target_pairs={{4,8},{8,12},{5,9},{9,13},{6,10},{10,14},{7,11},{11,15},{20,24},{2... | collective-permute-start | bytes 1867784 | tf_op jit(solution)/shard_map/ppermute | solution.py:28
  115.0 16.8 %collective-permute-start.30 = (bf16[1216,256]{1,0:T(8,128)(2,1)S(1)}, bf16[1216,256]{1,0:T(8,128)(2,1)S(1)}, u32[]{:S(2)}, u32[]{:S(2)}) collective-permute-start(bf16[1216,256]{1,0:T(8,128)(2,1)S(1)} %collective-permute-done.29.refs_4_), channel_id=1, source_target_pairs={{8,4},{4,0},{9,5},{5,1},{10,6},{6,2},{11,7},{7,3},{24,20},{20,16},... | collective-permute-start | bytes 1867784 | tf_op jit(solution)/shard_map/ppermute | solution.py:33
  122.2 10.9 %collective-permute-start.24 = (bf16[256,1024]{1,0:T(8,128)(2,1)S(1)}, bf16[256,1024]{1,0:T(8,128)(2,1)S(1)}, u32[]{:S(2)}, u32[]{:S(2)}) collective-permute-start(bf16[256,1024]{1,0:T(8,128)(2,1)S(1)} %get-tuple-element.92), channel_id=1, source_target_pairs={{12,8},{8,4},{13,9},{9,5},{14,10},{10,6},{15,11},{11,7},{28,24},{2... | collective-permute-start | bytes 1572872 | tf_op jit(solution)/shard_map/ppermute | solution.py:33
  122.9 15.6 %collective-permute-start.21 = (bf16[256,1024]{1,0:T(8,128)(2,1)S(1)}, bf16[256,1024]{1,0:T(8,128)(2,1)S(1)}, u32[]{:S(2)}, u32[]{:S(2)}) collective-permute-start(bf16[256,1024]{1,0:T(8,128)(2,1)S(1)} %get-tuple-element.93), channel_id=1, source_target_pairs={{0,4},{4,8},{1,5},{5,9},{2,6},{6,10},{3,7},{7,11},{16,20},{20,24},... | collective-permute-start | bytes 1572872 | tf_op jit(solution)/shard_map/ppermute | solution.py:28
  128.0 31.0 %collective-permute-start.28 = (bf16[1216,256]{1,0:T(8,128)(2,1)S(1)}, bf16[1216,256]{1,0:T(8,128)(2,1)S(1)}, u32[]{:S(2)}, u32[]{:S(2)}) collective-permute-start(bf16[1216,256]{1,0:T(8,128)(2,1)S(1)} %collective-permute-done.27.refs_2_), channel_id=1, source_target_pairs={{8,12},{9,13},{10,14},{11,15},{24,28},{25,29},{26,30},{27,31}} | collective-permute-start | bytes 1867784 | tf_op jit(solution)/shard_map/ppermute | solution.py:28
  131.8 27.1 %collective-permute-start.31 = (bf16[1216,256]{1,0:T(8,128)(2,1)S(1)}, bf16[1216,256]{1,0:T(8,128)(2,1)S(1)}, u32[]{:S(2)}, u32[]{:S(2)}) collective-permute-start(bf16[1216,256]{1,0:T(8,128)(2,1)S(1)} %collective-permute-done.30.refs_5_), channel_id=1, source_target_pairs={{4,0},{5,1},{6,2},{7,3},{20,16},{21,17},{22,18},{23,19}} | collective-permute-start | bytes 1867784 | tf_op jit(solution)/shard_map/ppermute | solution.py:33
  133.3 25.6 %collective-permute-start.25 = (bf16[256,1024]{1,0:T(8,128)(2,1)S(1)}, bf16[256,1024]{1,0:T(8,128)(2,1)S(1)}, u32[]{:S(2)}, u32[]{:S(2)}) collective-permute-start(bf16[256,1024]{1,0:T(8,128)(2,1)S(1)} %add.187), channel_id=1, source_target_pairs={{12,8},{8,4},{4,0},{13,9},{9,5},{5,1},{14,10},{10,6},{6,2},{15,11}... | collective-permute-start | bytes 1572872 | tf_op jit(solution)/shard_map/ppermute | solution.py:33
  138.7 20.2 %collective-permute-start.22 = (bf16[256,1024]{1,0:T(8,128)(2,1)S(1)}, bf16[256,1024]{1,0:T(8,128)(2,1)S(1)}, u32[]{:S(2)}, u32[]{:S(2)}) collective-permute-start(bf16[256,1024]{1,0:T(8,128)(2,1)S(1)} %add.185), channel_id=1, source_target_pairs={{0,4},{4,8},{8,12},{1,5},{5,9},{9,13},{2,6},{6,10},{10,14},{3,7},{... | collective-permute-start | bytes 1572872 | tf_op jit(solution)/shard_map/ppermute | solution.py:28
  159.2 22.5 %collective-permute-start.33 = (bf16[256,1024]{1,0:T(8,128)(2,1)S(1)}, bf16[256,1024]{1,0:T(8,128)(2,1)S(1)}, u32[]{:S(2)}, u32[]{:S(2)}) collective-permute-start(bf16[256,1024]{1,0:T(8,128)(2,1)S(1)} %shard_map.134.refs_0_), channel_id=1, source_target_pairs={{0,8},{4,12},{8,0},{12,4},{1,9},{5,13},{9,1},{13,5},{2,10},{6,14},... | collective-permute-start | bytes 1572872 | tf_op jit(solution)/shard_map/ppermute | solution.py:24
  183.9 14.5 %collective-permute-start.32 = (bf16[256,1024]{1,0:T(8,128)(2,1)S(1)}, bf16[256,1024]{1,0:T(8,128)(2,1)S(1)}, u32[]{:S(2)}, u32[]{:S(2)}) collective-permute-start(bf16[256,1024]{1,0:T(8,128)(2,1)S(1)} %shard_map.134.refs_0_), channel_id=1, source_target_pairs={{0,12},{4,0},{8,4},{12,8},{1,13},{5,1},{9,5},{13,9},{2,14},{6,2},{... | collective-permute-start | bytes 1572872 | tf_op jit(solution)/shard_map/ppermute | solution.py:24
  187.0 9.8 %collective-permute-start.35 = (bf16[128,1280]{1,0:T(8,128)(2,1)S(1)}, bf16[128,1280]{1,0:T(8,128)(2,1)S(1)}, u32[]{:S(2)}, u32[]{:S(2)}) collective-permute-start(bf16[128,1280]{1,0:T(8,128)(2,1)S(1)} %get-tuple-element.66), channel_id=1, source_target_pairs={{0,2},{1,3},{2,0},{3,1},{4,6},{5,7},{6,4},{7,5},{8,10},{9,11},{10,... | collective-permute-start | bytes 983048 | tf_op jit(solution)/shard_map/ppermute | solution.py:64
  188.8 21.1 %collective-permute-start.40 = (bf16[256,1024]{1,0:T(8,128)(2,1)S(1)}, bf16[256,1024]{1,0:T(8,128)(2,1)S(1)}, u32[]{:S(2)}, u32[]{:S(2)}) collective-permute-start(bf16[256,1024]{1,0:T(8,128)(2,1)S(1)} %shard_map.134.refs_0_), channel_id=1, source_target_pairs={{0,4},{4,8},{8,12},{12,0},{1,5},{5,9},{9,13},{13,1},{2,6},{6,10},{... | collective-permute-start | bytes 1572872 | tf_op jit(solution)/shard_map/ppermute | solution.py:24
  211.3 14.5 %collective-permute-start.39 = (bf16[64,1280]{1,0:T(8,128)(2,1)S(1)}, bf16[64,1280]{1,0:T(8,128)(2,1)S(1)}, u32[]{:S(2)}, u32[]{:S(2)}) collective-permute-start(bf16[64,1280]{1,0:T(8,128)(2,1)S(1)} %get-tuple-element.67.refs_2_), channel_id=1, source_target_pairs={{0,8},{4,12},{8,0},{12,4},{1,9},{5,13},{9,1},{13,5},{2,10},{6,14},... | collective-permute-start | bytes 491528 | tf_op jit(solution)/shard_map/ppermute | solution.py:24
  214.1 11.8 %collective-permute-start.38 = (bf16[64,1280]{1,0:T(8,128)(2,1)S(1)}, bf16[64,1280]{1,0:T(8,128)(2,1)S(1)}, u32[]{:S(2)}, u32[]{:S(2)}) collective-permute-start(bf16[64,1280]{1,0:T(8,128)(2,1)S(1)} %shard_map.141.refs_1_), channel_id=1, source_target_pairs={{0,4},{4,8},{8,12},{12,0},{1,5},{5,9},{9,13},{13,1},{2,6},{6,10},{... | collective-permute-start | bytes 491528 | tf_op jit(solution)/shard_map/ppermute | solution.py:24
  216.3 9.6 %collective-permute-start.42 = (bf16[64,1280]{1,0:T(8,128)(2,1)S(1)}, bf16[64,1280]{1,0:T(8,128)(2,1)S(1)}, u32[]{:S(2)}, u32[]{:S(2)}) collective-permute-start(bf16[64,1280]{1,0:T(8,128)(2,1)S(1)} %get-tuple-element.75), channel_id=1, source_target_pairs={{0,2},{1,3},{2,0},{3,1},{4,6},{5,7},{6,4},{7,5},{8,10},{9,11},{10,... | collective-permute-start | bytes 491528 | tf_op jit(solution)/shard_map/ppermute | solution.py:64
  (33 other events, 349.1 us)
